TPU v7x, 32 devices: a whole 2x2x4 slice. The times are simulated.
32 devices in a mesh: hil: 8 (over z, x), vec: 4 (over y, core).
Axes of the slice: x: 2, y: 2, z: 4, core: 2. Of those that a mesh axis runs over, the one named last changes fastest.
Arguments:
- start_block: float32 [1024, 64, 1024], P('hil', 'vec'), may hold values from -10800 to 10800
- down_matrix: float32 [1024, 1024], replicated, may hold values from -1 to 1, as said below
- hop_partner: int32 [10, 1024], replicated, may hold values from 0 to 1023, as said below
- hop_sign: int32 [10, 1024], replicated, may hold values from -1 to 1
- bond_hop: float32 [10], replicated, may hold values from 0.3 to 1
- onsite_u: float32 [10], replicated, may hold values from 0.5 to 2
Outputs:
- filtered_vectors: float32 [1024, 64, 1024], P('hil', 'vec')
Inputs may be any that keep to these rules, and one draw needn't show every extreme that they name: down_matrix is symmetric. For every b and u: hop_partner[b, hop_partner[b, u]] = u, hop_sign[b, hop_partner[b, u]] = hop_sign[b, u], and hop_partner[b, u] = u wherever hop_sign[b, u] = 0.
All inputs are finite; a program needn't handle non-finite values.
Results may differ from a plain program's by a relative error of at most 0.0002.
Values sent between devices are 32-bit elements; how exact they have to be, the bound alone decides.
No kernel may reach another device: no remote copies, remote signals or barrier semaphores. Data moves between devices by JAX's collectives and lax.ppermute only.
A program may use at most 192 MiB of HBM per device.

v0:
```python
import math

import jax
import jax.numpy as jnp
from jax import lax
from jax.sharding import PartitionSpec as P

SITES = 10
NU = 1024
ND = 1024
DEGREE = 2
NS_ITERS = 4


highest = lax.Precision.HIGHEST
center_shift = 6.0
half_range = 12.0


def site_bits(states):
    shifts = jnp.arange(SITES, dtype=jnp.int32)
    return jnp.bitwise_and(jnp.right_shift(states[:, None], shifts[None, :]), 1).astype(jnp.float32)


def split_down(local_block):
    hil_parts = lax.axis_size("hil")
    up_local, vec_local, down_count = local_block.shape
    down_local = down_count // hil_parts
    arranged = local_block.reshape(up_local, vec_local, hil_parts, down_local).transpose(2, 0, 1, 3)
    arranged = arranged.reshape(hil_parts, up_local, vec_local * down_local)
    received = lax.all_to_all(arranged, "hil", split_axis=0, concat_axis=1, tiled=True)
    return received.reshape(hil_parts * up_local, vec_local * down_local)


def split_up(spread, up_local, vec_local):
    hil_parts = lax.axis_size("hil")
    total_up, columns = spread.shape
    down_local = columns // vec_local
    received = lax.all_to_all(
        spread.reshape(1, total_up, columns), "hil", split_axis=1, concat_axis=0, tiled=True
    )
    arranged = received.reshape(hil_parts, up_local, vec_local, down_local).transpose(1, 2, 0, 3)
    return arranged.reshape(up_local, vec_local, hil_parts * down_local)


def to_panel_cut(block):
    return lax.all_to_all(block, "vec", split_axis=2, concat_axis=1, tiled=True)


def up_hops(spread, hop_coef, hop_partner):
    result = hop_coef[0][:, None] * jnp.take(spread, hop_partner[0], axis=0)
    for bond_index in range(1, hop_partner.shape[0]):
        result = result + hop_coef[bond_index][:, None] * jnp.take(
            spread, hop_partner[bond_index], axis=0
        )
    return result


def down_part(local_block, down_matrix, interaction):
    up_local, vec_local, down_count = local_block.shape
    flat_rows = local_block.reshape(up_local * vec_local, down_count)
    mixed = lax.dot_general(
        flat_rows,
        down_matrix,
        (((1,), (1,)), ((), ())),
        precision=highest,
        preferred_element_type=jnp.float32,
    )
    return mixed.reshape(local_block.shape) + interaction[:, None, :] * local_block


def advance(applied, present, earlier, degree_step):
    if degree_step == 0:
        return (applied - center_shift * present) / half_range
    return 2.0 * (applied - center_shift * present) / half_range - earlier


def gram_of(row_panel):
    return jnp.einsum("ukd,uld->kl", row_panel, row_panel, precision=highest)


def rotate(row_panel, mixing):
    return jnp.einsum("ukd,kl->uld", row_panel, mixing, precision=highest)


def frobenius_scale(gram_sum):
    return 1.0 / jnp.sqrt(jnp.sqrt(jnp.sum(gram_sum * gram_sum)) + 1e-06)


def on_device(start_block, down_matrix, hop_partner, hop_sign, bond_hop, onsite_u):
    up_local, vec_local, down_count = start_block.shape
    hop_coef = -bond_hop[:, None] * hop_sign.astype(jnp.float32)
    current = start_block
    local_states = lax.axis_index("hil") * up_local + jnp.arange(up_local, dtype=jnp.int32)
    interaction = jnp.dot(
        site_bits(local_states) * onsite_u[None, :],
        site_bits(jnp.arange(down_count, dtype=jnp.int32)).T,
        precision=highest,
        preferred_element_type=jnp.float32,
    )
    current_cut = split_down(current)
    previous = current
    previous_cut = current_cut
    for degree_step in range(DEGREE):
        local_part = down_part(current, down_matrix, interaction)
        hopped = up_hops(current_cut, hop_coef, hop_partner)
        applied = local_part + split_up(hopped, up_local, vec_local)
        following = advance(applied, current, previous, degree_step)
        if degree_step + 1 < DEGREE:
            applied_cut = split_down(local_part) + hopped
            following_cut = advance(applied_cut, current_cut, previous_cut, degree_step)
            previous_cut, current_cut = (current_cut, following_cut)
        previous, current = (current, following)
    row_panel = to_panel_cut(current)
    identity = jnp.eye(row_panel.shape[1], dtype=jnp.float32)
    gram_sum = lax.psum(gram_of(row_panel), ("hil", "vec"))
    norm_scale = frobenius_scale(gram_sum)
    gram_sum = norm_scale * norm_scale * gram_sum
    product_total = identity
    for newton_step in range(NS_ITERS):
        mixing = 1.5 * identity - 0.5 * gram_sum
        product_total = jnp.dot(
            product_total, mixing, precision=highest, preferred_element_type=jnp.float32
        )
        gram_sum = jnp.dot(
            mixing,
            jnp.dot(gram_sum, mixing, precision=highest, preferred_element_type=jnp.float32),
            precision=highest,
            preferred_element_type=jnp.float32,
        )
    row_panel = rotate(row_panel, norm_scale * product_total)
    current = lax.all_to_all(row_panel, "vec", split_axis=1, concat_axis=2, tiled=True)
    return current * math.sqrt(NU * ND)


def solution(mesh):
    in_specs = (P("hil", "vec", None), P(), P(), P(), P(), P())
    out_specs = P("hil", "vec", None)
    return jax.shard_map(
        on_device, mesh=mesh, in_specs=in_specs, out_specs=out_specs, check_vma=False
    )
```

profile of v0, /device:TPU:0, one launch (start us, length us, event | category | flops | bytes accessed | tf_op | source)
XLA Modules:
  0.0 1205.9 jit_solution(2733694062459211588)
XLA Ops:
  30.3 40.0 %multiply_add_fusion = f32[128,16,1024]{2,0,1:T(8,128)S(1)} fusion(f32[128,16,1024]{2,1,0:T(8,128)} %param.8, f32[128,1024]{1,0:T(8,128)S(1)} %get-tuple-element.29, f32[1024,1024]{1,0:T(8,128)} %param.9), kind=kOutput, calls=%fused_computation.69 | convolution fusion | flops 25773998080 | bytes 21495808 | tf_op jit(solution)/shard_map/dot_general | solution.py:62
  85.7 126.1 %all-to-all-done = f32[8,128,2048]{2,1,0:T(8,128)} async-done(((f32[8,128,2048]{2,1,0:T(8,128)}), f32[8,128,2048]{2,1,0:T(8,128)}, u32[]{:S(2)}, u32[]{:S(2)}) %all-to-all-start) | async-done | bytes 8388640 | tf_op jit(solution)/shard_map/all_to_all | solution.py:31
  222.2 12.4 %gather_fusion.9 = f32[1024,2048]{1,0:T(8,128)} fusion(f32[1024,2048]{1,0:T(8,128)} %bitcast.4, s32[1024]{0:T(1024)S(1)} %fusion.103), kind=kCustom, calls=%fused_computation.9.clone | custom fusion | bytes 16781312 | tf_op jit(solution)/shard_map/jit(_take)/gather | solution.py:53
  234.6 12.3 %gather_fusion.8 = f32[1024,2048]{1,0:T(8,128)} fusion(f32[1024,2048]{1,0:T(8,128)} %bitcast.4, s32[1024]{0:T(1024)S(1)} %fusion.102), kind=kCustom, calls=%fused_computation.8.clone | custom fusion | bytes 16781312 | tf_op jit(solution)/shard_map/jit(_take)/gather | solution.py:53
  247.0 12.4 %gather_fusion.7 = f32[1024,2048]{1,0:T(8,128)} fusion(f32[1024,2048]{1,0:T(8,128)} %bitcast.4, s32[1024]{0:T(1024)S(1)} %fusion.101), kind=kCustom, calls=%fused_computation.7.clone | custom fusion | bytes 16781312 | tf_op jit(solution)/shard_map/jit(_take)/gather | solution.py:53
  259.3 12.4 %gather_fusion.6 = f32[1024,2048]{1,0:T(8,128)} fusion(f32[1024,2048]{1,0:T(8,128)} %bitcast.4, s32[1024]{0:T(1024)S(1)} %fusion.100), kind=kCustom, calls=%fused_computation.6.clone | custom fusion | bytes 16781312 | tf_op jit(solution)/shard_map/jit(_take)/gather | solution.py:53
  271.7 12.4 %gather_fusion.5 = f32[1024,2048]{1,0:T(8,128)} fusion(f32[1024,2048]{1,0:T(8,128)} %bitcast.4, s32[1024]{0:T(1024)S(1)} %fusion.99), kind=kCustom, calls=%fused_computation.5.clone | custom fusion | bytes 16781312 | tf_op jit(solution)/shard_map/jit(_take)/gather | solution.py:53
  284.1 12.4 %gather_fusion.4 = f32[1024,2048]{1,0:T(8,128)} fusion(f32[1024,2048]{1,0:T(8,128)} %bitcast.4, s32[1024]{0:T(1024)S(1)} %fusion.98), kind=kCustom, calls=%fused_computation.4.clone | custom fusion | bytes 16781312 | tf_op jit(solution)/shard_map/jit(_take)/gather | solution.py:53
  296.5 12.4 %gather_fusion.3 = f32[1024,2048]{1,0:T(8,128)} fusion(f32[1024,2048]{1,0:T(8,128)} %bitcast.4, s32[1024]{0:T(1024)S(1)} %fusion.97), kind=kCustom, calls=%fused_computation.3.clone | custom fusion | bytes 16781312 | tf_op jit(solution)/shard_map/jit(_take)/gather | solution.py:53
  308.9 12.4 %gather_fusion.2 = f32[1024,2048]{1,0:T(8,128)} fusion(f32[1024,2048]{1,0:T(8,128)} %bitcast.4, s32[1024]{0:T(1024)S(1)} %fusion.96), kind=kCustom, calls=%fused_computation.2.clone | custom fusion | bytes 16781312 | tf_op jit(solution)/shard_map/jit(_take)/gather | solution.py:53
  321.3 12.4 %gather_fusion.1 = f32[1024,2048]{1,0:T(8,128)} fusion(f32[1024,2048]{1,0:T(8,128)} %bitcast.4, s32[1024]{0:T(1024)S(1)} %copy-done.26), kind=kCustom, calls=%fused_computation.1.clone | custom fusion | bytes 16781312 | tf_op jit(solution)/shard_map/jit(_take)/gather | solution.py:53
  333.7 12.4 %gather_fusion = f32[1024,2048]{1,0:T(8,128)} fusion(f32[1024,2048]{1,0:T(8,128)} %bitcast.4, s32[1024]{0:T(1024)S(1)} %copy-done.24), kind=kCustom, calls=%fused_computation.clone | custom fusion | bytes 16781312 | tf_op jit(solution)/shard_map/jit(_take)/gather | solution.py:51
  346.3 53.0 %all-to-all-done.2 = f32[8,128,2048]{1,2,0:T(8,128)} async-done(((f32[8,128,2048]{1,2,0:T(8,128)}), f32[8,128,2048]{1,2,0:T(8,128)}, u32[]{:S(2)}, u32[]{:S(2)}) %all-to-all-start.2) | async-done | bytes 8388640 | tf_op jit(solution)/shard_map/all_to_all | solution.py:31
  408.5 36.9 %fusion.1 = (f32[1024,2048]{1,0:T(8,128)}, f32[1024,2048]{1,0:T(8,128)}) fusion(f32[8,128,2048]{2,1,0:T(8,128)} %copy.53, f32[8,128,2048]{2,1,0:T(8,128)} %all-to-all-done, f32[1024,2048]{1,0:T(8,128)} %gather_fusion.9, pred[1024]{0:T(1024)(128)(4,1)S(1)} %copy-done.61, f32[1024]{0:T(1024)S(1)} %bitcast.115, f32[1024,2048]{1,0:T(8,128)} %gather_fusion.8, ...), kind=kLoop, calls=%fused_computation.23 | loop fusion | flops 69206016 | bytes 117491712 | tf_op jit(solution)/shard_map/div | solution.py:74
  461.7 12.2 %gather_fusion.19 = f32[1024,2048]{1,0:T(8,128)} fusion(f32[1024,2048]{1,0:T(8,128)} %get-tuple-element.6, s32[1024]{0:T(1024)S(1)} %copy-done.43), kind=kCustom, calls=%fused_computation.19.clone | custom fusion | bytes 16781312 | tf_op jit(solution)/shard_map/jit(_take)/gather | solution.py:53
  474.0 12.4 %gather_fusion.18 = f32[1024,2048]{1,0:T(8,128)} fusion(f32[1024,2048]{1,0:T(8,128)} %get-tuple-element.6, s32[1024]{0:T(1024)S(1)} %copy-done.41), kind=kCustom, calls=%fused_computation.18.clone | custom fusion | bytes 16781312 | tf_op jit(solution)/shard_map/jit(_take)/gather | solution.py:53
  486.4 12.4 %gather_fusion.17 = f32[1024,2048]{1,0:T(8,128)} fusion(f32[1024,2048]{1,0:T(8,128)} %get-tuple-element.6, s32[1024]{0:T(1024)S(1)} %copy-done.37), kind=kCustom, calls=%fused_computation.17.clone | custom fusion | bytes 16781312 | tf_op jit(solution)/shard_map/jit(_take)/gather | solution.py:53
  498.7 12.4 %gather_fusion.16 = f32[1024,2048]{1,0:T(8,128)} fusion(f32[1024,2048]{1,0:T(8,128)} %get-tuple-element.6, s32[1024]{0:T(1024)S(1)} %copy-done.31), kind=kCustom, calls=%fused_computation.16.clone | custom fusion | bytes 16781312 | tf_op jit(solution)/shard_map/jit(_take)/gather | solution.py:53
  511.1 12.4 %gather_fusion.15 = f32[1024,2048]{1,0:T(8,128)} fusion(f32[1024,2048]{1,0:T(8,128)} %get-tuple-element.6, s32[1024]{0:T(1024)S(1)} %copy-done.39), kind=kCustom, calls=%fused_computation.15.clone | custom fusion | bytes 16781312 | tf_op jit(solution)/shard_map/jit(_take)/gather | solution.py:53
  523.5 12.4 %gather_fusion.14 = f32[1024,2048]{1,0:T(8,128)} fusion(f32[1024,2048]{1,0:T(8,128)} %get-tuple-element.6, s32[1024]{0:T(1024)S(1)} %copy-done.33), kind=kCustom, calls=%fused_computation.14.clone | custom fusion | bytes 16781312 | tf_op jit(solution)/shard_map/jit(_take)/gather | solution.py:53
  535.9 12.4 %gather_fusion.13 = f32[1024,2048]{1,0:T(8,128)} fusion(f32[1024,2048]{1,0:T(8,128)} %get-tuple-element.6, s32[1024]{0:T(1024)S(1)} %copy-done.35), kind=kCustom, calls=%fused_computation.13.clone | custom fusion | bytes 16781312 | tf_op jit(solution)/shard_map/jit(_take)/gather | solution.py:53
  548.3 12.4 %gather_fusion.12 = f32[1024,2048]{1,0:T(8,128)} fusion(f32[1024,2048]{1,0:T(8,128)} %get-tuple-element.6, s32[1024]{0:T(1024)S(1)} %copy-done.29), kind=kCustom, calls=%fused_computation.12.clone | custom fusion | bytes 16781312 | tf_op jit(solution)/shard_map/jit(_take)/gather | solution.py:53
  560.7 12.4 %gather_fusion.11 = f32[1024,2048]{1,0:T(8,128)} fusion(f32[1024,2048]{1,0:T(8,128)} %get-tuple-element.6, s32[1024]{0:T(1024)S(1)} %copy-done.27), kind=kCustom, calls=%fused_computation.11.clone | custom fusion | bytes 16781312 | tf_op jit(solution)/shard_map/jit(_take)/gather | solution.py:53
  573.3 12.4 %gather_fusion.10 = f32[1024,2048]{1,0:T(8,128)} fusion(f32[1024,2048]{1,0:T(8,128)} %get-tuple-element.6, s32[1024]{0:T(1024)S(1)} %copy-done.25), kind=kCustom, calls=%fused_computation.10.clone | custom fusion | bytes 16781312 | tf_op jit(solution)/shard_map/jit(_take)/gather | solution.py:51
  585.9 31.3 %fusion.3 = f32[1,1024,2048]{2,1,0:T(8,128)} fusion(f32[1024,2048]{1,0:T(8,128)} %gather_fusion.19, f32[1024,2048]{1,0:T(8,128)} %gather_fusion.18, f32[1024,2048]{1,0:T(8,128)} %gather_fusion.17, f32[1024,2048]{1,0:T(8,128)} %gather_fusion.16, f32[1024,2048]{1,0:T(8,128)} %gather_fusion.15, f32[1024,2048]{1,0:T(8,128)} %gather_fusion.14, ...), kind=kLoop, calls=%fused_computation.28 | loop fusion | flops 60817408 | bytes 92325888 | tf_op jit(solution)/shard_map/reshape | solution.py:40
  628.1 15.7 %all-to-all-done.1 = f32[1,1024,2048]{2,0,1:T(1,128)} async-done(((f32[1,1024,2048]{2,0,1:T(1,128)}), f32[1,1024,2048]{2,0,1:T(1,128)}, u32[]{:S(2)}, u32[]{:S(2)}) %all-to-all-start.1) | async-done | bytes 8388640 | tf_op jit(solution)/shard_map/all_to_all | solution.py:39
  669.6 161.3 %all-to-all-done.3 = f32[1,1024,2048]{2,0,1:T(1,128)} async-done(((f32[1,1024,2048]{2,0,1:T(1,128)}), f32[1,1024,2048]{2,0,1:T(1,128)}, u32[]{:S(2)}, u32[]{:S(2)}) %all-to-all-start.3) | async-done | bytes 8388640 | tf_op jit(solution)/shard_map/all_to_all | solution.py:39
  852.0 46.6 %multiply_subtract_fusion = f32[128,16,1024]{2,0,1:T(8,128)} fusion(f32[128,16,1024]{2,0,1:T(8,128)} %reshape.98, f32[128,16,1024]{2,1,0:T(8,128)} %param.8, f32[128,1024]{1,0:T(8,128)S(1)} %copy-done.2, f32[1024,1024]{1,0:T(8,128)} %param.9, f32[128,16,1024]{2,0,1:T(8,128)} %copy-done.1, f32[128,16,1024]{2,0,1:T(8,128)} %reshape.92), kind=kOutput, calls=%fused_computation.65 | convolution fusion | flops 25799163904 | bytes 46661632 | tf_op jit(solution)/shard_map/dot_general | solution.py:62
  907.8 97.6 %all_to_all.63 = f32[128,16,1024]{0,1,2:T(8,128)S(1)} all-to-all(f32[128,16,1024]{0,1,2:T(8,128)} %copy.57), channel_id=1, replica_groups=mesh['hil'=8,'vec'=4] {'vec'}, dimensions={2} | all-to-all | bytes 16777216 | tf_op jit(solution)/shard_map/all_to_all | solution.py:47
  1026.1 38.2 %psum.7 = f32[64,64]{1,0:T(8,128)S(1)} all-reduce(f32[64,64]{1,0:T(8,128)S(1)} %convolution_bitcast_fusion.1), channel_id=1, replica_groups=mesh['hil'=8,'vec'=4] {'hil','vec'}, use_global_device_ids=true, to_apply=%region_0.0 | all-reduce | flops 4096 | bytes 32768 | tf_op jit(solution)/shard_map/psum | solution.py:116
  1082.1 96.7 %all_to_all.64 = f32[128,64,256]{2,0,1:T(8,128)S(1)} all-to-all(f32[128,64,256]{2,0,1:T(8,128)S(1)} %copy.61), channel_id=1, replica_groups=mesh['hil'=8,'vec'=4] {'vec'}, dimensions={1} | all-to-all | bytes 16777216 | tf_op jit(solution)/shard_map/all_to_all | solution.py:132
  1182.8 12.1 %copy.62 = f32[128,16,4,256]{3,2,1,0:T(4,128)} copy(f32[128,16,4,256]{3,0,1,2:T(8,128)} %bitcast.108) | data formatting | bytes 16777216 | tf_op jit(solution)/shard_map/mul | solution.py:133
  (191 shorter events, 200.8 us)
Async XLA Ops:
  20.7 191.1 %all-to-all-start = ((f32[8,128,2048]{2,1,0:T(8,128)}), f32[8,128,2048]{2,1,0:T(8,128)}, u32[]{:S(2)}, u32[]{:S(2)}) async-start(f32[8,128,2048]{2,1,0:T(8,128)} %reshape.88), calls=%async_computation | async-start | bytes 16777216 | tf_op jit(solution)/shard_map/all_to_all | solution.py:31
  211.8 187.4 %all-to-all-start.2 = ((f32[8,128,2048]{1,2,0:T(8,128)}), f32[8,128,2048]{1,2,0:T(8,128)}, u32[]{:S(2)}, u32[]{:S(2)}) async-start(f32[8,128,2048]{1,2,0:T(8,128)} %bitcast.104), calls=%async_computation.2 | async-start | bytes 16777216 | tf_op jit(solution)/shard_map/all_to_all | solution.py:31
  217.1 42.2 %copy-start.30 = (s32[1024]{0:T(1024)}, s32[1024]{0:T(1024)S(1)}, u32[]{:S(2)}) copy-start(s32[1024]{0:T(1024)S(1)} %fusion.100) | copy-start | bytes 12292
  217.2 29.8 %copy-start.36 = (s32[1024]{0:T(1024)}, s32[1024]{0:T(1024)S(1)}, u32[]{:S(2)}) copy-start(s32[1024]{0:T(1024)S(1)} %fusion.101) | copy-start | bytes 12292
  218.4 65.7 %copy-start.32 = (s32[1024]{0:T(1024)}, s32[1024]{0:T(1024)S(1)}, u32[]{:S(2)}) copy-start(s32[1024]{0:T(1024)S(1)} %fusion.98) | copy-start | bytes 12292
  218.4 53.3 %copy-start.38 = (s32[1024]{0:T(1024)}, s32[1024]{0:T(1024)S(1)}, u32[]{:S(2)}) copy-start(s32[1024]{0:T(1024)S(1)} %fusion.99) | copy-start | bytes 12292
  218.4 90.5 %copy-start.28 = (s32[1024]{0:T(1024)}, s32[1024]{0:T(1024)S(1)}, u32[]{:S(2)}) copy-start(s32[1024]{0:T(1024)S(1)} %fusion.96) | copy-start | bytes 12292
  218.4 78.0 %copy-start.34 = (s32[1024]{0:T(1024)}, s32[1024]{0:T(1024)S(1)}, u32[]{:S(2)}) copy-start(s32[1024]{0:T(1024)S(1)} %fusion.97) | copy-start | bytes 12292
  218.5 16.2 %copy-start.40 = (s32[1024]{0:T(1024)}, s32[1024]{0:T(1024)S(1)}, u32[]{:S(2)}) copy-start(s32[1024]{0:T(1024)S(1)} %fusion.102) | copy-start | bytes 12292
  218.5 16.1 %copy-start.42 = (s32[1024]{0:T(1024)}, s32[1024]{0:T(1024)S(1)}, u32[]{:S(2)}) copy-start(s32[1024]{0:T(1024)S(1)} %fusion.103) | copy-start | bytes 12292
  346.1 62.3 %copy-start.4 = (f32[1,1024]{1,0:T(1,128)S(1)}, f32[1,1024]{1,0:T(1,128)}, u32[]{:S(2)}) copy-start(f32[1,1024]{1,0:T(1,128)} %get-tuple-element.8) | copy-start | bytes 12292
  346.1 62.3 %copy-start.6 = (f32[1,1024]{1,0:T(1,128)S(1)}, f32[1,1024]{1,0:T(1,128)}, u32[]{:S(2)}) copy-start(f32[1,1024]{1,0:T(1,128)} %get-tuple-element.9) | copy-start | bytes 12292
  346.1 62.3 %copy-start.8 = (f32[1,1024]{1,0:T(1,128)S(1)}, f32[1,1024]{1,0:T(1,128)}, u32[]{:S(2)}) copy-start(f32[1,1024]{1,0:T(1,128)} %get-tuple-element.10) | copy-start | bytes 12292
  346.1 62.3 %copy-start.10 = (f32[1,1024]{1,0:T(1,128)S(1)}, f32[1,1024]{1,0:T(1,128)}, u32[]{:S(2)}) copy-start(f32[1,1024]{1,0:T(1,128)} %get-tuple-element.11) | copy-start | bytes 12292
  346.1 62.3 %copy-start.12 = (f32[1,1024]{1,0:T(1,128)S(1)}, f32[1,1024]{1,0:T(1,128)}, u32[]{:S(2)}) copy-start(f32[1,1024]{1,0:T(1,128)} %get-tuple-element.12) | copy-start | bytes 12292
  346.1 62.3 %copy-start.14 = (f32[1,1024]{1,0:T(1,128)S(1)}, f32[1,1024]{1,0:T(1,128)}, u32[]{:S(2)}) copy-start(f32[1,1024]{1,0:T(1,128)} %get-tuple-element.13) | copy-start | bytes 12292
  346.1 62.3 %copy-start.16 = (f32[1,1024]{1,0:T(1,128)S(1)}, f32[1,1024]{1,0:T(1,128)}, u32[]{:S(2)}) copy-start(f32[1,1024]{1,0:T(1,128)} %get-tuple-element.14) | copy-start | bytes 12292
  346.1 62.3 %copy-start.18 = (f32[1,1024]{1,0:T(1,128)S(1)}, f32[1,1024]{1,0:T(1,128)}, u32[]{:S(2)}) copy-start(f32[1,1024]{1,0:T(1,128)} %get-tuple-element.15) | copy-start | bytes 12292
  346.1 62.3 %copy-start.20 = (f32[1,1024]{1,0:T(1,128)S(1)}, f32[1,1024]{1,0:T(1,128)}, u32[]{:S(2)}) copy-start(f32[1,1024]{1,0:T(1,128)} %get-tuple-element.16) | copy-start | bytes 12292
  346.2 62.3 %copy-start.22 = (f32[1,1024]{1,0:T(1,128)S(1)}, f32[1,1024]{1,0:T(1,128)}, u32[]{:S(2)}) copy-start(f32[1,1024]{1,0:T(1,128)} %get-tuple-element.17) | copy-start | bytes 12292
  346.2 62.3 %copy-start.45 = (pred[1024]{0:T(1024)(128)(4,1)S(1)}, pred[1024]{0:T(1024)(128)(4,1)}, u32[]{:S(2)}) copy-start(pred[1024]{0:T(1024)(128)(4,1)} %get-tuple-element.32) | copy-start | bytes 3076
  346.2 62.3 %copy-start.47 = (pred[1024]{0:T(1024)(128)(4,1)S(1)}, pred[1024]{0:T(1024)(128)(4,1)}, u32[]{:S(2)}) copy-start(pred[1024]{0:T(1024)(128)(4,1)} %get-tuple-element.33) | copy-start | bytes 3076
  346.2 62.3 %copy-start.49 = (pred[1024]{0:T(1024)(128)(4,1)S(1)}, pred[1024]{0:T(1024)(128)(4,1)}, u32[]{:S(2)}) copy-start(pred[1024]{0:T(1024)(128)(4,1)} %get-tuple-element.38) | copy-start | bytes 3076
  346.2 62.3 %copy-start.51 = (pred[1024]{0:T(1024)(128)(4,1)S(1)}, pred[1024]{0:T(1024)(128)(4,1)}, u32[]{:S(2)}) copy-start(pred[1024]{0:T(1024)(128)(4,1)} %get-tuple-element.39) | copy-start | bytes 3076
  346.2 62.3 %copy-start.53 = (pred[1024]{0:T(1024)(128)(4,1)S(1)}, pred[1024]{0:T(1024)(128)(4,1)}, u32[]{:S(2)}) copy-start(pred[1024]{0:T(1024)(128)(4,1)} %get-tuple-element.34) | copy-start | bytes 3076
  346.2 62.3 %copy-start.55 = (pred[1024]{0:T(1024)(128)(4,1)S(1)}, pred[1024]{0:T(1024)(128)(4,1)}, u32[]{:S(2)}) copy-start(pred[1024]{0:T(1024)(128)(4,1)} %get-tuple-element.35) | copy-start | bytes 3076
  346.2 62.3 %copy-start.57 = (pred[1024]{0:T(1024)(128)(4,1)S(1)}, pred[1024]{0:T(1024)(128)(4,1)}, u32[]{:S(2)}) copy-start(pred[1024]{0:T(1024)(128)(4,1)} %get-tuple-element.36) | copy-start | bytes 3076
  346.2 62.3 %copy-start.59 = (pred[1024]{0:T(1024)(128)(4,1)S(1)}, pred[1024]{0:T(1024)(128)(4,1)}, u32[]{:S(2)}) copy-start(pred[1024]{0:T(1024)(128)(4,1)} %get-tuple-element.37) | copy-start | bytes 3076
  346.2 62.3 %copy-start.61 = (pred[1024]{0:T(1024)(128)(4,1)S(1)}, pred[1024]{0:T(1024)(128)(4,1)}, u32[]{:S(2)}) copy-start(pred[1024]{0:T(1024)(128)(4,1)} %get-tuple-element.30) | copy-start | bytes 3076
  346.3 62.3 %copy-start.63 = (pred[1024]{0:T(1024)(128)(4,1)S(1)}, pred[1024]{0:T(1024)(128)(4,1)}, u32[]{:S(2)}) copy-start(pred[1024]{0:T(1024)(128)(4,1)} %get-tuple-element.31) | copy-start | bytes 3076
  456.8 187.0 %all-to-all-start.1 = ((f32[1,1024,2048]{2,0,1:T(1,128)}), f32[1,1024,2048]{2,0,1:T(1,128)}, u32[]{:S(2)}, u32[]{:S(2)}) async-start(f32[1,1024,2048]{2,0,1:T(1,128)} %copy.49), calls=%async_computation.1 | async-start | bytes 16777216 | tf_op jit(solution)/shard_map/all_to_all | solution.py:39
  643.7 187.2 %all-to-all-start.3 = ((f32[1,1024,2048]{2,0,1:T(1,128)}), f32[1,1024,2048]{2,0,1:T(1,128)}, u32[]{:S(2)}, u32[]{:S(2)}) async-start(f32[1,1024,2048]{2,0,1:T(1,128)} %copy.54), calls=%async_computation.3 | async-start | bytes 16777216 | tf_op jit(solution)/shard_map/all_to_all | solution.py:39
  (39 other events, 439.5 us)
where the time goes:
time: 1210 us
  local copies, waits for them, and re-layouts  409 us (34%)
  waiting for transfers between devices  356 us (29%)
  blocking collectives  232 us (19%)
  matrix products  106 us (9%)
  other arithmetic  77.2 us (6%)
  starting transfers between devices  23.1 us (2%)
    gather x18, local copies, waits for them, and re-layouts, up_hops(): jnp.take(spread, hop_partner[bond_index], axis=0)  223 us
    all_to_all x2, waiting for transfers between devices, split_down(): lax.all_to_all(arranged, 'hil', split_axis=0, concat_axis=1, tiled=True)  179 us
    all_to_all x2, waiting for transfers between devices, split_up(): lax.all_to_all(spread.reshape(1, total_up, columns), 'hil', split_axis=1,...  177 us
    all_to_all x1, blocking collectives, to_panel_cut(): return lax.all_to_all(block, 'vec', split_axis=2, concat_axis=1, tiled=True)  97.6 us
    all_to_all x1, blocking collectives, on_device(): lax.all_to_all(row_panel, 'vec', split_axis=1, concat_axis=2, tiled=True)  96.7 us
    dot_general x2, matrix products, down_part(): lax.dot_general(flat_rows, down_matrix, (((1,), (1,)), ((), ())), precisi...  86.6 us
    psum x1, blocking collectives, on_device(): gram_sum = lax.psum(gram_of(row_panel), ('hil', 'vec'))  38.2 us
    div x1, other arithmetic, advance(): return (applied - center_shift * present) / half_range  36.9 us
  transfers between devices with their start and end apart: 4, of which 4 were waited for; matrix products, arithmetic and copies ran while one was open for 31% of the time, Pallas kernels for 0%

commit v1 on v0

v1 whole, which is shorter than its diff:
```python
import functools
import math

import jax
import jax.numpy as jnp
from jax import lax
from jax.experimental import pallas as pl
from jax.experimental.pallas import tpu as pltpu
from jax.sharding import PartitionSpec as P

DEGREE = 2
NS_ITERS = 4
STACK = 4

highest = lax.Precision.HIGHEST
high = lax.Precision.HIGH
center_shift = 6.0
half_range = 12.0


def site_bits(states, sites):
    shifts = jnp.arange(sites, dtype=jnp.int32)
    return jnp.bitwise_and(jnp.right_shift(states[:, None], shifts[None, :]), 1).astype(jnp.float32)


def hop_matrix(hop_coef, hop_partner):
    up_count = hop_partner.shape[1]
    columns = jnp.arange(up_count, dtype=jnp.int32)
    total = jnp.zeros((up_count, up_count), jnp.float32)
    for bond in range(hop_partner.shape[0]):
        total = total + jnp.where(hop_partner[bond][:, None] == columns[None, :], hop_coef[bond][:, None], 0.0)
    return total


def dot(left, right, contract, precision):
    return lax.dot_general(
        left, right, ((contract[:1], contract[1:]), ((), ())), precision=precision, preferred_element_type=jnp.float32
    )


def filter_vector(vector, down_matrix, up_matrix, diagonal, cuts):
    previous, current = vector, vector
    for degree_step in range(DEGREE):
        last = degree_step + 1 == DEGREE
        width = current.shape[1] // (cuts if last else 1)
        pieces = []
        for cut in range(cuts if last else 1):
            columns = slice(cut * width, (cut + 1) * width)
            applied = dot(current, down_matrix[columns], (1, 1), high)
            applied = applied + dot(up_matrix, current[:, columns], (1, 0), high)
            applied = applied + diagonal[:, columns] * current[:, columns]
            if degree_step == 0:
                pieces.append(applied / half_range)
            else:
                pieces.append(2.0 * applied / half_range - previous[:, columns])
        if last:
            return pieces
        previous, current = current, pieces[0]


def spread_step(held, step):
    pairs = [(i, i ^ step) for i in range(lax.axis_size("vec"))]
    return [lax.ppermute(piece, "vec", pairs) for piece in held]


def split(values):
    top = values.astype(jnp.bfloat16)
    return top, (values - top.astype(jnp.float32)).astype(jnp.bfloat16)


def stacked(refs, first, count):
    return jnp.concatenate([ref[first + u] for u in range(count) for ref in refs], axis=0)


def gram_kernel(groups, start_ref, *refs):
    inputs, (top_ref, cross_ref) = refs[:-2], refs[-2:]

    @pl.when(pl.program_id(0) == 0)
    def _():
        top_ref[...] = jnp.zeros_like(top_ref)
        cross_ref[...] = jnp.zeros_like(cross_ref)

    per_group = len(inputs) // groups
    rows = inputs[0].shape[0]
    for first in range(0, rows, STACK):
        for group in range(groups):
            top, low = split(stacked(inputs[group * per_group : (group + 1) * per_group], first, STACK))
            top_ref[...] += dot(top, top, (1, 1), None)
            cross_ref[...] += dot(top, low, (1, 1), None)


def rotate_kernel(groups, mix_ref, *refs):
    inputs, out_ref = refs[:-1], refs[-1]
    per_group = len(inputs) // groups
    rows, width = inputs[0].shape[0], inputs[0].shape[2]
    mix_top, mix_low = split(mix_ref[...])
    count = mix_top.shape[0]
    both = jnp.concatenate([mix_top, mix_low], axis=0)
    for first in range(0, rows, STACK):
        for group in range(groups):
            top, low = split(stacked(inputs[group * per_group : (group + 1) * per_group], first, STACK))
            wide = dot(both, top, (1, 0), None)
            result = wide[:count] + wide[count:] + dot(mix_top, low, (1, 0), None)
            out_ref[first : first + STACK, :, group * width : (group + 1) * width] = result.reshape(
                STACK, count // STACK, width
            )


def gram_partial(groups, start, row_count):
    flat = [array for group in groups for array in group]
    vectors = sum(array.shape[1] for array in groups[0])
    block = min(row_count, 8)
    specs = [pl.BlockSpec((block,) + array.shape[1:], lambda i, first: (first[0] + i, 0, 0)) for array in flat]
    size = STACK * vectors
    out = jax.ShapeDtypeStruct((size, size), jnp.float32)
    top, cross = pl.pallas_call(
        functools.partial(gram_kernel, len(groups)),
        out_shape=(out, out),
        grid_spec=pltpu.PrefetchScalarGridSpec(
            num_scalar_prefetch=1,
            grid=(row_count // block,),
            in_specs=specs,
            out_specs=[pl.BlockSpec((size, size), lambda i, first: (0, 0))] * 2,
        ),
        compiler_params=pltpu.CompilerParams(vmem_limit_bytes=48 * 1024 * 1024),
    )((start * (row_count // block)).reshape(1).astype(jnp.int32), *flat)
    cross = cross + cross.T
    total = (top + cross).reshape(STACK, vectors, STACK, vectors)
    return sum(total[u, :, u, :] for u in range(STACK))


def rotate(groups, mixing, up_local, down_count):
    flat = [array for group in groups for array in group]
    block = 8
    specs = [pl.BlockSpec((block,) + array.shape[1:], lambda i: (i, 0, 0)) for array in flat]
    own = mixing.shape[1]
    wide_mixing = jnp.kron(jnp.eye(STACK, dtype=jnp.float32), mixing.T)
    return pl.pallas_call(
        functools.partial(rotate_kernel, len(groups)),
        out_shape=jax.ShapeDtypeStruct((up_local, own, down_count), jnp.float32),
        grid=(up_local // block,),
        in_specs=[pl.BlockSpec(wide_mixing.shape, lambda i: (0, 0))] + specs,
        out_specs=pl.BlockSpec((block, own, down_count), lambda i: (i, 0, 0)),
        compiler_params=pltpu.CompilerParams(vmem_limit_bytes=48 * 1024 * 1024),
    )(wide_mixing, *flat)


def newton_schulz(gram_sum):
    identity = jnp.eye(gram_sum.shape[0], dtype=jnp.float32)
    norm_scale = 1.0 / jnp.sqrt(jnp.sqrt(jnp.sum(gram_sum * gram_sum)) + 1e-06)
    gram_sum = norm_scale * norm_scale * gram_sum
    product_total = identity
    for _ in range(NS_ITERS):
        mixing = 1.5 * identity - 0.5 * gram_sum
        product_total = dot(product_total, mixing, (1, 0), highest)
        gram_sum = dot(mixing, dot(gram_sum, mixing, (1, 0), highest), (1, 0), highest)
    return norm_scale * product_total


def vector_cut(start_block, down_matrix, hop_coef, hop_partner, onsite_u):
    hil_parts, vec_parts = lax.axis_size("hil"), lax.axis_size("vec")
    up_local, vec_local, down_count = start_block.shape
    up_count = up_local * hil_parts
    rounds = vec_local // hil_parts
    cuts = 2
    arrived = []
    for turn in range(rounds):
        block = start_block[:, turn * hil_parts : (turn + 1) * hil_parts].transpose(1, 0, 2)
        arrived.append(lax.all_to_all(block, "hil", split_axis=0, concat_axis=0, tiled=True))
    up_matrix = hop_matrix(hop_coef, hop_partner)
    sites = onsite_u.shape[0]
    diagonal = -center_shift + jnp.dot(
        site_bits(jnp.arange(up_count, dtype=jnp.int32), sites) * onsite_u[None, :],
        site_bits(jnp.arange(down_count, dtype=jnp.int32), sites).T,
        precision=highest,
        preferred_element_type=jnp.float32,
    )
    sent = []
    for turn in range(rounds):
        vector = arrived[turn].reshape(up_count, down_count)
        for piece in filter_vector(vector, down_matrix, up_matrix, diagonal, cuts):
            piece = piece.reshape(hil_parts, up_local, down_count // cuts)
            now = len(sent)
            for stage, earlier in enumerate(range(now - 2, -1, -1)):
                if stage < len(sent[earlier]) - 1:
                    piece, sent[earlier][stage + 1] = lax.optimization_barrier((piece, sent[earlier][stage + 1]))
            back = lax.all_to_all(piece, "hil", split_axis=0, concat_axis=0, tiled=True)
            sent.append([[back.transpose(1, 0, 2)]])
            step = vec_parts // 2
            while step >= 1:
                sent[now].append(spread_step([p for stage in sent[now] for p in stage], step))
                step //= 2
    groups = [[] for _ in range(cuts)]
    distances = [0]
    step = vec_parts // 2
    while step >= 1:
        distances += [distance ^ step for distance in distances]
        step //= 2
    for number, stages in enumerate(sent):
        held = [piece for stage in stages for piece in stage]
        groups[number % cuts].extend(held[distances.index(distance)] for distance in range(vec_parts))
    own = lax.axis_index("vec")
    near = jnp.bitwise_xor(jnp.arange(vec_parts, dtype=jnp.int32), own)
    exchange = (near[:, None] == jnp.arange(vec_parts, dtype=jnp.int32)[None, :]).astype(jnp.float32)
    order = jnp.kron(jnp.eye(rounds, dtype=jnp.float32), jnp.kron(exchange, jnp.eye(hil_parts, dtype=jnp.float32)))
    partial = gram_partial(groups, own, up_local // vec_parts)
    partial = dot(order, dot(partial, order, (1, 0), highest), (0, 0), highest)
    mixing = newton_schulz(lax.psum(partial, ("hil", "vec")))
    mixing = dot(dot(order, mixing, (1, 0), highest), order, (1, 1), highest)
    mixing = mixing.reshape(-1, rounds, vec_parts, hil_parts)[:, :, 0].reshape(-1, vec_local)
    return rotate(groups, mixing * math.sqrt(up_count * down_count), up_local, down_count)


def split_down(local_block):
    hil_parts = lax.axis_size("hil")
    up_local, vec_local, down_count = local_block.shape
    down_local = down_count // hil_parts
    arranged = local_block.reshape(up_local, vec_local, hil_parts, down_local).transpose(2, 0, 1, 3)
    arranged = arranged.reshape(hil_parts, up_local, vec_local * down_local)
    received = lax.all_to_all(arranged, "hil", split_axis=0, concat_axis=1, tiled=True)
    return received.reshape(hil_parts * up_local, vec_local * down_local)


def split_up(spread, up_local, vec_local):
    hil_parts = lax.axis_size("hil")
    total_up, columns = spread.shape
    down_local = columns // vec_local
    received = lax.all_to_all(
        spread.reshape(1, total_up, columns), "hil", split_axis=1, concat_axis=0, tiled=True
    )
    arranged = received.reshape(hil_parts, up_local, vec_local, down_local).transpose(1, 2, 0, 3)
    return arranged.reshape(up_local, vec_local, hil_parts * down_local)


def advance(applied, present, earlier, degree_step):
    if degree_step == 0:
        return (applied - center_shift * present) / half_range
    return 2.0 * (applied - center_shift * present) / half_range - earlier


def down_cut(start_block, down_matrix, hop_coef, hop_partner, onsite_u):
    up_local, vec_local, down_count = start_block.shape
    up_matrix = hop_matrix(hop_coef, hop_partner)
    sites = onsite_u.shape[0]
    local_states = lax.axis_index("hil") * up_local + jnp.arange(up_local, dtype=jnp.int32)
    interaction = jnp.dot(
        site_bits(local_states, sites) * onsite_u[None, :],
        site_bits(jnp.arange(down_count, dtype=jnp.int32), sites).T,
        precision=highest,
        preferred_element_type=jnp.float32,
    )
    current = previous = start_block
    current_cut = previous_cut = split_down(current)
    for degree_step in range(DEGREE):
        local_part = dot(current.reshape(up_local * vec_local, down_count), down_matrix, (1, 1), high)
        local_part = local_part.reshape(current.shape) + interaction[:, None, :] * current
        hopped = dot(up_matrix, current_cut, (1, 0), high)
        applied = local_part + split_up(hopped, up_local, vec_local)
        following = advance(applied, current, previous, degree_step)
        if degree_step + 1 < DEGREE:
            applied_cut = split_down(local_part) + hopped
            following_cut = advance(applied_cut, current_cut, previous_cut, degree_step)
            previous_cut, current_cut = current_cut, following_cut
        previous, current = current, following
    row_panel = lax.all_to_all(current, "vec", split_axis=2, concat_axis=1, tiled=True)
    gram_sum = lax.psum(jnp.einsum("ukd,uld->kl", row_panel, row_panel, precision=highest), ("hil", "vec"))
    mixing = newton_schulz(gram_sum) * math.sqrt(up_matrix.shape[0] * down_count)
    row_panel = jnp.einsum("ukd,kl->uld", row_panel, mixing, precision=highest)
    return lax.all_to_all(row_panel, "vec", split_axis=1, concat_axis=2, tiled=True)


def on_device(start_block, down_matrix, hop_partner, hop_sign, bond_hop, onsite_u):
    hil_parts, vec_parts = lax.axis_size("hil"), lax.axis_size("vec")
    up_local, vec_local, _ = start_block.shape
    hop_coef = -bond_hop[:, None] * hop_sign.astype(jnp.float32)
    whole_vectors = vec_local % hil_parts == 0 and vec_parts & (vec_parts - 1) == 0
    plan = vector_cut if whole_vectors and up_local % (8 * vec_parts) == 0 else down_cut
    return plan(start_block, down_matrix, hop_coef, hop_partner, onsite_u)


def solution(mesh):
    in_specs = (P("hil", "vec", None), P(), P(), P(), P(), P())
    out_specs = P("hil", "vec", None)
    return jax.shard_map(
        on_device, mesh=mesh, in_specs=in_specs, out_specs=out_specs, check_vma=False
    )
```

time: 1210 us -> 573 us (0.47)
  local copies, waits for them, and re-layouts: 409 us -> 39 us
  blocking collectives: 232 us -> 41 us
  other arithmetic: 77.2 us -> 1.23 us
  waiting for transfers between devices: 356 us -> 295 us
  Pallas kernels: 0 us -> 26.1 us
  starting transfers between devices: 23.1 us -> 40.2 us
  matrix products: 106 us -> 122 us
    gather x20 -> x0, local copies, waits for them, and re-layouts: 248 us -> none  [the longest x18 223 us: up_hops(): jnp.take(spread, hop_partner[bond_index], axis=0)]
    all_to_all x2 -> x0, blocking collectives: 194 us -> none  [the longest x1 97.6 us: to_panel_cut(): return lax.all_to_all(block, 'vec', split_axis=2, concat_axis=1, tiled=True)]
    all_to_all x4 -> x6, waiting for transfers between devices: 356 us -> 204 us  [the longest x2 133 us: vector_cut(): lax.all_to_all(block, 'hil', split_axis=0, concat_axis=0, tiled=True)]
    ppermute x0 -> x12, waiting for transfers between devices: none -> 91.6 us  [spread_step(): return [lax.ppermute(piece, 'vec', pairs) for piece in held]]
    reshape x8 -> x1, local copies, waits for them, and re-layouts: 82.6 us -> 0.23 us  [gram_partial(): total = (top + cross).reshape(STACK, vectors, STACK, vectors)]
    div x1 -> x0, other arithmetic: 36.9 us -> none  [advance(): return (applied - center_shift * present) / half_range]
    reshape x1 -> x0, other arithmetic: 31.3 us -> none  [split_up(): spread.reshape(1, total_up, columns)]
    pallas_call x0 -> x2, Pallas kernels: none -> 26.1 us  [the longest x1 20.2 us: rotate(): pl.pallas_call(functools.partial(rotate_kernel, len(groups)), out_shape=j...]
  transfers between devices with their start and end apart: 4 -> 18, of which waited for: 4 -> 9; matrix products, arithmetic and copies ran while one was open for 31% -> 25% of each run, Pallas kernels for 0% -> 0%
where the time goes in v1:
time: 573 us; the launch traced here: 567 us
  waiting for transfers between devices  295 us (51%)
  matrix products  122 us (21%)
  blocking collectives  41 us (7%)
  starting transfers between devices  40.2 us (7%)
  local copies, waits for them, and re-layouts  39 us (7%)
  Pallas kernels  26.1 us (5%)
    all_to_all x2, waiting for transfers between devices, vector_cut(): lax.all_to_all(block, 'hil', split_axis=0, concat_axis=0, tiled=True)  133 us
    dot_general x25, matrix products, dot(): lax.dot_general(left, right, ((contract[:1], contract[1:]), ((), ())), pr...  118 us
    ppermute x12, waiting for transfers between devices, spread_step(): return [lax.ppermute(piece, 'vec', pairs) for piece in held]  91.6 us
    all_to_all x4, waiting for transfers between devices, vector_cut(): back = lax.all_to_all(piece, 'hil', split_axis=0, concat_axis=0, tiled=True)  71.1 us
    psum x1, blocking collectives, vector_cut(): mixing = newton_schulz(lax.psum(partial, ('hil', 'vec')))  41 us
    all_to_all x4, starting transfers between devices, vector_cut(): back = lax.all_to_all(piece, 'hil', split_axis=0, concat_axis=0, tiled=True)  20.7 us
    pallas_call x1, Pallas kernels, rotate(): pl.pallas_call(functools.partial(rotate_kernel, len(groups)), out_shape=j...  20.2 us
    unnamed x46, local copies, waits for them, and re-layouts  17 us
  transfers between devices with their start and end apart: 18, of which 9 were waited for; matrix products, arithmetic and copies ran while one was open for 25% of the time, Pallas kernels for 0%

profile of v1, /device:TPU:0, one launch (start us, length us, event | category | flops | bytes accessed | tf_op | source)
XLA Modules:
  0.0 566.7 jit_solution(12936003179106119033)
XLA Ops:
  0.0 6.7 %fusion.110 = (f32[128,8,1024]{2,1,0:T(8,128)}, f32[128,8,1024]{2,1,0:T(8,128)S(1)}) fusion(f32[128,16,1024]{2,1,0:T(8,128)} %param.6), kind=kLoop, calls=%fused_computation.148 | loop fusion | bytes 16777216 | tf_op jit(solution)/shard_map/slice | solution.py:168
  6.7 4.4 copy.34
  11.1 7.3 %all-to-all-start = ((f32[8,128,1024]{2,1,0:T(8,128)}), f32[8,128,1024]{2,1,0:T(8,128)}, u32[]{:S(2)}, u32[]{:S(2)}) async-start(f32[8,128,1024]{2,1,0:T(8,128)} %bitcast.93), calls=%async_computation | async-start | bytes 8388608 | tf_op jit(solution)/shard_map/all_to_all | solution.py:169
  18.4 6.6 %copy.33 = f32[128,8,1024]{2,0,1:T(8,128)} copy(f32[128,8,1024]{2,1,0:T(8,128)} %get-tuple-element.23) | data formatting | bytes 8388608
  25.0 86.6 %all-to-all-done = f32[8,128,1024]{2,1,0:T(8,128)} async-done(((f32[8,128,1024]{2,1,0:T(8,128)}), f32[8,128,1024]{2,1,0:T(8,128)}, u32[]{:S(2)}, u32[]{:S(2)}) %all-to-all-start) | async-done | bytes 4194336 | tf_op jit(solution)/shard_map/all_to_all | solution.py:169
  111.7 5.0 all-to-all-start.2
  120.5 10.5 %fusion.113 = f32[1024,1024]{1,0:T(8,128)S(1)} fusion(f32[1024,1024]{1,0:T(8,128)} %bitcast.2, f32[1024,1024]{1,0:T(8,128)S(1)} %copy-done.8), kind=kOutput, calls=%fused_computation.151 | convolution fusion | flops 6442450944 | bytes 12582912 | tf_op jit(solution)/shard_map/dot_general | solution.py:36
  131.0 17.4 %add_multiply_fusion.1 = f32[1024,1024]{1,0:T(8,128)S(1)} fusion(f32[1024,1024]{1,0:T(8,128)S(1)} %convolution_add_fusion, f32[1024,1024]{1,0:T(8,128)} %bitcast.2, f32[1024,1024]{1,0:T(8,128)S(1)} %fusion.113, f32[1024]{0:T(1024)S(1)} %bitcast.163, s32[1024]{0:T(1024)S(1)} %bitcast.145, f32[1024]{0:T(1024)S(1)} %bitcast.169, s32[1024]{0:T(1024)S(1)} %bitcast.151, ...), kind=kOutput, calls=%fused_computation.3 | convolution fusion | flops 6477053952 | bytes 16859136 | tf_op jit(solution)/shard_map/dot_general | solution.py:36
  148.4 8.3 %fusion.6 = f32[1024,512]{1,0:T(8,128)S(1)} fusion(f32[1024,1024]{1,0:T(8,128)S(1)} %add_multiply_fusion.1, f32[1024]{0:T(1024)S(1)} %bitcast.164, s32[1024]{0:T(1024)S(1)} %bitcast.146, f32[1024]{0:T(1024)S(1)} %bitcast.170, s32[1024]{0:T(1024)S(1)} %bitcast.152, f32[1024]{0:T(1024)S(1)} %bitcast.176, s32[1024]{0:T(1024)S(1)} %bitcast.104, ...), kind=kOutput, calls=%fused_computation.30 | convolution fusion | flops 3251634176 | bytes 4276224 | tf_op jit(solution)/shard_map/dot_general | solution.py:36
  156.7 6.5 %slice_subtract_fusion.3 = f32[1024,512]{1,0:T(8,128)} fusion(f32[1024,1024]{1,0:T(8,128)} %bitcast.2, f32[1024,512]{1,0:T(8,128)S(1)} %fusion.6, f32[1024,1024]{1,0:T(8,128)S(1)} %convolution_add_fusion, f32[1024,1024]{1,0:T(8,128)S(1)} %add_multiply_fusion.1, f32[1024,1024]{1,0:T(8,128)S(1)} %copy-done.8), kind=kOutput, calls=%fused_computation.19 | convolution fusion | flops 3223846912 | bytes 16777216 | tf_op jit(solution)/shard_map/dot_general | solution.py:36
  163.2 46.0 %all-to-all-done.2 = f32[8,128,1024]{2,1,0:T(8,128)} async-done(((f32[8,128,1024]{2,1,0:T(8,128)}), f32[8,128,1024]{2,1,0:T(8,128)}, u32[]{:S(2)}, u32[]{:S(2)}) %all-to-all-start.2) | async-done | bytes 4194336 | tf_op jit(solution)/shard_map/all_to_all | solution.py:169
  213.1 10.0 %fusion.2 = f32[1024,512]{1,0:T(8,128)S(1)} fusion(f32[1024,1024]{1,0:T(8,128)} %copy-done.14, f32[1024]{0:T(1024)S(1)} %bitcast.165, s32[1024]{0:T(1024)S(1)} %bitcast.147, f32[1024]{0:T(1024)S(1)} %bitcast.171, s32[1024]{0:T(1024)S(1)} %bitcast.153, f32[1024]{0:T(1024)S(1)} %bitcast.177, s32[1024]{0:T(1024)S(1)} %bitcast.105, f32[1024]{0:T(1024)S(1)} %bitcast.183, ...), kind=kOutput, calls=%fused_computation.26 | convolution fusion | flops 3251634176 | bytes 4276224 | tf_op jit(solution)/shard_map/dot_general | solution.py:36
  223.2 6.5 %slice_subtract_fusion.1 = f32[1024,512]{1,0:T(8,128)} fusion(f32[1024,1024]{1,0:T(8,128)} %bitcast.2, f32[1024,512]{1,0:T(8,128)S(1)} %fusion.2, f32[1024,1024]{1,0:T(8,128)S(1)} %copy-done.15, f32[1024,1024]{1,0:T(8,128)S(1)} %copy-done.4, f32[1024,1024]{1,0:T(8,128)S(1)} %copy-done.9), kind=kOutput, calls=%fused_computation.17 | convolution fusion | flops 3223846912 | bytes 16777216 | tf_op jit(solution)/shard_map/dot_general | solution.py:36
  229.7 31.8 %all-to-all-done.1 = f32[8,128,512]{2,1,0:T(8,128)S(1)} async-done(((f32[8,128,512]{2,1,0:T(8,128)}), f32[8,128,512]{2,1,0:T(8,128)S(1)}, u32[]{:S(2)}, u32[]{:S(2)}) %all-to-all-start.1) | async-done | bytes 2097184 | tf_op jit(solution)/shard_map/all_to_all | solution.py:187
  261.5 4.8 all-to-all-start.3
  266.3 10.5 %fusion.114 = f32[1024,1024]{1,0:T(8,128)S(1)} fusion(f32[1024,1024]{1,0:T(8,128)} %bitcast.26, f32[1024,1024]{1,0:T(8,128)} %param.7), kind=kOutput, calls=%fused_computation.152 | convolution fusion | flops 6442450944 | bytes 12582912 | tf_op jit(solution)/shard_map/dot_general | solution.py:36
  281.3 16.9 %add_multiply_fusion = f32[1024,1024]{1,0:T(8,128)S(1)} fusion(f32[1024,1024]{1,0:T(8,128)S(1)} %copy-done.5, f32[1024,1024]{1,0:T(8,128)} %bitcast.26, f32[1024,1024]{1,0:T(8,128)S(1)} %fusion.114, f32[1024]{0:T(1024)S(1)} %bitcast.166, s32[1024]{0:T(1024)S(1)} %bitcast.148, f32[1024]{0:T(1024)S(1)} %bitcast.172, s32[1024]{0:T(1024)S(1)} %bitcast.154, ...), kind=kOutput, calls=%fused_computation.2 | convolution fusion | flops 6477053952 | bytes 16859136 | tf_op jit(solution)/shard_map/dot_general | solution.py:36
  298.3 8.3 %fusion = f32[1024,512]{1,0:T(8,128)S(1)} fusion(f32[1024,1024]{1,0:T(8,128)S(1)} %add_multiply_fusion, f32[1024]{0:T(1024)S(1)} %bitcast.167, s32[1024]{0:T(1024)S(1)} %bitcast.149, f32[1024]{0:T(1024)S(1)} %bitcast.173, s32[1024]{0:T(1024)S(1)} %bitcast.155, f32[1024]{0:T(1024)S(1)} %bitcast.179, s32[1024]{0:T(1024)S(1)} %bitcast.107, ...), kind=kOutput, calls=%fused_computation.24 | convolution fusion | flops 3251634176 | bytes 4276224 | tf_op jit(solution)/shard_map/dot_general | solution.py:36
  306.6 6.5 %slice_subtract_fusion = f32[1024,512]{1,0:T(8,128)} fusion(f32[1024,1024]{1,0:T(8,128)} %bitcast.26, f32[1024,512]{1,0:T(8,128)S(1)} %fusion, f32[1024,1024]{1,0:T(8,128)S(1)} %add_multiply_fusion, f32[1024,1024]{1,0:T(8,128)S(1)} %copy-done.5, f32[1024,1024]{1,0:T(8,128)S(1)} %copy-done.10), kind=kOutput, calls=%fused_computation.16 | convolution fusion | flops 3223846912 | bytes 16777216 | tf_op jit(solution)/shard_map/dot_general | solution.py:36
  313.1 13.3 %collective-permute-done.2.refs_2_ = f32[128,8,512]{2,1,0:T(8,128)S(1)} collective-permute-done((f32[128,8,512]{2,1,0:T(8,128)S(1)}, f32[128,8,512]{2,1,0:T(8,128)S(1)}, u32[]{:S(2)}, u32[]{:S(2)}) %collective-permute-start.2) | collective-permute-done | bytes 2097184 | tf_op jit(solution)/shard_map/ppermute | solution.py:63
  327.8 6.0 %all-to-all-start.4 = ((f32[8,128,512]{2,1,0:T(8,128)}), f32[8,128,512]{2,1,0:T(8,128)}, u32[]{:S(2)}, u32[]{:S(2)}) async-start(f32[8,128,512]{2,1,0:T(8,128)} %bitcast.94), calls=%async_computation.4 | async-start | bytes 4194304 | tf_op jit(solution)/shard_map/all_to_all | solution.py:187
  338.9 8.3 %fusion.4 = f32[1024,512]{1,0:T(8,128)S(1)} fusion(f32[1024,1024]{1,0:T(8,128)S(1)} %copy-done.13, f32[1024]{0:T(1024)S(1)} %bitcast.168, s32[1024]{0:T(1024)S(1)} %bitcast.150, f32[1024]{0:T(1024)S(1)} %bitcast.174, s32[1024]{0:T(1024)S(1)} %bitcast.156, f32[1024]{0:T(1024)S(1)} %bitcast.180, s32[1024]{0:T(1024)S(1)} %bitcast.108, f32[1024]{0:T(1024)S(1)} %bitcast.186, ...), kind=kOutput, calls=%fused_computation.28 | convolution fusion | flops 3251634176 | bytes 4276224 | tf_op jit(solution)/shard_map/dot_general | solution.py:36
  347.2 6.6 %slice_subtract_fusion.2 = f32[1024,512]{1,0:T(8,128)} fusion(f32[1024,1024]{1,0:T(8,128)} %bitcast.26, f32[1024,512]{1,0:T(8,128)S(1)} %fusion.4, f32[1024,1024]{1,0:T(8,128)S(1)} %copy-done.6, f32[1024,1024]{1,0:T(8,128)S(1)} %copy-done.13, f32[1024,1024]{1,0:T(8,128)S(1)} %copy-done.11), kind=kOutput, calls=%fused_computation.18 | convolution fusion | flops 3223846912 | bytes 16777216 | tf_op jit(solution)/shard_map/dot_general | solution.py:36
  353.8 28.3 %collective-permute-done.refs_10_ = f32[128,8,512]{2,1,0:T(8,128)} collective-permute-done((f32[128,8,512]{2,1,0:T(8,128)S(1)}, f32[128,8,512]{2,1,0:T(8,128)}, u32[]{:S(2)}, u32[]{:S(2)}) %collective-permute-start) | collective-permute-done | bytes 2097184 | tf_op jit(solution)/shard_map/ppermute | solution.py:63
  383.4 6.0 %all-to-all-start.5 = ((f32[8,128,512]{2,1,0:T(8,128)}), f32[8,128,512]{2,1,0:T(8,128)}, u32[]{:S(2)}, u32[]{:S(2)}) async-start(f32[8,128,512]{2,1,0:T(8,128)} %bitcast.95), calls=%async_computation.5 | async-start | bytes 4194304 | tf_op jit(solution)/shard_map/all_to_all | solution.py:187
  389.5 4.2 copy.36
  395.2 39.3 %all-to-all-done.5 = f32[8,128,512]{2,1,0:T(8,128)} async-done(((f32[8,128,512]{2,1,0:T(8,128)}), f32[8,128,512]{2,1,0:T(8,128)}, u32[]{:S(2)}, u32[]{:S(2)}) %all-to-all-start.5) | async-done | bytes 2097184 | tf_op jit(solution)/shard_map/all_to_all | solution.py:187
  434.5 4.2 copy.35
  442.4 44.5 %collective-permute-done.10.refs_14_ = f32[128,8,512]{2,1,0:T(8,128)} collective-permute-done((f32[128,8,512]{2,1,0:T(8,128)}, f32[128,8,512]{2,1,0:T(8,128)}, u32[]{:S(2)}, u32[]{:S(2)}) %collective-permute-start.10) | collective-permute-done | bytes 2097184 | tf_op jit(solution)/shard_map/ppermute | solution.py:63
  493.1 5.9 %shard_map.64 = (f32[256,256]{1,0:T(8,128)S(1)}, f32[256,256]{1,0:T(8,128)S(1)}) custom-call(s32[1]{0:T(128)} %bitcast.start_ref, f32[128,8,512]{2,1,0:T(8,128)S(1)} %bitcast.86, f32[128,8,512]{2,1,0:T(8,128)S(1)} %copy-done.1, f32[128,8,512]{2,1,0:T(8,128)} %copy-done.16, f32[128,8,512]{2,1,0:T(8,128)} %collective-permute-done.3.refs_3_, ...), custom_call_target="tpu_custom_call" | custom-call | tf_op jit(solution)/shard_map/pallas_call | solution.py:116
  499.9 41.0 %psum.7 = f32[64,64]{1,0:T(8,128)S(1)} all-reduce(f32[64,64]{1,0:T(8,128)S(1)} %fusion.116), channel_id=1, replica_groups=mesh['hil'=8,'vec'=4] {'hil','vec'}, use_global_device_ids=true, to_apply=%region_0.1 | all-reduce | flops 4096 | bytes 32768 | tf_op jit(solution)/shard_map/psum | solution.py:208
  546.1 20.2 %shard_map.65 = f32[128,16,1024]{2,1,0:T(8,128)} custom-call(f32[64,256]{1,0:T(8,128)S(1)} %mul.232.mix_ref, f32[128,8,512]{2,1,0:T(8,128)S(1)} %bitcast.87, f32[128,8,512]{2,1,0:T(8,128)S(1)} %copy-done.2, f32[128,8,512]{2,1,0:T(8,128)} %copy-done.16, f32[128,8,512]{2,1,0:T(8,128)} %collective-permute-done.3.refs_3_, f32[128,8,512]{2,1,0:T(8,128)} %bitcast.81.refs_4_, ...), custom_call_target="tpu_custom_call" | custom-call | tf_op jit(solution)/shard_map/pallas_call | solution.py:138
  (109 shorter events, 36.6 us)
Async XLA Ops:
  11.1 100.5 %all-to-all-start = ((f32[8,128,1024]{2,1,0:T(8,128)}), f32[8,128,1024]{2,1,0:T(8,128)}, u32[]{:S(2)}, u32[]{:S(2)}) async-start(f32[8,128,1024]{2,1,0:T(8,128)} %bitcast.93), calls=%async_computation | async-start | bytes 8388608 | tf_op jit(solution)/shard_map/all_to_all | solution.py:169
  111.7 5.0 copy-start.19
  111.7 5.1 copy-start.18
  111.7 5.2 copy-start.20
  111.7 97.5 %all-to-all-start.2 = ((f32[8,128,1024]{2,1,0:T(8,128)}), f32[8,128,1024]{2,1,0:T(8,128)}, u32[]{:S(2)}, u32[]{:S(2)}) async-start(f32[8,128,1024]{2,1,0:T(8,128)} %bitcast.92), calls=%async_computation.2 | async-start | bytes 8388608 | tf_op jit(solution)/shard_map/all_to_all | solution.py:169
  120.5 36.2 %copy-start.3 = (f32[1024,1024]{1,0:T(8,128)}, f32[1024,1024]{1,0:T(8,128)S(1)}, u32[]{:S(2)}) copy-start(f32[1024,1024]{1,0:T(8,128)S(1)} %convolution_add_fusion) | copy-start | bytes 12582916
  148.4 8.3 %copy-start.14 = (f32[1024,1024]{1,0:T(8,128)}, f32[1024,1024]{1,0:T(8,128)S(1)}, u32[]{:S(2)}) copy-start(f32[1024,1024]{1,0:T(8,128)S(1)} %add_multiply_fusion.1) | copy-start | bytes 12582916
  209.2 52.2 %all-to-all-start.1 = ((f32[8,128,512]{2,1,0:T(8,128)}), f32[8,128,512]{2,1,0:T(8,128)S(1)}, u32[]{:S(2)}, u32[]{:S(2)}) async-start(f32[8,128,512]{2,1,0:T(8,128)} %bitcast.23), calls=%async_computation.1 | async-start | bytes 4194304 | tf_op jit(solution)/shard_map/all_to_all | solution.py:187
  213.1 10.0 %copy-start.4 = (f32[1024,1024]{1,0:T(8,128)S(1)}, f32[1024,1024]{1,0:T(8,128)}, u32[]{:S(2)}) copy-start(f32[1024,1024]{1,0:T(8,128)} %copy-done.3) | copy-start | bytes 12582916
  213.1 10.0 %copy-start.9 = (f32[1024,1024]{1,0:T(8,128)S(1)}, f32[1024,1024]{1,0:T(8,128)}, u32[]{:S(2)}) copy-start(f32[1024,1024]{1,0:T(8,128)} %param.7) | copy-start | bytes 12582916
  213.1 10.0 %copy-start.15 = (f32[1024,1024]{1,0:T(8,128)S(1)}, f32[1024,1024]{1,0:T(8,128)}, u32[]{:S(2)}) copy-start(f32[1024,1024]{1,0:T(8,128)} %copy-done.14) | copy-start | bytes 12582916
  261.5 66.3 %all-to-all-start.3 = ((f32[8,128,512]{2,1,0:T(8,128)}), f32[8,128,512]{2,1,0:T(8,128)}, u32[]{:S(2)}, u32[]{:S(2)}) async-start(f32[8,128,512]{2,1,0:T(8,128)} %bitcast.28), calls=%async_computation.3 | async-start | bytes 4194304 | tf_op jit(solution)/shard_map/all_to_all | solution.py:187
  279.7 46.7 %collective-permute-start.2 = (f32[128,8,512]{2,1,0:T(8,128)S(1)}, f32[128,8,512]{2,1,0:T(8,128)S(1)}, u32[]{:S(2)}, u32[]{:S(2)}) collective-permute-start(f32[128,8,512]{2,1,0:T(8,128)S(1)} %bitcast.84), channel_id=1, source_target_pairs={{0,2},{1,3},{2,0},{3,1},{4,6},{5,7},{6,4},{7,5},{8,10},{9,11},{10,... | collective-permute-start | bytes 6291464 | tf_op jit(solution)/shard_map/ppermute | solution.py:63
  298.3 8.3 %copy-start.12 = (f32[1024,1024]{1,0:T(8,128)}, f32[1024,1024]{1,0:T(8,128)S(1)}, u32[]{:S(2)}) copy-start(f32[1024,1024]{1,0:T(8,128)S(1)} %add_multiply_fusion) | copy-start | bytes 12582916
  298.3 8.3 %copy-start.10 = (f32[1024,1024]{1,0:T(8,128)S(1)}, f32[1024,1024]{1,0:T(8,128)}, u32[]{:S(2)}) copy-start(f32[1024,1024]{1,0:T(8,128)} %param.7) | copy-start | bytes 12582916
  327.8 55.7 %all-to-all-start.4 = ((f32[8,128,512]{2,1,0:T(8,128)}), f32[8,128,512]{2,1,0:T(8,128)}, u32[]{:S(2)}, u32[]{:S(2)}) async-start(f32[8,128,512]{2,1,0:T(8,128)} %bitcast.94), calls=%async_computation.4 | async-start | bytes 4194304 | tf_op jit(solution)/shard_map/all_to_all | solution.py:187
  333.7 5.1 copy-start.13
  336.7 10.5 %copy-start.7 = (f32[8,128,512]{2,0,1:T(8,128)}, f32[8,128,512]{2,0,1:T(8,128)S(1)}, u32[]{:S(2)}) copy-start(f32[8,128,512]{2,0,1:T(8,128)S(1)} %copy.37) | copy-start | bytes 6291460
  336.7 10.5 %copy-start.6 = (f32[1024,1024]{1,0:T(8,128)S(1)}, f32[1024,1024]{1,0:T(8,128)}, u32[]{:S(2)}) copy-start(f32[1024,1024]{1,0:T(8,128)} %copy-done.3) | copy-start | bytes 12582916
  336.7 10.5 %copy-start.11 = (f32[1024,1024]{1,0:T(8,128)S(1)}, f32[1024,1024]{1,0:T(8,128)}, u32[]{:S(2)}) copy-start(f32[1024,1024]{1,0:T(8,128)} %param.7) | copy-start | bytes 12582916
  336.8 45.3 %collective-permute-start = (f32[128,8,512]{2,1,0:T(8,128)S(1)}, f32[128,8,512]{2,1,0:T(8,128)}, u32[]{:S(2)}, u32[]{:S(2)}) collective-permute-start(f32[128,8,512]{2,1,0:T(8,128)S(1)} %bitcast.88), channel_id=1, source_target_pairs={{0,2},{1,3},{2,0},{3,1},{4,6},{5,7},{6,4},{7,5},{8,10},{9,11},{10,... | collective-permute-start | bytes 6291464 | tf_op jit(solution)/shard_map/ppermute | solution.py:63
  338.3 43.7 %collective-permute-start.1 = (f32[128,8,512]{2,1,0:T(8,128)S(1)}, f32[128,8,512]{2,1,0:T(8,128)S(1)}, u32[]{:S(2)}, u32[]{:S(2)}) collective-permute-start(f32[128,8,512]{2,1,0:T(8,128)S(1)} %bitcast.85), channel_id=1, source_target_pairs={{0,1},{1,0},{2,3},{3,2},{4,5},{5,4},{6,7},{7,6},{8,9},{9,8},{10,11... | collective-permute-start | bytes 6291464 | tf_op jit(solution)/shard_map/ppermute | solution.py:63
  338.3 45.1 %collective-permute-start.3 = (f32[128,8,512]{2,1,0:T(8,128)}, f32[128,8,512]{2,1,0:T(8,128)}, u32[]{:S(2)}, u32[]{:S(2)}) collective-permute-start(f32[128,8,512]{2,1,0:T(8,128)} %copy-done.16), channel_id=1, source_target_pairs={{0,1},{1,0},{2,3},{3,2},{4,5},{5,4},{6,7},{7,6},{8,9},{9,8},{10,11... | collective-permute-start | bytes 6291464 | tf_op jit(solution)/shard_map/ppermute | solution.py:63
  383.4 51.1 %all-to-all-start.5 = ((f32[8,128,512]{2,1,0:T(8,128)}), f32[8,128,512]{2,1,0:T(8,128)}, u32[]{:S(2)}, u32[]{:S(2)}) async-start(f32[8,128,512]{2,1,0:T(8,128)} %bitcast.95), calls=%async_computation.5 | async-start | bytes 4194304 | tf_op jit(solution)/shard_map/all_to_all | solution.py:187
  389.4 51.3 %collective-permute-start.7 = (f32[128,8,512]{2,1,0:T(8,128)}, f32[128,8,512]{2,1,0:T(8,128)}, u32[]{:S(2)}, u32[]{:S(2)}) collective-permute-start(f32[128,8,512]{2,1,0:T(8,128)} %bitcast.89), channel_id=1, source_target_pairs={{0,1},{1,0},{2,3},{3,2},{4,5},{5,4},{6,7},{7,6},{8,9},{9,8},{10,11... | collective-permute-start | bytes 6291464 | tf_op jit(solution)/shard_map/ppermute | solution.py:63
  393.7 48.7 %collective-permute-start.5 = (f32[128,8,512]{2,1,0:T(8,128)}, f32[128,8,512]{2,1,0:T(8,128)}, u32[]{:S(2)}, u32[]{:S(2)}) collective-permute-start(f32[128,8,512]{2,1,0:T(8,128)} %bitcast.81.refs_4_), channel_id=1, source_target_pairs={{0,2},{1,3},{2,0},{3,1},{4,6},{5,7},{6,4},{7,5},{8,10},{9,11},{10,... | collective-permute-start | bytes 6291464 | tf_op jit(solution)/shard_map/ppermute | solution.py:63
  438.7 48.2 %collective-permute-start.10 = (f32[128,8,512]{2,1,0:T(8,128)}, f32[128,8,512]{2,1,0:T(8,128)}, u32[]{:S(2)}, u32[]{:S(2)}) collective-permute-start(f32[128,8,512]{2,1,0:T(8,128)} %bitcast.80.refs_12_), channel_id=1, source_target_pairs={{0,2},{1,3},{2,0},{3,1},{4,6},{5,7},{6,4},{7,5},{8,10},{9,11},{10,... | collective-permute-start | bytes 6291464 | tf_op jit(solution)/shard_map/ppermute | solution.py:63
  440.3 47.5 %collective-permute-start.8 = (f32[128,8,512]{2,1,0:T(8,128)}, f32[128,8,512]{2,1,0:T(8,128)}, u32[]{:S(2)}, u32[]{:S(2)}) collective-permute-start(f32[128,8,512]{2,1,0:T(8,128)} %collective-permute-done.refs_10_), channel_id=1, source_target_pairs={{0,1},{1,0},{2,3},{3,2},{4,5},{5,4},{6,7},{7,6},{8,9},{9,8},{10,11... | collective-permute-start | bytes 6291464 | tf_op jit(solution)/shard_map/ppermute | solution.py:63
  440.3 47.5 %collective-permute-start.4 = (f32[128,8,512]{2,1,0:T(8,128)}, f32[128,8,512]{2,1,0:T(8,128)}, u32[]{:S(2)}, u32[]{:S(2)}) collective-permute-start(f32[128,8,512]{2,1,0:T(8,128)} %bitcast.81.refs_4_), channel_id=1, source_target_pairs={{0,1},{1,0},{2,3},{3,2},{4,5},{5,4},{6,7},{7,6},{8,9},{9,8},{10,11... | collective-permute-start | bytes 6291464 | tf_op jit(solution)/shard_map/ppermute | solution.py:63
  440.8 47.0 %collective-permute-start.9 = (f32[128,8,512]{2,1,0:T(8,128)}, f32[128,8,512]{2,1,0:T(8,128)}, u32[]{:S(2)}, u32[]{:S(2)}) collective-permute-start(f32[128,8,512]{2,1,0:T(8,128)} %bitcast.80.refs_12_), channel_id=1, source_target_pairs={{0,1},{1,0},{2,3},{3,2},{4,5},{5,4},{6,7},{7,6},{8,9},{9,8},{10,11... | collective-permute-start | bytes 6291464 | tf_op jit(solution)/shard_map/ppermute | solution.py:63
  442.4 45.3 %collective-permute-start.6 = (f32[128,8,512]{2,1,0:T(8,128)}, f32[128,8,512]{2,1,0:T(8,128)}, u32[]{:S(2)}, u32[]{:S(2)}) collective-permute-start(f32[128,8,512]{2,1,0:T(8,128)} %collective-permute-done.5.refs_6_), channel_id=1, source_target_pairs={{0,1},{1,0},{2,3},{3,2},{4,5},{5,4},{6,7},{7,6},{8,9},{9,8},{10,11... | collective-permute-start | bytes 6291464 | tf_op jit(solution)/shard_map/ppermute | solution.py:63
  487.0 4.5 collective-permute-start.11
  (8 other events, 24.0 us)

commit v2 on v1

v2 whole, which is shorter than its diff:
```python
import functools
import math

import jax
import jax.numpy as jnp
from jax import lax
from jax.experimental import pallas as pl
from jax.experimental.pallas import tpu as pltpu
from jax.sharding import PartitionSpec as P

DEGREE = 2
NS_ITERS = 4
STACK = 4

highest = lax.Precision.HIGHEST
high = lax.Precision.HIGH
center_shift = 6.0
half_range = 12.0


def site_bits(states, sites):
    shifts = jnp.arange(sites, dtype=jnp.int32)
    return jnp.bitwise_and(jnp.right_shift(states[:, None], shifts[None, :]), 1).astype(jnp.float32)


def hop_matrix(hop_coef, hop_partner):
    up_count = hop_partner.shape[1]
    columns = jnp.arange(up_count, dtype=jnp.int32)
    total = jnp.zeros((up_count, up_count), jnp.float32)
    for bond in range(hop_partner.shape[0]):
        total = total + jnp.where(hop_partner[bond][:, None] == columns[None, :], hop_coef[bond][:, None], 0.0)
    return total


def dot(left, right, contract, precision):
    return lax.dot_general(
        left, right, ((contract[:1], contract[1:]), ((), ())), precision=precision, preferred_element_type=jnp.float32
    )


def apply_rows(vector, vector_rows, down_matrix, up_rows, diagonal_rows):
    applied = dot(vector_rows, down_matrix, (1, 1), high) + dot(up_rows, vector, (1, 0), high)
    return applied + diagonal_rows * vector_rows


def spread_step(held, step):
    pairs = [(i, i ^ step) for i in range(lax.axis_size("vec"))]
    return [lax.ppermute(piece, "vec", pairs) for piece in held]


def split(values):
    top = values.astype(jnp.bfloat16)
    return top, (values - top.astype(jnp.float32)).astype(jnp.bfloat16)


def vectors_first_kernel(start_ref, block_ref, out_ref):
    out_ref[...] = jnp.swapaxes(block_ref[...], 0, 1)


def vectors_first(start_block, turn, count, swapped):
    up_local, _, down_count = start_block.shape
    rows = 16
    blocks = up_local // rows
    return pl.pallas_call(
        vectors_first_kernel,
        out_shape=jax.ShapeDtypeStruct((count, up_local, down_count), jnp.float32),
        grid_spec=pltpu.PrefetchScalarGridSpec(
            num_scalar_prefetch=1,
            grid=(blocks,),
            in_specs=[
                pl.BlockSpec(
                    (rows, count, down_count),
                    lambda i, swap: (lax.rem(i + swap[0] * (blocks // 2), blocks), turn, 0),
                )
            ],
            out_specs=pl.BlockSpec((count, rows, down_count), lambda i, swap: (0, i, 0)),
        ),
        compiler_params=pltpu.CompilerParams(vmem_limit_bytes=56 * 1024 * 1024),
    )(swapped, start_block)


def stacked(refs):
    return jnp.concatenate([jnp.swapaxes(ref[...], 0, 1) for ref in refs], axis=1)


def gram_kernel(start_ref, *refs):
    inputs, (top_ref, cross_ref) = refs[:-2], refs[-2:]

    @pl.when(pl.program_id(0) == 0)
    def _():
        top_ref[...] = jnp.zeros_like(top_ref)
        cross_ref[...] = jnp.zeros_like(cross_ref)

    values = stacked(inputs)
    rows, vectors, columns = values.shape
    for first in range(0, rows, STACK):
        top, low = split(values[first : first + STACK].reshape(STACK * vectors, columns))
        top_ref[...] += dot(top, top, (1, 1), None)
        cross_ref[...] += dot(top, low, (1, 1), None)


def gram_partial(pieces, part, parts):
    vectors = sum(piece.shape[0] for piece in pieces)
    block = 8
    blocks = pieces[0].shape[1] // parts // block
    specs = [
        pl.BlockSpec((piece.shape[0], block, piece.shape[2]), lambda i, first: (0, first[0] + i, 0)) for piece in pieces
    ]
    size = STACK * vectors
    out = jax.ShapeDtypeStruct((size, size), jnp.float32)
    top, cross = pl.pallas_call(
        gram_kernel,
        out_shape=(out, out),
        grid_spec=pltpu.PrefetchScalarGridSpec(
            num_scalar_prefetch=1,
            grid=(blocks,),
            in_specs=specs,
            out_specs=[pl.BlockSpec((size, size), lambda i, first: (0, 0))] * 2,
        ),
        compiler_params=pltpu.CompilerParams(vmem_limit_bytes=48 * 1024 * 1024),
    )((part * blocks).reshape(1), *pieces)
    cross = cross + cross.T
    total = (top + cross).reshape(STACK, vectors, STACK, vectors)
    return sum(total[u, :, u, :] for u in range(STACK))


def rotate_kernel(half_blocks, swap_ref, mix_ref, *refs):
    inputs, out_ref = refs[:-1], refs[-1]
    mix_top, mix_low = split(mix_ref[...])
    count = mix_top.shape[0]
    both = jnp.concatenate([mix_top, mix_low], axis=0)

    def run(half):
        values = stacked(half)
        rows, vectors, columns = values.shape
        for first in range(0, rows, STACK):
            top, low = split(values[first : first + STACK].reshape(STACK * vectors, columns))
            wide = dot(both, top, (1, 0), None)
            result = wide[:count] + wide[count:] + dot(mix_top, low, (1, 0), None)
            out_ref[first : first + STACK] = result.reshape(STACK, count // STACK, result.shape[1])

    pl.when(pl.program_id(0) < half_blocks)(lambda: run(inputs[: len(inputs) // 2]))
    pl.when(pl.program_id(0) >= half_blocks)(lambda: run(inputs[len(inputs) // 2 :]))


def rotate(halves, mixing, swapped):
    half_rows, down_count = halves[0][0].shape[1:]
    block = 8
    half_blocks = half_rows // block
    own = mixing.shape[1]
    wide_mixing = jnp.kron(jnp.eye(STACK, dtype=jnp.float32), mixing.T)
    specs = [pl.BlockSpec(wide_mixing.shape, lambda i, swap: (0, 0))]
    for piece in halves[0]:
        shape = (piece.shape[0], block, down_count)
        specs.append(pl.BlockSpec(shape, lambda i, swap: (0, jnp.minimum(i, half_blocks - 1), 0)))
    for piece in halves[1]:
        shape = (piece.shape[0], block, down_count)
        specs.append(pl.BlockSpec(shape, lambda i, swap: (0, jnp.maximum(i - half_blocks, 0), 0)))
    return pl.pallas_call(
        functools.partial(rotate_kernel, half_blocks),
        out_shape=jax.ShapeDtypeStruct((2 * half_rows, own, down_count), jnp.float32),
        grid_spec=pltpu.PrefetchScalarGridSpec(
            num_scalar_prefetch=1,
            grid=(2 * half_blocks,),
            in_specs=specs,
            out_specs=pl.BlockSpec(
                (block, own, down_count),
                lambda i, swap: (lax.rem(i + swap[0] * half_blocks, 2 * half_blocks), 0, 0),
            ),
        ),
        compiler_params=pltpu.CompilerParams(vmem_limit_bytes=48 * 1024 * 1024),
    )(swapped, wide_mixing, *halves[0], *halves[1])


def newton_schulz(gram_sum):
    identity = jnp.eye(gram_sum.shape[0], dtype=jnp.float32)
    norm_scale = 1.0 / jnp.sqrt(jnp.sqrt(jnp.sum(gram_sum * gram_sum)) + 1e-06)
    gram_sum = norm_scale * norm_scale * gram_sum
    product_total = identity
    for _ in range(NS_ITERS):
        mixing = 1.5 * identity - 0.5 * gram_sum
        product_total = dot(product_total, mixing, (1, 0), highest)
        gram_sum = dot(mixing, dot(gram_sum, mixing, (1, 0), highest), (1, 0), highest)
    return norm_scale * product_total


def vector_cut(start_block, down_matrix, hop_coef, hop_partner, onsite_u):
    hil_parts, vec_parts = lax.axis_size("hil"), lax.axis_size("vec")
    up_local, vec_local, down_count = start_block.shape
    up_count = up_local * hil_parts
    rounds = vec_local // hil_parts
    half_rows = up_local // 2
    side = vec_parts // 2
    own = lax.axis_index("vec")
    swap = own // side
    swapped = swap.reshape(1).astype(jnp.int32)

    def ordered(values):
        cut = values.reshape(values.shape[:-1] + (hil_parts, 2, half_rows))
        return jnp.where(swap == 1, cut[..., ::-1, :], cut).reshape(values.shape)

    arrived = []
    for turn in range(rounds):
        block = vectors_first(start_block, turn, hil_parts, swapped)
        block = lax.all_to_all(block, "hil", split_axis=0, concat_axis=0, tiled=True)
        arrived.append(block.reshape(up_count, down_count))
    other = jnp.where((hop_partner // half_rows) % 2 == 0, hop_partner + half_rows, hop_partner - half_rows)
    up_matrix = hop_matrix(ordered(hop_coef), ordered(jnp.where(swap == 1, other, hop_partner)))
    sites = onsite_u.shape[0]
    diagonal = -center_shift + jnp.dot(
        site_bits(ordered(jnp.arange(up_count, dtype=jnp.int32)), sites) * onsite_u[None, :],
        site_bits(jnp.arange(down_count, dtype=jnp.int32), sites).T,
        precision=highest,
        preferred_element_type=jnp.float32,
    )

    def rows(values, half):
        return values.reshape(hil_parts, 2, half_rows, -1)[:, half].reshape(hil_parts * half_rows, -1)

    def first_step(vector):
        return apply_rows(vector, vector, down_matrix, up_matrix, diagonal) / half_range

    def second_step(vector, before, half):
        applied = apply_rows(vector, rows(vector, half), down_matrix, rows(up_matrix, half), rows(diagonal, half))
        return (2.0 * applied / half_range - rows(before, half)).reshape(hil_parts, half_rows, down_count)

    mine, theirs = 0, 1
    once = first_step(arrived[0])
    crossed = []
    held = [[], []]
    for turn in range(rounds):
        pieces = {half: second_step(once, arrived[turn], half) for half in (theirs, mine)}
        pieces[theirs], pieces[mine] = lax.optimization_barrier((pieces[theirs], pieces[mine]))
        for half in (theirs, mine):
            piece = pieces[half]
            if half == mine and turn + 1 < rounds:
                once = first_step(arrived[turn + 1])
                piece, once = lax.optimization_barrier((piece, once))
            if len(crossed) > 1:
                piece, crossed[-2][0] = lax.optimization_barrier((piece, crossed[-2][0]))
            back = lax.all_to_all(piece, "hil", split_axis=0, concat_axis=0, tiled=True)
            held[half].append(back)
            crossed.append(spread_step([back], side))
    halves = []
    for half in (mine, theirs):
        arrays = []
        for turn in range(rounds):
            near = [held[half][turn], crossed[2 * turn + (0 if half == mine else 1)][0]]
            step = side // 2
            while step >= 1:
                near = near + spread_step(near, step)
                step //= 2
            arrays.extend(near)
        halves.append(arrays)
    distances = [0, side]
    step = side // 2
    while step >= 1:
        distances += [distance ^ step for distance in distances]
        step //= 2
    near = jnp.bitwise_xor(jnp.array(distances, dtype=jnp.int32), own)
    exchange = (near[:, None] == jnp.arange(vec_parts, dtype=jnp.int32)[None, :]).astype(jnp.float32)
    order = jnp.kron(jnp.eye(rounds, dtype=jnp.float32), jnp.kron(exchange, jnp.eye(hil_parts, dtype=jnp.float32)))
    partial = gram_partial(halves[mine], lax.rem(own, side), side)
    partial = dot(order, dot(partial, order, (1, 0), highest), (0, 0), highest)
    mixing = newton_schulz(lax.psum(partial, ("hil", "vec")))
    mixing = dot(dot(order, mixing, (1, 0), highest), order, (1, 1), highest)
    mixing = mixing.reshape(-1, rounds, vec_parts, hil_parts)[:, :, 0].reshape(-1, vec_local)
    return rotate(halves, mixing * math.sqrt(up_count * down_count), swapped)


def split_down(local_block):
    hil_parts = lax.axis_size("hil")
    up_local, vec_local, down_count = local_block.shape
    down_local = down_count // hil_parts
    arranged = local_block.reshape(up_local, vec_local, hil_parts, down_local).transpose(2, 0, 1, 3)
    arranged = arranged.reshape(hil_parts, up_local, vec_local * down_local)
    received = lax.all_to_all(arranged, "hil", split_axis=0, concat_axis=1, tiled=True)
    return received.reshape(hil_parts * up_local, vec_local * down_local)


def split_up(spread, up_local, vec_local):
    hil_parts = lax.axis_size("hil")
    total_up, columns = spread.shape
    down_local = columns // vec_local
    received = lax.all_to_all(
        spread.reshape(1, total_up, columns), "hil", split_axis=1, concat_axis=0, tiled=True
    )
    arranged = received.reshape(hil_parts, up_local, vec_local, down_local).transpose(1, 2, 0, 3)
    return arranged.reshape(up_local, vec_local, hil_parts * down_local)


def advance(applied, present, earlier, degree_step):
    if degree_step == 0:
        return (applied - center_shift * present) / half_range
    return 2.0 * (applied - center_shift * present) / half_range - earlier


def down_cut(start_block, down_matrix, hop_coef, hop_partner, onsite_u):
    up_local, vec_local, down_count = start_block.shape
    up_matrix = hop_matrix(hop_coef, hop_partner)
    sites = onsite_u.shape[0]
    local_states = lax.axis_index("hil") * up_local + jnp.arange(up_local, dtype=jnp.int32)
    interaction = jnp.dot(
        site_bits(local_states, sites) * onsite_u[None, :],
        site_bits(jnp.arange(down_count, dtype=jnp.int32), sites).T,
        precision=highest,
        preferred_element_type=jnp.float32,
    )
    current = previous = start_block
    current_cut = previous_cut = split_down(current)
    for degree_step in range(DEGREE):
        local_part = dot(current.reshape(up_local * vec_local, down_count), down_matrix, (1, 1), high)
        local_part = local_part.reshape(current.shape) + interaction[:, None, :] * current
        hopped = dot(up_matrix, current_cut, (1, 0), high)
        applied = local_part + split_up(hopped, up_local, vec_local)
        following = advance(applied, current, previous, degree_step)
        if degree_step + 1 < DEGREE:
            applied_cut = split_down(local_part) + hopped
            following_cut = advance(applied_cut, current_cut, previous_cut, degree_step)
            previous_cut, current_cut = current_cut, following_cut
        previous, current = current, following
    row_panel = lax.all_to_all(current, "vec", split_axis=2, concat_axis=1, tiled=True)
    gram_sum = lax.psum(jnp.einsum("ukd,uld->kl", row_panel, row_panel, precision=highest), ("hil", "vec"))
    mixing = newton_schulz(gram_sum) * math.sqrt(up_matrix.shape[0] * down_count)
    row_panel = jnp.einsum("ukd,kl->uld", row_panel, mixing, precision=highest)
    return lax.all_to_all(row_panel, "vec", split_axis=1, concat_axis=2, tiled=True)


def on_device(start_block, down_matrix, hop_partner, hop_sign, bond_hop, onsite_u):
    hil_parts, vec_parts = lax.axis_size("hil"), lax.axis_size("vec")
    up_local, vec_local, _ = start_block.shape
    hop_coef = -bond_hop[:, None] * hop_sign.astype(jnp.float32)
    whole_vectors = vec_local % hil_parts == 0 and hil_parts % 8 == 0
    halved = vec_parts > 1 and vec_parts & (vec_parts - 1) == 0 and up_local % (16 * vec_parts) == 0
    plan = vector_cut if whole_vectors and halved else down_cut
    return plan(start_block, down_matrix, hop_coef, hop_partner, onsite_u)


def solution(mesh):
    in_specs = (P("hil", "vec", None), P(), P(), P(), P(), P())
    out_specs = P("hil", "vec", None)
    return jax.shard_map(
        on_device, mesh=mesh, in_specs=in_specs, out_specs=out_specs, check_vma=False
    )
```

time: 573 us -> 551 us (0.962)
  local copies, waits for them, and re-layouts: 39 us -> 21.2 us
  Pallas kernels: 26.1 us -> 43.4 us
  matrix products: 122 us -> 108 us
  waiting for transfers between devices: 295 us -> 283 us
    all_to_all x2, waiting for transfers between devices: 133 us -> 101 us  [vector_cut(): lax.all_to_all(block, 'hil', split_axis=0, concat_axis=0, tiled=True)]
    ppermute x12, waiting for transfers between devices: 91.6 us -> 115 us  [spread_step(): return [lax.ppermute(piece, 'vec', pairs) for piece in held]]
    pallas_call x2 -> x4, Pallas kernels: 26.1 us -> 43.4 us  [the longest x1 23.7 us: rotate(): pl.pallas_call(functools.partial(rotate_kernel, half_blocks), out_shape=j...]
    dot_general x25, matrix products: 118 us -> 103 us  [dot(): lax.dot_general(left, right, ((contract[:1], contract[1:]), ((), ())), pr...]
    all_to_all x4 -> x0, local copies, waits for them, and re-layouts: 14.3 us -> none  [vector_cut(): back = lax.all_to_all(piece, 'hil', split_axis=0, concat_axis=0, tiled=True)]
    unnamed x46 -> x40, local copies, waits for them, and re-layouts: 17 us -> 8.37 us
  transfers between devices with their start and end apart: 18 -> 18, of which waited for: 9 -> 8; matrix products, arithmetic and copies ran while one was open for 25% -> 24% of each run, Pallas kernels for 0% -> 2%
where the time goes in v2:
time: 551 us; the launch traced here: 542 us
  waiting for transfers between devices  283 us (51%)
  matrix products  108 us (20%)
  Pallas kernels  43.4 us (8%)
  blocking collectives  40 us (7%)
  starting transfers between devices  37.8 us (7%)
  local copies, waits for them, and re-layouts  21.2 us (4%)
  other arithmetic  6.76 us (1%)
    ppermute x12, waiting for transfers between devices, spread_step(): return [lax.ppermute(piece, 'vec', pairs) for piece in held]  115 us
    dot_general x25, matrix products, dot(): lax.dot_general(left, right, ((contract[:1], contract[1:]), ((), ())), pr...  103 us
    all_to_all x2, waiting for transfers between devices, vector_cut(): lax.all_to_all(block, 'hil', split_axis=0, concat_axis=0, tiled=True)  101 us
    all_to_all x4, waiting for transfers between devices, vector_cut(): back = lax.all_to_all(piece, 'hil', split_axis=0, concat_axis=0, tiled=True)  66.4 us
    psum x1, blocking collectives, vector_cut(): mixing = newton_schulz(lax.psum(partial, ('hil', 'vec')))  40 us
    pallas_call x1, Pallas kernels, rotate(): pl.pallas_call(functools.partial(rotate_kernel, half_blocks), out_shape=j...  23.7 us
    all_to_all x4, starting transfers between devices, vector_cut(): back = lax.all_to_all(piece, 'hil', split_axis=0, concat_axis=0, tiled=True)  17.8 us
    pallas_call x2, Pallas kernels, vectors_first(): pl.pallas_call(vectors_first_kernel, out_shape=jax.ShapeDtypeStruct((coun...  13.9 us
  transfers between devices with their start and end apart: 18, of which 8 were waited for; matrix products, arithmetic and copies ran while one was open for 24% of the time, Pallas kernels for 2%

profile of v2, /device:TPU:0, one launch (start us, length us, event | category | flops | bytes accessed | tf_op | source)
XLA Modules:
  0.0 542.1 jit_solution(8200700669202606168)
XLA Ops:
  0.0 6.9 %shard_map.73 = f32[8,128,1024]{2,1,0:T(8,128)} custom-call(s32[1]{0:T(128)} %bitcast.start_ref.swap_ref, f32[128,16,1024]{2,1,0:T(8,128)} %block_ref.3), custom_call_target="tpu_custom_call" | custom-call | tf_op jit(solution)/shard_map/pallas_call | solution.py:64
  6.9 7.3 %all-to-all-start = ((f32[8,128,1024]{2,1,0:T(8,128)}), f32[8,128,1024]{2,1,0:T(8,128)}, u32[]{:S(2)}, u32[]{:S(2)}) async-start(f32[8,128,1024]{2,1,0:T(8,128)} %shard_map.73), calls=%async_computation | async-start | bytes 8388608 | tf_op jit(solution)/shard_map/all_to_all | solution.py:205
  14.2 7.0 %shard_map.74 = f32[8,128,1024]{2,1,0:T(8,128)} custom-call(s32[1]{0:T(128)} %bitcast.start_ref.swap_ref, f32[128,16,1024]{2,1,0:T(8,128)} %block_ref.3), custom_call_target="tpu_custom_call" | custom-call | tf_op jit(solution)/shard_map/pallas_call | solution.py:64
  23.8 5.3 convolution_add_fusion
  29.1 78.3 %all-to-all-done = f32[8,128,1024]{2,1,0:T(8,128)} async-done(((f32[8,128,1024]{2,1,0:T(8,128)}), f32[8,128,1024]{2,1,0:T(8,128)}, u32[]{:S(2)}, u32[]{:S(2)}) %all-to-all-start) | async-done | bytes 4194336 | tf_op jit(solution)/shard_map/all_to_all | solution.py:205
  107.4 4.6 all-to-all-start.1
  112.0 5.4 select_add_fusion
  124.8 8.9 %fusion.111 = f32[1024,1024]{1,0:T(8,128)S(1)} fusion(f32[1024,1024]{1,0:T(8,128)} %bitcast.2, f32[1024,1024]{1,0:T(8,128)S(1)} %copy-done), kind=kOutput, calls=%fused_computation.199 | convolution fusion | flops 6442450944 | bytes 12582912 | tf_op jit(solution)/shard_map/dot_general | solution.py:36
  133.8 16.9 %add_multiply_fusion.1 = f32[1024,1024]{1,0:T(8,128)S(1)} fusion(f32[1024,1024]{1,0:T(8,128)S(1)} %copy-done.11, f32[1024,1024]{1,0:T(8,128)} %bitcast.2, f32[1024,1024]{1,0:T(8,128)S(1)} %fusion.111, f32[1024]{0:T(1024)S(1)} %broadcast_in_dim.176, s32[1024]{0:T(1024)S(1)} %eq.347, f32[1024]{0:T(1024)S(1)} %broadcast_in_dim.174, s32[1024]{0:T(1024)S(1)} %eq.343, ...), kind=kOutput, calls=%fused_computation.12 | convolution fusion | flops 6477053952 | bytes 16859136 | tf_op jit(solution)/shard_map/dot_general | solution.py:36
  153.8 3.6 fusion.112
  157.5 3.6 fusion.113
  161.2 5.5 %bitcast_subtract_fusion.3 = f32[512,1024]{1,0:T(8,128)} fusion(f32[8,1,64,1024]{3,2,1,0:T(8,128)S(1)} %get-tuple-element.40, f32[512,1024]{1,0:T(8,128)S(1)} %bitcast.163, f32[8,1,64,1024]{3,2,1,0:T(8,128)S(1)} %get-tuple-element.36, f32[512,1024]{1,0:T(8,128)S(1)} %fusion.112, f32[512,1024]{1,0:T(8,128)S(1)} %bitcast.166, ...), kind=kOutput, calls=%fused_computation.34 | convolution fusion | flops 3223846912 | bytes 16777216 | tf_op jit(solution)/shard_map/dot_general | solution.py:36
  166.7 15.0 %bitcast_subtract_fusion.2 = f32[512,1024]{1,0:T(8,128)} fusion(f32[8,1,64,1024]{3,2,1,0:T(8,128)S(1)} %get-tuple-element.39, f32[512,1024]{1,0:T(8,128)S(1)} %bitcast.159, f32[8,1,64,1024]{3,2,1,0:T(8,128)S(1)} %get-tuple-element.35, f32[512,1024]{1,0:T(8,128)S(1)} %fusion.113, f32[512,1024]{1,0:T(8,128)S(1)} %bitcast.164, ...), kind=kOutput, calls=%fused_computation.27 | convolution fusion | flops 3223846912 | bytes 16777216 | tf_op jit(solution)/shard_map/dot_general | solution.py:36
  181.7 22.9 %all-to-all-done.1 = f32[8,128,1024]{2,1,0:T(8,128)} async-done(((f32[8,128,1024]{2,1,0:T(8,128)}), f32[8,128,1024]{2,1,0:T(8,128)}, u32[]{:S(2)}, u32[]{:S(2)}) %all-to-all-start.1) | async-done | bytes 4194336 | tf_op jit(solution)/shard_map/all_to_all | solution.py:205
  204.6 3.6 all-to-all-start.3
  208.2 10.7 %fusion.114 = f32[1024,1024]{1,0:T(8,128)S(1)} fusion(f32[1024,1024]{1,0:T(8,128)} %bitcast.36, f32[1024,1024]{1,0:T(8,128)} %param.8), kind=kOutput, calls=%fused_computation.202 | convolution fusion | flops 6442450944 | bytes 12582912 | tf_op jit(solution)/shard_map/dot_general | solution.py:36
  218.9 18.0 %add_multiply_fusion = f32[1024,1024]{1,0:T(8,128)} fusion(f32[1024,1024]{1,0:T(8,128)S(1)} %copy-done.12, f32[1024,1024]{1,0:T(8,128)} %bitcast.36, f32[1024,1024]{1,0:T(8,128)S(1)} %fusion.114, f32[1024]{0:T(1024)S(1)} %broadcast_in_dim.176, s32[1024]{0:T(1024)S(1)} %eq.347, f32[1024]{0:T(1024)S(1)} %broadcast_in_dim.174, s32[1024]{0:T(1024)S(1)} %eq.343, ...), kind=kOutput, calls=%fused_computation | convolution fusion | flops 6477053952 | bytes 16859136 | tf_op jit(solution)/shard_map/dot_general | solution.py:36
  236.9 19.7 %all-to-all-done.3.refs_8_ = f32[8,64,1024]{2,1,0:T(8,128)S(1)} async-done(((f32[8,64,1024]{2,1,0:T(8,128)}), f32[8,64,1024]{2,1,0:T(8,128)S(1)}, u32[]{:S(2)}, u32[]{:S(2)}) %all-to-all-start.3) | async-done | bytes 2097184 | tf_op jit(solution)/shard_map/all_to_all | solution.py:241
  258.0 3.8 all-to-all-start.2
  265.3 3.5 fusion.115
  273.0 3.5 fusion.116
  276.6 5.5 %bitcast_subtract_fusion.1 = f32[512,1024]{1,0:T(8,128)} fusion(f32[8,1,64,1024]{3,2,1,0:T(8,128)S(1)} %get-tuple-element.32, f32[512,1024]{1,0:T(8,128)S(1)} %bitcast.161, f32[8,1,64,1024]{3,2,1,0:T(8,128)S(1)} %copy-done.10, f32[512,1024]{1,0:T(8,128)S(1)} %fusion.115, f32[512,1024]{1,0:T(8,128)S(1)} %bitcast.167, f32[1024,1024]{1,0:T(8,128)S(1)} %copy-done.2), kind=kOutput, calls=%fused_computation.26 | convolution fusion | flops 3223846912 | bytes 16777216 | tf_op jit(solution)/shard_map/dot_general | solution.py:36
  282.1 5.8 %bitcast_subtract_fusion = f32[512,1024]{1,0:T(8,128)} fusion(f32[8,1,64,1024]{3,2,1,0:T(8,128)S(1)} %get-tuple-element.31, f32[512,1024]{1,0:T(8,128)S(1)} %bitcast.157, f32[8,1,64,1024]{3,2,1,0:T(8,128)S(1)} %copy-done.6, f32[512,1024]{1,0:T(8,128)S(1)} %fusion.116, f32[512,1024]{1,0:T(8,128)S(1)} %bitcast.165, f32[1024,1024]{1,0:T(8,128)S(1)} %copy-done.2), kind=kOutput, calls=%fused_computation.25 | convolution fusion | flops 3223846912 | bytes 16777216 | tf_op jit(solution)/shard_map/dot_general | solution.py:36
  287.9 28.3 %collective-permute-done.refs_1_ = f32[8,64,1024]{2,1,0:T(8,128)} collective-permute-done((f32[8,64,1024]{2,1,0:T(8,128)S(1)}, f32[8,64,1024]{2,1,0:T(8,128)}, u32[]{:S(2)}, u32[]{:S(2)}) %collective-permute-start) | collective-permute-done | bytes 2097184 | tf_op jit(solution)/shard_map/ppermute | solution.py:48
  316.3 5.7 %all-to-all-start.5 = ((f32[8,64,1024]{2,1,0:T(8,128)}), f32[8,64,1024]{2,1,0:T(8,128)}, u32[]{:S(2)}, u32[]{:S(2)}) async-start(f32[8,64,1024]{2,1,0:T(8,128)} %bitcast.172), calls=%async_computation.5 | async-start | bytes 4194304 | tf_op jit(solution)/shard_map/all_to_all | solution.py:241
  323.5 44.4 %collective-permute-done.3.refs_9_ = f32[8,64,1024]{2,1,0:T(8,128)} collective-permute-done((f32[8,64,1024]{2,1,0:T(8,128)S(1)}, f32[8,64,1024]{2,1,0:T(8,128)}, u32[]{:S(2)}, u32[]{:S(2)}) %collective-permute-start.3) | collective-permute-done | bytes 2097184 | tf_op jit(solution)/shard_map/ppermute | solution.py:48
  369.0 4.6 all-to-all-start.4
  375.6 45.6 %all-to-all-done.4.refs_4_ = f32[8,64,1024]{2,1,0:T(8,128)} async-done(((f32[8,64,1024]{2,1,0:T(8,128)}), f32[8,64,1024]{2,1,0:T(8,128)}, u32[]{:S(2)}, u32[]{:S(2)}) %all-to-all-start.4) | async-done | bytes 2097184 | tf_op jit(solution)/shard_map/all_to_all | solution.py:241
  424.5 42.4 %collective-permute-done.9.refs_13_ = f32[8,64,1024]{2,1,0:T(8,128)} collective-permute-done((f32[8,64,1024]{2,1,0:T(8,128)}, f32[8,64,1024]{2,1,0:T(8,128)}, u32[]{:S(2)}, u32[]{:S(2)}) %collective-permute-start.9) | collective-permute-done | bytes 2097184 | tf_op jit(solution)/shard_map/ppermute | solution.py:48
  467.5 5.9 %shard_map.75 = (f32[256,256]{1,0:T(8,128)S(1)}, f32[256,256]{1,0:T(8,128)S(1)}) custom-call(s32[1]{0:T(128)} %bitcast.1.start_ref, f32[8,64,1024]{2,1,0:T(8,128)S(1)} %all-to-all-done.2.refs_0_, f32[8,64,1024]{2,1,0:T(8,128)} %collective-permute-done.refs_1_, f32[8,64,1024]{2,1,0:T(8,128)} %collective-permute-done.1.refs_2_, ...), custom_call_target="tpu_custom_call" | custom-call | tf_op jit(solution)/shard_map/pallas_call | solution.py:111
  474.3 40.0 %psum.7 = f32[64,64]{1,0:T(8,128)S(1)} all-reduce(f32[64,64]{1,0:T(8,128)S(1)} %fusion.118), channel_id=1, replica_groups=mesh['hil'=8,'vec'=4] {'hil','vec'}, use_global_device_ids=true, to_apply=%region_0.1 | all-reduce | flops 4096 | bytes 32768 | tf_op jit(solution)/shard_map/psum | solution.py:265
  518.0 23.7 %shard_map.76 = f32[128,16,1024]{2,1,0:T(8,128)} custom-call(s32[1]{0:T(128)} %bitcast.start_ref.swap_ref, f32[64,256]{1,0:T(8,128)S(1)} %mul.232.mix_ref, f32[8,64,1024]{2,1,0:T(8,128)S(1)} %all-to-all-done.2.refs_0_, f32[8,64,1024]{2,1,0:T(8,128)} %collective-permute-done.refs_1_, f32[8,64,1024]{2,1,0:T(8,128)} %collective-permute-done.1.refs_2_, ...), custom_call_target="tpu_custom_call" | custom-call | tf_op jit(solution)/shard_map/pallas_call | solution.py:159
  (140 shorter events, 34.2 us)
Async XLA Ops:
  6.9 100.5 %all-to-all-start = ((f32[8,128,1024]{2,1,0:T(8,128)}), f32[8,128,1024]{2,1,0:T(8,128)}, u32[]{:S(2)}, u32[]{:S(2)}) async-start(f32[8,128,1024]{2,1,0:T(8,128)} %shard_map.73), calls=%async_computation | async-start | bytes 8388608 | tf_op jit(solution)/shard_map/all_to_all | solution.py:205
  14.1 7.0 %copy-start.18 = (f32[10]{0:T(128)S(1)}, f32[10]{0:T(128)}, u32[]{:S(2)}) copy-start(f32[10]{0:T(128)} %param.11) | copy-start | bytes 124
  14.2 7.2 %copy-start.15 = (s32[10,1024]{1,0:T(8,128)S(1)}, s32[10,1024]{1,0:T(8,128)}, u32[]{:S(2)}) copy-start(s32[10,1024]{1,0:T(8,128)} %param.10) | copy-start | bytes 122884
  14.2 7.4 %copy-start.16 = (s32[10,1024]{1,0:T(8,128)S(1)}, s32[10,1024]{1,0:T(8,128)}, u32[]{:S(2)}) copy-start(s32[10,1024]{1,0:T(8,128)} %param.9) | copy-start | bytes 122884
  14.2 9.7 %copy-start.17 = (f32[10]{0:T(128)S(1)}, f32[10]{0:T(128)}, u32[]{:S(2)}) copy-start(f32[10]{0:T(128)} %param.12) | copy-start | bytes 124
  107.4 97.1 %all-to-all-start.1 = ((f32[8,128,1024]{2,1,0:T(8,128)}), f32[8,128,1024]{2,1,0:T(8,128)}, u32[]{:S(2)}, u32[]{:S(2)}) async-start(f32[8,128,1024]{2,1,0:T(8,128)} %shard_map.74), calls=%async_computation.1 | async-start | bytes 8388608 | tf_op jit(solution)/shard_map/all_to_all | solution.py:205
  117.4 3.7 copy-start.11
  118.0 43.1 %copy-start.7 = (f32[8,1,64,1024]{3,2,1,0:T(8,128)}, f32[8,1,64,1024]{3,2,1,0:T(8,128)S(1)}, u32[]{:S(2)}) copy-start(f32[8,1,64,1024]{3,2,1,0:T(8,128)S(1)} %get-tuple-element.34) | copy-start | bytes 6291460
  118.0 48.7 %copy-start.3 = (f32[8,1,64,1024]{3,2,1,0:T(8,128)}, f32[8,1,64,1024]{3,2,1,0:T(8,128)S(1)}, u32[]{:S(2)}) copy-start(f32[8,1,64,1024]{3,2,1,0:T(8,128)S(1)} %get-tuple-element.33) | copy-start | bytes 6291460
  121.1 3.7 copy-start
  121.7 39.5 %copy-start.9 = (f32[8,1,64,1024]{3,2,1,0:T(8,128)}, f32[8,1,64,1024]{3,2,1,0:T(8,128)S(1)}, u32[]{:S(2)}) copy-start(f32[8,1,64,1024]{3,2,1,0:T(8,128)S(1)} %get-tuple-element.36) | copy-start | bytes 6291460
  121.7 45.0 %copy-start.5 = (f32[8,1,64,1024]{3,2,1,0:T(8,128)}, f32[8,1,64,1024]{3,2,1,0:T(8,128)S(1)}, u32[]{:S(2)}) copy-start(f32[8,1,64,1024]{3,2,1,0:T(8,128)S(1)} %get-tuple-element.35) | copy-start | bytes 6291460
  204.6 52.0 %all-to-all-start.3 = ((f32[8,64,1024]{2,1,0:T(8,128)}), f32[8,64,1024]{2,1,0:T(8,128)S(1)}, u32[]{:S(2)}, u32[]{:S(2)}) async-start(f32[8,64,1024]{2,1,0:T(8,128)} %bitcast.171), calls=%async_computation.3 | async-start | bytes 4194304 | tf_op jit(solution)/shard_map/all_to_all | solution.py:241
  208.2 10.7 %copy-start.12 = (f32[1024,1024]{1,0:T(8,128)S(1)}, f32[1024,1024]{1,0:T(8,128)}, u32[]{:S(2)}) copy-start(f32[1024,1024]{1,0:T(8,128)} %convolution_add_fusion) | copy-start | bytes 12582916
  258.0 58.3 %all-to-all-start.2 = ((f32[8,64,1024]{2,1,0:T(8,128)}), f32[8,64,1024]{2,1,0:T(8,128)S(1)}, u32[]{:S(2)}, u32[]{:S(2)}) async-start(f32[8,64,1024]{2,1,0:T(8,128)} %bitcast.169), calls=%async_computation.2 | async-start | bytes 4194304 | tf_op jit(solution)/shard_map/all_to_all | solution.py:241
  268.8 47.4 %collective-permute-start = (f32[8,64,1024]{2,1,0:T(8,128)S(1)}, f32[8,64,1024]{2,1,0:T(8,128)}, u32[]{:S(2)}, u32[]{:S(2)}) collective-permute-start(f32[8,64,1024]{2,1,0:T(8,128)S(1)} %copy-done.14), channel_id=1, source_target_pairs={{0,2},{1,3},{2,0},{3,1},{4,6},{5,7},{6,4},{7,5},{8,10},{9,11},{10,... | collective-permute-start | bytes 6291464 | tf_op jit(solution)/shard_map/ppermute | solution.py:48
  276.5 5.5 %copy-start.4 = (f32[8,1,64,1024]{3,2,1,0:T(8,128)S(1)}, f32[8,1,64,1024]{3,2,1,0:T(8,128)}, u32[]{:S(2)}) copy-start(f32[8,1,64,1024]{3,2,1,0:T(8,128)} %copy-done.3) | copy-start | bytes 6291460
  276.6 5.5 %copy-start.6 = (f32[8,1,64,1024]{3,2,1,0:T(8,128)S(1)}, f32[8,1,64,1024]{3,2,1,0:T(8,128)}, u32[]{:S(2)}) copy-start(f32[8,1,64,1024]{3,2,1,0:T(8,128)} %copy-done.5) | copy-start | bytes 6291460
  287.9 135.5 %copy-start.19 = (s32[4]{0:T(128)S(1)}, s32[4]{0:T(128)}, u32[]{:S(2)}) copy-start(s32[4]{0:T(128)} %constant.86.clone) | copy-start | bytes 52
  316.3 52.8 %all-to-all-start.5 = ((f32[8,64,1024]{2,1,0:T(8,128)}), f32[8,64,1024]{2,1,0:T(8,128)}, u32[]{:S(2)}, u32[]{:S(2)}) async-start(f32[8,64,1024]{2,1,0:T(8,128)} %bitcast.172), calls=%async_computation.5 | async-start | bytes 4194304 | tf_op jit(solution)/shard_map/all_to_all | solution.py:241
  322.0 45.9 %collective-permute-start.3 = (f32[8,64,1024]{2,1,0:T(8,128)S(1)}, f32[8,64,1024]{2,1,0:T(8,128)}, u32[]{:S(2)}, u32[]{:S(2)}) collective-permute-start(f32[8,64,1024]{2,1,0:T(8,128)S(1)} %all-to-all-done.2.refs_0_), channel_id=1, source_target_pairs={{0,2},{1,3},{2,0},{3,1},{4,6},{5,7},{6,4},{7,5},{8,10},{9,11},{10,... | collective-permute-start | bytes 6291464 | tf_op jit(solution)/shard_map/ppermute | solution.py:48
  369.0 52.2 %all-to-all-start.4 = ((f32[8,64,1024]{2,1,0:T(8,128)}), f32[8,64,1024]{2,1,0:T(8,128)}, u32[]{:S(2)}, u32[]{:S(2)}) async-start(f32[8,64,1024]{2,1,0:T(8,128)} %bitcast.170), calls=%async_computation.4 | async-start | bytes 4194304 | tf_op jit(solution)/shard_map/all_to_all | solution.py:241
  373.6 49.1 %collective-permute-start.4 = (f32[8,64,1024]{2,1,0:T(8,128)}, f32[8,64,1024]{2,1,0:T(8,128)}, u32[]{:S(2)}, u32[]{:S(2)}) collective-permute-start(f32[8,64,1024]{2,1,0:T(8,128)} %all-to-all-done.5.refs_12_), channel_id=1, source_target_pairs={{0,2},{1,3},{2,0},{3,1},{4,6},{5,7},{6,4},{7,5},{8,10},{9,11},{10,... | collective-permute-start | bytes 6291464 | tf_op jit(solution)/shard_map/ppermute | solution.py:48
  375.1 48.8 %collective-permute-start.1 = (f32[8,64,1024]{2,1,0:T(8,128)S(1)}, f32[8,64,1024]{2,1,0:T(8,128)}, u32[]{:S(2)}, u32[]{:S(2)}) collective-permute-start(f32[8,64,1024]{2,1,0:T(8,128)S(1)} %all-to-all-done.2.refs_0_), channel_id=1, source_target_pairs={{0,1},{1,0},{2,3},{3,2},{4,5},{5,4},{6,7},{7,6},{8,9},{9,8},{10,11... | collective-permute-start | bytes 6291464 | tf_op jit(solution)/shard_map/ppermute | solution.py:48
  375.1 48.9 %collective-permute-start.2 = (f32[8,64,1024]{2,1,0:T(8,128)}, f32[8,64,1024]{2,1,0:T(8,128)}, u32[]{:S(2)}, u32[]{:S(2)}) collective-permute-start(f32[8,64,1024]{2,1,0:T(8,128)} %collective-permute-done.refs_1_), channel_id=1, source_target_pairs={{0,1},{1,0},{2,3},{3,2},{4,5},{5,4},{6,7},{7,6},{8,9},{9,8},{10,11... | collective-permute-start | bytes 6291464 | tf_op jit(solution)/shard_map/ppermute | solution.py:48
  421.2 45.8 %collective-permute-start.9 = (f32[8,64,1024]{2,1,0:T(8,128)}, f32[8,64,1024]{2,1,0:T(8,128)}, u32[]{:S(2)}, u32[]{:S(2)}) collective-permute-start(f32[8,64,1024]{2,1,0:T(8,128)} %all-to-all-done.4.refs_4_), channel_id=1, source_target_pairs={{0,2},{1,3},{2,0},{3,1},{4,6},{5,7},{6,4},{7,5},{8,10},{9,11},{10,... | collective-permute-start | bytes 6291464 | tf_op jit(solution)/shard_map/ppermute | solution.py:48
  422.7 44.3 %collective-permute-start.5 = (f32[8,64,1024]{2,1,0:T(8,128)}, f32[8,64,1024]{2,1,0:T(8,128)}, u32[]{:S(2)}, u32[]{:S(2)}) collective-permute-start(f32[8,64,1024]{2,1,0:T(8,128)} %all-to-all-done.4.refs_4_), channel_id=1, source_target_pairs={{0,1},{1,0},{2,3},{3,2},{4,5},{5,4},{6,7},{7,6},{8,9},{9,8},{10,11... | collective-permute-start | bytes 6291464 | tf_op jit(solution)/shard_map/ppermute | solution.py:48
  422.7 44.8 %collective-permute-start.6 = (f32[8,64,1024]{2,1,0:T(8,128)}, f32[8,64,1024]{2,1,0:T(8,128)}, u32[]{:S(2)}, u32[]{:S(2)}) collective-permute-start(f32[8,64,1024]{2,1,0:T(8,128)} %collective-permute-done.4.refs_5_), channel_id=1, source_target_pairs={{0,1},{1,0},{2,3},{3,2},{4,5},{5,4},{6,7},{7,6},{8,9},{9,8},{10,11... | collective-permute-start | bytes 6291464 | tf_op jit(solution)/shard_map/ppermute | solution.py:48
  424.0 94.0 %collective-permute-start.7 = (f32[8,64,1024]{2,1,0:T(8,128)}, f32[8,64,1024]{2,1,0:T(8,128)}, u32[]{:S(2)}, u32[]{:S(2)}) collective-permute-start(f32[8,64,1024]{2,1,0:T(8,128)} %copy-done.13), channel_id=1, source_target_pairs={{0,1},{1,0},{2,3},{3,2},{4,5},{5,4},{6,7},{7,6},{8,9},{9,8},{10,11... | collective-permute-start | bytes 6291464 | tf_op jit(solution)/shard_map/ppermute | solution.py:48
  424.0 93.9 %collective-permute-start.8 = (f32[8,64,1024]{2,1,0:T(8,128)}, f32[8,64,1024]{2,1,0:T(8,128)}, u32[]{:S(2)}, u32[]{:S(2)}) collective-permute-start(f32[8,64,1024]{2,1,0:T(8,128)} %collective-permute-done.3.refs_9_), channel_id=1, source_target_pairs={{0,1},{1,0},{2,3},{3,2},{4,5},{5,4},{6,7},{7,6},{8,9},{9,8},{10,11... | collective-permute-start | bytes 6291464 | tf_op jit(solution)/shard_map/ppermute | solution.py:48
  467.0 51.0 %collective-permute-start.10 = (f32[8,64,1024]{2,1,0:T(8,128)}, f32[8,64,1024]{2,1,0:T(8,128)}, u32[]{:S(2)}, u32[]{:S(2)}) collective-permute-start(f32[8,64,1024]{2,1,0:T(8,128)} %all-to-all-done.5.refs_12_), channel_id=1, source_target_pairs={{0,1},{1,0},{2,3},{3,2},{4,5},{5,4},{6,7},{7,6},{8,9},{9,8},{10,11... | collective-permute-start | bytes 6291464 | tf_op jit(solution)/shard_map/ppermute | solution.py:48
  467.0 51.0 %collective-permute-start.11 = (f32[8,64,1024]{2,1,0:T(8,128)}, f32[8,64,1024]{2,1,0:T(8,128)}, u32[]{:S(2)}, u32[]{:S(2)}) collective-permute-start(f32[8,64,1024]{2,1,0:T(8,128)} %collective-permute-done.9.refs_13_), channel_id=1, source_target_pairs={{0,1},{1,0},{2,3},{3,2},{4,5},{5,4},{6,7},{7,6},{8,9},{9,8},{10,11... | collective-permute-start | bytes 6291464 | tf_op jit(solution)/shard_map/ppermute | solution.py:48
  (6 other events, 19.1 us)

commit v3 on v2

--- a/solution.py
+++ b/solution.py
@@ -10,6 +10,7 @@
 
 DEGREE = 2
 NS_ITERS = 4
+SUBLANES = 8
 STACK = 4
 
 highest = lax.Precision.HIGHEST
@@ -124,52 +125,61 @@
     return sum(total[u, :, u, :] for u in range(STACK))
 
 
-def rotate_kernel(half_blocks, swap_ref, mix_ref, *refs):
-    inputs, out_ref = refs[:-1], refs[-1]
+def rotate_kernel(swap_ref, mix_ref, *refs):
+    inputs, out_ref = [ref for ref in refs[:-1] if ref.ndim == 3 and ref.shape[1] == SUBLANES], refs[-1]
+    columns = out_ref.shape[2]
     mix_top, mix_low = split(mix_ref[...])
     count = mix_top.shape[0]
     both = jnp.concatenate([mix_top, mix_low], axis=0)
-
-    def run(half):
-        values = stacked(half)
-        rows, vectors, columns = values.shape
-        for first in range(0, rows, STACK):
-            top, low = split(values[first : first + STACK].reshape(STACK * vectors, columns))
-            wide = dot(both, top, (1, 0), None)
-            result = wide[:count] + wide[count:] + dot(mix_top, low, (1, 0), None)
-            out_ref[first : first + STACK] = result.reshape(STACK, count // STACK, result.shape[1])
-
-    pl.when(pl.program_id(0) < half_blocks)(lambda: run(inputs[: len(inputs) // 2]))
-    pl.when(pl.program_id(0) >= half_blocks)(lambda: run(inputs[len(inputs) // 2 :]))
-
-
-def rotate(halves, mixing, swapped):
-    half_rows, down_count = halves[0][0].shape[1:]
-    block = 8
-    half_blocks = half_rows // block
-    own = mixing.shape[1]
-    wide_mixing = jnp.kron(jnp.eye(STACK, dtype=jnp.float32), mixing.T)
+    top, low = split(jnp.concatenate([ref[...].reshape(-1, columns) for ref in inputs], axis=0))
+    wide = dot(both, top, (1, 0), None)
+    result = wide[:count] + wide[count:] + dot(mix_top, low, (1, 0), None)
+    out_ref[...] = jnp.swapaxes(result.reshape(-1, SUBLANES, columns), 0, 1)
+
+
+def rotate_half(pieces, wide_mixing, swapped, half, earlier):
+    half_rows, down_count = pieces[0].shape[1:]
+    blocks = half_rows // SUBLANES
+    own = wide_mixing.shape[0] // SUBLANES
     specs = [pl.BlockSpec(wide_mixing.shape, lambda i, swap: (0, 0))]
-    for piece in halves[0]:
-        shape = (piece.shape[0], block, down_count)
-        specs.append(pl.BlockSpec(shape, lambda i, swap: (0, jnp.minimum(i, half_blocks - 1), 0)))
-    for piece in halves[1]:
-        shape = (piece.shape[0], block, down_count)
-        specs.append(pl.BlockSpec(shape, lambda i, swap: (0, jnp.maximum(i - half_blocks, 0), 0)))
+    for piece in pieces:
+        specs.append(pl.BlockSpec((piece.shape[0], SUBLANES, down_count), lambda i, swap: (0, i, 0)))
+    operands = [swapped, wide_mixing, *pieces]
+    aliases = {}
+    if earlier is not None:
+        specs.append(pl.BlockSpec(memory_space=pl.ANY))
+        aliases = {len(operands): 0}
+        operands.append(earlier)
     return pl.pallas_call(
-        functools.partial(rotate_kernel, half_blocks),
+        rotate_kernel,
         out_shape=jax.ShapeDtypeStruct((2 * half_rows, own, down_count), jnp.float32),
         grid_spec=pltpu.PrefetchScalarGridSpec(
             num_scalar_prefetch=1,
-            grid=(2 * half_blocks,),
+            grid=(blocks,),
             in_specs=specs,
             out_specs=pl.BlockSpec(
-                (block, own, down_count),
-                lambda i, swap: (lax.rem(i + swap[0] * half_blocks, 2 * half_blocks), 0, 0),
+                (SUBLANES, own, down_count), lambda i, swap: (i + lax.rem(swap[0] + half, 2) * blocks, 0, 0)
             ),
         ),
-        compiler_params=pltpu.CompilerParams(vmem_limit_bytes=48 * 1024 * 1024),
-    )(swapped, wide_mixing, *halves[0], *halves[1])
+        input_output_aliases=aliases,
+        compiler_params=pltpu.CompilerParams(vmem_limit_bytes=56 * 1024 * 1024),
+    )(*operands)
+
+
+def small_sum(values, axis):
+    parts = lax.axis_size(axis)
+    if parts & (parts - 1):
+        return lax.psum(values, axis)
+    step = 1
+    while step < parts:
+        count = min(4, parts // step)
+        moved = []
+        for distance in range(step, count * step, step):
+            moved.append(lax.ppermute(values, axis, [(i, i ^ distance) for i in range(parts)]))
+        for other in moved:
+            values = values + other
+        step *= count
+    return values
 
 
 def newton_schulz(gram_sum):
@@ -226,32 +236,36 @@
 
     mine, theirs = 0, 1
     once = first_step(arrived[0])
+    pieces = [second_step(once, arrived[0], half) for half in (mine, theirs)]
+    pieces[theirs], pieces[mine] = lax.optimization_barrier((pieces[theirs], pieces[mine]))
     crossed = []
     held = [[], []]
     for turn in range(rounds):
-        pieces = {half: second_step(once, arrived[turn], half) for half in (theirs, mine)}
-        pieces[theirs], pieces[mine] = lax.optimization_barrier((pieces[theirs], pieces[mine]))
+        upcoming = [None, None]
         for half in (theirs, mine):
             piece = pieces[half]
             if half == mine and turn + 1 < rounds:
                 once = first_step(arrived[turn + 1])
-                piece, once = lax.optimization_barrier((piece, once))
+                upcoming[theirs] = second_step(once, arrived[turn + 1], theirs)
+                piece, once, upcoming[theirs] = lax.optimization_barrier((piece, once, upcoming[theirs]))
+                upcoming[mine] = second_step(once, arrived[turn + 1], mine)
             if len(crossed) > 1:
-                piece, crossed[-2][0] = lax.optimization_barrier((piece, crossed[-2][0]))
+                piece, crossed[-2] = lax.optimization_barrier((piece, crossed[-2]))
             back = lax.all_to_all(piece, "hil", split_axis=0, concat_axis=0, tiled=True)
             held[half].append(back)
-            crossed.append(spread_step([back], side))
-    halves = []
-    for half in (mine, theirs):
-        arrays = []
-        for turn in range(rounds):
-            near = [held[half][turn], crossed[2 * turn + (0 if half == mine else 1)][0]]
-            step = side // 2
-            while step >= 1:
-                near = near + spread_step(near, step)
-                step //= 2
-            arrays.extend(near)
-        halves.append(arrays)
+            crossed.append(spread_step([back], side)[0])
+        pieces = upcoming
+
+    def on_side(near):
+        step = side // 2
+        while step >= 1:
+            near = near + spread_step(near, step)
+            step //= 2
+        return near
+
+    halves = [[], []]
+    for turn in range(rounds):
+        halves[mine].extend(on_side([held[mine][turn], crossed[2 * turn]]))
     distances = [0, side]
     step = side // 2
     while step >= 1:
@@ -262,10 +276,17 @@
     order = jnp.kron(jnp.eye(rounds, dtype=jnp.float32), jnp.kron(exchange, jnp.eye(hil_parts, dtype=jnp.float32)))
     partial = gram_partial(halves[mine], lax.rem(own, side), side)
     partial = dot(order, dot(partial, order, (1, 0), highest), (0, 0), highest)
-    mixing = newton_schulz(lax.psum(partial, ("hil", "vec")))
+    gram_sum = small_sum(small_sum(partial, "vec"), "hil")
+    gram_sum, crossed[-1] = lax.optimization_barrier((gram_sum, crossed[-1]))
+    for turn in range(rounds):
+        halves[theirs].extend(on_side([held[theirs][turn], crossed[2 * turn + 1]]))
+    mixing = newton_schulz(gram_sum)
     mixing = dot(dot(order, mixing, (1, 0), highest), order, (1, 1), highest)
     mixing = mixing.reshape(-1, rounds, vec_parts, hil_parts)[:, :, 0].reshape(-1, vec_local)
-    return rotate(halves, mixing * math.sqrt(up_count * down_count), swapped)
+    mixing = mixing * math.sqrt(up_count * down_count)
+    wide_mixing = jnp.kron(mixing.T, jnp.eye(SUBLANES, dtype=jnp.float32))
+    result = rotate_half(halves[mine], wide_mixing, swapped, mine, None)
+    return rotate_half(halves[theirs], wide_mixing, swapped, theirs, result)
 
 
 def split_down(local_block):

time: 551 us -> 520 us (0.944)
  blocking collectives: 40 us -> 0 us
  starting transfers between devices: 37.8 us -> 46.8 us
  waiting for transfers between devices: 283 us -> 274 us
  local copies, waits for them, and re-layouts: 21.2 us -> 27.6 us
    psum x1 -> x0, blocking collectives: 40 us -> none  [vector_cut(): mixing = newton_schulz(lax.psum(partial, ('hil', 'vec')))]
    ppermute x0 -> x7, waiting for transfers between devices: none -> 38.3 us  [small_sum(): lax.ppermute(values, axis, [(i, i ^ distance) for i in range(parts)])]
    ppermute x12, waiting for transfers between devices: 115 us -> 83.5 us  [spread_step(): return [lax.ppermute(piece, 'vec', pairs) for piece in held]]
    all_to_all x4, waiting for transfers between devices: 66.4 us -> 50.5 us  [vector_cut(): back = lax.all_to_all(piece, 'hil', split_axis=0, concat_axis=0, tiled=True)]
    ppermute x0 -> x7, starting transfers between devices: none -> 7.91 us  [small_sum(): lax.ppermute(values, axis, [(i, i ^ distance) for i in range(parts)])]
    slice x6 -> x7, local copies, waits for them, and re-layouts: 9.49 us -> 11.5 us  [rows(): values.reshape(hil_parts, 2, half_rows, -1)[:, half]]
    pallas_call x1 -> x2, Pallas kernels: 23.7 us -> 23.1 us  [rotate_half(): pl.pallas_call(rotate_kernel, out_shape=jax.ShapeDtypeStruct((2 * half_ro...]
  transfers between devices with their start and end apart: 18 -> 25, of which waited for: 8 -> 14; matrix products, arithmetic and copies ran while one was open for 24% -> 27% of each run, Pallas kernels for 2% -> 5%
where the time goes in v3:
time: 520 us; the launch traced here: 511 us
  waiting for transfers between devices  274 us (53%)
  matrix products  108 us (21%)
  starting transfers between devices  46.8 us (9%)
  Pallas kernels  42.8 us (8%)
  local copies, waits for them, and re-layouts  27.6 us (5%)
  other arithmetic  9.3 us (2%)
    dot_general x25, matrix products, dot(): lax.dot_general(left, right, ((contract[:1], contract[1:]), ((), ())), pr...  103 us
    all_to_all x2, waiting for transfers between devices, vector_cut(): lax.all_to_all(block, 'hil', split_axis=0, concat_axis=0, tiled=True)  102 us
    ppermute x12, waiting for transfers between devices, spread_step(): return [lax.ppermute(piece, 'vec', pairs) for piece in held]  83.5 us
    all_to_all x4, waiting for transfers between devices, vector_cut(): back = lax.all_to_all(piece, 'hil', split_axis=0, concat_axis=0, tiled=True)  50.5 us
    ppermute x7, waiting for transfers between devices, small_sum(): lax.ppermute(values, axis, [(i, i ^ distance) for i in range(parts)])  38.3 us
    pallas_call x2, Pallas kernels, rotate_half(): pl.pallas_call(rotate_kernel, out_shape=jax.ShapeDtypeStruct((2 * half_ro...  23.1 us
    all_to_all x4, starting transfers between devices, vector_cut(): back = lax.all_to_all(piece, 'hil', split_axis=0, concat_axis=0, tiled=True)  19.2 us
    pallas_call x2, Pallas kernels, vectors_first(): pl.pallas_call(vectors_first_kernel, out_shape=jax.ShapeDtypeStruct((coun...  13.9 us
  transfers between devices with their start and end apart: 25, of which 14 were waited for; matrix products, arithmetic and copies ran while one was open for 27% of the time, Pallas kernels for 5%

profile of v3, /device:TPU:0, one launch (start us, length us, event | category | flops | bytes accessed | tf_op | source)
XLA Modules:
  0.0 510.9 jit_solution(15672025923309475210)
XLA Ops:
  0.0 6.9 %shard_map.73 = f32[8,128,1024]{2,1,0:T(8,128)} custom-call(s32[1]{0:T(128)} %bitcast.start_ref.swap_ref, f32[128,16,1024]{2,1,0:T(8,128)} %block_ref.3), custom_call_target="tpu_custom_call" | custom-call | tf_op jit(solution)/shard_map/pallas_call | solution.py:65
  6.9 7.3 %all-to-all-start = ((f32[8,128,1024]{2,1,0:T(8,128)}), f32[8,128,1024]{2,1,0:T(8,128)}, u32[]{:S(2)}, u32[]{:S(2)}) async-start(f32[8,128,1024]{2,1,0:T(8,128)} %shard_map.73), calls=%async_computation | async-start | bytes 8388608 | tf_op jit(solution)/shard_map/all_to_all | solution.py:215
  14.2 7.0 %shard_map.74 = f32[8,128,1024]{2,1,0:T(8,128)} custom-call(s32[1]{0:T(128)} %bitcast.start_ref.swap_ref, f32[128,16,1024]{2,1,0:T(8,128)} %block_ref.3), custom_call_target="tpu_custom_call" | custom-call | tf_op jit(solution)/shard_map/pallas_call | solution.py:65
  23.8 5.3 %convolution_add_fusion = f32[1024,1024]{1,0:T(8,128)} fusion(f32[10]{0:T(128)S(1)} %copy-done.18, s32[1024]{0:T(1024)S(1)} %shift_right_arithmetic.28), kind=kOutput, calls=%fused_computation.24 | convolution fusion | flops 126949376 | bytes 4198440 | tf_op jit(solution)/shard_map/dot_general | solution.py:220
  29.1 78.4 %all-to-all-done = f32[8,128,1024]{2,1,0:T(8,128)} async-done(((f32[8,128,1024]{2,1,0:T(8,128)}), f32[8,128,1024]{2,1,0:T(8,128)}, u32[]{:S(2)}, u32[]{:S(2)}) %all-to-all-start) | async-done | bytes 4194336 | tf_op jit(solution)/shard_map/all_to_all | solution.py:215
  107.4 4.6 all-to-all-start.1
  112.0 5.4 %select_add_fusion = f32[8,2,64,1024]{3,2,1,0:T(8,128)S(1)} fusion(f32[8,2,64]{2,1,0:T(2,128)S(1)} %get-tuple-element.69, s32[8,2,64]{2,1,0:T(2,128)S(1)} %get-tuple-element.50, f32[8,2,64]{2,1,0:T(2,128)S(1)} %get-tuple-element.68, s32[8,2,64]{2,1,0:T(2,128)S(1)} %get-tuple-element.49, f32[8,2,64]{2,1,0:T(2,128)S(1)} %get-tuple-element.67, ...), kind=kLoop, calls=%fused_computation.1 | loop fusion | flops 30408704 | bytes 4276224 | tf_op jit(solution)/shard_map/add | solution.py:32
  124.1 8.9 %fusion.109 = f32[1024,1024]{1,0:T(8,128)S(1)} fusion(f32[1024,1024]{1,0:T(8,128)} %bitcast.2, f32[1024,1024]{1,0:T(8,128)S(1)} %copy-done.1), kind=kOutput, calls=%fused_computation.198 | convolution fusion | flops 6442450944 | bytes 12582912 | tf_op jit(solution)/shard_map/dot_general | solution.py:37
  133.0 17.0 %add_multiply_fusion.1 = f32[1024,1024]{1,0:T(8,128)S(1)} fusion(f32[1024,1024]{1,0:T(8,128)S(1)} %copy-done.12, f32[1024,1024]{1,0:T(8,128)} %bitcast.2, f32[1024,1024]{1,0:T(8,128)S(1)} %fusion.109, f32[1024]{0:T(1024)S(1)} %broadcast_in_dim.176, s32[1024]{0:T(1024)S(1)} %eq.342, f32[1024]{0:T(1024)S(1)} %broadcast_in_dim.174, s32[1024]{0:T(1024)S(1)} %eq.338, ...), kind=kOutput, calls=%fused_computation.12 | convolution fusion | flops 6477053952 | bytes 16859136 | tf_op jit(solution)/shard_map/dot_general | solution.py:37
  153.2 3.6 fusion.111
  156.8 3.6 fusion.110
  160.5 5.5 %bitcast_subtract_fusion.2 = f32[512,1024]{1,0:T(8,128)} fusion(f32[8,1,64,1024]{3,2,1,0:T(8,128)S(1)} %get-tuple-element.39, f32[512,1024]{1,0:T(8,128)S(1)} %bitcast.167, f32[8,1,64,1024]{3,2,1,0:T(8,128)S(1)} %get-tuple-element.35, f32[512,1024]{1,0:T(8,128)S(1)} %fusion.111, f32[512,1024]{1,0:T(8,128)S(1)} %bitcast.168, ...), kind=kOutput, calls=%fused_computation.27 | convolution fusion | flops 3223846912 | bytes 16777216 | tf_op jit(solution)/shard_map/dot_general | solution.py:37
  166.0 15.0 %bitcast_subtract_fusion.3 = f32[512,1024]{1,0:T(8,128)} fusion(f32[8,1,64,1024]{3,2,1,0:T(8,128)S(1)} %get-tuple-element.40, f32[512,1024]{1,0:T(8,128)S(1)} %bitcast.165, f32[8,1,64,1024]{3,2,1,0:T(8,128)S(1)} %get-tuple-element.36, f32[512,1024]{1,0:T(8,128)S(1)} %fusion.110, f32[512,1024]{1,0:T(8,128)S(1)} %bitcast.170, ...), kind=kOutput, calls=%fused_computation.34 | convolution fusion | flops 3223846912 | bytes 16777216 | tf_op jit(solution)/shard_map/dot_general | solution.py:37
  181.0 23.5 %all-to-all-done.1 = f32[8,128,1024]{2,1,0:T(8,128)} async-done(((f32[8,128,1024]{2,1,0:T(8,128)}), f32[8,128,1024]{2,1,0:T(8,128)}, u32[]{:S(2)}, u32[]{:S(2)}) %all-to-all-start.1) | async-done | bytes 4194336 | tf_op jit(solution)/shard_map/all_to_all | solution.py:215
  204.6 4.3 all-to-all-start.3
  208.9 10.6 %fusion.112 = f32[1024,1024]{1,0:T(8,128)S(1)} fusion(f32[1024,1024]{1,0:T(8,128)} %bitcast.36, f32[1024,1024]{1,0:T(8,128)} %param.8), kind=kOutput, calls=%fused_computation.201 | convolution fusion | flops 6442450944 | bytes 12582912 | tf_op jit(solution)/shard_map/dot_general | solution.py:37
  219.6 17.0 %add_multiply_fusion = f32[1024,1024]{1,0:T(8,128)S(1)} fusion(f32[1024,1024]{1,0:T(8,128)S(1)} %copy-done.13, f32[1024,1024]{1,0:T(8,128)} %bitcast.36, f32[1024,1024]{1,0:T(8,128)S(1)} %fusion.112, f32[1024]{0:T(1024)S(1)} %broadcast_in_dim.176, s32[1024]{0:T(1024)S(1)} %eq.342, f32[1024]{0:T(1024)S(1)} %broadcast_in_dim.174, s32[1024]{0:T(1024)S(1)} %eq.338, ...), kind=kOutput, calls=%fused_computation | convolution fusion | flops 6477053952 | bytes 16859136 | tf_op jit(solution)/shard_map/dot_general | solution.py:37
  236.8 5.4 %fusion.104 = (f32[8,1,64,1024]{3,2,1,0:T(8,128)}, f32[8,1,64,1024]{3,2,1,0:T(8,128)S(1)}) fusion(f32[8,2,64,1024]{3,2,1,0:T(8,128)} %bitcast.39), kind=kLoop, calls=%fused_computation.193 | loop fusion | bytes 8388608 | tf_op jit(solution)/shard_map/slice | solution.py:228
  245.8 5.5 %bitcast_subtract_fusion.1 = f32[512,1024]{1,0:T(8,128)} fusion(f32[8,1,64,1024]{3,2,1,0:T(8,128)S(1)} %get-tuple-element.32, f32[512,1024]{1,0:T(8,128)S(1)} %bitcast.161, f32[8,1,64,1024]{3,2,1,0:T(8,128)S(1)} %copy-done.11, f32[512,1024]{1,0:T(8,128)S(1)} %fusion.113, f32[512,1024]{1,0:T(8,128)S(1)} %bitcast.171, f32[1024,1024]{1,0:T(8,128)S(1)} %add_multiply_fusion), kind=kOutput, calls=%fused_computation.26 | convolution fusion | flops 3223846912 | bytes 16777216 | tf_op jit(solution)/shard_map/dot_general | solution.py:37
  251.3 5.4 %all-to-all-done.3.refs_0_ = f32[8,64,1024]{2,1,0:T(8,128)} async-done(((f32[8,64,1024]{2,1,0:T(8,128)}), f32[8,64,1024]{2,1,0:T(8,128)}, u32[]{:S(2)}, u32[]{:S(2)}) %all-to-all-start.3) | async-done | bytes 2097184 | tf_op jit(solution)/shard_map/all_to_all | solution.py:254
  261.9 46.0 %collective-permute-done.refs_1_ = f32[8,64,1024]{2,1,0:T(8,128)} collective-permute-done((f32[8,64,1024]{2,1,0:T(8,128)}, f32[8,64,1024]{2,1,0:T(8,128)}, u32[]{:S(2)}, u32[]{:S(2)}) %collective-permute-start) | collective-permute-done | bytes 2097184 | tf_op jit(solution)/shard_map/ppermute | solution.py:49
  308.8 5.2 %all-to-all-start.5 = ((f32[8,64,1024]{2,1,0:T(8,128)}), f32[8,64,1024]{2,1,0:T(8,128)}, u32[]{:S(2)}, u32[]{:S(2)}) async-start(f32[8,64,1024]{2,1,0:T(8,128)} %bitcast.175), calls=%async_computation.5 | async-start | bytes 4194304 | tf_op jit(solution)/shard_map/all_to_all | solution.py:254
  317.3 3.7 fusion.114
  321.1 6.5 %bitcast_subtract_fusion = f32[512,1024]{1,0:T(8,128)} fusion(f32[8,1,64,1024]{3,2,1,0:T(8,128)} %get-tuple-element.31, f32[512,1024]{1,0:T(8,128)S(1)} %bitcast.163, f32[8,1,64,1024]{3,2,1,0:T(8,128)S(1)} %copy-done.9, f32[512,1024]{1,0:T(8,128)S(1)} %fusion.114, f32[512,1024]{1,0:T(8,128)S(1)} %bitcast.169, f32[1024,1024]{1,0:T(8,128)S(1)} %copy-done.5), kind=kOutput, calls=%fused_computation.25 | convolution fusion | flops 3223846912 | bytes 16777216 | tf_op jit(solution)/shard_map/dot_general | solution.py:37
  327.6 32.5 %collective-permute-done.3.refs_1_ = f32[8,64,1024]{2,1,0:T(8,128)S(1)} collective-permute-done((f32[8,64,1024]{2,1,0:T(8,128)S(1)}, f32[8,64,1024]{2,1,0:T(8,128)S(1)}, u32[]{:S(2)}, u32[]{:S(2)}) %collective-permute-start.3) | collective-permute-done | bytes 2097184 | tf_op jit(solution)/shard_map/ppermute | solution.py:49
  361.4 6.1 %all-to-all-start.4 = ((f32[8,64,1024]{2,1,0:T(8,128)}), f32[8,64,1024]{2,1,0:T(8,128)}, u32[]{:S(2)}, u32[]{:S(2)}) async-start(f32[8,64,1024]{2,1,0:T(8,128)} %bitcast.176), calls=%async_computation.4 | async-start | bytes 4194304 | tf_op jit(solution)/shard_map/all_to_all | solution.py:254
  369.6 44.2 %all-to-all-done.4.refs_4_ = f32[8,64,1024]{2,1,0:T(8,128)} async-done(((f32[8,64,1024]{2,1,0:T(8,128)}), f32[8,64,1024]{2,1,0:T(8,128)}, u32[]{:S(2)}, u32[]{:S(2)}) %all-to-all-start.4) | async-done | bytes 2097184 | tf_op jit(solution)/shard_map/all_to_all | solution.py:254
  421.3 5.9 %shard_map.75 = (f32[256,256]{1,0:T(8,128)S(1)}, f32[256,256]{1,0:T(8,128)S(1)}) custom-call(s32[1]{0:T(128)} %bitcast.1.start_ref, f32[8,64,1024]{2,1,0:T(8,128)S(1)} %all-to-all-done.2.refs_0_, f32[8,64,1024]{2,1,0:T(8,128)} %collective-permute-done.refs_1_, f32[8,64,1024]{2,1,0:T(8,128)} %collective-permute-done.1.refs_2_, ...), custom_call_target="tpu_custom_call" | custom-call | tf_op jit(solution)/shard_map/pallas_call | solution.py:112
  430.1 33.1 %collective-permute-done.8 = f32[64,64]{1,0:T(8,128)S(1)} collective-permute-done((f32[64,64]{1,0:T(8,128)S(1)}, f32[64,64]{1,0:T(8,128)S(1)}, u32[]{:S(2)}, u32[]{:S(2)}) %collective-permute-start.8) | collective-permute-done | bytes 16416 | tf_op jit(solution)/shard_map/ppermute | solution.py:178
  481.3 4.6 mul.232.mix_ref
  485.9 11.6 %shard_map.76.refs_8_ = f32[128,16,1024]{2,1,0:T(8,128)} custom-call(s32[1]{0:T(128)} %bitcast.start_ref.swap_ref, f32[128,512]{1,0:T(8,128)} %mul.232.mix_ref, f32[8,64,1024]{2,1,0:T(8,128)} %copy-done, f32[8,64,1024]{2,1,0:T(8,128)} %collective-permute-done.refs_1_, f32[8,64,1024]{2,1,0:T(8,128)} %collective-permute-done.1.refs_2_, ...), custom_call_target="tpu_custom_call" | custom-call | tf_op jit(solution)/shard_map/pallas_call | solution.py:153
  498.9 11.5 %shard_map.77 = f32[128,16,1024]{2,1,0:T(8,128)} custom-call(s32[1]{0:T(128)} %bitcast.start_ref.swap_ref, f32[128,512]{1,0:T(8,128)} %mul.232.mix_ref, f32[8,64,1024]{2,1,0:T(8,128)} %all-to-all-done.3.refs_0_, f32[8,64,1024]{2,1,0:T(8,128)} %copy-done.14, f32[8,64,1024]{2,1,0:T(8,128)} %copy-done.15, ...), custom_call_target="tpu_custom_call", output_to_operand_aliasing={{}: (10, {})} | custom-call | tf_op jit(solution)/shard_map/pallas_call | solution.py:153
  (159 shorter events, 57.8 us)
Async XLA Ops:
  6.9 100.5 %all-to-all-start = ((f32[8,128,1024]{2,1,0:T(8,128)}), f32[8,128,1024]{2,1,0:T(8,128)}, u32[]{:S(2)}, u32[]{:S(2)}) async-start(f32[8,128,1024]{2,1,0:T(8,128)} %shard_map.73), calls=%async_computation | async-start | bytes 8388608 | tf_op jit(solution)/shard_map/all_to_all | solution.py:215
  14.2 9.6 %copy-start.18 = (f32[10]{0:T(128)S(1)}, f32[10]{0:T(128)}, u32[]{:S(2)}) copy-start(f32[10]{0:T(128)} %param.12) | copy-start | bytes 124
  107.4 97.1 %all-to-all-start.1 = ((f32[8,128,1024]{2,1,0:T(8,128)}), f32[8,128,1024]{2,1,0:T(8,128)}, u32[]{:S(2)}, u32[]{:S(2)}) async-start(f32[8,128,1024]{2,1,0:T(8,128)} %shard_map.74), calls=%async_computation.1 | async-start | bytes 8388608 | tf_op jit(solution)/shard_map/all_to_all | solution.py:215
  117.9 42.6 %copy-start.6 = (f32[8,1,64,1024]{3,2,1,0:T(8,128)}, f32[8,1,64,1024]{3,2,1,0:T(8,128)S(1)}, u32[]{:S(2)}) copy-start(f32[8,1,64,1024]{3,2,1,0:T(8,128)S(1)} %get-tuple-element.33) | copy-start | bytes 6291460
  121.0 39.6 %copy-start.8 = (f32[8,1,64,1024]{3,2,1,0:T(8,128)}, f32[8,1,64,1024]{3,2,1,0:T(8,128)S(1)}, u32[]{:S(2)}) copy-start(f32[8,1,64,1024]{3,2,1,0:T(8,128)S(1)} %get-tuple-element.35) | copy-start | bytes 6291460
  121.0 45.1 %copy-start.10 = (f32[8,1,64,1024]{3,2,1,0:T(8,128)}, f32[8,1,64,1024]{3,2,1,0:T(8,128)S(1)}, u32[]{:S(2)}) copy-start(f32[8,1,64,1024]{3,2,1,0:T(8,128)S(1)} %get-tuple-element.36) | copy-start | bytes 6291460
  204.6 52.2 %all-to-all-start.3 = ((f32[8,64,1024]{2,1,0:T(8,128)}), f32[8,64,1024]{2,1,0:T(8,128)}, u32[]{:S(2)}, u32[]{:S(2)}) async-start(f32[8,64,1024]{2,1,0:T(8,128)} %bitcast.174), calls=%async_computation.3 | async-start | bytes 4194304 | tf_op jit(solution)/shard_map/all_to_all | solution.py:254
  208.9 10.7 %copy-start.13 = (f32[1024,1024]{1,0:T(8,128)S(1)}, f32[1024,1024]{1,0:T(8,128)}, u32[]{:S(2)}) copy-start(f32[1024,1024]{1,0:T(8,128)} %convolution_add_fusion) | copy-start | bytes 12582916
  256.7 52.0 %all-to-all-start.2 = ((f32[8,64,1024]{2,1,0:T(8,128)}), f32[8,64,1024]{2,1,0:T(8,128)S(1)}, u32[]{:S(2)}, u32[]{:S(2)}) async-start(f32[8,64,1024]{2,1,0:T(8,128)} %bitcast.173), calls=%async_computation.2 | async-start | bytes 4194304 | tf_op jit(solution)/shard_map/all_to_all | solution.py:254
  260.3 47.6 %collective-permute-start = (f32[8,64,1024]{2,1,0:T(8,128)}, f32[8,64,1024]{2,1,0:T(8,128)}, u32[]{:S(2)}, u32[]{:S(2)}) collective-permute-start(f32[8,64,1024]{2,1,0:T(8,128)} %all-to-all-done.3.refs_0_), channel_id=1, source_target_pairs={{0,2},{1,3},{2,0},{3,1},{4,6},{5,7},{6,4},{7,5},{8,10},{9,11},{10,... | collective-permute-start | bytes 6291464 | tf_op jit(solution)/shard_map/ppermute | solution.py:49
  308.8 112.6 %copy-start = (f32[8,64,1024]{2,1,0:T(8,128)}, f32[8,64,1024]{2,1,0:T(8,128)S(1)}, u32[]{:S(2)}) copy-start(f32[8,64,1024]{2,1,0:T(8,128)S(1)} %all-to-all-done.2.refs_0_) | copy-start | bytes 6291460
  308.8 52.7 %all-to-all-start.5 = ((f32[8,64,1024]{2,1,0:T(8,128)}), f32[8,64,1024]{2,1,0:T(8,128)}, u32[]{:S(2)}, u32[]{:S(2)}) async-start(f32[8,64,1024]{2,1,0:T(8,128)} %bitcast.175), calls=%async_computation.5 | async-start | bytes 4194304 | tf_op jit(solution)/shard_map/all_to_all | solution.py:254
  314.0 46.1 %collective-permute-start.3 = (f32[8,64,1024]{2,1,0:T(8,128)S(1)}, f32[8,64,1024]{2,1,0:T(8,128)S(1)}, u32[]{:S(2)}, u32[]{:S(2)}) collective-permute-start(f32[8,64,1024]{2,1,0:T(8,128)S(1)} %all-to-all-done.2.refs_0_), channel_id=1, source_target_pairs={{0,2},{1,3},{2,0},{3,1},{4,6},{5,7},{6,4},{7,5},{8,10},{9,11},{10,... | collective-permute-start | bytes 6291464 | tf_op jit(solution)/shard_map/ppermute | solution.py:49
  327.6 86.8 %copy-start.20 = (s32[4]{0:T(128)S(1)}, s32[4]{0:T(128)}, u32[]{:S(2)}) copy-start(s32[4]{0:T(128)} %constant.86.clone) | copy-start | bytes 52
  361.4 52.4 %all-to-all-start.4 = ((f32[8,64,1024]{2,1,0:T(8,128)}), f32[8,64,1024]{2,1,0:T(8,128)}, u32[]{:S(2)}, u32[]{:S(2)}) async-start(f32[8,64,1024]{2,1,0:T(8,128)} %bitcast.176), calls=%async_computation.4 | async-start | bytes 4194304 | tf_op jit(solution)/shard_map/all_to_all | solution.py:254
  367.5 46.3 %collective-permute-start.4 = (f32[8,64,1024]{2,1,0:T(8,128)}, f32[8,64,1024]{2,1,0:T(8,128)}, u32[]{:S(2)}, u32[]{:S(2)}) collective-permute-start(f32[8,64,1024]{2,1,0:T(8,128)} %all-to-all-done.5.refs_4_), channel_id=1, source_target_pairs={{0,2},{1,3},{2,0},{3,1},{4,6},{5,7},{6,4},{7,5},{8,10},{9,11},{10,... | collective-permute-start | bytes 6291464 | tf_op jit(solution)/shard_map/ppermute | solution.py:49
  369.1 47.3 %collective-permute-start.1 = (f32[8,64,1024]{2,1,0:T(8,128)S(1)}, f32[8,64,1024]{2,1,0:T(8,128)}, u32[]{:S(2)}, u32[]{:S(2)}) collective-permute-start(f32[8,64,1024]{2,1,0:T(8,128)S(1)} %all-to-all-done.2.refs_0_), channel_id=1, source_target_pairs={{0,1},{1,0},{2,3},{3,2},{4,5},{5,4},{6,7},{7,6},{8,9},{9,8},{10,11... | collective-permute-start | bytes 6291464 | tf_op jit(solution)/shard_map/ppermute | solution.py:49
  369.1 47.3 %collective-permute-start.2 = (f32[8,64,1024]{2,1,0:T(8,128)}, f32[8,64,1024]{2,1,0:T(8,128)}, u32[]{:S(2)}, u32[]{:S(2)}) collective-permute-start(f32[8,64,1024]{2,1,0:T(8,128)} %collective-permute-done.refs_1_), channel_id=1, source_target_pairs={{0,1},{1,0},{2,3},{3,2},{4,5},{5,4},{6,7},{7,6},{8,9},{9,8},{10,11... | collective-permute-start | bytes 6291464 | tf_op jit(solution)/shard_map/ppermute | solution.py:49
  413.8 4.5 collective-permute-start.5
  413.9 7.5 %collective-permute-start.6 = (f32[8,64,1024]{2,1,0:T(8,128)}, f32[8,64,1024]{2,1,0:T(8,128)}, u32[]{:S(2)}, u32[]{:S(2)}) collective-permute-start(f32[8,64,1024]{2,1,0:T(8,128)} %collective-permute-done.4.refs_5_), channel_id=1, source_target_pairs={{0,1},{1,0},{2,3},{3,2},{4,5},{5,4},{6,7},{7,6},{8,9},{9,8},{10,11... | collective-permute-start | bytes 6291464 | tf_op jit(solution)/shard_map/ppermute | solution.py:49
  414.4 60.8 %collective-permute-start.14 = (f32[8,64,1024]{2,1,0:T(8,128)}, f32[8,64,1024]{2,1,0:T(8,128)}, u32[]{:S(2)}, u32[]{:S(2)}) collective-permute-start(f32[8,64,1024]{2,1,0:T(8,128)} %all-to-all-done.4.refs_4_), channel_id=1, source_target_pairs={{0,2},{1,3},{2,0},{3,1},{4,6},{5,7},{6,4},{7,5},{8,10},{9,11},{10,... | collective-permute-start | bytes 6291464 | tf_op jit(solution)/shard_map/ppermute | solution.py:49
  428.2 1.9 collective-permute-start.7
  428.4 34.9 %collective-permute-start.8 = (f32[64,64]{1,0:T(8,128)S(1)}, f32[64,64]{1,0:T(8,128)S(1)}, u32[]{:S(2)}, u32[]{:S(2)}) collective-permute-start(f32[64,64]{1,0:T(8,128)S(1)} %fusion.116), channel_id=1, source_target_pairs={{0,2},{1,3},{2,0},{3,1},{4,6},{5,7},{6,4},{7,5},{8,10},{9,11},{10,... | collective-permute-start | bytes 49160 | tf_op jit(solution)/shard_map/ppermute | solution.py:178
  429.9 33.3 %collective-permute-start.9 = (f32[64,64]{1,0:T(8,128)S(1)}, f32[64,64]{1,0:T(8,128)S(1)}, u32[]{:S(2)}, u32[]{:S(2)}) collective-permute-start(f32[64,64]{1,0:T(8,128)S(1)} %fusion.116), channel_id=1, source_target_pairs={{0,3},{1,2},{2,1},{3,0},{4,7},{5,6},{6,5},{7,4},{8,11},{9,10},{10,... | collective-permute-start | bytes 49160 | tf_op jit(solution)/shard_map/ppermute | solution.py:178
  463.3 4.0 collective-permute-start.10
  464.5 3.9 collective-permute-start.11
  465.5 4.8 collective-permute-start.12
  470.3 4.9 collective-permute-start.13
  473.0 24.5 %collective-permute-start.15 = (f32[8,64,1024]{2,1,0:T(8,128)}, f32[8,64,1024]{2,1,0:T(8,128)S(1)}, u32[]{:S(2)}, u32[]{:S(2)}) collective-permute-start(f32[8,64,1024]{2,1,0:T(8,128)} %all-to-all-done.3.refs_0_), channel_id=1, source_target_pairs={{0,1},{1,0},{2,3},{3,2},{4,5},{5,4},{6,7},{7,6},{8,9},{9,8},{10,11... | collective-permute-start | bytes 6291464 | tf_op jit(solution)/shard_map/ppermute | solution.py:49
  473.0 24.5 %collective-permute-start.16 = (f32[8,64,1024]{2,1,0:T(8,128)}, f32[8,64,1024]{2,1,0:T(8,128)}, u32[]{:S(2)}, u32[]{:S(2)}) collective-permute-start(f32[8,64,1024]{2,1,0:T(8,128)} %copy-done.14), channel_id=1, source_target_pairs={{0,1},{1,0},{2,3},{3,2},{4,5},{5,4},{6,7},{7,6},{8,9},{9,8},{10,11... | collective-permute-start | bytes 6291464 | tf_op jit(solution)/shard_map/ppermute | solution.py:49
  473.5 24.0 %collective-permute-start.17 = (f32[8,64,1024]{2,1,0:T(8,128)}, f32[8,64,1024]{2,1,0:T(8,128)}, u32[]{:S(2)}, u32[]{:S(2)}) collective-permute-start(f32[8,64,1024]{2,1,0:T(8,128)} %all-to-all-done.5.refs_4_), channel_id=1, source_target_pairs={{0,1},{1,0},{2,3},{3,2},{4,5},{5,4},{6,7},{7,6},{8,9},{9,8},{10,11... | collective-permute-start | bytes 6291464 | tf_op jit(solution)/shard_map/ppermute | solution.py:49
  477.1 20.5 %collective-permute-start.18 = (f32[8,64,1024]{2,1,0:T(8,128)}, f32[8,64,1024]{2,1,0:T(8,128)}, u32[]{:S(2)}, u32[]{:S(2)}) collective-permute-start(f32[8,64,1024]{2,1,0:T(8,128)} %collective-permute-done.14.refs_5_), channel_id=1, source_target_pairs={{0,1},{1,0},{2,3},{3,2},{4,5},{5,4},{6,7},{7,6},{8,9},{9,8},{10,11... | collective-permute-start | bytes 6291464 | tf_op jit(solution)/shard_map/ppermute | solution.py:49
  (14 other events, 65.6 us)

commit v4 on v3

--- a/solution.py
+++ b/solution.py
@@ -54,37 +54,50 @@
     return top, (values - top.astype(jnp.float32)).astype(jnp.bfloat16)
 
 
-def vectors_first_kernel(start_ref, block_ref, out_ref):
-    out_ref[...] = jnp.swapaxes(block_ref[...], 0, 1)
-
-
-def vectors_first(start_block, turn, count, swapped):
+def vectors_first_kernel(place_ref, block_ref, *refs):
+    out_refs, scratch_ref = refs[:-1], refs[-1]
+    scratch_ref[...] = jnp.swapaxes(block_ref[...], 0, 1)
+    for distance, out_ref in enumerate(out_refs):
+        out_ref[...] = scratch_ref[jnp.bitwise_xor(place_ref[1], distance)]
+
+
+def vectors_first(start_block, turn, count, place):
     up_local, _, down_count = start_block.shape
     rows = 16
     blocks = up_local // rows
     return pl.pallas_call(
         vectors_first_kernel,
-        out_shape=jax.ShapeDtypeStruct((count, up_local, down_count), jnp.float32),
+        out_shape=[jax.ShapeDtypeStruct((up_local, down_count), jnp.float32)] * count,
         grid_spec=pltpu.PrefetchScalarGridSpec(
             num_scalar_prefetch=1,
             grid=(blocks,),
             in_specs=[
                 pl.BlockSpec(
                     (rows, count, down_count),
-                    lambda i, swap: (lax.rem(i + swap[0] * (blocks // 2), blocks), turn, 0),
+                    lambda i, place: (lax.rem(i + place[0] * (blocks // 2), blocks), turn, 0),
                 )
             ],
-            out_specs=pl.BlockSpec((count, rows, down_count), lambda i, swap: (0, i, 0)),
+            out_specs=[pl.BlockSpec((rows, down_count), lambda i, place: (i, 0))] * count,
+            scratch_shapes=[pltpu.VMEM((count, rows, down_count), jnp.float32)],
         ),
         compiler_params=pltpu.CompilerParams(vmem_limit_bytes=56 * 1024 * 1024),
-    )(swapped, start_block)
-
-
-def stacked(refs):
-    return jnp.concatenate([jnp.swapaxes(ref[...], 0, 1) for ref in refs], axis=1)
-
-
-def gram_kernel(start_ref, *refs):
+    )(place, start_block)
+
+
+def joined(refs):
+    return jnp.concatenate([ref[...] for ref in refs], axis=-1)
+
+
+def grouped(refs, counts):
+    ends = [sum(counts[: i + 1]) for i in range(len(counts))]
+    return [refs[end - count : end] for end, count in zip(ends, counts)]
+
+
+def stacked(refs, counts):
+    return jnp.concatenate([jnp.swapaxes(joined(cuts), 0, 1) for cuts in grouped(refs, counts)], axis=1)
+
+
+def gram_kernel(counts, start_ref, *refs):
     inputs, (top_ref, cross_ref) = refs[:-2], refs[-2:]
 
     @pl.when(pl.program_id(0) == 0)
@@ -92,7 +105,7 @@
         top_ref[...] = jnp.zeros_like(top_ref)
         cross_ref[...] = jnp.zeros_like(cross_ref)
 
-    values = stacked(inputs)
+    values = stacked(inputs, counts)
     rows, vectors, columns = values.shape
     for first in range(0, rows, STACK):
         top, low = split(values[first : first + STACK].reshape(STACK * vectors, columns))
@@ -101,16 +114,16 @@
 
 
 def gram_partial(pieces, part, parts):
-    vectors = sum(piece.shape[0] for piece in pieces)
-    block = 8
-    blocks = pieces[0].shape[1] // parts // block
+    vectors = sum(cuts[0].shape[0] for cuts in pieces)
+    blocks = pieces[0][0].shape[1] // parts // SUBLANES
+    flat = [cut for cuts in pieces for cut in cuts]
     specs = [
-        pl.BlockSpec((piece.shape[0], block, piece.shape[2]), lambda i, first: (0, first[0] + i, 0)) for piece in pieces
+        pl.BlockSpec((cut.shape[0], SUBLANES, cut.shape[2]), lambda i, first: (0, first[0] + i, 0)) for cut in flat
     ]
     size = STACK * vectors
     out = jax.ShapeDtypeStruct((size, size), jnp.float32)
     top, cross = pl.pallas_call(
-        gram_kernel,
+        functools.partial(gram_kernel, [len(cuts) for cuts in pieces]),
         out_shape=(out, out),
         grid_spec=pltpu.PrefetchScalarGridSpec(
             num_scalar_prefetch=1,
@@ -119,46 +132,48 @@
             out_specs=[pl.BlockSpec((size, size), lambda i, first: (0, 0))] * 2,
         ),
         compiler_params=pltpu.CompilerParams(vmem_limit_bytes=48 * 1024 * 1024),
-    )((part * blocks).reshape(1), *pieces)
+    )((part * blocks).reshape(1), *flat)
     cross = cross + cross.T
     total = (top + cross).reshape(STACK, vectors, STACK, vectors)
     return sum(total[u, :, u, :] for u in range(STACK))
 
 
-def rotate_kernel(swap_ref, mix_ref, *refs):
-    inputs, out_ref = [ref for ref in refs[:-1] if ref.ndim == 3 and ref.shape[1] == SUBLANES], refs[-1]
+def rotate_kernel(counts, place_ref, mix_ref, *refs):
+    inputs, out_ref = refs[: sum(counts)], refs[-1]
     columns = out_ref.shape[2]
     mix_top, mix_low = split(mix_ref[...])
     count = mix_top.shape[0]
     both = jnp.concatenate([mix_top, mix_low], axis=0)
-    top, low = split(jnp.concatenate([ref[...].reshape(-1, columns) for ref in inputs], axis=0))
+    top, low = split(jnp.concatenate([joined(cuts).reshape(-1, columns) for cuts in grouped(inputs, counts)], axis=0))
     wide = dot(both, top, (1, 0), None)
     result = wide[:count] + wide[count:] + dot(mix_top, low, (1, 0), None)
     out_ref[...] = jnp.swapaxes(result.reshape(-1, SUBLANES, columns), 0, 1)
 
 
-def rotate_half(pieces, wide_mixing, swapped, half, earlier):
-    half_rows, down_count = pieces[0].shape[1:]
+def rotate_half(pieces, wide_mixing, place, half, earlier):
+    half_rows = pieces[0][0].shape[1]
+    down_count = sum(cut.shape[2] for cut in pieces[0])
     blocks = half_rows // SUBLANES
     own = wide_mixing.shape[0] // SUBLANES
-    specs = [pl.BlockSpec(wide_mixing.shape, lambda i, swap: (0, 0))]
-    for piece in pieces:
-        specs.append(pl.BlockSpec((piece.shape[0], SUBLANES, down_count), lambda i, swap: (0, i, 0)))
-    operands = [swapped, wide_mixing, *pieces]
+    flat = [cut for cuts in pieces for cut in cuts]
+    specs = [pl.BlockSpec(wide_mixing.shape, lambda i, place: (0, 0))]
+    for cut in flat:
+        specs.append(pl.BlockSpec((cut.shape[0], SUBLANES, cut.shape[2]), lambda i, place: (0, i, 0)))
+    operands = [place, wide_mixing, *flat]
     aliases = {}
     if earlier is not None:
         specs.append(pl.BlockSpec(memory_space=pl.ANY))
         aliases = {len(operands): 0}
         operands.append(earlier)
     return pl.pallas_call(
-        rotate_kernel,
+        functools.partial(rotate_kernel, [len(cuts) for cuts in pieces]),
         out_shape=jax.ShapeDtypeStruct((2 * half_rows, own, down_count), jnp.float32),
         grid_spec=pltpu.PrefetchScalarGridSpec(
             num_scalar_prefetch=1,
             grid=(blocks,),
             in_specs=specs,
             out_specs=pl.BlockSpec(
-                (SUBLANES, own, down_count), lambda i, swap: (i + lax.rem(swap[0] + half, 2) * blocks, 0, 0)
+                (SUBLANES, own, down_count), lambda i, place: (i + lax.rem(place[0] + half, 2) * blocks, 0, 0)
             ),
         ),
         input_output_aliases=aliases,
@@ -194,6 +209,11 @@
     return norm_scale * product_total
 
 
+def after(value, cell):
+    value, cell[0] = lax.optimization_barrier((value, cell[0]))
+    return value
+
+
 def vector_cut(start_block, down_matrix, hop_coef, hop_partner, onsite_u):
     hil_parts, vec_parts = lax.axis_size("hil"), lax.axis_size("vec")
     up_local, vec_local, down_count = start_block.shape
@@ -201,21 +221,55 @@
     rounds = vec_local // hil_parts
     half_rows = up_local // 2
     side = vec_parts // 2
-    own = lax.axis_index("vec")
+    row, own = lax.axis_index("hil"), lax.axis_index("vec")
     swap = own // side
-    swapped = swap.reshape(1).astype(jnp.int32)
+    place = jnp.stack([swap, row]).astype(jnp.int32)
 
     def ordered(values):
-        cut = values.reshape(values.shape[:-1] + (hil_parts, 2, half_rows))
-        return jnp.where(swap == 1, cut[..., ::-1, :], cut).reshape(values.shape)
-
-    arrived = []
-    for turn in range(rounds):
-        block = vectors_first(start_block, turn, hil_parts, swapped)
-        block = lax.all_to_all(block, "hil", split_axis=0, concat_axis=0, tiled=True)
-        arrived.append(block.reshape(up_count, down_count))
-    other = jnp.where((hop_partner // half_rows) % 2 == 0, hop_partner + half_rows, hop_partner - half_rows)
-    up_matrix = hop_matrix(ordered(hop_coef), ordered(jnp.where(swap == 1, other, hop_partner)))
+        lead = values.shape[:-1]
+        cut = values.reshape(lead + (hil_parts, 2, half_rows))
+        cut = jnp.where(swap == 1, cut[..., ::-1, :], cut)
+        step = 1
+        while step < hil_parts:
+            cut = cut.reshape(lead + (hil_parts // step // 2, 2, step * up_local))
+            cut = jnp.where((row // step) % 2 == 1, cut[..., ::-1, :], cut)
+            step *= 2
+        return cut.reshape(values.shape)
+
+    def position(states):
+        inner = states % up_local
+        inner = jnp.where(swap == 1, jnp.where(inner < half_rows, inner + half_rows, inner - half_rows), inner)
+        return jnp.bitwise_xor(states // up_local, row) * up_local + inner
+
+    flight = 2 * 1024 * 1024
+    sent = []
+
+    def send(blocks, extra):
+        cells = [[blocks[0]]] + [None] * (hil_parts - 1)
+        order = []
+        far, near = list(range(hil_parts - 1, hil_parts // 2 - 1, -1)), list(range(hil_parts // 2 - 1, 0, -1))
+        while far or near:
+            order += far[:1] + near[:1]
+            far, near = far[1:], near[1:]
+        for number, distance in enumerate(order):
+            block = blocks[distance]
+            size = 4 * block.size
+            ahead, waiting = 0, len(sent)
+            while waiting > 0 and ahead + size <= flight:
+                waiting -= 1
+                ahead += 4 * sent[waiting][0].size
+            if waiting > 0:
+                block = after(block, sent[waiting - 1])
+            if number == len(order) // 2 and extra is not None:
+                block = after(block, extra)
+            cell = [lax.ppermute(block, "hil", [(i, i ^ distance) for i in range(hil_parts)])]
+            sent.append(cell)
+            cells[distance] = cell
+        return cells
+
+    inward = [send(vectors_first(start_block, turn, hil_parts, place), None) for turn in range(rounds)]
+    arrived = [jnp.concatenate([cell[0] for cell in cells], axis=0) for cells in inward]
+    up_matrix = hop_matrix(ordered(hop_coef), ordered(position(hop_partner)))
     sites = onsite_u.shape[0]
     diagonal = -center_shift + jnp.dot(
         site_bits(ordered(jnp.arange(up_count, dtype=jnp.int32)), sites) * onsite_u[None, :],
@@ -238,8 +292,7 @@
     once = first_step(arrived[0])
     pieces = [second_step(once, arrived[0], half) for half in (mine, theirs)]
     pieces[theirs], pieces[mine] = lax.optimization_barrier((pieces[theirs], pieces[mine]))
-    crossed = []
-    held = [[], []]
+    work = []
     for turn in range(rounds):
         upcoming = [None, None]
         for half in (theirs, mine):
@@ -249,11 +302,14 @@
                 upcoming[theirs] = second_step(once, arrived[turn + 1], theirs)
                 piece, once, upcoming[theirs] = lax.optimization_barrier((piece, once, upcoming[theirs]))
                 upcoming[mine] = second_step(once, arrived[turn + 1], mine)
-            if len(crossed) > 1:
-                piece, crossed[-2] = lax.optimization_barrier((piece, crossed[-2]))
-            back = lax.all_to_all(piece, "hil", split_axis=0, concat_axis=0, tiled=True)
-            held[half].append(back)
-            crossed.append(spread_step([back], side)[0])
+            cuts = 2 if (turn, half) in ((0, theirs), (rounds - 1, mine)) else 1
+            width = down_count // cuts
+            for cut in range(cuts):
+                blocks = [piece[distance, :, cut * width : (cut + 1) * width] for distance in range(hil_parts)]
+                extra = work[-2][3] if len(work) > 1 else None
+                back = jnp.stack([cell[0] for cell in send(blocks, extra)])
+                last = (turn, half, cut) == (rounds - 1, mine, cuts - 1)
+                work.append((half, turn, back, [None if last else spread_step([back], side)[0]]))
         pieces = upcoming
 
     def on_side(near):
@@ -263,30 +319,44 @@
             step //= 2
         return near
 
-    halves = [[], []]
-    for turn in range(rounds):
-        halves[mine].extend(on_side([held[mine][turn], crossed[2 * turn]]))
-    distances = [0, side]
-    step = side // 2
+    def gathered(half):
+        result = []
+        for turn in range(rounds):
+            here = [on_side([back]) for h, t, back, _ in work if (h, t) == (half, turn)]
+            there = [on_side([cell[0]]) for h, t, _, cell in work if (h, t) == (1 - half, turn)]
+            result += [list(cuts) for cuts in zip(*here)]
+            result += [list(cuts) for cuts in zip(*there)]
+        return result
+
+    step, distances = side // 2, [0]
     while step >= 1:
         distances += [distance ^ step for distance in distances]
         step //= 2
+    distances += [distance ^ side for distance in distances]
     near = jnp.bitwise_xor(jnp.array(distances, dtype=jnp.int32), own)
-    exchange = (near[:, None] == jnp.arange(vec_parts, dtype=jnp.int32)[None, :]).astype(jnp.float32)
-    order = jnp.kron(jnp.eye(rounds, dtype=jnp.float32), jnp.kron(exchange, jnp.eye(hil_parts, dtype=jnp.float32)))
-    partial = gram_partial(halves[mine], lax.rem(own, side), side)
+    over_vec = (near[:, None] == jnp.arange(vec_parts, dtype=jnp.int32)[None, :]).astype(jnp.float32)
+    near = jnp.bitwise_xor(jnp.arange(hil_parts, dtype=jnp.int32), row)
+    over_hil = (near[:, None] == jnp.arange(hil_parts, dtype=jnp.int32)[None, :]).astype(jnp.float32)
+    turns = jnp.eye(rounds, dtype=jnp.float32)
+    order = jnp.kron(turns, jnp.kron(over_vec, over_hil))
+    order_out = jnp.kron(turns, jnp.kron(over_vec, jnp.eye(hil_parts, dtype=jnp.float32)))
+    order_out = order_out.reshape(rounds, vec_parts, hil_parts, -1)[:, 0].reshape(vec_local, -1)
+    own_pieces = gathered(mine)
+    partial = gram_partial(own_pieces, lax.rem(own, side), side)
     partial = dot(order, dot(partial, order, (1, 0), highest), (0, 0), highest)
-    gram_sum = small_sum(small_sum(partial, "vec"), "hil")
-    gram_sum, crossed[-1] = lax.optimization_barrier((gram_sum, crossed[-1]))
-    for turn in range(rounds):
-        halves[theirs].extend(on_side([held[theirs][turn], crossed[2 * turn + 1]]))
-    mixing = newton_schulz(gram_sum)
-    mixing = dot(dot(order, mixing, (1, 0), highest), order, (1, 1), highest)
-    mixing = mixing.reshape(-1, rounds, vec_parts, hil_parts)[:, :, 0].reshape(-1, vec_local)
-    mixing = mixing * math.sqrt(up_count * down_count)
-    wide_mixing = jnp.kron(mixing.T, jnp.eye(SUBLANES, dtype=jnp.float32))
-    result = rotate_half(halves[mine], wide_mixing, swapped, mine, None)
-    return rotate_half(halves[theirs], wide_mixing, swapped, theirs, result)
+    partial = small_sum(partial, "vec")
+    back, partial = lax.optimization_barrier((work[-1][2], partial))
+    work[-1][3][0] = spread_step([back], side)[0]
+    mixing = newton_schulz(small_sum(partial, "hil")) * math.sqrt(up_count * down_count)
+    mixing = dot(dot(order_out, mixing, (1, 1), highest), order, (1, 1), highest)
+    wide = jnp.arange(vec_local * SUBLANES, dtype=jnp.int32)
+    long = jnp.arange(order.shape[0] * SUBLANES, dtype=jnp.int32)
+    left = (wide[:, None] // SUBLANES == jnp.arange(vec_local, dtype=jnp.int32)[None, :]).astype(jnp.float32)
+    right = (jnp.arange(order.shape[0], dtype=jnp.int32)[:, None] == long[None, :] // SUBLANES).astype(jnp.float32)
+    wide_mixing = dot(left, dot(mixing, right, (1, 0), highest), (1, 0), highest)
+    wide_mixing = jnp.where(wide[:, None] % SUBLANES == long[None, :] % SUBLANES, wide_mixing, 0.0)
+    result = rotate_half(own_pieces, wide_mixing, place, mine, None)
+    return rotate_half(gathered(theirs), wide_mixing, place, theirs, result)
 
 
 def split_down(local_block):
@@ -351,7 +421,7 @@
     hil_parts, vec_parts = lax.axis_size("hil"), lax.axis_size("vec")
     up_local, vec_local, _ = start_block.shape
     hop_coef = -bond_hop[:, None] * hop_sign.astype(jnp.float32)
-    whole_vectors = vec_local % hil_parts == 0 and hil_parts % 8 == 0
+    whole_vectors = vec_local % hil_parts == 0 and hil_parts % 8 == 0 and hil_parts & (hil_parts - 1) == 0
     halved = vec_parts > 1 and vec_parts & (vec_parts - 1) == 0 and up_local % (16 * vec_parts) == 0
     plan = vector_cut if whole_vectors and halved else down_cut
     return plan(start_block, down_matrix, hop_coef, hop_partner, onsite_u)

time: 520 us -> 614 us (1.18)
  starting transfers between devices: 46.8 us -> 143 us
  matrix products: 108 us -> 96.4 us
  local copies, waits for them, and re-layouts: 27.6 us -> 38.7 us
    ppermute x0 -> x56, waiting for transfers between devices: none -> 183 us  [send(): lax.ppermute(block, 'hil', [(i, i ^ distance) for i in range(hil_parts)])]
    all_to_all x6 -> x0, waiting for transfers between devices: 152 us -> none  [the longest x2 102 us: vector_cut(): lax.all_to_all(block, 'hil', split_axis=0, concat_axis=0, tiled=True)]
    ppermute x0 -> x56, starting transfers between devices: none -> 129 us  [send(): lax.ppermute(block, 'hil', [(i, i ^ distance) for i in range(hil_parts)])]
    all_to_all x6 -> x0, starting transfers between devices: 31 us -> none  [the longest x4 19.2 us: vector_cut(): back = lax.all_to_all(piece, 'hil', split_axis=0, concat_axis=0, tiled=True)]
    ppermute x7, waiting for transfers between devices: 38.3 us -> 10.9 us  [small_sum(): lax.ppermute(values, axis, [(i, i ^ distance) for i in range(parts)])]
    unnamed x42 -> x141, local copies, waits for them, and re-layouts: 8.35 us -> 19 us
    dot_general x25 -> x28, matrix products: 103 us -> 92.9 us  [dot(): lax.dot_general(left, right, ((contract[:1], contract[1:]), ((), ())), pr...]
    ppermute x12 -> x18, waiting for transfers between devices: 83.5 us -> 75.2 us  [spread_step(): return [lax.ppermute(piece, 'vec', pairs) for piece in held]]
  transfers between devices with their start and end apart: 25 -> 81, of which waited for: 14 -> 31; matrix products, arithmetic and copies ran while one was open for 27% -> 22% of each run, Pallas kernels for 5% -> 3%
where the time goes in v4:
time: 614 us; the launch traced here: 606 us
  waiting for transfers between devices  269 us (44%)
  starting transfers between devices  143 us (23%)
  matrix products  96.4 us (16%)
  Pallas kernels  46.2 us (8%)
  local copies, waits for them, and re-layouts  38.7 us (6%)
  other arithmetic  9.68 us (2%)
    ppermute x56, waiting for transfers between devices, send(): lax.ppermute(block, 'hil', [(i, i ^ distance) for i in range(hil_parts)])  183 us
    ppermute x56, starting transfers between devices, send(): lax.ppermute(block, 'hil', [(i, i ^ distance) for i in range(hil_parts)])  129 us
    dot_general x28, matrix products, dot(): lax.dot_general(left, right, ((contract[:1], contract[1:]), ((), ())), pr...  92.9 us
    ppermute x18, waiting for transfers between devices, spread_step(): return [lax.ppermute(piece, 'vec', pairs) for piece in held]  75.2 us
    pallas_call x2, Pallas kernels, rotate_half(): pl.pallas_call(functools.partial(rotate_kernel, [len(cuts) for cuts in pi...  24.7 us
    unnamed x141, local copies, waits for them, and re-layouts  19 us
    pallas_call x2, Pallas kernels, vectors_first(): pl.pallas_call(vectors_first_kernel, out_shape=[jax.ShapeDtypeStruct((up_...  15.5 us
  transfers between devices with their start and end apart: 81, of which 31 were waited for; matrix products, arithmetic and copies ran while one was open for 22% of the time, Pallas kernels for 3%

profile of v4, /device:TPU:0, one launch (start us, length us, event | category | flops | bytes accessed | tf_op | source)
XLA Modules:
  0.0 606.1 jit_solution(3819850071950446836)
XLA Ops:
  0.6 7.7 %shard_map.73 = (f32[128,1024]{1,0:T(8,128)}, f32[128,1024]{1,0:T(8,128)}, f32[128,1024]{1,0:T(8,128)}, f32[128,1024]{1,0:T(8,128)}, f32[128,1024]{1,0:T(8,128)}...) custom-call(s32[2]{0:T(128)} %pad_add_fusion.place_ref, f32[128,16,1024]{2,1,0:T(8,128)} %block_ref.3), custom_call_target="tpu_custom_call" | custom-call | tf_op jit(solution)/shard_map/pallas_call | solution.py:68
  8.4 5.1 collective-permute-start.6
  24.3 6.6 %select_add_fusion = f32[8,2,64,1024]{3,2,1,0:T(8,128)} fusion(f32[8,2,64]{2,1,0:T(2,128)S(1)} %broadcast_in_dim.209, s32[8,2,64]{2,1,0:T(2,128)S(1)} %eq.468, f32[8,2,64]{2,1,0:T(2,128)S(1)} %broadcast_in_dim.207, s32[8,2,64]{2,1,0:T(2,128)S(1)} %eq.464, f32[8,2,64]{2,1,0:T(2,128)S(1)} %broadcast_in_dim.205, s32[8,2,64]{2,1,0:T(2,128)S(1)} %eq.460, ...), kind=kLoop, calls=%fused_computation.1 | loop fusion | flops 30408704 | bytes 4276224 | tf_op jit(solution)/shard_map/add | solution.py:32
  31.2 7.7 %collective-permute-done = f32[128,1024]{1,0:T(8,128)S(1)} collective-permute-done((f32[128,1024]{1,0:T(8,128)}, f32[128,1024]{1,0:T(8,128)S(1)}, u32[]{:S(2)}, u32[]{:S(2)}) %collective-permute-start) | collective-permute-done | bytes 524320 | tf_op jit(solution)/shard_map/ppermute | solution.py:265
  39.3 29.3 %collective-permute-done.3 = f32[128,1024]{1,0:T(8,128)S(1)} collective-permute-done((f32[128,1024]{1,0:T(8,128)}, f32[128,1024]{1,0:T(8,128)S(1)}, u32[]{:S(2)}, u32[]{:S(2)}) %collective-permute-start.3) | collective-permute-done | bytes 524320 | tf_op jit(solution)/shard_map/ppermute | solution.py:265
  68.6 19.2 %collective-permute-start.4 = (f32[128,1024]{1,0:T(8,128)}, f32[128,1024]{1,0:T(8,128)S(1)}, u32[]{:S(2)}, u32[]{:S(2)}) collective-permute-start(f32[128,1024]{1,0:T(8,128)} %get-tuple-element.93), channel_id=1, source_target_pairs={{0,16},{4,20},{8,24},{12,28},{16,0},{20,4},{24,8},{28,12},{1,17},{... | collective-permute-start | bytes 1572872 | tf_op jit(solution)/shard_map/ppermute | solution.py:265
  91.4 7.8 %shard_map.74 = (f32[128,1024]{1,0:T(8,128)}, f32[128,1024]{1,0:T(8,128)}, f32[128,1024]{1,0:T(8,128)}, f32[128,1024]{1,0:T(8,128)}, f32[128,1024]{1,0:T(8,128)}...) custom-call(s32[2]{0:T(128)} %pad_add_fusion.place_ref, f32[128,16,1024]{2,1,0:T(8,128)} %block_ref.3), custom_call_target="tpu_custom_call" | custom-call | tf_op jit(solution)/shard_map/pallas_call | solution.py:68
  108.7 12.8 %collective-permute-done.5 = f32[128,1024]{1,0:T(8,128)S(1)} collective-permute-done((f32[128,1024]{1,0:T(8,128)}, f32[128,1024]{1,0:T(8,128)S(1)}, u32[]{:S(2)}, u32[]{:S(2)}) %collective-permute-start.5) | collective-permute-done | bytes 524320 | tf_op jit(solution)/shard_map/ppermute | solution.py:265
  121.5 13.1 %collective-permute-done.4 = f32[128,1024]{1,0:T(8,128)S(1)} collective-permute-done((f32[128,1024]{1,0:T(8,128)}, f32[128,1024]{1,0:T(8,128)S(1)}, u32[]{:S(2)}, u32[]{:S(2)}) %collective-permute-start.4) | collective-permute-done | bytes 524320 | tf_op jit(solution)/shard_map/ppermute | solution.py:265
  135.9 14.6 %fusion.11 = f32[1024,1024]{1,0:T(8,128)} fusion(f32[1024,1024]{1,0:T(8,128)S(1)} %constant_dynamic-update-slice_fusion, f32[1024]{0:T(1024)S(1)} %bitcast.488, s32[1024]{0:T(1024)S(1)} %bitcast.468, f32[1024]{0:T(1024)S(1)} %bitcast.486, s32[1024]{0:T(1024)S(1)} %bitcast.466, f32[1024]{0:T(1024)S(1)} %bitcast.484, s32[1024]{0:T(1024)S(1)} %bitcast.464, ...), kind=kOutput, calls=%fused_computation.47 | convolution fusion | flops 6472859648 | bytes 8470528 | tf_op jit(solution)/shard_map/dot_general | solution.py:37
  150.5 10.4 %add_multiply_fusion.1 = f32[1024,1024]{1,0:T(8,128)S(1)} fusion(f32[1024,1024]{1,0:T(8,128)S(1)} %convolution_add_fusion, f32[1024,1024]{1,0:T(8,128)S(1)} %constant_dynamic-update-slice_fusion, f32[1024,1024]{1,0:T(8,128)} %fusion.11, f32[1024,1024]{1,0:T(8,128)S(1)} %copy-done.6), kind=kOutput, calls=%fused_computation.12 | convolution fusion | flops 6446645248 | bytes 20971520 | tf_op jit(solution)/shard_map/dot_general | solution.py:37
  175.1 8.9 %bitcast_subtract_fusion.2 = f32[512,1024]{1,0:T(8,128)} fusion(f32[8,1,64,1024]{3,2,1,0:T(8,128)} %get-tuple-element.256, f32[512,1024]{1,0:T(8,128)} %bitcast.424, f32[8,1,64,1024]{3,2,1,0:T(8,128)} %get-tuple-element.161, f32[512,1024]{1,0:T(8,128)} %fusion.126, f32[512,1024]{1,0:T(8,128)} %bitcast.425, f32[1024,1024]{1,0:T(8,128)S(1)} %add_multiply_fusion.1), kind=kOutput, calls=%fused_computation.27 | convolution fusion | flops 3223846912 | bytes 16777216 | tf_op jit(solution)/shard_map/dot_general | solution.py:37
  200.3 28.6 %collective-permute-done.31 = f32[64,512]{1,0:T(8,128)S(1)} collective-permute-done((f32[64,512]{1,0:T(8,128)S(1)}, f32[64,512]{1,0:T(8,128)S(1)}, u32[]{:S(2)}, u32[]{:S(2)}) %collective-permute-start.31) | collective-permute-done | bytes 131104 | tf_op jit(solution)/shard_map/ppermute | solution.py:265
  232.6 11.7 %collective-permute-done.32 = f32[64,512]{1,0:T(8,128)S(1)} collective-permute-done((f32[64,512]{1,0:T(8,128)S(1)}, f32[64,512]{1,0:T(8,128)S(1)}, u32[]{:S(2)}, u32[]{:S(2)}) %collective-permute-start.32) | collective-permute-done | bytes 131104 | tf_op jit(solution)/shard_map/ppermute | solution.py:265
  244.3 7.1 %collective-permute-done.33 = f32[64,512]{1,0:T(8,128)S(1)} collective-permute-done((f32[64,512]{1,0:T(8,128)S(1)}, f32[64,512]{1,0:T(8,128)S(1)}, u32[]{:S(2)}, u32[]{:S(2)}) %collective-permute-start.33) | collective-permute-done | bytes 131104 | tf_op jit(solution)/shard_map/ppermute | solution.py:265
  257.8 14.5 %fusion.10 = f32[1024,1024]{1,0:T(8,128)} fusion(f32[1024,1024]{1,0:T(8,128)S(1)} %constant_dynamic-update-slice_fusion.8, f32[1024]{0:T(1024)S(1)} %bitcast.489, s32[1024]{0:T(1024)S(1)} %bitcast.469, f32[1024]{0:T(1024)S(1)} %bitcast.487, s32[1024]{0:T(1024)S(1)} %bitcast.467, f32[1024]{0:T(1024)S(1)} %bitcast.485, s32[1024]{0:T(1024)S(1)} %bitcast.465, ...), kind=kOutput, calls=%fused_computation.46 | convolution fusion | flops 6472859648 | bytes 8470528 | tf_op jit(solution)/shard_map/dot_general | solution.py:37
  272.3 10.3 %add_multiply_fusion = f32[1024,1024]{1,0:T(8,128)S(1)} fusion(f32[1024,1024]{1,0:T(8,128)S(1)} %convolution_add_fusion, f32[1024,1024]{1,0:T(8,128)S(1)} %constant_dynamic-update-slice_fusion.8, f32[1024,1024]{1,0:T(8,128)} %fusion.10, f32[1024,1024]{1,0:T(8,128)S(1)} %copy-done.6), kind=kOutput, calls=%fused_computation | convolution fusion | flops 6446645248 | bytes 20971520 | tf_op jit(solution)/shard_map/dot_general | solution.py:37
  299.8 10.0 %collective-permute-done.20 = f32[64,512]{1,0:T(8,128)S(1)} collective-permute-done((f32[64,512]{1,0:T(8,128)S(1)}, f32[64,512]{1,0:T(8,128)S(1)}, u32[]{:S(2)}, u32[]{:S(2)}) %collective-permute-start.20) | collective-permute-done | bytes 131104 | tf_op jit(solution)/shard_map/ppermute | solution.py:265
  330.1 11.7 %collective-permute-done.34.refs_2_ = f32[8,64,512]{2,1,0:T(8,128)S(1)} collective-permute-done((f32[8,64,512]{2,1,0:T(8,128)S(1)}, f32[8,64,512]{2,1,0:T(8,128)S(1)}, u32[]{:S(2)}, u32[]{:S(2)}) %collective-permute-start.34) | collective-permute-done | bytes 1048608 | tf_op jit(solution)/shard_map/ppermute | solution.py:49
  370.9 8.2 %collective-permute-done.51 = f32[64,1024]{1,0:T(8,128)S(1)} collective-permute-done((f32[64,1024]{1,0:T(8,128)S(1)}, f32[64,1024]{1,0:T(8,128)S(1)}, u32[]{:S(2)}, u32[]{:S(2)}) %collective-permute-start.51) | collective-permute-done | bytes 262176 | tf_op jit(solution)/shard_map/ppermute | solution.py:265
  387.1 5.2 collective-permute-start.16
  392.8 17.9 %collective-permute-done.39 = f32[64,1024]{1,0:T(8,128)S(1)} collective-permute-done((f32[64,1024]{1,0:T(8,128)S(1)}, f32[64,1024]{1,0:T(8,128)S(1)}, u32[]{:S(2)}, u32[]{:S(2)}) %collective-permute-start.39) | collective-permute-done | bytes 262176 | tf_op jit(solution)/shard_map/ppermute | solution.py:265
  425.8 15.4 %collective-permute-done.56.refs_4_ = f32[8,64,1024]{2,1,0:T(8,128)S(1)} collective-permute-done((f32[8,64,1024]{2,1,0:T(8,128)}, f32[8,64,1024]{2,1,0:T(8,128)S(1)}, u32[]{:S(2)}, u32[]{:S(2)}) %collective-permute-start.56) | collective-permute-done | bytes 2097184 | tf_op jit(solution)/shard_map/ppermute | solution.py:49
  452.5 6.2 %collective-permute-done.59 = f32[64,512]{1,0:T(8,128)S(1)} collective-permute-done((f32[64,512]{1,0:T(8,128)S(1)}, f32[64,512]{1,0:T(8,128)S(1)}, u32[]{:S(2)}, u32[]{:S(2)}) %collective-permute-start.59) | collective-permute-done | bytes 131104 | tf_op jit(solution)/shard_map/ppermute | solution.py:265
  461.7 5.2 collective-permute-done.60
  470.9 5.1 collective-permute-done.43.refs_10_
  502.4 6.0 shard_map.75
  517.0 5.5 collective-permute-start.70
  535.5 18.9 %collective-permute-done.77.refs_8_ = f32[8,64,512]{2,1,0:T(8,128)} collective-permute-done((f32[8,64,512]{2,1,0:T(8,128)S(1)}, f32[8,64,512]{2,1,0:T(8,128)}, u32[]{:S(2)}, u32[]{:S(2)}) %collective-permute-start.77) | collective-permute-done | bytes 1048608 | tf_op jit(solution)/shard_map/ppermute | solution.py:49
  554.4 22.1 %collective-permute-done.78.refs_9_ = f32[8,64,512]{2,1,0:T(8,128)} collective-permute-done((f32[8,64,512]{2,1,0:T(8,128)}, f32[8,64,512]{2,1,0:T(8,128)}, u32[]{:S(2)}, u32[]{:S(2)}) %collective-permute-start.78) | collective-permute-done | bytes 1048608 | tf_op jit(solution)/shard_map/ppermute | solution.py:49
  578.1 12.3 %shard_map.76.refs_12_ = f32[128,16,1024]{2,1,0:T(8,128)} custom-call(s32[2]{0:T(128)} %pad_add_fusion.place_ref, f32[128,512]{1,0:T(8,128)} %convolution_select_fusion.mix_ref, f32[8,64,1024]{2,1,0:T(8,128)} %bitcast_dynamic-update-slice_fusion.refs_0_, f32[8,64,1024]{2,1,0:T(8,128)} %collective-permute-done.52.refs_1_, f32[8,64,512]{2,1,0:T(8,128)} %copy-done.1, ...), custom_call_target="tpu_custom_call" | custom-call | tf_op jit(solution)/shard_map/pallas_call | solution.py:168
  593.4 12.4 %shard_map.77 = f32[128,16,1024]{2,1,0:T(8,128)} custom-call(s32[2]{0:T(128)} %pad_add_fusion.place_ref, f32[128,512]{1,0:T(8,128)} %convolution_select_fusion.mix_ref, f32[8,64,512]{2,1,0:T(8,128)} %copy-done.20, f32[8,64,512]{2,1,0:T(8,128)} %copy-done.19, f32[8,64,512]{2,1,0:T(8,128)} %collective-permute-done.73.refs_2_, ...), custom_call_target="tpu_custom_call", output_to_operand_aliasing={{}: (14, {})} | custom-call | tf_op jit(solution)/shard_map/pallas_call | solution.py:168
  (413 shorter events, 226.0 us)
Async XLA Ops:
  8.4 96.0 %collective-permute-start.6 = (f32[128,1024]{1,0:T(8,128)}, f32[128,1024]{1,0:T(8,128)S(1)}, u32[]{:S(2)}, u32[]{:S(2)}) collective-permute-start(f32[128,1024]{1,0:T(8,128)} %get-tuple-element.99), channel_id=1, source_target_pairs={{0,24},{4,28},{8,16},{12,20},{16,8},{20,12},{24,0},{28,4},{1,25},{... | collective-permute-start | bytes 1572872 | tf_op jit(solution)/shard_map/ppermute | solution.py:265
  14.6 94.0 %collective-permute-start.2 = (f32[128,1024]{1,0:T(8,128)}, f32[128,1024]{1,0:T(8,128)S(1)}, u32[]{:S(2)}, u32[]{:S(2)}) collective-permute-start(f32[128,1024]{1,0:T(8,128)} %get-tuple-element.87), channel_id=1, source_target_pairs={{0,8},{4,12},{8,0},{12,4},{16,24},{20,28},{24,16},{28,20},{1,9},{5... | collective-permute-start | bytes 1572872 | tf_op jit(solution)/shard_map/ppermute | solution.py:265
  14.7 54.0 %collective-permute-start.3 = (f32[128,1024]{1,0:T(8,128)}, f32[128,1024]{1,0:T(8,128)S(1)}, u32[]{:S(2)}, u32[]{:S(2)}) collective-permute-start(f32[128,1024]{1,0:T(8,128)} %get-tuple-element.90), channel_id=1, source_target_pairs={{0,12},{4,8},{8,4},{12,0},{16,28},{20,24},{24,20},{28,16},{1,13},{... | collective-permute-start | bytes 1572872 | tf_op jit(solution)/shard_map/ppermute | solution.py:265
  16.5 105.0 %collective-permute-start.5 = (f32[128,1024]{1,0:T(8,128)}, f32[128,1024]{1,0:T(8,128)S(1)}, u32[]{:S(2)}, u32[]{:S(2)}) collective-permute-start(f32[128,1024]{1,0:T(8,128)} %get-tuple-element.96), channel_id=1, source_target_pairs={{0,20},{4,16},{8,28},{12,24},{16,4},{20,0},{24,12},{28,8},{1,21},{... | collective-permute-start | bytes 1572872 | tf_op jit(solution)/shard_map/ppermute | solution.py:265
  38.9 82.6 %collective-permute-start.1 = (f32[128,1024]{1,0:T(8,128)}, f32[128,1024]{1,0:T(8,128)}, u32[]{:S(2)}, u32[]{:S(2)}) collective-permute-start(f32[128,1024]{1,0:T(8,128)} %get-tuple-element.84), channel_id=1, source_target_pairs={{0,4},{4,0},{8,12},{12,8},{16,20},{20,16},{24,28},{28,24},{1,5},{5... | collective-permute-start | bytes 1572872 | tf_op jit(solution)/shard_map/ppermute | solution.py:265
  68.6 65.9 %collective-permute-start.4 = (f32[128,1024]{1,0:T(8,128)}, f32[128,1024]{1,0:T(8,128)S(1)}, u32[]{:S(2)}, u32[]{:S(2)}) collective-permute-start(f32[128,1024]{1,0:T(8,128)} %get-tuple-element.93), channel_id=1, source_target_pairs={{0,16},{4,20},{8,24},{12,28},{16,0},{20,4},{24,8},{28,12},{1,17},{... | collective-permute-start | bytes 1572872 | tf_op jit(solution)/shard_map/ppermute | solution.py:265
  104.3 89.4 %collective-permute-start.7 = (f32[128,1024]{1,0:T(8,128)}, f32[128,1024]{1,0:T(8,128)S(1)}, u32[]{:S(2)}, u32[]{:S(2)}) collective-permute-start(f32[128,1024]{1,0:T(8,128)} %get-tuple-element.105), channel_id=1, source_target_pairs={{0,28},{4,24},{8,20},{12,16},{16,12},{20,8},{24,4},{28,0},{1,29},{... | collective-permute-start | bytes 1572872 | tf_op jit(solution)/shard_map/ppermute | solution.py:265
  108.7 85.4 %collective-permute-start.10 = (f32[128,1024]{1,0:T(8,128)}, f32[128,1024]{1,0:T(8,128)S(1)}, u32[]{:S(2)}, u32[]{:S(2)}) collective-permute-start(f32[128,1024]{1,0:T(8,128)} %get-tuple-element.109), channel_id=1, source_target_pairs={{0,12},{4,8},{8,4},{12,0},{16,28},{20,24},{24,20},{28,16},{1,13},{... | collective-permute-start | bytes 1572872 | tf_op jit(solution)/shard_map/ppermute | solution.py:265
  121.5 73.7 %collective-permute-start.13 = (f32[128,1024]{1,0:T(8,128)}, f32[128,1024]{1,0:T(8,128)S(1)}, u32[]{:S(2)}, u32[]{:S(2)}) collective-permute-start(f32[128,1024]{1,0:T(8,128)} %get-tuple-element.113), channel_id=1, source_target_pairs={{0,24},{4,28},{8,16},{12,20},{16,8},{20,12},{24,0},{28,4},{1,25},{... | collective-permute-start | bytes 1572872 | tf_op jit(solution)/shard_map/ppermute | solution.py:265
  193.8 57.6 %collective-permute-start.8 = (f32[128,1024]{1,0:T(8,128)S(1)}, f32[128,1024]{1,0:T(8,128)S(1)}, u32[]{:S(2)}, u32[]{:S(2)}) collective-permute-start(f32[128,1024]{1,0:T(8,128)S(1)} %copy-done.33), channel_id=1, source_target_pairs={{0,4},{4,0},{8,12},{12,8},{16,20},{20,16},{24,28},{28,24},{1,5},{5... | collective-permute-start | bytes 1572872 | tf_op jit(solution)/shard_map/ppermute | solution.py:265
  194.1 59.6 %collective-permute-start.9 = (f32[128,1024]{1,0:T(8,128)S(1)}, f32[128,1024]{1,0:T(8,128)S(1)}, u32[]{:S(2)}, u32[]{:S(2)}) collective-permute-start(f32[128,1024]{1,0:T(8,128)S(1)} %copy-done.32), channel_id=1, source_target_pairs={{0,8},{4,12},{8,0},{12,4},{16,24},{20,28},{24,16},{28,20},{1,9},{5... | collective-permute-start | bytes 1572872 | tf_op jit(solution)/shard_map/ppermute | solution.py:265
  194.1 62.0 %collective-permute-start.11 = (f32[128,1024]{1,0:T(8,128)S(1)}, f32[128,1024]{1,0:T(8,128)S(1)}, u32[]{:S(2)}, u32[]{:S(2)}) collective-permute-start(f32[128,1024]{1,0:T(8,128)S(1)} %copy-done.31), channel_id=1, source_target_pairs={{0,16},{4,20},{8,24},{12,28},{16,0},{20,4},{24,8},{28,12},{1,17},{... | collective-permute-start | bytes 1572872 | tf_op jit(solution)/shard_map/ppermute | solution.py:265
  195.2 62.5 %collective-permute-start.12 = (f32[128,1024]{1,0:T(8,128)S(1)}, f32[128,1024]{1,0:T(8,128)S(1)}, u32[]{:S(2)}, u32[]{:S(2)}) collective-permute-start(f32[128,1024]{1,0:T(8,128)S(1)} %copy-done.30), channel_id=1, source_target_pairs={{0,20},{4,16},{8,28},{12,24},{16,4},{20,0},{24,12},{28,8},{1,21},{... | collective-permute-start | bytes 1572872 | tf_op jit(solution)/shard_map/ppermute | solution.py:265
  251.4 58.4 %collective-permute-start.21 = (f32[64,512]{1,0:T(8,128)S(1)}, f32[64,512]{1,0:T(8,128)}, u32[]{:S(2)}, u32[]{:S(2)}) collective-permute-start(f32[64,512]{1,0:T(8,128)S(1)} %get-tuple-element.210), channel_id=1, source_target_pairs={{0,8},{4,12},{8,0},{12,4},{16,24},{20,28},{24,16},{28,20},{1,9},{5... | collective-permute-start | bytes 393224 | tf_op jit(solution)/shard_map/ppermute | solution.py:265
  251.4 65.8 %collective-permute-start.23 = (f32[64,512]{1,0:T(8,128)S(1)}, f32[64,512]{1,0:T(8,128)}, u32[]{:S(2)}, u32[]{:S(2)}) collective-permute-start(f32[64,512]{1,0:T(8,128)S(1)} %get-tuple-element.208), channel_id=1, source_target_pairs={{0,16},{4,20},{8,24},{12,28},{16,0},{20,4},{24,8},{28,12},{1,17},{... | collective-permute-start | bytes 393224 | tf_op jit(solution)/shard_map/ppermute | solution.py:265
  253.7 42.5 %collective-permute-start.14 = (f32[64,512]{1,0:T(8,128)}, f32[64,512]{1,0:T(8,128)S(1)}, u32[]{:S(2)}, u32[]{:S(2)}) collective-permute-start(f32[64,512]{1,0:T(8,128)} %get-tuple-element.214), channel_id=1, source_target_pairs={{0,24},{4,28},{8,16},{12,20},{16,8},{20,12},{24,0},{28,4},{1,25},{... | collective-permute-start | bytes 393224 | tf_op jit(solution)/shard_map/ppermute | solution.py:265
  256.1 43.1 %collective-permute-start.18 = (f32[64,512]{1,0:T(8,128)}, f32[64,512]{1,0:T(8,128)S(1)}, u32[]{:S(2)}, u32[]{:S(2)}) collective-permute-start(f32[64,512]{1,0:T(8,128)} %get-tuple-element.122), channel_id=1, source_target_pairs={{0,28},{4,24},{8,20},{12,16},{16,12},{20,8},{24,4},{28,0},{1,29},{... | collective-permute-start | bytes 393224 | tf_op jit(solution)/shard_map/ppermute | solution.py:265
  318.3 48.5 %collective-permute-start.27 = (f32[8,64,512]{2,1,0:T(8,128)S(1)}, f32[8,64,512]{2,1,0:T(8,128)S(1)}, u32[]{:S(2)}, u32[]{:S(2)}) collective-permute-start(f32[8,64,512]{2,1,0:T(8,128)S(1)} %constant_dynamic-update-slice_fusion.16.refs_1_), channel_id=1, source_target_pairs={{0,2},{1,3},{2,0},{3,1},{4,6},{5,7},{6,4},{7,5},{8,10},{9,11},{10,... | collective-permute-start | bytes 3145736 | tf_op jit(solution)/shard_map/ppermute | solution.py:49
  320.2 33.2 %collective-permute-start.19 = (f32[64,1024]{1,0:T(8,128)S(1)}, f32[64,1024]{1,0:T(8,128)S(1)}, u32[]{:S(2)}, u32[]{:S(2)}) collective-permute-start(f32[64,1024]{1,0:T(8,128)S(1)} %get-tuple-element.123), channel_id=1, source_target_pairs={{0,12},{4,8},{8,4},{12,0},{16,28},{20,24},{24,20},{28,16},{1,13},{... | collective-permute-start | bytes 786440 | tf_op jit(solution)/shard_map/ppermute | solution.py:265
  357.7 34.6 %collective-permute-start.37 = (f32[64,1024]{1,0:T(8,128)S(1)}, f32[64,1024]{1,0:T(8,128)S(1)}, u32[]{:S(2)}, u32[]{:S(2)}) collective-permute-start(f32[64,1024]{1,0:T(8,128)S(1)} %get-tuple-element.133), channel_id=1, source_target_pairs={{0,12},{4,8},{8,4},{12,0},{16,28},{20,24},{24,20},{28,16},{1,13},{... | collective-permute-start | bytes 786440 | tf_op jit(solution)/shard_map/ppermute | solution.py:265
  362.1 50.8 %collective-permute-start.42 = (f32[64,1024]{1,0:T(8,128)S(1)}, f32[64,1024]{1,0:T(8,128)S(1)}, u32[]{:S(2)}, u32[]{:S(2)}) collective-permute-start(f32[64,1024]{1,0:T(8,128)S(1)} %get-tuple-element.137), channel_id=1, source_target_pairs={{0,28},{4,24},{8,20},{12,16},{16,12},{20,8},{24,4},{28,0},{1,29},{... | collective-permute-start | bytes 786440 | tf_op jit(solution)/shard_map/ppermute | solution.py:265
  366.7 46.1 %collective-permute-start.41 = (f32[64,1024]{1,0:T(8,128)S(1)}, f32[64,1024]{1,0:T(8,128)S(1)}, u32[]{:S(2)}, u32[]{:S(2)}) collective-permute-start(f32[64,1024]{1,0:T(8,128)S(1)} %get-tuple-element.136), channel_id=1, source_target_pairs={{0,24},{4,28},{8,16},{12,20},{16,8},{20,12},{24,0},{28,4},{1,25},{... | collective-permute-start | bytes 786440 | tf_op jit(solution)/shard_map/ppermute | solution.py:265
  392.3 48.8 %collective-permute-start.56 = (f32[8,64,1024]{2,1,0:T(8,128)}, f32[8,64,1024]{2,1,0:T(8,128)S(1)}, u32[]{:S(2)}, u32[]{:S(2)}) collective-permute-start(f32[8,64,1024]{2,1,0:T(8,128)} %bitcast_dynamic-update-slice_fusion.refs_0_), channel_id=1, source_target_pairs={{0,2},{1,3},{2,0},{3,1},{4,6},{5,7},{6,4},{7,5},{8,10},{9,11},{10,... | collective-permute-start | bytes 6291464 | tf_op jit(solution)/shard_map/ppermute | solution.py:49
  412.9 63.0 %collective-permute-start.43 = (f32[8,64,1024]{2,1,0:T(8,128)S(1)}, f32[8,64,1024]{2,1,0:T(8,128)}, u32[]{:S(2)}, u32[]{:S(2)}) collective-permute-start(f32[8,64,1024]{2,1,0:T(8,128)S(1)} %bitcast_dynamic-update-slice_fusion.7.refs_6_), channel_id=1, source_target_pairs={{0,2},{1,3},{2,0},{3,1},{4,6},{5,7},{6,4},{7,5},{8,10},{9,11},{10,... | collective-permute-start | bytes 6291464 | tf_op jit(solution)/shard_map/ppermute | solution.py:49
  420.4 32.0 %collective-permute-start.58 = (f32[64,512]{1,0:T(8,128)S(1)}, f32[64,512]{1,0:T(8,128)S(1)}, u32[]{:S(2)}, u32[]{:S(2)}) collective-permute-start(f32[64,512]{1,0:T(8,128)S(1)} %get-tuple-element.171), channel_id=1, source_target_pairs={{0,12},{4,8},{8,4},{12,0},{16,28},{20,24},{24,20},{28,16},{1,13},{... | collective-permute-start | bytes 393224 | tf_op jit(solution)/shard_map/ppermute | solution.py:265
  420.4 64.4 %collective-permute-start.46 = (f32[64,512]{1,0:T(8,128)S(1)}, f32[64,512]{1,0:T(8,128)S(1)}, u32[]{:S(2)}, u32[]{:S(2)}) collective-permute-start(f32[64,512]{1,0:T(8,128)S(1)} %get-tuple-element.178), channel_id=1, source_target_pairs={{0,16},{4,20},{8,24},{12,28},{16,0},{20,4},{24,8},{28,12},{1,17},{... | collective-permute-start | bytes 393224 | tf_op jit(solution)/shard_map/ppermute | solution.py:265
  441.2 45.5 %collective-permute-start.47 = (f32[64,512]{1,0:T(8,128)S(1)}, f32[64,512]{1,0:T(8,128)S(1)}, u32[]{:S(2)}, u32[]{:S(2)}) collective-permute-start(f32[64,512]{1,0:T(8,128)S(1)} %get-tuple-element.177), channel_id=1, source_target_pairs={{0,20},{4,16},{8,28},{12,24},{16,4},{20,0},{24,12},{28,8},{1,21},{... | collective-permute-start | bytes 393224 | tf_op jit(solution)/shard_map/ppermute | solution.py:265
  527.8 62.7 %collective-permute-start.76 = (f32[8,64,1024]{2,1,0:T(8,128)}, f32[8,64,1024]{2,1,0:T(8,128)S(1)}, u32[]{:S(2)}, u32[]{:S(2)}) collective-permute-start(f32[8,64,1024]{2,1,0:T(8,128)} %copy-done.16), channel_id=1, source_target_pairs={{0,1},{1,0},{2,3},{3,2},{4,5},{5,4},{6,7},{7,6},{8,9},{9,8},{10,11... | collective-permute-start | bytes 6291464 | tf_op jit(solution)/shard_map/ppermute | solution.py:49
  528.3 62.2 %collective-permute-start.75 = (f32[8,64,1024]{2,1,0:T(8,128)}, f32[8,64,1024]{2,1,0:T(8,128)}, u32[]{:S(2)}, u32[]{:S(2)}) collective-permute-start(f32[8,64,1024]{2,1,0:T(8,128)} %copy-done.17), channel_id=1, source_target_pairs={{0,1},{1,0},{2,3},{3,2},{4,5},{5,4},{6,7},{7,6},{8,9},{9,8},{10,11... | collective-permute-start | bytes 6291464 | tf_op jit(solution)/shard_map/ppermute | solution.py:49
  532.2 44.2 %collective-permute-start.78 = (f32[8,64,512]{2,1,0:T(8,128)}, f32[8,64,512]{2,1,0:T(8,128)}, u32[]{:S(2)}, u32[]{:S(2)}) collective-permute-start(f32[8,64,512]{2,1,0:T(8,128)} %constant_dynamic-update-slice_fusion.32.refs_7_), channel_id=1, source_target_pairs={{0,2},{1,3},{2,0},{3,1},{4,6},{5,7},{6,4},{7,5},{8,10},{9,11},{10,... | collective-permute-start | bytes 3145736 | tf_op jit(solution)/shard_map/ppermute | solution.py:49
  535.4 55.0 %collective-permute-start.74 = (f32[8,64,512]{2,1,0:T(8,128)}, f32[8,64,512]{2,1,0:T(8,128)S(1)}, u32[]{:S(2)}, u32[]{:S(2)}) collective-permute-start(f32[8,64,512]{2,1,0:T(8,128)} %copy-done.19), channel_id=1, source_target_pairs={{0,1},{1,0},{2,3},{3,2},{4,5},{5,4},{6,7},{7,6},{8,9},{9,8},{10,11... | collective-permute-start | bytes 3145736 | tf_op jit(solution)/shard_map/ppermute | solution.py:49
  554.4 36.1 %collective-permute-start.79 = (f32[8,64,512]{2,1,0:T(8,128)}, f32[8,64,512]{2,1,0:T(8,128)S(1)}, u32[]{:S(2)}, u32[]{:S(2)}) collective-permute-start(f32[8,64,512]{2,1,0:T(8,128)} %collective-permute-done.77.refs_8_), channel_id=1, source_target_pairs={{0,1},{1,0},{2,3},{3,2},{4,5},{5,4},{6,7},{7,6},{8,9},{9,8},{10,11... | collective-permute-start | bytes 3145736 | tf_op jit(solution)/shard_map/ppermute | solution.py:49
  (84 other events, 1473.9 us)

commit v5 on v3

--- a/solution.py
+++ b/solution.py
@@ -54,11 +54,11 @@
     return top, (values - top.astype(jnp.float32)).astype(jnp.bfloat16)
 
 
-def vectors_first_kernel(start_ref, block_ref, out_ref):
+def vectors_first_kernel(place_ref, block_ref, out_ref):
     out_ref[...] = jnp.swapaxes(block_ref[...], 0, 1)
 
 
-def vectors_first(start_block, turn, count, swapped):
+def vectors_first(start_block, turn, count, place):
     up_local, _, down_count = start_block.shape
     rows = 16
     blocks = up_local // rows
@@ -71,20 +71,29 @@
             in_specs=[
                 pl.BlockSpec(
                     (rows, count, down_count),
-                    lambda i, swap: (lax.rem(i + swap[0] * (blocks // 2), blocks), turn, 0),
+                    lambda i, place: (lax.rem(i + place[0] * (blocks // 2), blocks), turn, 0),
                 )
             ],
-            out_specs=pl.BlockSpec((count, rows, down_count), lambda i, swap: (0, i, 0)),
+            out_specs=pl.BlockSpec((count, rows, down_count), lambda i, place: (0, i, 0)),
         ),
         compiler_params=pltpu.CompilerParams(vmem_limit_bytes=56 * 1024 * 1024),
-    )(swapped, start_block)
-
-
-def stacked(refs):
-    return jnp.concatenate([jnp.swapaxes(ref[...], 0, 1) for ref in refs], axis=1)
-
-
-def gram_kernel(start_ref, *refs):
+    )(place, start_block)
+
+
+def joined(refs):
+    return jnp.concatenate([ref[...] for ref in refs], axis=-1)
+
+
+def grouped(refs, counts):
+    ends = [sum(counts[: i + 1]) for i in range(len(counts))]
+    return [refs[end - count : end] for end, count in zip(ends, counts)]
+
+
+def stacked(refs, counts):
+    return jnp.concatenate([jnp.swapaxes(joined(cuts), 0, 1) for cuts in grouped(refs, counts)], axis=1)
+
+
+def gram_kernel(counts, start_ref, *refs):
     inputs, (top_ref, cross_ref) = refs[:-2], refs[-2:]
 
     @pl.when(pl.program_id(0) == 0)
@@ -92,7 +101,7 @@
         top_ref[...] = jnp.zeros_like(top_ref)
         cross_ref[...] = jnp.zeros_like(cross_ref)
 
-    values = stacked(inputs)
+    values = stacked(inputs, counts)
     rows, vectors, columns = values.shape
     for first in range(0, rows, STACK):
         top, low = split(values[first : first + STACK].reshape(STACK * vectors, columns))
@@ -101,16 +110,16 @@
 
 
 def gram_partial(pieces, part, parts):
-    vectors = sum(piece.shape[0] for piece in pieces)
-    block = 8
-    blocks = pieces[0].shape[1] // parts // block
+    vectors = sum(cuts[0].shape[0] for cuts in pieces)
+    blocks = pieces[0][0].shape[1] // parts // SUBLANES
+    flat = [cut for cuts in pieces for cut in cuts]
     specs = [
-        pl.BlockSpec((piece.shape[0], block, piece.shape[2]), lambda i, first: (0, first[0] + i, 0)) for piece in pieces
+        pl.BlockSpec((cut.shape[0], SUBLANES, cut.shape[2]), lambda i, first: (0, first[0] + i, 0)) for cut in flat
     ]
     size = STACK * vectors
     out = jax.ShapeDtypeStruct((size, size), jnp.float32)
     top, cross = pl.pallas_call(
-        gram_kernel,
+        functools.partial(gram_kernel, [len(cuts) for cuts in pieces]),
         out_shape=(out, out),
         grid_spec=pltpu.PrefetchScalarGridSpec(
             num_scalar_prefetch=1,
@@ -119,50 +128,62 @@
             out_specs=[pl.BlockSpec((size, size), lambda i, first: (0, 0))] * 2,
         ),
         compiler_params=pltpu.CompilerParams(vmem_limit_bytes=48 * 1024 * 1024),
-    )((part * blocks).reshape(1), *pieces)
+        cost_estimate=pl.CostEstimate(
+            flops=4 * size * size * flat[0].shape[2] * blocks * SUBLANES // STACK,
+            bytes_accessed=4 * sum(cut.size for cut in flat) // parts,
+            transcendentals=0,
+        ),
+    )((part * blocks).reshape(1), *flat)
     cross = cross + cross.T
     total = (top + cross).reshape(STACK, vectors, STACK, vectors)
     return sum(total[u, :, u, :] for u in range(STACK))
 
 
-def rotate_kernel(swap_ref, mix_ref, *refs):
-    inputs, out_ref = [ref for ref in refs[:-1] if ref.ndim == 3 and ref.shape[1] == SUBLANES], refs[-1]
+def rotate_kernel(counts, place_ref, mix_ref, *refs):
+    inputs, out_ref = refs[: sum(counts)], refs[-1]
     columns = out_ref.shape[2]
     mix_top, mix_low = split(mix_ref[...])
     count = mix_top.shape[0]
     both = jnp.concatenate([mix_top, mix_low], axis=0)
-    top, low = split(jnp.concatenate([ref[...].reshape(-1, columns) for ref in inputs], axis=0))
+    top, low = split(jnp.concatenate([joined(cuts).reshape(-1, columns) for cuts in grouped(inputs, counts)], axis=0))
     wide = dot(both, top, (1, 0), None)
     result = wide[:count] + wide[count:] + dot(mix_top, low, (1, 0), None)
-    out_ref[...] = jnp.swapaxes(result.reshape(-1, SUBLANES, columns), 0, 1)
-
-
-def rotate_half(pieces, wide_mixing, swapped, half, earlier):
-    half_rows, down_count = pieces[0].shape[1:]
+    out_ref[...] = result.reshape(SUBLANES, -1, columns)
+
+
+def rotate_half(pieces, wide_mixing, place, half, earlier):
+    half_rows = pieces[0][0].shape[1]
+    down_count = sum(cut.shape[2] for cut in pieces[0])
     blocks = half_rows // SUBLANES
     own = wide_mixing.shape[0] // SUBLANES
-    specs = [pl.BlockSpec(wide_mixing.shape, lambda i, swap: (0, 0))]
-    for piece in pieces:
-        specs.append(pl.BlockSpec((piece.shape[0], SUBLANES, down_count), lambda i, swap: (0, i, 0)))
-    operands = [swapped, wide_mixing, *pieces]
+    flat = [cut for cuts in pieces for cut in cuts]
+    specs = [pl.BlockSpec(wide_mixing.shape, lambda i, place: (0, 0))]
+    for cut in flat:
+        specs.append(pl.BlockSpec((cut.shape[0], SUBLANES, cut.shape[2]), lambda i, place: (0, i, 0)))
+    operands = [place, wide_mixing, *flat]
     aliases = {}
     if earlier is not None:
         specs.append(pl.BlockSpec(memory_space=pl.ANY))
         aliases = {len(operands): 0}
         operands.append(earlier)
     return pl.pallas_call(
-        rotate_kernel,
+        functools.partial(rotate_kernel, [len(cuts) for cuts in pieces]),
         out_shape=jax.ShapeDtypeStruct((2 * half_rows, own, down_count), jnp.float32),
         grid_spec=pltpu.PrefetchScalarGridSpec(
             num_scalar_prefetch=1,
             grid=(blocks,),
             in_specs=specs,
             out_specs=pl.BlockSpec(
-                (SUBLANES, own, down_count), lambda i, swap: (i + lax.rem(swap[0] + half, 2) * blocks, 0, 0)
+                (SUBLANES, own, down_count), lambda i, place: (i + lax.rem(place[0] + half, 2) * blocks, 0, 0)
             ),
         ),
         input_output_aliases=aliases,
         compiler_params=pltpu.CompilerParams(vmem_limit_bytes=56 * 1024 * 1024),
+        cost_estimate=pl.CostEstimate(
+            flops=6 * wide_mixing.size * down_count * blocks,
+            bytes_accessed=4 * (sum(cut.size for cut in flat) + half_rows * own * down_count),
+            transcendentals=0,
+        ),
     )(*operands)
 
 
@@ -203,7 +224,7 @@
     side = vec_parts // 2
     own = lax.axis_index("vec")
     swap = own // side
-    swapped = swap.reshape(1).astype(jnp.int32)
+    place = swap.reshape(1).astype(jnp.int32)
 
     def ordered(values):
         cut = values.reshape(values.shape[:-1] + (hil_parts, 2, half_rows))
@@ -211,7 +232,7 @@
 
     arrived = []
     for turn in range(rounds):
-        block = vectors_first(start_block, turn, hil_parts, swapped)
+        block = vectors_first(start_block, turn, hil_parts, place)
         block = lax.all_to_all(block, "hil", split_axis=0, concat_axis=0, tiled=True)
         arrived.append(block.reshape(up_count, down_count))
     other = jnp.where((hop_partner // half_rows) % 2 == 0, hop_partner + half_rows, hop_partner - half_rows)
@@ -253,7 +274,12 @@
                 piece, crossed[-2] = lax.optimization_barrier((piece, crossed[-2]))
             back = lax.all_to_all(piece, "hil", split_axis=0, concat_axis=0, tiled=True)
             held[half].append(back)
-            crossed.append(spread_step([back], side)[0])
+            if (turn, half) == (rounds - 1, mine):
+                bounds = [0, down_count // 4, down_count // 8 * 5, down_count]
+                cuts = [back[:, :, begin:end] for begin, end in zip(bounds, bounds[1:])]
+                crossed.append(spread_step(cuts[:1], side)[0])
+            else:
+                crossed.append(spread_step([back], side)[0])
         pieces = upcoming
 
     def on_side(near):
@@ -263,30 +289,42 @@
             step //= 2
         return near
 
-    halves = [[], []]
+    own_pieces = []
     for turn in range(rounds):
-        halves[mine].extend(on_side([held[mine][turn], crossed[2 * turn]]))
-    distances = [0, side]
-    step = side // 2
+        own_pieces += [[piece] for piece in on_side([held[mine][turn]]) + on_side([crossed[2 * turn]])]
+    step, distances = side // 2, [0]
     while step >= 1:
         distances += [distance ^ step for distance in distances]
         step //= 2
+    distances += [distance ^ side for distance in distances]
     near = jnp.bitwise_xor(jnp.array(distances, dtype=jnp.int32), own)
     exchange = (near[:, None] == jnp.arange(vec_parts, dtype=jnp.int32)[None, :]).astype(jnp.float32)
     order = jnp.kron(jnp.eye(rounds, dtype=jnp.float32), jnp.kron(exchange, jnp.eye(hil_parts, dtype=jnp.float32)))
-    partial = gram_partial(halves[mine], lax.rem(own, side), side)
+    order_own = order.reshape(rounds, vec_parts, hil_parts, -1)[:, 0].reshape(vec_local, -1)
+    partial = gram_partial(own_pieces, lax.rem(own, side), side)
     partial = dot(order, dot(partial, order, (1, 0), highest), (0, 0), highest)
-    gram_sum = small_sum(small_sum(partial, "vec"), "hil")
-    gram_sum, crossed[-1] = lax.optimization_barrier((gram_sum, crossed[-1]))
+    partial, cuts[0] = lax.optimization_barrier((partial, crossed[-1]))
+    partial, cuts[1] = lax.optimization_barrier((small_sum(partial, "vec"), cuts[1]))
+    cuts[1] = spread_step(cuts[1:2], side)[0]
+    gram_sum, cuts[1], cuts[2] = lax.optimization_barrier((small_sum(partial, "hil"), cuts[1], cuts[2]))
+    cuts[2] = spread_step(cuts[2:], side)[0]
+    mixing = newton_schulz(gram_sum) * math.sqrt(up_count * down_count)
+    mixing = dot(dot(order_own, mixing, (1, 1), highest), order, (1, 1), highest)
+    wide = jnp.arange(vec_local * SUBLANES, dtype=jnp.int32)
+    long = jnp.arange(order.shape[0] * SUBLANES, dtype=jnp.int32)
+    left = (wide[:, None] % vec_local == jnp.arange(vec_local, dtype=jnp.int32)[None, :]).astype(jnp.float32)
+    right = (jnp.arange(order.shape[0], dtype=jnp.int32)[:, None] == long[None, :] // SUBLANES).astype(jnp.float32)
+    wide_mixing = dot(left, dot(mixing, right, (1, 0), highest), (1, 0), highest)
+    wide_mixing = jnp.where(wide[:, None] // vec_local == long[None, :] % SUBLANES, wide_mixing, 0.0)
+    result = rotate_half(own_pieces, wide_mixing, place, mine, None)
+    result, cuts[2] = lax.optimization_barrier((result, cuts[2]))
+    other_pieces = []
     for turn in range(rounds):
-        halves[theirs].extend(on_side([held[theirs][turn], crossed[2 * turn + 1]]))
-    mixing = newton_schulz(gram_sum)
-    mixing = dot(dot(order, mixing, (1, 0), highest), order, (1, 1), highest)
-    mixing = mixing.reshape(-1, rounds, vec_parts, hil_parts)[:, :, 0].reshape(-1, vec_local)
-    mixing = mixing * math.sqrt(up_count * down_count)
-    wide_mixing = jnp.kron(mixing.T, jnp.eye(SUBLANES, dtype=jnp.float32))
-    result = rotate_half(halves[mine], wide_mixing, swapped, mine, None)
-    return rotate_half(halves[theirs], wide_mixing, swapped, theirs, result)
+        there = cuts if turn == rounds - 1 else [crossed[2 * turn + 1]]
+        here = [[piece] for piece in on_side([held[theirs][turn]])]
+        there = [list(group) for group in zip(*[on_side([cut]) for cut in there])]
+        other_pieces += here + there
+    return rotate_half(other_pieces, wide_mixing, place, theirs, result)
 
 
 def split_down(local_block):

time: 520 us -> 502 us (0.965)
  waiting for transfers between devices: 274 us -> 255 us
    ppermute x7, waiting for transfers between devices: 38.3 us -> 6.14 us  [small_sum(): lax.ppermute(values, axis, [(i, i ^ distance) for i in range(parts)])]
    ppermute x12 -> x16, waiting for transfers between devices: 83.5 us -> 96.3 us  [spread_step(): return [lax.ppermute(piece, 'vec', pairs) for piece in held]]
    dot_general x25 -> x28, matrix products: 103 us -> 104 us  [dot(): lax.dot_general(left, right, ((contract[:1], contract[1:]), ((), ())), pr...]
  transfers between devices with their start and end apart: 25 -> 29, of which waited for: 14 -> 18; matrix products, arithmetic and copies ran while one was open for 27% -> 27% of each run, Pallas kernels for 5% -> 5%
where the time goes in v5:
time: 502 us; the launch traced here: 493 us
  waiting for transfers between devices  255 us (51%)
  matrix products  110 us (22%)
  starting transfers between devices  49.5 us (10%)
  Pallas kernels  42.8 us (9%)
  local copies, waits for them, and re-layouts  27.9 us (6%)
  other arithmetic  6.67 us (1%)
    dot_general x28, matrix products, dot(): lax.dot_general(left, right, ((contract[:1], contract[1:]), ((), ())), pr...  104 us
    all_to_all x2, waiting for transfers between devices, vector_cut(): lax.all_to_all(block, 'hil', split_axis=0, concat_axis=0, tiled=True)  102 us
    ppermute x16, waiting for transfers between devices, spread_step(): return [lax.ppermute(piece, 'vec', pairs) for piece in held]  96.3 us
    all_to_all x4, waiting for transfers between devices, vector_cut(): back = lax.all_to_all(piece, 'hil', split_axis=0, concat_axis=0, tiled=True)  50.3 us
    pallas_call x2, Pallas kernels, rotate_half(): pl.pallas_call(functools.partial(rotate_kernel, [len(cuts) for cuts in pi...  23 us
    all_to_all x4, starting transfers between devices, vector_cut(): back = lax.all_to_all(piece, 'hil', split_axis=0, concat_axis=0, tiled=True)  19.2 us
    pallas_call x2, Pallas kernels, vectors_first(): pl.pallas_call(vectors_first_kernel, out_shape=jax.ShapeDtypeStruct((coun...  13.9 us
    all_to_all x2, starting transfers between devices, vector_cut(): lax.all_to_all(block, 'hil', split_axis=0, concat_axis=0, tiled=True)  11.8 us
  transfers between devices with their start and end apart: 29, of which 18 were waited for; matrix products, arithmetic and copies ran while one was open for 27% of the time, Pallas kernels for 5%

profile of v5, /device:TPU:0, one launch (start us, length us, event | category | flops | bytes accessed | tf_op | source)
XLA Modules:
  0.0 492.9 jit_solution(8324404245952062877)
XLA Ops:
  0.0 6.9 %shard_map.73 = f32[8,128,1024]{2,1,0:T(8,128)} custom-call(s32[1]{0:T(128)} %bitcast.place_ref, f32[128,16,1024]{2,1,0:T(8,128)} %block_ref.3), custom_call_target="tpu_custom_call" | custom-call | tf_op jit(solution)/shard_map/pallas_call | solution.py:65
  6.9 7.3 %all-to-all-start = ((f32[8,128,1024]{2,1,0:T(8,128)}), f32[8,128,1024]{2,1,0:T(8,128)}, u32[]{:S(2)}, u32[]{:S(2)}) async-start(f32[8,128,1024]{2,1,0:T(8,128)} %shard_map.73), calls=%async_computation | async-start | bytes 8388608 | tf_op jit(solution)/shard_map/all_to_all | solution.py:236
  14.2 7.0 %shard_map.74 = f32[8,128,1024]{2,1,0:T(8,128)} custom-call(s32[1]{0:T(128)} %bitcast.place_ref, f32[128,16,1024]{2,1,0:T(8,128)} %block_ref.3), custom_call_target="tpu_custom_call" | custom-call | tf_op jit(solution)/shard_map/pallas_call | solution.py:65
  23.8 5.3 %convolution_add_fusion = f32[1024,1024]{1,0:T(8,128)} fusion(f32[10]{0:T(128)S(1)} %copy-done.22, s32[1024]{0:T(1024)S(1)} %shift_right_arithmetic.28), kind=kOutput, calls=%fused_computation.24 | convolution fusion | flops 126949376 | bytes 4198440 | tf_op jit(solution)/shard_map/dot_general | solution.py:241
  29.1 78.3 %all-to-all-done = f32[8,128,1024]{2,1,0:T(8,128)} async-done(((f32[8,128,1024]{2,1,0:T(8,128)}), f32[8,128,1024]{2,1,0:T(8,128)}, u32[]{:S(2)}, u32[]{:S(2)}) %all-to-all-start) | async-done | bytes 4194336 | tf_op jit(solution)/shard_map/all_to_all | solution.py:236
  107.4 4.6 all-to-all-start.1
  112.0 5.4 %select_add_fusion = f32[8,2,64,1024]{3,2,1,0:T(8,128)S(1)} fusion(f32[8,2,64]{2,1,0:T(2,128)S(1)} %get-tuple-element.85, s32[8,2,64]{2,1,0:T(2,128)S(1)} %get-tuple-element.66, f32[8,2,64]{2,1,0:T(2,128)S(1)} %get-tuple-element.84, s32[8,2,64]{2,1,0:T(2,128)S(1)} %get-tuple-element.65, f32[8,2,64]{2,1,0:T(2,128)S(1)} %get-tuple-element.83, ...), kind=kLoop, calls=%fused_computation.1 | loop fusion | flops 30408704 | bytes 4276224 | tf_op jit(solution)/shard_map/add | solution.py:32
  124.1 8.9 %fusion.120 = f32[1024,1024]{1,0:T(8,128)S(1)} fusion(f32[1024,1024]{1,0:T(8,128)} %bitcast.3, f32[1024,1024]{1,0:T(8,128)S(1)} %copy-done.1), kind=kOutput, calls=%fused_computation.219 | convolution fusion | flops 6442450944 | bytes 12582912 | tf_op jit(solution)/shard_map/dot_general | solution.py:37
  133.0 17.0 %add_multiply_fusion.1 = f32[1024,1024]{1,0:T(8,128)S(1)} fusion(f32[1024,1024]{1,0:T(8,128)S(1)} %copy-done.12, f32[1024,1024]{1,0:T(8,128)} %bitcast.3, f32[1024,1024]{1,0:T(8,128)S(1)} %fusion.120, f32[1024]{0:T(1024)S(1)} %broadcast_in_dim.182, s32[1024]{0:T(1024)S(1)} %eq.388, f32[1024]{0:T(1024)S(1)} %broadcast_in_dim.180, s32[1024]{0:T(1024)S(1)} %eq.384, ...), kind=kOutput, calls=%fused_computation.12 | convolution fusion | flops 6477053952 | bytes 16859136 | tf_op jit(solution)/shard_map/dot_general | solution.py:37
  153.2 3.6 fusion.122
  156.8 3.6 fusion.121
  160.5 5.5 %bitcast_subtract_fusion.2 = f32[512,1024]{1,0:T(8,128)} fusion(f32[8,1,64,1024]{3,2,1,0:T(8,128)S(1)} %get-tuple-element.53, f32[512,1024]{1,0:T(8,128)S(1)} %bitcast.162, f32[8,1,64,1024]{3,2,1,0:T(8,128)S(1)} %get-tuple-element.49, f32[512,1024]{1,0:T(8,128)S(1)} %fusion.122, f32[512,1024]{1,0:T(8,128)S(1)} %bitcast.163, ...), kind=kOutput, calls=%fused_computation.27 | convolution fusion | flops 3223846912 | bytes 16777216 | tf_op jit(solution)/shard_map/dot_general | solution.py:37
  166.0 14.9 %bitcast_subtract_fusion.3 = f32[512,1024]{1,0:T(8,128)} fusion(f32[8,1,64,1024]{3,2,1,0:T(8,128)S(1)} %get-tuple-element.54, f32[512,1024]{1,0:T(8,128)S(1)} %bitcast.160, f32[8,1,64,1024]{3,2,1,0:T(8,128)S(1)} %get-tuple-element.50, f32[512,1024]{1,0:T(8,128)S(1)} %fusion.121, f32[512,1024]{1,0:T(8,128)S(1)} %bitcast.165, ...), kind=kOutput, calls=%fused_computation.34 | convolution fusion | flops 3223846912 | bytes 16777216 | tf_op jit(solution)/shard_map/dot_general | solution.py:37
  180.9 23.6 %all-to-all-done.1 = f32[8,128,1024]{2,1,0:T(8,128)} async-done(((f32[8,128,1024]{2,1,0:T(8,128)}), f32[8,128,1024]{2,1,0:T(8,128)}, u32[]{:S(2)}, u32[]{:S(2)}) %all-to-all-start.1) | async-done | bytes 4194336 | tf_op jit(solution)/shard_map/all_to_all | solution.py:236
  204.6 4.3 all-to-all-start.3
  208.9 10.6 %fusion.123 = f32[1024,1024]{1,0:T(8,128)S(1)} fusion(f32[1024,1024]{1,0:T(8,128)} %bitcast.37, f32[1024,1024]{1,0:T(8,128)} %param.8), kind=kOutput, calls=%fused_computation.222 | convolution fusion | flops 6442450944 | bytes 12582912 | tf_op jit(solution)/shard_map/dot_general | solution.py:37
  219.6 17.0 %add_multiply_fusion = f32[1024,1024]{1,0:T(8,128)S(1)} fusion(f32[1024,1024]{1,0:T(8,128)S(1)} %copy-done.13, f32[1024,1024]{1,0:T(8,128)} %bitcast.37, f32[1024,1024]{1,0:T(8,128)S(1)} %fusion.123, f32[1024]{0:T(1024)S(1)} %broadcast_in_dim.182, s32[1024]{0:T(1024)S(1)} %eq.388, f32[1024]{0:T(1024)S(1)} %broadcast_in_dim.180, s32[1024]{0:T(1024)S(1)} %eq.384, ...), kind=kOutput, calls=%fused_computation | convolution fusion | flops 6477053952 | bytes 16859136 | tf_op jit(solution)/shard_map/dot_general | solution.py:37
  236.9 5.3 %fusion.114 = (f32[8,1,64,1024]{3,2,1,0:T(8,128)}, f32[8,1,64,1024]{3,2,1,0:T(8,128)S(1)}) fusion(f32[8,2,64,1024]{3,2,1,0:T(8,128)} %bitcast.40), kind=kLoop, calls=%fused_computation.213 | loop fusion | bytes 8388608 | tf_op jit(solution)/shard_map/slice | solution.py:249
  245.8 5.7 %bitcast_subtract_fusion.1 = f32[512,1024]{1,0:T(8,128)} fusion(f32[8,1,64,1024]{3,2,1,0:T(8,128)S(1)} %get-tuple-element.46, f32[512,1024]{1,0:T(8,128)S(1)} %bitcast.156, f32[8,1,64,1024]{3,2,1,0:T(8,128)S(1)} %copy-done.11, f32[512,1024]{1,0:T(8,128)S(1)} %fusion.124, f32[512,1024]{1,0:T(8,128)S(1)} %bitcast.166, f32[1024,1024]{1,0:T(8,128)S(1)} %add_multiply_fusion), kind=kOutput, calls=%fused_computation.26 | convolution fusion | flops 3223846912 | bytes 16777216 | tf_op jit(solution)/shard_map/dot_general | solution.py:37
  251.5 5.3 %all-to-all-done.3.refs_0_ = f32[8,64,1024]{2,1,0:T(8,128)} async-done(((f32[8,64,1024]{2,1,0:T(8,128)}), f32[8,64,1024]{2,1,0:T(8,128)}, u32[]{:S(2)}, u32[]{:S(2)}) %all-to-all-start.3) | async-done | bytes 2097184 | tf_op jit(solution)/shard_map/all_to_all | solution.py:275
  256.7 3.6 all-to-all-start.2
  261.9 46.0 %collective-permute-done.1.refs_2_ = f32[8,64,1024]{2,1,0:T(8,128)} collective-permute-done((f32[8,64,1024]{2,1,0:T(8,128)}, f32[8,64,1024]{2,1,0:T(8,128)}, u32[]{:S(2)}, u32[]{:S(2)}) %collective-permute-start.1) | collective-permute-done | bytes 2097184 | tf_op jit(solution)/shard_map/ppermute | solution.py:49
  308.8 5.2 %all-to-all-start.5 = ((f32[8,64,1024]{2,1,0:T(8,128)}), f32[8,64,1024]{2,1,0:T(8,128)}, u32[]{:S(2)}, u32[]{:S(2)}) async-start(f32[8,64,1024]{2,1,0:T(8,128)} %bitcast.170), calls=%async_computation.5 | async-start | bytes 4194304 | tf_op jit(solution)/shard_map/all_to_all | solution.py:275
  317.3 3.7 fusion.125
  321.1 6.5 %bitcast_subtract_fusion = f32[512,1024]{1,0:T(8,128)} fusion(f32[8,1,64,1024]{3,2,1,0:T(8,128)} %get-tuple-element.45, f32[512,1024]{1,0:T(8,128)S(1)} %bitcast.158, f32[8,1,64,1024]{3,2,1,0:T(8,128)S(1)} %copy-done.9, f32[512,1024]{1,0:T(8,128)S(1)} %fusion.125, f32[512,1024]{1,0:T(8,128)S(1)} %bitcast.164, f32[1024,1024]{1,0:T(8,128)S(1)} %copy-done.5), kind=kOutput, calls=%fused_computation.25 | convolution fusion | flops 3223846912 | bytes 16777216 | tf_op jit(solution)/shard_map/dot_general | solution.py:37
  327.6 32.5 %collective-permute-done.3.refs_2_ = f32[8,64,1024]{2,1,0:T(8,128)S(1)} collective-permute-done((f32[8,64,1024]{2,1,0:T(8,128)S(1)}, f32[8,64,1024]{2,1,0:T(8,128)S(1)}, u32[]{:S(2)}, u32[]{:S(2)}) %collective-permute-start.3) | collective-permute-done | bytes 2097184 | tf_op jit(solution)/shard_map/ppermute | solution.py:49
  361.4 6.1 %all-to-all-start.4 = ((f32[8,64,1024]{2,1,0:T(8,128)}), f32[8,64,1024]{2,1,0:T(8,128)}, u32[]{:S(2)}, u32[]{:S(2)}) async-start(f32[8,64,1024]{2,1,0:T(8,128)} %bitcast.171), calls=%async_computation.4 | async-start | bytes 4194304 | tf_op jit(solution)/shard_map/all_to_all | solution.py:275
  369.6 44.2 %all-to-all-done.4.refs_4_ = f32[8,64,1024]{2,1,0:T(8,128)} async-done(((f32[8,64,1024]{2,1,0:T(8,128)}), f32[8,64,1024]{2,1,0:T(8,128)}, u32[]{:S(2)}, u32[]{:S(2)}) %all-to-all-start.4) | async-done | bytes 2097184 | tf_op jit(solution)/shard_map/all_to_all | solution.py:275
  421.3 5.9 %shard_map.75 = (f32[256,256]{1,0:T(8,128)S(1)}, f32[256,256]{1,0:T(8,128)S(1)}) custom-call(s32[1]{0:T(128)} %bitcast.2.start_ref, f32[8,64,1024]{2,1,0:T(8,128)S(1)} %all-to-all-done.2.refs_0_, f32[8,64,1024]{2,1,0:T(8,128)} %collective-permute-done.refs_1_, f32[8,64,1024]{2,1,0:T(8,128)} %collective-permute-done.1.refs_2_, ...), custom_call_target="tpu_custom_call" | custom-call | flops 2147483648 | bytes 8388608 | tf_op jit(solution)/shard_map/pallas_call | solution.py:121
  448.9 6.2 %collective-permute-done.15.refs_7_ = f32[8,64,384]{2,1,0:T(8,128)} collective-permute-done((f32[8,64,384]{2,1,0:T(8,128)}, f32[8,64,384]{2,1,0:T(8,128)}, u32[]{:S(2)}, u32[]{:S(2)}) %collective-permute-start.15) | collective-permute-done | bytes 786464 | tf_op jit(solution)/shard_map/ppermute | solution.py:49
  461.1 11.5 %shard_map.76.refs_12_ = f32[128,16,1024]{2,1,0:T(8,128)} custom-call(s32[1]{0:T(128)} %bitcast.place_ref, f32[128,512]{1,0:T(8,128)} %convolution_select_fusion.mix_ref, f32[8,64,1024]{2,1,0:T(8,128)} %copy-done, f32[8,64,1024]{2,1,0:T(8,128)} %collective-permute-done.refs_1_, f32[8,64,1024]{2,1,0:T(8,128)} %collective-permute-done.1.refs_2_, ...), custom_call_target="tpu_custom_call" | custom-call | flops 3221225472 | bytes 20971520 | tf_op jit(solution)/shard_map/pallas_call | solution.py:169
  480.9 11.5 %shard_map.77 = f32[128,16,1024]{2,1,0:T(8,128)} custom-call(s32[1]{0:T(128)} %bitcast.place_ref, f32[128,512]{1,0:T(8,128)} %convolution_select_fusion.mix_ref, f32[8,64,1024]{2,1,0:T(8,128)} %all-to-all-done.3.refs_0_, f32[8,64,1024]{2,1,0:T(8,128)} %collective-permute-done.16.refs_1_, f32[8,64,1024]{2,1,0:T(8,128)} %copy-done.14, ...), custom_call_target="tpu_custom_call", output_to_operand_aliasing={{}: (14, {})} | custom-call | flops 3221225472 | bytes 20971520 | tf_op jit(solution)/shard_map/pallas_call | solution.py:169
  (179 shorter events, 67.8 us)
Async XLA Ops:
  6.9 100.5 %all-to-all-start = ((f32[8,128,1024]{2,1,0:T(8,128)}), f32[8,128,1024]{2,1,0:T(8,128)}, u32[]{:S(2)}, u32[]{:S(2)}) async-start(f32[8,128,1024]{2,1,0:T(8,128)} %shard_map.73), calls=%async_computation | async-start | bytes 8388608 | tf_op jit(solution)/shard_map/all_to_all | solution.py:236
  107.4 97.1 %all-to-all-start.1 = ((f32[8,128,1024]{2,1,0:T(8,128)}), f32[8,128,1024]{2,1,0:T(8,128)}, u32[]{:S(2)}, u32[]{:S(2)}) async-start(f32[8,128,1024]{2,1,0:T(8,128)} %shard_map.74), calls=%async_computation.1 | async-start | bytes 8388608 | tf_op jit(solution)/shard_map/all_to_all | solution.py:236
  117.9 42.6 %copy-start.6 = (f32[8,1,64,1024]{3,2,1,0:T(8,128)}, f32[8,1,64,1024]{3,2,1,0:T(8,128)S(1)}, u32[]{:S(2)}) copy-start(f32[8,1,64,1024]{3,2,1,0:T(8,128)S(1)} %get-tuple-element.47) | copy-start | bytes 6291460
  121.0 45.1 %copy-start.10 = (f32[8,1,64,1024]{3,2,1,0:T(8,128)}, f32[8,1,64,1024]{3,2,1,0:T(8,128)S(1)}, u32[]{:S(2)}) copy-start(f32[8,1,64,1024]{3,2,1,0:T(8,128)S(1)} %get-tuple-element.50) | copy-start | bytes 6291460
  204.6 52.2 %all-to-all-start.3 = ((f32[8,64,1024]{2,1,0:T(8,128)}), f32[8,64,1024]{2,1,0:T(8,128)}, u32[]{:S(2)}, u32[]{:S(2)}) async-start(f32[8,64,1024]{2,1,0:T(8,128)} %bitcast.169), calls=%async_computation.3 | async-start | bytes 4194304 | tf_op jit(solution)/shard_map/all_to_all | solution.py:275
  256.7 52.0 %all-to-all-start.2 = ((f32[8,64,1024]{2,1,0:T(8,128)}), f32[8,64,1024]{2,1,0:T(8,128)S(1)}, u32[]{:S(2)}, u32[]{:S(2)}) async-start(f32[8,64,1024]{2,1,0:T(8,128)} %bitcast.168), calls=%async_computation.2 | async-start | bytes 4194304 | tf_op jit(solution)/shard_map/all_to_all | solution.py:275
  260.3 47.6 %collective-permute-start.1 = (f32[8,64,1024]{2,1,0:T(8,128)}, f32[8,64,1024]{2,1,0:T(8,128)}, u32[]{:S(2)}, u32[]{:S(2)}) collective-permute-start(f32[8,64,1024]{2,1,0:T(8,128)} %all-to-all-done.3.refs_0_), channel_id=1, source_target_pairs={{0,2},{1,3},{2,0},{3,1},{4,6},{5,7},{6,4},{7,5},{8,10},{9,11},{10,... | collective-permute-start | bytes 6291464 | tf_op jit(solution)/shard_map/ppermute | solution.py:49
  308.8 112.6 %copy-start = (f32[8,64,1024]{2,1,0:T(8,128)}, f32[8,64,1024]{2,1,0:T(8,128)S(1)}, u32[]{:S(2)}) copy-start(f32[8,64,1024]{2,1,0:T(8,128)S(1)} %all-to-all-done.2.refs_0_) | copy-start | bytes 6291460
  308.8 52.7 %all-to-all-start.5 = ((f32[8,64,1024]{2,1,0:T(8,128)}), f32[8,64,1024]{2,1,0:T(8,128)}, u32[]{:S(2)}, u32[]{:S(2)}) async-start(f32[8,64,1024]{2,1,0:T(8,128)} %bitcast.170), calls=%async_computation.5 | async-start | bytes 4194304 | tf_op jit(solution)/shard_map/all_to_all | solution.py:275
  314.0 46.1 %collective-permute-start.3 = (f32[8,64,1024]{2,1,0:T(8,128)S(1)}, f32[8,64,1024]{2,1,0:T(8,128)S(1)}, u32[]{:S(2)}, u32[]{:S(2)}) collective-permute-start(f32[8,64,1024]{2,1,0:T(8,128)S(1)} %all-to-all-done.2.refs_0_), channel_id=1, source_target_pairs={{0,2},{1,3},{2,0},{3,1},{4,6},{5,7},{6,4},{7,5},{8,10},{9,11},{10,... | collective-permute-start | bytes 6291464 | tf_op jit(solution)/shard_map/ppermute | solution.py:49
  361.4 52.4 %all-to-all-start.4 = ((f32[8,64,1024]{2,1,0:T(8,128)}), f32[8,64,1024]{2,1,0:T(8,128)}, u32[]{:S(2)}, u32[]{:S(2)}) async-start(f32[8,64,1024]{2,1,0:T(8,128)} %bitcast.171), calls=%async_computation.4 | async-start | bytes 4194304 | tf_op jit(solution)/shard_map/all_to_all | solution.py:275
  367.5 46.4 %collective-permute-start.5 = (f32[8,64,1024]{2,1,0:T(8,128)}, f32[8,64,1024]{2,1,0:T(8,128)}, u32[]{:S(2)}, u32[]{:S(2)}) collective-permute-start(f32[8,64,1024]{2,1,0:T(8,128)} %all-to-all-done.5.refs_4_), channel_id=1, source_target_pairs={{0,2},{1,3},{2,0},{3,1},{4,6},{5,7},{6,4},{7,5},{8,10},{9,11},{10,... | collective-permute-start | bytes 6291464 | tf_op jit(solution)/shard_map/ppermute | solution.py:49
  369.1 49.1 %collective-permute-start = (f32[8,64,1024]{2,1,0:T(8,128)S(1)}, f32[8,64,1024]{2,1,0:T(8,128)}, u32[]{:S(2)}, u32[]{:S(2)}) collective-permute-start(f32[8,64,1024]{2,1,0:T(8,128)S(1)} %all-to-all-done.2.refs_0_), channel_id=1, source_target_pairs={{0,1},{1,0},{2,3},{3,2},{4,5},{5,4},{6,7},{7,6},{8,9},{9,8},{10,11... | collective-permute-start | bytes 6291464 | tf_op jit(solution)/shard_map/ppermute | solution.py:49
  369.1 49.1 %collective-permute-start.2 = (f32[8,64,1024]{2,1,0:T(8,128)}, f32[8,64,1024]{2,1,0:T(8,128)}, u32[]{:S(2)}, u32[]{:S(2)}) collective-permute-start(f32[8,64,1024]{2,1,0:T(8,128)} %collective-permute-done.1.refs_2_), channel_id=1, source_target_pairs={{0,1},{1,0},{2,3},{3,2},{4,5},{5,4},{6,7},{7,6},{8,9},{9,8},{10,11... | collective-permute-start | bytes 6291464 | tf_op jit(solution)/shard_map/ppermute | solution.py:49
  413.8 4.5 collective-permute-start.4
  413.9 7.5 %collective-permute-start.6 = (f32[8,64,1024]{2,1,0:T(8,128)}, f32[8,64,1024]{2,1,0:T(8,128)}, u32[]{:S(2)}, u32[]{:S(2)}) collective-permute-start(f32[8,64,1024]{2,1,0:T(8,128)} %collective-permute-done.5.refs_6_), channel_id=1, source_target_pairs={{0,1},{1,0},{2,3},{3,2},{4,5},{5,4},{6,7},{7,6},{8,9},{9,8},{10,11... | collective-permute-start | bytes 6291464 | tf_op jit(solution)/shard_map/ppermute | solution.py:49
  416.7 14.2 %collective-permute-start.7 = (f32[8,64,256]{2,1,0:T(8,128)}, f32[8,64,256]{2,1,0:T(8,128)}, u32[]{:S(2)}, u32[]{:S(2)}) collective-permute-start(f32[8,64,256]{2,1,0:T(8,128)} %slice.221), channel_id=1, source_target_pairs={{0,2},{1,3},{2,0},{3,1},{4,6},{5,7},{6,4},{7,5},{8,10},{9,11},{10,... | collective-permute-start | bytes 1572872 | tf_op jit(solution)/shard_map/ppermute | solution.py:49
  430.8 4.5 collective-permute-start.10
  431.1 4.3 collective-permute-start.8
  432.5 3.9 collective-permute-start.9
  436.4 18.7 %collective-permute-start.15 = (f32[8,64,384]{2,1,0:T(8,128)}, f32[8,64,384]{2,1,0:T(8,128)}, u32[]{:S(2)}, u32[]{:S(2)}) collective-permute-start(f32[8,64,384]{2,1,0:T(8,128)} %get-tuple-element.37), channel_id=1, source_target_pairs={{0,2},{1,3},{2,0},{3,1},{4,6},{5,7},{6,4},{7,5},{8,10},{9,11},{10,... | collective-permute-start | bytes 2359304 | tf_op jit(solution)/shard_map/ppermute | solution.py:49
  437.0 3.9 collective-permute-start.11
  438.2 3.9 collective-permute-start.12
  439.2 4.8 collective-permute-start.13
  444.0 4.9 collective-permute-start.14
  446.7 28.9 %collective-permute-start.16 = (f32[8,64,1024]{2,1,0:T(8,128)}, f32[8,64,1024]{2,1,0:T(8,128)}, u32[]{:S(2)}, u32[]{:S(2)}) collective-permute-start(f32[8,64,1024]{2,1,0:T(8,128)} %all-to-all-done.3.refs_0_), channel_id=1, source_target_pairs={{0,1},{1,0},{2,3},{3,2},{4,5},{5,4},{6,7},{7,6},{8,9},{9,8},{10,11... | collective-permute-start | bytes 6291464 | tf_op jit(solution)/shard_map/ppermute | solution.py:49
  446.7 29.4 %collective-permute-start.17 = (f32[8,64,1024]{2,1,0:T(8,128)S(1)}, f32[8,64,1024]{2,1,0:T(8,128)}, u32[]{:S(2)}, u32[]{:S(2)}) collective-permute-start(f32[8,64,1024]{2,1,0:T(8,128)S(1)} %copy-done.15), channel_id=1, source_target_pairs={{0,1},{1,0},{2,3},{3,2},{4,5},{5,4},{6,7},{7,6},{8,9},{9,8},{10,11... | collective-permute-start | bytes 6291464 | tf_op jit(solution)/shard_map/ppermute | solution.py:49
  447.2 28.9 %collective-permute-start.18 = (f32[8,64,1024]{2,1,0:T(8,128)}, f32[8,64,1024]{2,1,0:T(8,128)}, u32[]{:S(2)}, u32[]{:S(2)}) collective-permute-start(f32[8,64,1024]{2,1,0:T(8,128)} %all-to-all-done.5.refs_4_), channel_id=1, source_target_pairs={{0,1},{1,0},{2,3},{3,2},{4,5},{5,4},{6,7},{7,6},{8,9},{9,8},{10,11... | collective-permute-start | bytes 6291464 | tf_op jit(solution)/shard_map/ppermute | solution.py:49
  457.6 18.0 %collective-permute-start.19 = (f32[8,64,384]{2,1,0:T(8,128)S(1)}, f32[8,64,384]{2,1,0:T(8,128)S(1)}, u32[]{:S(2)}, u32[]{:S(2)}) collective-permute-start(f32[8,64,384]{2,1,0:T(8,128)S(1)} %get-tuple-element.42), channel_id=1, source_target_pairs={{0,2},{1,3},{2,0},{3,1},{4,6},{5,7},{6,4},{7,5},{8,10},{9,11},{10,... | collective-permute-start | bytes 2359304 | tf_op jit(solution)/shard_map/ppermute | solution.py:49
  459.9 19.0 %collective-permute-start.21 = (f32[8,64,384]{2,1,0:T(8,128)}, f32[8,64,384]{2,1,0:T(8,128)S(1)}, u32[]{:S(2)}, u32[]{:S(2)}) collective-permute-start(f32[8,64,384]{2,1,0:T(8,128)} %collective-permute-done.15.refs_7_), channel_id=1, source_target_pairs={{0,1},{1,0},{2,3},{3,2},{4,5},{5,4},{6,7},{7,6},{8,9},{9,8},{10,11... | collective-permute-start | bytes 2359304 | tf_op jit(solution)/shard_map/ppermute | solution.py:49
  475.6 3.3 collective-permute-start.22
  475.6 3.2 collective-permute-start.20
  (21 other events, 149.7 us)

commit v6 on v5

--- a/solution.py
+++ b/solution.py
@@ -60,7 +60,7 @@
 
 def vectors_first(start_block, turn, count, place):
     up_local, _, down_count = start_block.shape
-    rows = 16
+    rows = min(32, up_local // 2)
     blocks = up_local // rows
     return pl.pallas_call(
         vectors_first_kernel,
@@ -151,15 +151,18 @@
     out_ref[...] = result.reshape(SUBLANES, -1, columns)
 
 
-def rotate_half(pieces, wide_mixing, place, half, earlier):
+def rotate_part(pieces, wide_mixing, place, half, segment, segments, earlier):
     half_rows = pieces[0][0].shape[1]
-    down_count = sum(cut.shape[2] for cut in pieces[0])
+    down_count = pieces[0][0].shape[2]
+    width = down_count // segments
     blocks = half_rows // SUBLANES
     own = wide_mixing.shape[0] // SUBLANES
     flat = [cut for cuts in pieces for cut in cuts]
     specs = [pl.BlockSpec(wide_mixing.shape, lambda i, place: (0, 0))]
     for cut in flat:
-        specs.append(pl.BlockSpec((cut.shape[0], SUBLANES, cut.shape[2]), lambda i, place: (0, i, 0)))
+        column = segment if cut.shape[2] == down_count else 0
+        shape = (cut.shape[0], SUBLANES, min(cut.shape[2], width))
+        specs.append(pl.BlockSpec(shape, lambda i, place, column=column: (0, i, column)))
     operands = [place, wide_mixing, *flat]
     aliases = {}
     if earlier is not None:
@@ -174,14 +177,14 @@
             grid=(blocks,),
             in_specs=specs,
             out_specs=pl.BlockSpec(
-                (SUBLANES, own, down_count), lambda i, place: (i + lax.rem(place[0] + half, 2) * blocks, 0, 0)
+                (SUBLANES, own, width), lambda i, place: (i + lax.rem(place[0] + half, 2) * blocks, 0, segment)
             ),
         ),
         input_output_aliases=aliases,
         compiler_params=pltpu.CompilerParams(vmem_limit_bytes=56 * 1024 * 1024),
         cost_estimate=pl.CostEstimate(
-            flops=6 * wide_mixing.size * down_count * blocks,
-            bytes_accessed=4 * (sum(cut.size for cut in flat) + half_rows * own * down_count),
+            flops=6 * wide_mixing.size * width * blocks,
+            bytes_accessed=4 * half_rows * width * (sum(cuts[0].shape[0] for cuts in pieces) + own),
             transcendentals=0,
         ),
     )(*operands)
@@ -275,7 +278,7 @@
             back = lax.all_to_all(piece, "hil", split_axis=0, concat_axis=0, tiled=True)
             held[half].append(back)
             if (turn, half) == (rounds - 1, mine):
-                bounds = [0, down_count // 4, down_count // 8 * 5, down_count]
+                bounds = [0, down_count // 4, down_count // 2, down_count]
                 cuts = [back[:, :, begin:end] for begin, end in zip(bounds, bounds[1:])]
                 crossed.append(spread_step(cuts[:1], side)[0])
             else:
@@ -316,15 +319,21 @@
     right = (jnp.arange(order.shape[0], dtype=jnp.int32)[:, None] == long[None, :] // SUBLANES).astype(jnp.float32)
     wide_mixing = dot(left, dot(mixing, right, (1, 0), highest), (1, 0), highest)
     wide_mixing = jnp.where(wide[:, None] // vec_local == long[None, :] % SUBLANES, wide_mixing, 0.0)
-    result = rotate_half(own_pieces, wide_mixing, place, mine, None)
+    first = [list(pair) for pair in zip(on_side([cuts[0]]), on_side([cuts[1]]))]
+    wide_mixing, first = lax.optimization_barrier((wide_mixing, first))
+    result = rotate_part(own_pieces, wide_mixing, place, mine, 0, 1, None)
+    here = [[piece] for turn in range(rounds) for piece in on_side([held[theirs][turn]])]
+    there = [[piece] for turn in range(rounds - 1) for piece in on_side([crossed[2 * turn + 1]])]
+    per_turn = len(first)
+    columns = [there + first]
     result, cuts[2] = lax.optimization_barrier((result, cuts[2]))
-    other_pieces = []
-    for turn in range(rounds):
-        there = cuts if turn == rounds - 1 else [crossed[2 * turn + 1]]
-        here = [[piece] for piece in on_side([held[theirs][turn]])]
-        there = [list(group) for group in zip(*[on_side([cut]) for cut in there])]
-        other_pieces += here + there
-    return rotate_half(other_pieces, wide_mixing, place, theirs, result)
+    columns.append(there + [[piece] for piece in on_side([cuts[2]])])
+    for segment, arrays in enumerate(columns):
+        pieces = []
+        for begin in range(0, rounds * per_turn, per_turn):
+            pieces += here[begin : begin + per_turn] + arrays[begin : begin + per_turn]
+        result = rotate_part(pieces, wide_mixing, place, theirs, segment, 2, result)
+    return result
 
 
 def split_down(local_block):

time: 502 us -> 506 us (level)
    pallas_call x2 -> x3, Pallas kernels: 23 us -> 28.7 us  [rotate_part(): pl.pallas_call(functools.partial(rotate_kernel, [len(cuts) for cuts in pi...]
    unnamed x48 -> x54, local copies, waits for them, and re-layouts: 9.02 us -> 11.3 us
  transfers between devices with their start and end apart: 29 -> 29, of which waited for: 18 -> 18; matrix products, arithmetic and copies ran while one was open for 27% -> 27% of each run, Pallas kernels for 5% -> 6%
where the time goes in v6:
time: 506 us; the launch traced here: 497 us
  waiting for transfers between devices  256 us (51%)
  matrix products  109 us (22%)
  starting transfers between devices  49.1 us (10%)
  Pallas kernels  44.7 us (9%)
  local copies, waits for them, and re-layouts  29.6 us (6%)
  other arithmetic  6.67 us (1%)
    dot_general x28, matrix products, dot(): lax.dot_general(left, right, ((contract[:1], contract[1:]), ((), ())), pr...  104 us
    all_to_all x2, waiting for transfers between devices, vector_cut(): lax.all_to_all(block, 'hil', split_axis=0, concat_axis=0, tiled=True)  103 us
    ppermute x16, waiting for transfers between devices, spread_step(): return [lax.ppermute(piece, 'vec', pairs) for piece in held]  94.6 us
    all_to_all x4, waiting for transfers between devices, vector_cut(): back = lax.all_to_all(piece, 'hil', split_axis=0, concat_axis=0, tiled=True)  51 us
    pallas_call x3, Pallas kernels, rotate_part(): pl.pallas_call(functools.partial(rotate_kernel, [len(cuts) for cuts in pi...  28.7 us
    all_to_all x4, starting transfers between devices, vector_cut(): back = lax.all_to_all(piece, 'hil', split_axis=0, concat_axis=0, tiled=True)  18.5 us
    all_to_all x2, starting transfers between devices, vector_cut(): lax.all_to_all(block, 'hil', split_axis=0, concat_axis=0, tiled=True)  11.8 us
    slice x7, local copies, waits for them, and re-layouts, rows(): values.reshape(hil_parts, 2, half_rows, -1)[:, half]  11.5 us
  transfers between devices with their start and end apart: 29, of which 18 were waited for; matrix products, arithmetic and copies ran while one was open for 27% of the time, Pallas kernels for 6%

profile of v6, /device:TPU:0, one launch (start us, length us, event | category | flops | bytes accessed | tf_op | source)
XLA Modules:
  0.0 497.1 jit_solution(17579318267776986298)
XLA Ops:
  0.0 5.0 %shard_map.73 = f32[8,128,1024]{2,1,0:T(8,128)} custom-call(s32[1]{0:T(128)} %bitcast.place_ref, f32[128,16,1024]{2,1,0:T(8,128)} %block_ref.3), custom_call_target="tpu_custom_call" | custom-call | tf_op jit(solution)/shard_map/pallas_call | solution.py:65
  5.0 7.3 %all-to-all-start = ((f32[8,128,1024]{2,1,0:T(8,128)}), f32[8,128,1024]{2,1,0:T(8,128)}, u32[]{:S(2)}, u32[]{:S(2)}) async-start(f32[8,128,1024]{2,1,0:T(8,128)} %shard_map.73), calls=%async_computation | async-start | bytes 8388608 | tf_op jit(solution)/shard_map/all_to_all | solution.py:239
  12.3 5.1 %shard_map.74 = f32[8,128,1024]{2,1,0:T(8,128)} custom-call(s32[1]{0:T(128)} %bitcast.place_ref, f32[128,16,1024]{2,1,0:T(8,128)} %block_ref.3), custom_call_target="tpu_custom_call" | custom-call | tf_op jit(solution)/shard_map/pallas_call | solution.py:65
  20.1 5.2 %convolution_add_fusion = f32[1024,1024]{1,0:T(8,128)} fusion(f32[10]{0:T(128)S(1)} %copy-done.25, s32[1024]{0:T(1024)S(1)} %shift_right_arithmetic.28), kind=kOutput, calls=%fused_computation.24 | convolution fusion | flops 126949376 | bytes 4198440 | tf_op jit(solution)/shard_map/dot_general | solution.py:244
  25.3 80.3 %all-to-all-done = f32[8,128,1024]{2,1,0:T(8,128)} async-done(((f32[8,128,1024]{2,1,0:T(8,128)}), f32[8,128,1024]{2,1,0:T(8,128)}, u32[]{:S(2)}, u32[]{:S(2)}) %all-to-all-start) | async-done | bytes 4194336 | tf_op jit(solution)/shard_map/all_to_all | solution.py:239
  105.5 4.6 all-to-all-start.1
  110.1 5.4 %select_add_fusion = f32[8,2,64,1024]{3,2,1,0:T(8,128)S(1)} fusion(f32[8,2,64]{2,1,0:T(2,128)S(1)} %get-tuple-element.95, s32[8,2,64]{2,1,0:T(2,128)S(1)} %get-tuple-element.76, f32[8,2,64]{2,1,0:T(2,128)S(1)} %get-tuple-element.94, s32[8,2,64]{2,1,0:T(2,128)S(1)} %get-tuple-element.75, f32[8,2,64]{2,1,0:T(2,128)S(1)} %get-tuple-element.93, ...), kind=kLoop, calls=%fused_computation.1 | loop fusion | flops 30408704 | bytes 4276224 | tf_op jit(solution)/shard_map/add | solution.py:32
  122.9 8.9 %fusion.120 = f32[1024,1024]{1,0:T(8,128)S(1)} fusion(f32[1024,1024]{1,0:T(8,128)} %bitcast.3, f32[1024,1024]{1,0:T(8,128)S(1)} %copy-done.1), kind=kOutput, calls=%fused_computation.219 | convolution fusion | flops 6442450944 | bytes 12582912 | tf_op jit(solution)/shard_map/dot_general | solution.py:37
  131.9 17.0 %add_multiply_fusion.1 = f32[1024,1024]{1,0:T(8,128)S(1)} fusion(f32[1024,1024]{1,0:T(8,128)S(1)} %copy-done.15, f32[1024,1024]{1,0:T(8,128)} %bitcast.3, f32[1024,1024]{1,0:T(8,128)S(1)} %fusion.120, f32[1024]{0:T(1024)S(1)} %broadcast_in_dim.182, s32[1024]{0:T(1024)S(1)} %eq.388, f32[1024]{0:T(1024)S(1)} %broadcast_in_dim.180, s32[1024]{0:T(1024)S(1)} %eq.384, ...), kind=kOutput, calls=%fused_computation.12 | convolution fusion | flops 6477053952 | bytes 16859136 | tf_op jit(solution)/shard_map/dot_general | solution.py:37
  152.0 3.6 fusion.122
  155.7 3.6 fusion.121
  159.3 5.5 %bitcast_subtract_fusion.2 = f32[512,1024]{1,0:T(8,128)} fusion(f32[8,1,64,1024]{3,2,1,0:T(8,128)S(1)} %get-tuple-element.63, f32[512,1024]{1,0:T(8,128)S(1)} %bitcast.162, f32[8,1,64,1024]{3,2,1,0:T(8,128)S(1)} %get-tuple-element.59, f32[512,1024]{1,0:T(8,128)S(1)} %fusion.122, f32[512,1024]{1,0:T(8,128)S(1)} %bitcast.163, ...), kind=kOutput, calls=%fused_computation.27 | convolution fusion | flops 3223846912 | bytes 16777216 | tf_op jit(solution)/shard_map/dot_general | solution.py:37
  164.9 14.9 %bitcast_subtract_fusion.3 = f32[512,1024]{1,0:T(8,128)} fusion(f32[8,1,64,1024]{3,2,1,0:T(8,128)S(1)} %get-tuple-element.64, f32[512,1024]{1,0:T(8,128)S(1)} %bitcast.160, f32[8,1,64,1024]{3,2,1,0:T(8,128)S(1)} %get-tuple-element.60, f32[512,1024]{1,0:T(8,128)S(1)} %fusion.121, f32[512,1024]{1,0:T(8,128)S(1)} %bitcast.165, ...), kind=kOutput, calls=%fused_computation.34 | convolution fusion | flops 3223846912 | bytes 16777216 | tf_op jit(solution)/shard_map/dot_general | solution.py:37
  179.7 22.9 %all-to-all-done.1 = f32[8,128,1024]{2,1,0:T(8,128)} async-done(((f32[8,128,1024]{2,1,0:T(8,128)}), f32[8,128,1024]{2,1,0:T(8,128)}, u32[]{:S(2)}, u32[]{:S(2)}) %all-to-all-start.1) | async-done | bytes 4194336 | tf_op jit(solution)/shard_map/all_to_all | solution.py:239
  206.3 10.6 %fusion.123 = f32[1024,1024]{1,0:T(8,128)S(1)} fusion(f32[1024,1024]{1,0:T(8,128)} %bitcast.37, f32[1024,1024]{1,0:T(8,128)} %param.8), kind=kOutput, calls=%fused_computation.222 | convolution fusion | flops 6442450944 | bytes 12582912 | tf_op jit(solution)/shard_map/dot_general | solution.py:37
  216.9 17.1 %add_multiply_fusion = f32[1024,1024]{1,0:T(8,128)S(1)} fusion(f32[1024,1024]{1,0:T(8,128)S(1)} %copy-done.16, f32[1024,1024]{1,0:T(8,128)} %bitcast.37, f32[1024,1024]{1,0:T(8,128)S(1)} %fusion.123, f32[1024]{0:T(1024)S(1)} %broadcast_in_dim.182, s32[1024]{0:T(1024)S(1)} %eq.388, f32[1024]{0:T(1024)S(1)} %broadcast_in_dim.180, s32[1024]{0:T(1024)S(1)} %eq.384, ...), kind=kOutput, calls=%fused_computation | convolution fusion | flops 6477053952 | bytes 16859136 | tf_op jit(solution)/shard_map/dot_general | solution.py:37
  234.3 5.3 %fusion.114 = (f32[8,1,64,1024]{3,2,1,0:T(8,128)}, f32[8,1,64,1024]{3,2,1,0:T(8,128)S(1)}) fusion(f32[8,2,64,1024]{3,2,1,0:T(8,128)} %bitcast.40), kind=kLoop, calls=%fused_computation.213 | loop fusion | bytes 8388608 | tf_op jit(solution)/shard_map/slice | solution.py:252
  243.2 5.6 %bitcast_subtract_fusion.1 = f32[512,1024]{1,0:T(8,128)} fusion(f32[8,1,64,1024]{3,2,1,0:T(8,128)S(1)} %get-tuple-element.56, f32[512,1024]{1,0:T(8,128)S(1)} %bitcast.156, f32[8,1,64,1024]{3,2,1,0:T(8,128)S(1)} %copy-done.14, f32[512,1024]{1,0:T(8,128)S(1)} %fusion.124, f32[512,1024]{1,0:T(8,128)S(1)} %bitcast.166, f32[1024,1024]{1,0:T(8,128)S(1)} %add_multiply_fusion), kind=kOutput, calls=%fused_computation.26 | convolution fusion | flops 3223846912 | bytes 16777216 | tf_op jit(solution)/shard_map/dot_general | solution.py:37
  248.8 5.9 %all-to-all-done.3.refs_0_ = f32[8,64,1024]{2,1,0:T(8,128)S(1)} async-done(((f32[8,64,1024]{2,1,0:T(8,128)}), f32[8,64,1024]{2,1,0:T(8,128)S(1)}, u32[]{:S(2)}, u32[]{:S(2)}) %all-to-all-start.3) | async-done | bytes 2097184 | tf_op jit(solution)/shard_map/all_to_all | solution.py:278
  261.2 46.0 %collective-permute-done.1.refs_2_ = f32[8,64,1024]{2,1,0:T(8,128)} collective-permute-done((f32[8,64,1024]{2,1,0:T(8,128)}, f32[8,64,1024]{2,1,0:T(8,128)}, u32[]{:S(2)}, u32[]{:S(2)}) %collective-permute-start.1) | collective-permute-done | bytes 2097184 | tf_op jit(solution)/shard_map/ppermute | solution.py:49
  308.1 5.2 %all-to-all-start.5 = ((f32[8,64,1024]{2,1,0:T(8,128)}), f32[8,64,1024]{2,1,0:T(8,128)}, u32[]{:S(2)}, u32[]{:S(2)}) async-start(f32[8,64,1024]{2,1,0:T(8,128)} %bitcast.170), calls=%async_computation.5 | async-start | bytes 4194304 | tf_op jit(solution)/shard_map/all_to_all | solution.py:278
  316.7 3.7 fusion.125
  320.4 6.5 %bitcast_subtract_fusion = f32[512,1024]{1,0:T(8,128)} fusion(f32[8,1,64,1024]{3,2,1,0:T(8,128)} %get-tuple-element.55, f32[512,1024]{1,0:T(8,128)S(1)} %bitcast.158, f32[8,1,64,1024]{3,2,1,0:T(8,128)S(1)} %copy-done.10, f32[512,1024]{1,0:T(8,128)S(1)} %fusion.125, f32[512,1024]{1,0:T(8,128)S(1)} %bitcast.164, f32[1024,1024]{1,0:T(8,128)S(1)} %copy-done.5), kind=kOutput, calls=%fused_computation.25 | convolution fusion | flops 3223846912 | bytes 16777216 | tf_op jit(solution)/shard_map/dot_general | solution.py:37
  326.9 32.5 %collective-permute-done.3.refs_2_ = f32[8,64,1024]{2,1,0:T(8,128)S(1)} collective-permute-done((f32[8,64,1024]{2,1,0:T(8,128)S(1)}, f32[8,64,1024]{2,1,0:T(8,128)S(1)}, u32[]{:S(2)}, u32[]{:S(2)}) %collective-permute-start.3) | collective-permute-done | bytes 2097184 | tf_op jit(solution)/shard_map/ppermute | solution.py:49
  360.8 6.1 %all-to-all-start.4 = ((f32[8,64,1024]{2,1,0:T(8,128)}), f32[8,64,1024]{2,1,0:T(8,128)}, u32[]{:S(2)}, u32[]{:S(2)}) async-start(f32[8,64,1024]{2,1,0:T(8,128)} %bitcast.171), calls=%async_computation.4 | async-start | bytes 4194304 | tf_op jit(solution)/shard_map/all_to_all | solution.py:278
  368.9 44.2 %all-to-all-done.4.refs_4_ = f32[8,64,1024]{2,1,0:T(8,128)} async-done(((f32[8,64,1024]{2,1,0:T(8,128)}), f32[8,64,1024]{2,1,0:T(8,128)}, u32[]{:S(2)}, u32[]{:S(2)}) %all-to-all-start.4) | async-done | bytes 2097184 | tf_op jit(solution)/shard_map/all_to_all | solution.py:278
  420.7 5.9 %shard_map.75 = (f32[256,256]{1,0:T(8,128)S(1)}, f32[256,256]{1,0:T(8,128)S(1)}) custom-call(s32[1]{0:T(128)} %bitcast.2.start_ref, f32[8,64,1024]{2,1,0:T(8,128)S(1)} %all-to-all-done.2.refs_0_, f32[8,64,1024]{2,1,0:T(8,128)} %collective-permute-done.refs_1_, f32[8,64,1024]{2,1,0:T(8,128)} %collective-permute-done.1.refs_2_, ...), custom_call_target="tpu_custom_call" | custom-call | flops 2147483648 | bytes 8388608 | tf_op jit(solution)/shard_map/pallas_call | solution.py:121
  453.6 4.2 collective-permute-done.16.refs_8_
  459.9 11.6 %shard_map.76.refs_10_ = f32[128,16,1024]{2,1,0:T(8,128)} custom-call(s32[1]{0:T(128)} %bitcast.place_ref, f32[128,512]{1,0:T(8,128)} %convolution_select_fusion.mix_ref, f32[8,64,1024]{2,1,0:T(8,128)} %copy-done, f32[8,64,1024]{2,1,0:T(8,128)} %collective-permute-done.refs_1_, f32[8,64,1024]{2,1,0:T(8,128)} %collective-permute-done.1.refs_2_, ...), custom_call_target="tpu_custom_call" | custom-call | flops 3221225472 | bytes 20971520 | tf_op jit(solution)/shard_map/pallas_call | solution.py:172
  471.6 5.5 %collective-permute-done.21.refs_6_ = f32[8,64,512]{2,1,0:T(8,128)S(1)} collective-permute-done((f32[8,64,512]{2,1,0:T(8,128)S(1)}, f32[8,64,512]{2,1,0:T(8,128)S(1)}, u32[]{:S(2)}, u32[]{:S(2)}) %collective-permute-start.21) | collective-permute-done | bytes 1048608 | tf_op jit(solution)/shard_map/ppermute | solution.py:49
  478.5 8.5 %shard_map.77.refs_8_ = f32[128,16,1024]{2,1,0:T(8,128)} custom-call(s32[1]{0:T(128)} %bitcast.place_ref, f32[128,512]{1,0:T(8,128)} %convolution_select_fusion.mix_ref, f32[8,64,1024]{2,1,0:T(8,128)} %copy-done.6, f32[8,64,1024]{2,1,0:T(8,128)} %copy-done.18, f32[8,64,1024]{2,1,0:T(8,128)} %copy-done.17, ...), custom_call_target="tpu_custom_call", output_to_operand_aliasing={{}: (12, {})} | custom-call | flops 1610612736 | bytes 10485760 | tf_op jit(solution)/shard_map/pallas_call | solution.py:172
  488.0 8.6 %shard_map.78 = f32[128,16,1024]{2,1,0:T(8,128)} custom-call(s32[1]{0:T(128)} %bitcast.place_ref, f32[128,512]{1,0:T(8,128)} %convolution_select_fusion.mix_ref, f32[8,64,1024]{2,1,0:T(8,128)} %copy-done.6, f32[8,64,1024]{2,1,0:T(8,128)} %copy-done.18, f32[8,64,1024]{2,1,0:T(8,128)} %copy-done.17, ...), custom_call_target="tpu_custom_call", output_to_operand_aliasing={{}: (10, {})} | custom-call | flops 1610612736 | bytes 10485760 | tf_op jit(solution)/shard_map/pallas_call | solution.py:172
  (186 shorter events, 72.8 us)
Async XLA Ops:
  5.0 100.5 %all-to-all-start = ((f32[8,128,1024]{2,1,0:T(8,128)}), f32[8,128,1024]{2,1,0:T(8,128)}, u32[]{:S(2)}, u32[]{:S(2)}) async-start(f32[8,128,1024]{2,1,0:T(8,128)} %shard_map.73), calls=%async_computation | async-start | bytes 8388608 | tf_op jit(solution)/shard_map/all_to_all | solution.py:239
  105.5 97.1 %all-to-all-start.1 = ((f32[8,128,1024]{2,1,0:T(8,128)}), f32[8,128,1024]{2,1,0:T(8,128)}, u32[]{:S(2)}, u32[]{:S(2)}) async-start(f32[8,128,1024]{2,1,0:T(8,128)} %shard_map.74), calls=%async_computation.1 | async-start | bytes 8388608 | tf_op jit(solution)/shard_map/all_to_all | solution.py:239
  116.1 48.7 %copy-start.11 = (f32[8,1,64,1024]{3,2,1,0:T(8,128)}, f32[8,1,64,1024]{3,2,1,0:T(8,128)S(1)}, u32[]{:S(2)}) copy-start(f32[8,1,64,1024]{3,2,1,0:T(8,128)S(1)} %get-tuple-element.58) | copy-start | bytes 6291460
  119.8 45.0 %copy-start.13 = (f32[8,1,64,1024]{3,2,1,0:T(8,128)}, f32[8,1,64,1024]{3,2,1,0:T(8,128)S(1)}, u32[]{:S(2)}) copy-start(f32[8,1,64,1024]{3,2,1,0:T(8,128)S(1)} %get-tuple-element.60) | copy-start | bytes 6291460
  202.6 52.0 %all-to-all-start.3 = ((f32[8,64,1024]{2,1,0:T(8,128)}), f32[8,64,1024]{2,1,0:T(8,128)S(1)}, u32[]{:S(2)}, u32[]{:S(2)}) async-start(f32[8,64,1024]{2,1,0:T(8,128)} %bitcast.169), calls=%async_computation.3 | async-start | bytes 4194304 | tf_op jit(solution)/shard_map/all_to_all | solution.py:278
  256.0 52.1 %all-to-all-start.2 = ((f32[8,64,1024]{2,1,0:T(8,128)}), f32[8,64,1024]{2,1,0:T(8,128)S(1)}, u32[]{:S(2)}, u32[]{:S(2)}) async-start(f32[8,64,1024]{2,1,0:T(8,128)} %bitcast.168), calls=%async_computation.2 | async-start | bytes 4194304 | tf_op jit(solution)/shard_map/all_to_all | solution.py:278
  259.7 47.6 %collective-permute-start.1 = (f32[8,64,1024]{2,1,0:T(8,128)}, f32[8,64,1024]{2,1,0:T(8,128)}, u32[]{:S(2)}, u32[]{:S(2)}) collective-permute-start(f32[8,64,1024]{2,1,0:T(8,128)} %copy-done.6), channel_id=1, source_target_pairs={{0,2},{1,3},{2,0},{3,1},{4,6},{5,7},{6,4},{7,5},{8,10},{9,11},{10,... | collective-permute-start | bytes 6291464 | tf_op jit(solution)/shard_map/ppermute | solution.py:49
  308.1 112.6 %copy-start = (f32[8,64,1024]{2,1,0:T(8,128)}, f32[8,64,1024]{2,1,0:T(8,128)S(1)}, u32[]{:S(2)}) copy-start(f32[8,64,1024]{2,1,0:T(8,128)S(1)} %all-to-all-done.2.refs_0_) | copy-start | bytes 6291460
  308.1 52.7 %all-to-all-start.5 = ((f32[8,64,1024]{2,1,0:T(8,128)}), f32[8,64,1024]{2,1,0:T(8,128)}, u32[]{:S(2)}, u32[]{:S(2)}) async-start(f32[8,64,1024]{2,1,0:T(8,128)} %bitcast.170), calls=%async_computation.5 | async-start | bytes 4194304 | tf_op jit(solution)/shard_map/all_to_all | solution.py:278
  313.3 46.1 %collective-permute-start.3 = (f32[8,64,1024]{2,1,0:T(8,128)S(1)}, f32[8,64,1024]{2,1,0:T(8,128)S(1)}, u32[]{:S(2)}, u32[]{:S(2)}) collective-permute-start(f32[8,64,1024]{2,1,0:T(8,128)S(1)} %all-to-all-done.2.refs_0_), channel_id=1, source_target_pairs={{0,2},{1,3},{2,0},{3,1},{4,6},{5,7},{6,4},{7,5},{8,10},{9,11},{10,... | collective-permute-start | bytes 6291464 | tf_op jit(solution)/shard_map/ppermute | solution.py:49
  360.8 52.4 %all-to-all-start.4 = ((f32[8,64,1024]{2,1,0:T(8,128)}), f32[8,64,1024]{2,1,0:T(8,128)}, u32[]{:S(2)}, u32[]{:S(2)}) async-start(f32[8,64,1024]{2,1,0:T(8,128)} %bitcast.171), calls=%async_computation.4 | async-start | bytes 4194304 | tf_op jit(solution)/shard_map/all_to_all | solution.py:278
  366.8 46.3 %collective-permute-start.5 = (f32[8,64,1024]{2,1,0:T(8,128)}, f32[8,64,1024]{2,1,0:T(8,128)}, u32[]{:S(2)}, u32[]{:S(2)}) collective-permute-start(f32[8,64,1024]{2,1,0:T(8,128)} %all-to-all-done.5.refs_4_), channel_id=1, source_target_pairs={{0,2},{1,3},{2,0},{3,1},{4,6},{5,7},{6,4},{7,5},{8,10},{9,11},{10,... | collective-permute-start | bytes 6291464 | tf_op jit(solution)/shard_map/ppermute | solution.py:49
  368.4 49.5 %collective-permute-start = (f32[8,64,1024]{2,1,0:T(8,128)S(1)}, f32[8,64,1024]{2,1,0:T(8,128)}, u32[]{:S(2)}, u32[]{:S(2)}) collective-permute-start(f32[8,64,1024]{2,1,0:T(8,128)S(1)} %all-to-all-done.2.refs_0_), channel_id=1, source_target_pairs={{0,1},{1,0},{2,3},{3,2},{4,5},{5,4},{6,7},{7,6},{8,9},{9,8},{10,11... | collective-permute-start | bytes 6291464 | tf_op jit(solution)/shard_map/ppermute | solution.py:49
  368.4 49.5 %collective-permute-start.2 = (f32[8,64,1024]{2,1,0:T(8,128)}, f32[8,64,1024]{2,1,0:T(8,128)}, u32[]{:S(2)}, u32[]{:S(2)}) collective-permute-start(f32[8,64,1024]{2,1,0:T(8,128)} %collective-permute-done.1.refs_2_), channel_id=1, source_target_pairs={{0,1},{1,0},{2,3},{3,2},{4,5},{5,4},{6,7},{7,6},{8,9},{9,8},{10,11... | collective-permute-start | bytes 6291464 | tf_op jit(solution)/shard_map/ppermute | solution.py:49
  413.2 4.8 collective-permute-start.4
  413.2 7.5 %collective-permute-start.6 = (f32[8,64,1024]{2,1,0:T(8,128)}, f32[8,64,1024]{2,1,0:T(8,128)}, u32[]{:S(2)}, u32[]{:S(2)}) collective-permute-start(f32[8,64,1024]{2,1,0:T(8,128)} %collective-permute-done.5.refs_6_), channel_id=1, source_target_pairs={{0,1},{1,0},{2,3},{3,2},{4,5},{5,4},{6,7},{7,6},{8,9},{9,8},{10,11... | collective-permute-start | bytes 6291464 | tf_op jit(solution)/shard_map/ppermute | solution.py:49
  416.4 14.1 %collective-permute-start.7 = (f32[8,64,256]{2,1,0:T(8,128)}, f32[8,64,256]{2,1,0:T(8,128)S(1)}, u32[]{:S(2)}, u32[]{:S(2)}) collective-permute-start(f32[8,64,256]{2,1,0:T(8,128)} %get-tuple-element.66), channel_id=1, source_target_pairs={{0,2},{1,3},{2,0},{3,1},{4,6},{5,7},{6,4},{7,5},{8,10},{9,11},{10,... | collective-permute-start | bytes 1572872 | tf_op jit(solution)/shard_map/ppermute | solution.py:49
  430.5 3.6 collective-permute-start.10
  430.7 3.3 collective-permute-start.8
  432.1 3.9 collective-permute-start.9
  436.0 13.1 %collective-permute-start.15 = (f32[8,64,256]{2,1,0:T(8,128)}, f32[8,64,256]{2,1,0:T(8,128)}, u32[]{:S(2)}, u32[]{:S(2)}) collective-permute-start(f32[8,64,256]{2,1,0:T(8,128)} %get-tuple-element.42), channel_id=1, source_target_pairs={{0,2},{1,3},{2,0},{3,1},{4,6},{5,7},{6,4},{7,5},{8,10},{9,11},{10,... | collective-permute-start | bytes 1572872 | tf_op jit(solution)/shard_map/ppermute | solution.py:49
  436.6 3.9 collective-permute-start.11
  437.8 3.9 collective-permute-start.12
  438.8 4.8 collective-permute-start.13
  443.6 4.9 collective-permute-start.14
  446.5 30.5 %collective-permute-start.18 = (f32[8,64,1024]{2,1,0:T(8,128)}, f32[8,64,1024]{2,1,0:T(8,128)S(1)}, u32[]{:S(2)}, u32[]{:S(2)}) collective-permute-start(f32[8,64,1024]{2,1,0:T(8,128)} %copy-done.6), channel_id=1, source_target_pairs={{0,1},{1,0},{2,3},{3,2},{4,5},{5,4},{6,7},{7,6},{8,9},{9,8},{10,11... | collective-permute-start | bytes 6291464 | tf_op jit(solution)/shard_map/ppermute | solution.py:49
  446.5 30.6 %collective-permute-start.19 = (f32[8,64,1024]{2,1,0:T(8,128)}, f32[8,64,1024]{2,1,0:T(8,128)}, u32[]{:S(2)}, u32[]{:S(2)}) collective-permute-start(f32[8,64,1024]{2,1,0:T(8,128)} %copy-done.17), channel_id=1, source_target_pairs={{0,1},{1,0},{2,3},{3,2},{4,5},{5,4},{6,7},{7,6},{8,9},{9,8},{10,11... | collective-permute-start | bytes 6291464 | tf_op jit(solution)/shard_map/ppermute | solution.py:49
  448.4 28.7 %collective-permute-start.20 = (f32[8,64,1024]{2,1,0:T(8,128)}, f32[8,64,1024]{2,1,0:T(8,128)}, u32[]{:S(2)}, u32[]{:S(2)}) collective-permute-start(f32[8,64,1024]{2,1,0:T(8,128)} %all-to-all-done.5.refs_4_), channel_id=1, source_target_pairs={{0,1},{1,0},{2,3},{3,2},{4,5},{5,4},{6,7},{7,6},{8,9},{9,8},{10,11... | collective-permute-start | bytes 6291464 | tf_op jit(solution)/shard_map/ppermute | solution.py:49
  448.5 9.3 %collective-permute-start.16 = (f32[8,64,256]{2,1,0:T(8,128)}, f32[8,64,256]{2,1,0:T(8,128)}, u32[]{:S(2)}, u32[]{:S(2)}) collective-permute-start(f32[8,64,256]{2,1,0:T(8,128)} %copy-done.21), channel_id=1, source_target_pairs={{0,1},{1,0},{2,3},{3,2},{4,5},{5,4},{6,7},{7,6},{8,9},{9,8},{10,11... | collective-permute-start | bytes 1572872 | tf_op jit(solution)/shard_map/ppermute | solution.py:49
  452.0 25.1 %collective-permute-start.21 = (f32[8,64,512]{2,1,0:T(8,128)S(1)}, f32[8,64,512]{2,1,0:T(8,128)S(1)}, u32[]{:S(2)}, u32[]{:S(2)}) collective-permute-start(f32[8,64,512]{2,1,0:T(8,128)S(1)} %slice.223), channel_id=1, source_target_pairs={{0,2},{1,3},{2,0},{3,1},{4,6},{5,7},{6,4},{7,5},{8,10},{9,11},{10,... | collective-permute-start | bytes 3145736 | tf_op jit(solution)/shard_map/ppermute | solution.py:49
  457.8 2.1 collective-permute-start.17
  477.1 9.9 %collective-permute-start.22 = (f32[8,64,512]{2,1,0:T(8,128)S(1)}, f32[8,64,512]{2,1,0:T(8,128)S(1)}, u32[]{:S(2)}, u32[]{:S(2)}) collective-permute-start(f32[8,64,512]{2,1,0:T(8,128)S(1)} %collective-permute-done.21.refs_6_), channel_id=1, source_target_pairs={{0,1},{1,0},{2,3},{3,2},{4,5},{5,4},{6,7},{7,6},{8,9},{9,8},{10,11... | collective-permute-start | bytes 3145736 | tf_op jit(solution)/shard_map/ppermute | solution.py:49
  (24 other events, 205.5 us)

commit v7 on v5

--- a/solution.py
+++ b/solution.py
@@ -60,7 +60,7 @@
 
 def vectors_first(start_block, turn, count, place):
     up_local, _, down_count = start_block.shape
-    rows = 16
+    rows = min(32, up_local // 2)
     blocks = up_local // rows
     return pl.pallas_call(
         vectors_first_kernel,
@@ -140,26 +140,37 @@
 
 
 def rotate_kernel(counts, place_ref, mix_ref, *refs):
-    inputs, out_ref = refs[: sum(counts)], refs[-1]
-    columns = out_ref.shape[2]
-    mix_top, mix_low = split(mix_ref[...])
-    count = mix_top.shape[0]
-    both = jnp.concatenate([mix_top, mix_low], axis=0)
-    top, low = split(jnp.concatenate([joined(cuts).reshape(-1, columns) for cuts in grouped(inputs, counts)], axis=0))
-    wide = dot(both, top, (1, 0), None)
-    result = wide[:count] + wide[count:] + dot(mix_top, low, (1, 0), None)
-    out_ref[...] = result.reshape(SUBLANES, -1, columns)
+    inputs, out_ref, both_ref = refs[: sum(counts)], refs[-2], refs[-1]
+    rows, _, columns = out_ref.shape
+    count = mix_ref.shape[0]
+
+    @pl.when(pl.program_id(0) == 0)
+    def _():
+        mix_top, mix_low = split(mix_ref[...])
+        both_ref[:count] = mix_top
+        both_ref[count:] = mix_low
+
+    for first in range(0, rows, SUBLANES):
+        blocks = []
+        for cuts in grouped(inputs, counts):
+            block = jnp.concatenate([ref[:, first : first + SUBLANES, :] for ref in cuts], axis=-1)
+            blocks.append(block.reshape(-1, columns))
+        top, low = split(jnp.concatenate(blocks, axis=0))
+        wide = dot(both_ref[...], top, (1, 0), None)
+        result = wide[:count] + wide[count:] + dot(both_ref[:count], low, (1, 0), None)
+        out_ref[first : first + SUBLANES] = result.reshape(SUBLANES, -1, columns)
 
 
 def rotate_half(pieces, wide_mixing, place, half, earlier):
     half_rows = pieces[0][0].shape[1]
     down_count = sum(cut.shape[2] for cut in pieces[0])
-    blocks = half_rows // SUBLANES
+    step_rows = 2 * SUBLANES
+    blocks = half_rows // step_rows
     own = wide_mixing.shape[0] // SUBLANES
     flat = [cut for cuts in pieces for cut in cuts]
     specs = [pl.BlockSpec(wide_mixing.shape, lambda i, place: (0, 0))]
     for cut in flat:
-        specs.append(pl.BlockSpec((cut.shape[0], SUBLANES, cut.shape[2]), lambda i, place: (0, i, 0)))
+        specs.append(pl.BlockSpec((cut.shape[0], step_rows, cut.shape[2]), lambda i, place: (0, i, 0)))
     operands = [place, wide_mixing, *flat]
     aliases = {}
     if earlier is not None:
@@ -174,13 +185,14 @@
             grid=(blocks,),
             in_specs=specs,
             out_specs=pl.BlockSpec(
-                (SUBLANES, own, down_count), lambda i, place: (i + lax.rem(place[0] + half, 2) * blocks, 0, 0)
+                (step_rows, own, down_count), lambda i, place: (i + lax.rem(place[0] + half, 2) * blocks, 0, 0)
             ),
+            scratch_shapes=[pltpu.VMEM((2 * wide_mixing.shape[0], wide_mixing.shape[1]), jnp.bfloat16)],
         ),
         input_output_aliases=aliases,
         compiler_params=pltpu.CompilerParams(vmem_limit_bytes=56 * 1024 * 1024),
         cost_estimate=pl.CostEstimate(
-            flops=6 * wide_mixing.size * down_count * blocks,
+            flops=6 * wide_mixing.size * down_count * half_rows // SUBLANES,
             bytes_accessed=4 * (sum(cut.size for cut in flat) + half_rows * own * down_count),
             transcendentals=0,
         ),
@@ -275,7 +287,7 @@
             back = lax.all_to_all(piece, "hil", split_axis=0, concat_axis=0, tiled=True)
             held[half].append(back)
             if (turn, half) == (rounds - 1, mine):
-                bounds = [0, down_count // 4, down_count // 8 * 5, down_count]
+                bounds = [0, down_count // 8 * 3, down_count // 8 * 5, down_count]
                 cuts = [back[:, :, begin:end] for begin, end in zip(bounds, bounds[1:])]
                 crossed.append(spread_step(cuts[:1], side)[0])
             else:
@@ -304,10 +316,9 @@
     partial = gram_partial(own_pieces, lax.rem(own, side), side)
     partial = dot(order, dot(partial, order, (1, 0), highest), (0, 0), highest)
     partial, cuts[0] = lax.optimization_barrier((partial, crossed[-1]))
-    partial, cuts[1] = lax.optimization_barrier((small_sum(partial, "vec"), cuts[1]))
-    cuts[1] = spread_step(cuts[1:2], side)[0]
-    gram_sum, cuts[1], cuts[2] = lax.optimization_barrier((small_sum(partial, "hil"), cuts[1], cuts[2]))
-    cuts[2] = spread_step(cuts[2:], side)[0]
+    partial, cuts[1], cuts[2] = lax.optimization_barrier((small_sum(partial, "vec"), cuts[1], cuts[2]))
+    cuts[1:] = spread_step(cuts[1:], side)
+    gram_sum, cuts[1] = lax.optimization_barrier((small_sum(partial, "hil"), cuts[1]))
     mixing = newton_schulz(gram_sum) * math.sqrt(up_count * down_count)
     mixing = dot(dot(order_own, mixing, (1, 1), highest), order, (1, 1), highest)
     wide = jnp.arange(vec_local * SUBLANES, dtype=jnp.int32)

time: 502 us -> 498 us (level)
  Pallas kernels: 42.8 us -> 35.4 us
  transfers between devices with their start and end apart: 29 -> 29, of which waited for: 18 -> 14; matrix products, arithmetic and copies ran while one was open for 27% -> 29% of each run, Pallas kernels for 5% -> 4%
where the time goes in v7:
time: 498 us; the launch traced here: 490 us
  waiting for transfers between devices  253 us (51%)
  matrix products  111 us (22%)
  starting transfers between devices  50.2 us (10%)
  Pallas kernels  35.4 us (7%)
  local copies, waits for them, and re-layouts  29.1 us (6%)
  other arithmetic  8.31 us (2%)
    dot_general x28, matrix products, dot(): lax.dot_general(left, right, ((contract[:1], contract[1:]), ((), ())), pr...  106 us
    all_to_all x2, waiting for transfers between devices, vector_cut(): lax.all_to_all(block, 'hil', split_axis=0, concat_axis=0, tiled=True)  104 us
    ppermute x16, waiting for transfers between devices, spread_step(): return [lax.ppermute(piece, 'vec', pairs) for piece in held]  94.5 us
    all_to_all x4, waiting for transfers between devices, vector_cut(): back = lax.all_to_all(piece, 'hil', split_axis=0, concat_axis=0, tiled=True)  50.5 us
    pallas_call x2, Pallas kernels, rotate_half(): pl.pallas_call(functools.partial(rotate_kernel, [len(cuts) for cuts in pi...  19.4 us
    all_to_all x4, starting transfers between devices, vector_cut(): back = lax.all_to_all(piece, 'hil', split_axis=0, concat_axis=0, tiled=True)  19.2 us
    all_to_all x2, starting transfers between devices, vector_cut(): lax.all_to_all(block, 'hil', split_axis=0, concat_axis=0, tiled=True)  11.8 us
    slice x7, local copies, waits for them, and re-layouts, rows(): values.reshape(hil_parts, 2, half_rows, -1)[:, half]  11.5 us
  transfers between devices with their start and end apart: 29, of which 14 were waited for; matrix products, arithmetic and copies ran while one was open for 29% of the time, Pallas kernels for 4%

profile of v7, /device:TPU:0, one launch (start us, length us, event | category | flops | bytes accessed | tf_op | source)
XLA Modules:
  0.0 489.6 jit_solution(11329130668335265111)
XLA Ops:
  0.0 5.0 %shard_map.73 = f32[8,128,1024]{2,1,0:T(8,128)} custom-call(s32[1]{0:T(128)} %bitcast.place_ref, f32[128,16,1024]{2,1,0:T(8,128)} %block_ref.3), custom_call_target="tpu_custom_call" | custom-call | tf_op jit(solution)/shard_map/pallas_call | solution.py:65
  5.0 7.3 %all-to-all-start = ((f32[8,128,1024]{2,1,0:T(8,128)}), f32[8,128,1024]{2,1,0:T(8,128)}, u32[]{:S(2)}, u32[]{:S(2)}) async-start(f32[8,128,1024]{2,1,0:T(8,128)} %shard_map.73), calls=%async_computation | async-start | bytes 8388608 | tf_op jit(solution)/shard_map/all_to_all | solution.py:248
  12.3 5.1 %shard_map.74 = f32[8,128,1024]{2,1,0:T(8,128)} custom-call(s32[1]{0:T(128)} %bitcast.place_ref, f32[128,16,1024]{2,1,0:T(8,128)} %block_ref.3), custom_call_target="tpu_custom_call" | custom-call | tf_op jit(solution)/shard_map/pallas_call | solution.py:65
  20.1 5.2 %convolution_add_fusion = f32[1024,1024]{1,0:T(8,128)} fusion(f32[10]{0:T(128)S(1)} %copy-done.23, s32[1024]{0:T(1024)S(1)} %shift_right_arithmetic.28), kind=kOutput, calls=%fused_computation.24 | convolution fusion | flops 126949376 | bytes 4198440 | tf_op jit(solution)/shard_map/dot_general | solution.py:253
  25.3 80.2 %all-to-all-done = f32[8,128,1024]{2,1,0:T(8,128)} async-done(((f32[8,128,1024]{2,1,0:T(8,128)}), f32[8,128,1024]{2,1,0:T(8,128)}, u32[]{:S(2)}, u32[]{:S(2)}) %all-to-all-start) | async-done | bytes 4194336 | tf_op jit(solution)/shard_map/all_to_all | solution.py:248
  105.5 4.6 all-to-all-start.1
  110.1 5.4 %select_add_fusion = f32[8,2,64,1024]{3,2,1,0:T(8,128)S(1)} fusion(f32[8,2,64]{2,1,0:T(2,128)S(1)} %get-tuple-element.85, s32[8,2,64]{2,1,0:T(2,128)S(1)} %get-tuple-element.66, f32[8,2,64]{2,1,0:T(2,128)S(1)} %get-tuple-element.84, s32[8,2,64]{2,1,0:T(2,128)S(1)} %get-tuple-element.65, f32[8,2,64]{2,1,0:T(2,128)S(1)} %get-tuple-element.83, ...), kind=kLoop, calls=%fused_computation.1 | loop fusion | flops 30408704 | bytes 4276224 | tf_op jit(solution)/shard_map/add | solution.py:32
  122.2 8.9 %fusion.120 = f32[1024,1024]{1,0:T(8,128)S(1)} fusion(f32[1024,1024]{1,0:T(8,128)} %bitcast.3, f32[1024,1024]{1,0:T(8,128)S(1)} %copy-done.1), kind=kOutput, calls=%fused_computation.219 | convolution fusion | flops 6442450944 | bytes 12582912 | tf_op jit(solution)/shard_map/dot_general | solution.py:37
  131.1 17.0 %add_multiply_fusion.1 = f32[1024,1024]{1,0:T(8,128)S(1)} fusion(f32[1024,1024]{1,0:T(8,128)S(1)} %copy-done.12, f32[1024,1024]{1,0:T(8,128)} %bitcast.3, f32[1024,1024]{1,0:T(8,128)S(1)} %fusion.120, f32[1024]{0:T(1024)S(1)} %broadcast_in_dim.182, s32[1024]{0:T(1024)S(1)} %eq.388, f32[1024]{0:T(1024)S(1)} %broadcast_in_dim.180, s32[1024]{0:T(1024)S(1)} %eq.384, ...), kind=kOutput, calls=%fused_computation.12 | convolution fusion | flops 6477053952 | bytes 16859136 | tf_op jit(solution)/shard_map/dot_general | solution.py:37
  151.2 3.6 fusion.122
  154.9 3.6 fusion.121
  158.6 5.5 %bitcast_subtract_fusion.2 = f32[512,1024]{1,0:T(8,128)} fusion(f32[8,1,64,1024]{3,2,1,0:T(8,128)S(1)} %get-tuple-element.53, f32[512,1024]{1,0:T(8,128)S(1)} %bitcast.162, f32[8,1,64,1024]{3,2,1,0:T(8,128)S(1)} %get-tuple-element.49, f32[512,1024]{1,0:T(8,128)S(1)} %fusion.122, f32[512,1024]{1,0:T(8,128)S(1)} %bitcast.163, ...), kind=kOutput, calls=%fused_computation.27 | convolution fusion | flops 3223846912 | bytes 16777216 | tf_op jit(solution)/shard_map/dot_general | solution.py:37
  164.1 15.0 %bitcast_subtract_fusion.3 = f32[512,1024]{1,0:T(8,128)} fusion(f32[8,1,64,1024]{3,2,1,0:T(8,128)S(1)} %get-tuple-element.54, f32[512,1024]{1,0:T(8,128)S(1)} %bitcast.160, f32[8,1,64,1024]{3,2,1,0:T(8,128)S(1)} %get-tuple-element.50, f32[512,1024]{1,0:T(8,128)S(1)} %fusion.121, f32[512,1024]{1,0:T(8,128)S(1)} %bitcast.165, ...), kind=kOutput, calls=%fused_computation.34 | convolution fusion | flops 3223846912 | bytes 16777216 | tf_op jit(solution)/shard_map/dot_general | solution.py:37
  179.0 23.6 %all-to-all-done.1 = f32[8,128,1024]{2,1,0:T(8,128)} async-done(((f32[8,128,1024]{2,1,0:T(8,128)}), f32[8,128,1024]{2,1,0:T(8,128)}, u32[]{:S(2)}, u32[]{:S(2)}) %all-to-all-start.1) | async-done | bytes 4194336 | tf_op jit(solution)/shard_map/all_to_all | solution.py:248
  202.6 4.3 all-to-all-start.3
  207.0 10.6 %fusion.123 = f32[1024,1024]{1,0:T(8,128)S(1)} fusion(f32[1024,1024]{1,0:T(8,128)} %bitcast.37, f32[1024,1024]{1,0:T(8,128)} %param.8), kind=kOutput, calls=%fused_computation.222 | convolution fusion | flops 6442450944 | bytes 12582912 | tf_op jit(solution)/shard_map/dot_general | solution.py:37
  217.7 17.0 %add_multiply_fusion = f32[1024,1024]{1,0:T(8,128)S(1)} fusion(f32[1024,1024]{1,0:T(8,128)S(1)} %copy-done.13, f32[1024,1024]{1,0:T(8,128)} %bitcast.37, f32[1024,1024]{1,0:T(8,128)S(1)} %fusion.123, f32[1024]{0:T(1024)S(1)} %broadcast_in_dim.182, s32[1024]{0:T(1024)S(1)} %eq.388, f32[1024]{0:T(1024)S(1)} %broadcast_in_dim.180, s32[1024]{0:T(1024)S(1)} %eq.384, ...), kind=kOutput, calls=%fused_computation | convolution fusion | flops 6477053952 | bytes 16859136 | tf_op jit(solution)/shard_map/dot_general | solution.py:37
  235.0 5.4 %fusion.114 = (f32[8,1,64,1024]{3,2,1,0:T(8,128)}, f32[8,1,64,1024]{3,2,1,0:T(8,128)S(1)}) fusion(f32[8,2,64,1024]{3,2,1,0:T(8,128)} %bitcast.40), kind=kLoop, calls=%fused_computation.213 | loop fusion | bytes 8388608 | tf_op jit(solution)/shard_map/slice | solution.py:261
  243.9 5.5 %bitcast_subtract_fusion.1 = f32[512,1024]{1,0:T(8,128)} fusion(f32[8,1,64,1024]{3,2,1,0:T(8,128)S(1)} %get-tuple-element.46, f32[512,1024]{1,0:T(8,128)S(1)} %bitcast.156, f32[8,1,64,1024]{3,2,1,0:T(8,128)S(1)} %copy-done.11, f32[512,1024]{1,0:T(8,128)S(1)} %fusion.124, f32[512,1024]{1,0:T(8,128)S(1)} %bitcast.166, f32[1024,1024]{1,0:T(8,128)S(1)} %add_multiply_fusion), kind=kOutput, calls=%fused_computation.26 | convolution fusion | flops 3223846912 | bytes 16777216 | tf_op jit(solution)/shard_map/dot_general | solution.py:37
  249.4 5.4 %all-to-all-done.3.refs_0_ = f32[8,64,1024]{2,1,0:T(8,128)} async-done(((f32[8,64,1024]{2,1,0:T(8,128)}), f32[8,64,1024]{2,1,0:T(8,128)}, u32[]{:S(2)}, u32[]{:S(2)}) %all-to-all-start.3) | async-done | bytes 2097184 | tf_op jit(solution)/shard_map/all_to_all | solution.py:287
  254.8 3.6 all-to-all-start.2
  260.0 46.0 %collective-permute-done.1.refs_2_ = f32[8,64,1024]{2,1,0:T(8,128)} collective-permute-done((f32[8,64,1024]{2,1,0:T(8,128)}, f32[8,64,1024]{2,1,0:T(8,128)}, u32[]{:S(2)}, u32[]{:S(2)}) %collective-permute-start.1) | collective-permute-done | bytes 2097184 | tf_op jit(solution)/shard_map/ppermute | solution.py:49
  306.9 5.2 %all-to-all-start.5 = ((f32[8,64,1024]{2,1,0:T(8,128)}), f32[8,64,1024]{2,1,0:T(8,128)}, u32[]{:S(2)}, u32[]{:S(2)}) async-start(f32[8,64,1024]{2,1,0:T(8,128)} %bitcast.170), calls=%async_computation.5 | async-start | bytes 4194304 | tf_op jit(solution)/shard_map/all_to_all | solution.py:287
  315.4 3.7 fusion.125
  319.2 6.5 %bitcast_subtract_fusion = f32[512,1024]{1,0:T(8,128)} fusion(f32[8,1,64,1024]{3,2,1,0:T(8,128)} %get-tuple-element.45, f32[512,1024]{1,0:T(8,128)S(1)} %bitcast.158, f32[8,1,64,1024]{3,2,1,0:T(8,128)S(1)} %copy-done.9, f32[512,1024]{1,0:T(8,128)S(1)} %fusion.125, f32[512,1024]{1,0:T(8,128)S(1)} %bitcast.164, f32[1024,1024]{1,0:T(8,128)S(1)} %copy-done.5), kind=kOutput, calls=%fused_computation.25 | convolution fusion | flops 3223846912 | bytes 16777216 | tf_op jit(solution)/shard_map/dot_general | solution.py:37
  325.7 32.5 %collective-permute-done.3.refs_2_ = f32[8,64,1024]{2,1,0:T(8,128)S(1)} collective-permute-done((f32[8,64,1024]{2,1,0:T(8,128)S(1)}, f32[8,64,1024]{2,1,0:T(8,128)S(1)}, u32[]{:S(2)}, u32[]{:S(2)}) %collective-permute-start.3) | collective-permute-done | bytes 2097184 | tf_op jit(solution)/shard_map/ppermute | solution.py:49
  359.5 6.1 %all-to-all-start.4 = ((f32[8,64,1024]{2,1,0:T(8,128)}), f32[8,64,1024]{2,1,0:T(8,128)}, u32[]{:S(2)}, u32[]{:S(2)}) async-start(f32[8,64,1024]{2,1,0:T(8,128)} %bitcast.171), calls=%async_computation.4 | async-start | bytes 4194304 | tf_op jit(solution)/shard_map/all_to_all | solution.py:287
  367.7 44.3 %all-to-all-done.4.refs_4_ = f32[8,64,1024]{2,1,0:T(8,128)} async-done(((f32[8,64,1024]{2,1,0:T(8,128)}), f32[8,64,1024]{2,1,0:T(8,128)}, u32[]{:S(2)}, u32[]{:S(2)}) %all-to-all-start.4) | async-done | bytes 2097184 | tf_op jit(solution)/shard_map/all_to_all | solution.py:287
  419.4 5.9 %shard_map.75 = (f32[256,256]{1,0:T(8,128)S(1)}, f32[256,256]{1,0:T(8,128)S(1)}) custom-call(s32[1]{0:T(128)} %bitcast.2.start_ref, f32[8,64,1024]{2,1,0:T(8,128)S(1)} %all-to-all-done.2.refs_0_, f32[8,64,1024]{2,1,0:T(8,128)} %collective-permute-done.refs_1_, f32[8,64,1024]{2,1,0:T(8,128)} %collective-permute-done.1.refs_2_, ...), custom_call_target="tpu_custom_call" | custom-call | flops 2147483648 | bytes 8388608 | tf_op jit(solution)/shard_map/pallas_call | solution.py:121
  426.3 9.0 %collective-permute-done.7.refs_6_ = f32[8,64,384]{2,1,0:T(8,128)} collective-permute-done((f32[8,64,384]{2,1,0:T(8,128)}, f32[8,64,384]{2,1,0:T(8,128)}, u32[]{:S(2)}, u32[]{:S(2)}) %collective-permute-start.7) | collective-permute-done | bytes 786464 | tf_op jit(solution)/shard_map/ppermute | solution.py:49
  462.8 9.7 %shard_map.76.refs_12_ = f32[128,16,1024]{2,1,0:T(8,128)} custom-call(s32[1]{0:T(128)} %bitcast.place_ref, f32[128,512]{1,0:T(8,128)} %convolution_select_fusion.mix_ref, f32[8,64,1024]{2,1,0:T(8,128)} %copy-done, f32[8,64,1024]{2,1,0:T(8,128)} %collective-permute-done.refs_1_, f32[8,64,1024]{2,1,0:T(8,128)} %collective-permute-done.1.refs_2_, ...), custom_call_target="tpu_custom_call" | custom-call | flops 3221225472 | bytes 20971520 | tf_op jit(solution)/shard_map/pallas_call | solution.py:180
  479.4 9.7 %shard_map.77 = f32[128,16,1024]{2,1,0:T(8,128)} custom-call(s32[1]{0:T(128)} %bitcast.place_ref, f32[128,512]{1,0:T(8,128)} %convolution_select_fusion.mix_ref, f32[8,64,1024]{2,1,0:T(8,128)} %all-to-all-done.3.refs_0_, f32[8,64,1024]{2,1,0:T(8,128)} %collective-permute-done.16.refs_1_, f32[8,64,1024]{2,1,0:T(8,128)} %copy-done.14, ...), custom_call_target="tpu_custom_call", output_to_operand_aliasing={{}: (14, {})} | custom-call | flops 3221225472 | bytes 20971520 | tf_op jit(solution)/shard_map/pallas_call | solution.py:180
  (181 shorter events, 67.1 us)
Async XLA Ops:
  5.0 100.5 %all-to-all-start = ((f32[8,128,1024]{2,1,0:T(8,128)}), f32[8,128,1024]{2,1,0:T(8,128)}, u32[]{:S(2)}, u32[]{:S(2)}) async-start(f32[8,128,1024]{2,1,0:T(8,128)} %shard_map.73), calls=%async_computation | async-start | bytes 8388608 | tf_op jit(solution)/shard_map/all_to_all | solution.py:248
  105.5 97.1 %all-to-all-start.1 = ((f32[8,128,1024]{2,1,0:T(8,128)}), f32[8,128,1024]{2,1,0:T(8,128)}, u32[]{:S(2)}, u32[]{:S(2)}) async-start(f32[8,128,1024]{2,1,0:T(8,128)} %shard_map.74), calls=%async_computation.1 | async-start | bytes 8388608 | tf_op jit(solution)/shard_map/all_to_all | solution.py:248
  116.0 42.6 %copy-start.6 = (f32[8,1,64,1024]{3,2,1,0:T(8,128)}, f32[8,1,64,1024]{3,2,1,0:T(8,128)S(1)}, u32[]{:S(2)}) copy-start(f32[8,1,64,1024]{3,2,1,0:T(8,128)S(1)} %get-tuple-element.47) | copy-start | bytes 6291460
  119.1 45.0 %copy-start.10 = (f32[8,1,64,1024]{3,2,1,0:T(8,128)}, f32[8,1,64,1024]{3,2,1,0:T(8,128)S(1)}, u32[]{:S(2)}) copy-start(f32[8,1,64,1024]{3,2,1,0:T(8,128)S(1)} %get-tuple-element.50) | copy-start | bytes 6291460
  202.6 52.2 %all-to-all-start.3 = ((f32[8,64,1024]{2,1,0:T(8,128)}), f32[8,64,1024]{2,1,0:T(8,128)}, u32[]{:S(2)}, u32[]{:S(2)}) async-start(f32[8,64,1024]{2,1,0:T(8,128)} %bitcast.169), calls=%async_computation.3 | async-start | bytes 4194304 | tf_op jit(solution)/shard_map/all_to_all | solution.py:287
  254.8 52.0 %all-to-all-start.2 = ((f32[8,64,1024]{2,1,0:T(8,128)}), f32[8,64,1024]{2,1,0:T(8,128)S(1)}, u32[]{:S(2)}, u32[]{:S(2)}) async-start(f32[8,64,1024]{2,1,0:T(8,128)} %bitcast.168), calls=%async_computation.2 | async-start | bytes 4194304 | tf_op jit(solution)/shard_map/all_to_all | solution.py:287
  258.4 47.6 %collective-permute-start.1 = (f32[8,64,1024]{2,1,0:T(8,128)}, f32[8,64,1024]{2,1,0:T(8,128)}, u32[]{:S(2)}, u32[]{:S(2)}) collective-permute-start(f32[8,64,1024]{2,1,0:T(8,128)} %all-to-all-done.3.refs_0_), channel_id=1, source_target_pairs={{0,2},{1,3},{2,0},{3,1},{4,6},{5,7},{6,4},{7,5},{8,10},{9,11},{10,... | collective-permute-start | bytes 6291464 | tf_op jit(solution)/shard_map/ppermute | solution.py:49
  306.9 112.6 %copy-start = (f32[8,64,1024]{2,1,0:T(8,128)}, f32[8,64,1024]{2,1,0:T(8,128)S(1)}, u32[]{:S(2)}) copy-start(f32[8,64,1024]{2,1,0:T(8,128)S(1)} %all-to-all-done.2.refs_0_) | copy-start | bytes 6291460
  306.9 52.7 %all-to-all-start.5 = ((f32[8,64,1024]{2,1,0:T(8,128)}), f32[8,64,1024]{2,1,0:T(8,128)}, u32[]{:S(2)}, u32[]{:S(2)}) async-start(f32[8,64,1024]{2,1,0:T(8,128)} %bitcast.170), calls=%async_computation.5 | async-start | bytes 4194304 | tf_op jit(solution)/shard_map/all_to_all | solution.py:287
  312.1 46.1 %collective-permute-start.3 = (f32[8,64,1024]{2,1,0:T(8,128)S(1)}, f32[8,64,1024]{2,1,0:T(8,128)S(1)}, u32[]{:S(2)}, u32[]{:S(2)}) collective-permute-start(f32[8,64,1024]{2,1,0:T(8,128)S(1)} %all-to-all-done.2.refs_0_), channel_id=1, source_target_pairs={{0,2},{1,3},{2,0},{3,1},{4,6},{5,7},{6,4},{7,5},{8,10},{9,11},{10,... | collective-permute-start | bytes 6291464 | tf_op jit(solution)/shard_map/ppermute | solution.py:49
  359.5 52.4 %all-to-all-start.4 = ((f32[8,64,1024]{2,1,0:T(8,128)}), f32[8,64,1024]{2,1,0:T(8,128)}, u32[]{:S(2)}, u32[]{:S(2)}) async-start(f32[8,64,1024]{2,1,0:T(8,128)} %bitcast.171), calls=%async_computation.4 | async-start | bytes 4194304 | tf_op jit(solution)/shard_map/all_to_all | solution.py:287
  365.6 46.4 %collective-permute-start.5 = (f32[8,64,1024]{2,1,0:T(8,128)}, f32[8,64,1024]{2,1,0:T(8,128)}, u32[]{:S(2)}, u32[]{:S(2)}) collective-permute-start(f32[8,64,1024]{2,1,0:T(8,128)} %all-to-all-done.5.refs_4_), channel_id=1, source_target_pairs={{0,2},{1,3},{2,0},{3,1},{4,6},{5,7},{6,4},{7,5},{8,10},{9,11},{10,... | collective-permute-start | bytes 6291464 | tf_op jit(solution)/shard_map/ppermute | solution.py:49
  367.2 49.9 %collective-permute-start = (f32[8,64,1024]{2,1,0:T(8,128)S(1)}, f32[8,64,1024]{2,1,0:T(8,128)}, u32[]{:S(2)}, u32[]{:S(2)}) collective-permute-start(f32[8,64,1024]{2,1,0:T(8,128)S(1)} %all-to-all-done.2.refs_0_), channel_id=1, source_target_pairs={{0,1},{1,0},{2,3},{3,2},{4,5},{5,4},{6,7},{7,6},{8,9},{9,8},{10,11... | collective-permute-start | bytes 6291464 | tf_op jit(solution)/shard_map/ppermute | solution.py:49
  367.2 49.9 %collective-permute-start.2 = (f32[8,64,1024]{2,1,0:T(8,128)}, f32[8,64,1024]{2,1,0:T(8,128)}, u32[]{:S(2)}, u32[]{:S(2)}) collective-permute-start(f32[8,64,1024]{2,1,0:T(8,128)} %collective-permute-done.1.refs_2_), channel_id=1, source_target_pairs={{0,1},{1,0},{2,3},{3,2},{4,5},{5,4},{6,7},{7,6},{8,9},{9,8},{10,11... | collective-permute-start | bytes 6291464 | tf_op jit(solution)/shard_map/ppermute | solution.py:49
  411.9 5.2 %collective-permute-start.4 = (f32[8,64,1024]{2,1,0:T(8,128)}, f32[8,64,1024]{2,1,0:T(8,128)}, u32[]{:S(2)}, u32[]{:S(2)}) collective-permute-start(f32[8,64,1024]{2,1,0:T(8,128)} %all-to-all-done.4.refs_4_), channel_id=1, source_target_pairs={{0,1},{1,0},{2,3},{3,2},{4,5},{5,4},{6,7},{7,6},{8,9},{9,8},{10,11... | collective-permute-start | bytes 6291464 | tf_op jit(solution)/shard_map/ppermute | solution.py:49
  411.9 7.5 %collective-permute-start.6 = (f32[8,64,1024]{2,1,0:T(8,128)}, f32[8,64,1024]{2,1,0:T(8,128)}, u32[]{:S(2)}, u32[]{:S(2)}) collective-permute-start(f32[8,64,1024]{2,1,0:T(8,128)} %collective-permute-done.5.refs_6_), channel_id=1, source_target_pairs={{0,1},{1,0},{2,3},{3,2},{4,5},{5,4},{6,7},{7,6},{8,9},{9,8},{10,11... | collective-permute-start | bytes 6291464 | tf_op jit(solution)/shard_map/ppermute | solution.py:49
  415.6 19.8 %collective-permute-start.7 = (f32[8,64,384]{2,1,0:T(8,128)}, f32[8,64,384]{2,1,0:T(8,128)}, u32[]{:S(2)}, u32[]{:S(2)}) collective-permute-start(f32[8,64,384]{2,1,0:T(8,128)} %get-tuple-element.56), channel_id=1, source_target_pairs={{0,2},{1,3},{2,0},{3,1},{4,6},{5,7},{6,4},{7,5},{8,10},{9,11},{10,... | collective-permute-start | bytes 2359304 | tf_op jit(solution)/shard_map/ppermute | solution.py:49
  435.4 4.0 collective-permute-start.10
  435.7 3.7 collective-permute-start.8
  437.0 3.9 collective-permute-start.9
  440.9 13.8 %collective-permute-start.15 = (f32[8,64,256]{2,1,0:T(8,128)}, f32[8,64,256]{2,1,0:T(8,128)S(1)}, u32[]{:S(2)}, u32[]{:S(2)}) collective-permute-start(f32[8,64,256]{2,1,0:T(8,128)} %slice.222), channel_id=1, source_target_pairs={{0,2},{1,3},{2,0},{3,1},{4,6},{5,7},{6,4},{7,5},{8,10},{9,11},{10,... | collective-permute-start | bytes 1572872 | tf_op jit(solution)/shard_map/ppermute | solution.py:49
  442.1 4.0 collective-permute-start.11
  443.3 3.9 collective-permute-start.12
  444.3 4.8 collective-permute-start.13
  449.1 5.1 %collective-permute-start.14 = (f32[64,64]{1,0:T(8,128)S(1)}, f32[64,64]{1,0:T(8,128)S(1)}, u32[]{:S(2)}, u32[]{:S(2)}) collective-permute-start(f32[64,64]{1,0:T(8,128)S(1)} %add_add_fusion), channel_id=1, source_target_pairs={{0,16},{4,20},{8,24},{12,28},{16,0},{20,4},{24,8},{28,12},{1,17},{... | collective-permute-start | bytes 49160 | tf_op jit(solution)/shard_map/ppermute | solution.py:211
  453.7 20.9 %collective-permute-start.16 = (f32[8,64,1024]{2,1,0:T(8,128)}, f32[8,64,1024]{2,1,0:T(8,128)}, u32[]{:S(2)}, u32[]{:S(2)}) collective-permute-start(f32[8,64,1024]{2,1,0:T(8,128)} %all-to-all-done.3.refs_0_), channel_id=1, source_target_pairs={{0,1},{1,0},{2,3},{3,2},{4,5},{5,4},{6,7},{7,6},{8,9},{9,8},{10,11... | collective-permute-start | bytes 6291464 | tf_op jit(solution)/shard_map/ppermute | solution.py:49
  453.7 21.4 %collective-permute-start.17 = (f32[8,64,1024]{2,1,0:T(8,128)S(1)}, f32[8,64,1024]{2,1,0:T(8,128)}, u32[]{:S(2)}, u32[]{:S(2)}) collective-permute-start(f32[8,64,1024]{2,1,0:T(8,128)S(1)} %copy-done.15), channel_id=1, source_target_pairs={{0,1},{1,0},{2,3},{3,2},{4,5},{5,4},{6,7},{7,6},{8,9},{9,8},{10,11... | collective-permute-start | bytes 6291464 | tf_op jit(solution)/shard_map/ppermute | solution.py:49
  454.2 20.9 %collective-permute-start.18 = (f32[8,64,1024]{2,1,0:T(8,128)}, f32[8,64,1024]{2,1,0:T(8,128)}, u32[]{:S(2)}, u32[]{:S(2)}) collective-permute-start(f32[8,64,1024]{2,1,0:T(8,128)} %all-to-all-done.5.refs_4_), channel_id=1, source_target_pairs={{0,1},{1,0},{2,3},{3,2},{4,5},{5,4},{6,7},{7,6},{8,9},{9,8},{10,11... | collective-permute-start | bytes 6291464 | tf_op jit(solution)/shard_map/ppermute | solution.py:49
  454.2 20.9 %collective-permute-start.20 = (f32[8,64,384]{2,1,0:T(8,128)}, f32[8,64,384]{2,1,0:T(8,128)S(1)}, u32[]{:S(2)}, u32[]{:S(2)}) collective-permute-start(f32[8,64,384]{2,1,0:T(8,128)} %collective-permute-done.7.refs_6_), channel_id=1, source_target_pairs={{0,1},{1,0},{2,3},{3,2},{4,5},{5,4},{6,7},{7,6},{8,9},{9,8},{10,11... | collective-permute-start | bytes 2359304 | tf_op jit(solution)/shard_map/ppermute | solution.py:49
  454.7 19.9 %collective-permute-start.19 = (f32[8,64,384]{2,1,0:T(8,128)}, f32[8,64,384]{2,1,0:T(8,128)}, u32[]{:S(2)}, u32[]{:S(2)}) collective-permute-start(f32[8,64,384]{2,1,0:T(8,128)} %get-tuple-element.42), channel_id=1, source_target_pairs={{0,2},{1,3},{2,0},{3,1},{4,6},{5,7},{6,4},{7,5},{8,10},{9,11},{10,... | collective-permute-start | bytes 2359304 | tf_op jit(solution)/shard_map/ppermute | solution.py:49
  474.6 3.0 collective-permute-start.22
  474.6 3.0 collective-permute-start.21
  (22 other events, 175.9 us)

commit v8 on v7

--- a/solution.py
+++ b/solution.py
@@ -161,16 +161,17 @@
         out_ref[first : first + SUBLANES] = result.reshape(SUBLANES, -1, columns)
 
 
-def rotate_half(pieces, wide_mixing, place, half, earlier):
+def rotate_part(pieces, wide_mixing, place, half, column, width, earlier):
     half_rows = pieces[0][0].shape[1]
-    down_count = sum(cut.shape[2] for cut in pieces[0])
+    down_count = pieces[0][0].shape[2]
     step_rows = 2 * SUBLANES
     blocks = half_rows // step_rows
     own = wide_mixing.shape[0] // SUBLANES
     flat = [cut for cuts in pieces for cut in cuts]
     specs = [pl.BlockSpec(wide_mixing.shape, lambda i, place: (0, 0))]
     for cut in flat:
-        specs.append(pl.BlockSpec((cut.shape[0], step_rows, cut.shape[2]), lambda i, place: (0, i, 0)))
+        shape = (cut.shape[0], step_rows, min(cut.shape[2], width))
+        specs.append(pl.BlockSpec(shape, lambda i, place, at=column if cut.shape[2] == down_count else 0: (0, i, at)))
     operands = [place, wide_mixing, *flat]
     aliases = {}
     if earlier is not None:
@@ -185,15 +186,15 @@
             grid=(blocks,),
             in_specs=specs,
             out_specs=pl.BlockSpec(
-                (step_rows, own, down_count), lambda i, place: (i + lax.rem(place[0] + half, 2) * blocks, 0, 0)
+                (step_rows, own, width), lambda i, place: (i + lax.rem(place[0] + half, 2) * blocks, 0, column)
             ),
             scratch_shapes=[pltpu.VMEM((2 * wide_mixing.shape[0], wide_mixing.shape[1]), jnp.bfloat16)],
         ),
         input_output_aliases=aliases,
         compiler_params=pltpu.CompilerParams(vmem_limit_bytes=56 * 1024 * 1024),
         cost_estimate=pl.CostEstimate(
-            flops=6 * wide_mixing.size * down_count * half_rows // SUBLANES,
-            bytes_accessed=4 * (sum(cut.size for cut in flat) + half_rows * own * down_count),
+            flops=6 * wide_mixing.size * width * half_rows // SUBLANES,
+            bytes_accessed=4 * half_rows * width * (sum(cuts[0].shape[0] for cuts in pieces) + own),
             transcendentals=0,
         ),
     )(*operands)
@@ -287,9 +288,8 @@
             back = lax.all_to_all(piece, "hil", split_axis=0, concat_axis=0, tiled=True)
             held[half].append(back)
             if (turn, half) == (rounds - 1, mine):
-                bounds = [0, down_count // 8 * 3, down_count // 8 * 5, down_count]
-                cuts = [back[:, :, begin:end] for begin, end in zip(bounds, bounds[1:])]
-                crossed.append(spread_step(cuts[:1], side)[0])
+                bounds = [down_count // 4 * number for number in range(5)]
+                crossed.append(spread_step([back[:, :, : bounds[1]]], side)[0])
             else:
                 crossed.append(spread_step([back], side)[0])
         pieces = upcoming
@@ -315,9 +315,10 @@
     order_own = order.reshape(rounds, vec_parts, hil_parts, -1)[:, 0].reshape(vec_local, -1)
     partial = gram_partial(own_pieces, lax.rem(own, side), side)
     partial = dot(order, dot(partial, order, (1, 0), highest), (0, 0), highest)
-    partial, cuts[0] = lax.optimization_barrier((partial, crossed[-1]))
-    partial, cuts[1], cuts[2] = lax.optimization_barrier((small_sum(partial, "vec"), cuts[1], cuts[2]))
-    cuts[1:] = spread_step(cuts[1:], side)
+    partial, first, back = lax.optimization_barrier((partial, crossed[-1], held[mine][-1]))
+    cuts = [back[:, :, begin:end] for begin, end in zip(bounds[1:], bounds[2:])]
+    partial, cuts = lax.optimization_barrier((small_sum(partial, "vec"), cuts))
+    cuts = [first] + spread_step(cuts, side)
     gram_sum, cuts[1] = lax.optimization_barrier((small_sum(partial, "hil"), cuts[1]))
     mixing = newton_schulz(gram_sum) * math.sqrt(up_count * down_count)
     mixing = dot(dot(order_own, mixing, (1, 1), highest), order, (1, 1), highest)
@@ -327,15 +328,20 @@
     right = (jnp.arange(order.shape[0], dtype=jnp.int32)[:, None] == long[None, :] // SUBLANES).astype(jnp.float32)
     wide_mixing = dot(left, dot(mixing, right, (1, 0), highest), (1, 0), highest)
     wide_mixing = jnp.where(wide[:, None] // vec_local == long[None, :] % SUBLANES, wide_mixing, 0.0)
-    result = rotate_half(own_pieces, wide_mixing, place, mine, None)
-    result, cuts[2] = lax.optimization_barrier((result, cuts[2]))
-    other_pieces = []
-    for turn in range(rounds):
-        there = cuts if turn == rounds - 1 else [crossed[2 * turn + 1]]
-        here = [[piece] for piece in on_side([held[theirs][turn]])]
-        there = [list(group) for group in zip(*[on_side([cut]) for cut in there])]
-        other_pieces += here + there
-    return rotate_half(other_pieces, wide_mixing, place, theirs, result)
+    wide_mixing, cuts[:3] = lax.optimization_barrier((wide_mixing, cuts[:3]))
+    result = rotate_part(own_pieces, wide_mixing, place, mine, 0, down_count, None)
+    result, cuts[3] = lax.optimization_barrier((result, cuts[3]))
+    here = [[piece] for turn in range(rounds) for piece in on_side([held[theirs][turn]])]
+    there = [[piece] for turn in range(rounds - 1) for piece in on_side([crossed[2 * turn + 1]])]
+    exchanged = [on_side([cut]) for cut in cuts]
+    early = there + [list(pair) for pair in zip(*exchanged[:3])]
+    late = there + [[piece] for piece in exchanged[3]]
+    for arrays, column, width in ((early, 0, bounds[3]), (late, 3, down_count - bounds[3])):
+        pieces = []
+        for begin in range(0, len(here), side):
+            pieces += here[begin : begin + side] + arrays[begin : begin + side]
+        result = rotate_part(pieces, wide_mixing, place, theirs, column, width, result)
+    return result
 
 
 def split_down(local_block):

time: 498 us -> 507 us (1.018)
  waiting for transfers between devices: 253 us -> 262 us
    ppermute x16 -> x18, waiting for transfers between devices: 94.5 us -> 101 us  [spread_step(): return [lax.ppermute(piece, 'vec', pairs) for piece in held]]
    pallas_call x2 -> x3, Pallas kernels: 19.4 us -> 22.7 us  [rotate_part(): pl.pallas_call(functools.partial(rotate_kernel, [len(cuts) for cuts in pi...]
    unnamed x50 -> x58, local copies, waits for them, and re-layouts: 8.76 us -> 11.5 us
    ppermute x16 -> x18, starting transfers between devices: 10.9 us -> 11.5 us  [spread_step(): return [lax.ppermute(piece, 'vec', pairs) for piece in held]]
  transfers between devices with their start and end apart: 29 -> 31, of which waited for: 14 -> 17; matrix products, arithmetic and copies ran while one was open for 29% -> 27% of each run, Pallas kernels for 4% -> 6%
where the time goes in v8:
time: 507 us; the launch traced here: 499 us
  waiting for transfers between devices  262 us (52%)
  matrix products  109 us (21%)
  starting transfers between devices  49.9 us (10%)
  Pallas kernels  38.7 us (8%)
  local copies, waits for them, and re-layouts  30.5 us (6%)
  other arithmetic  6.64 us (1%)
    dot_general x28, matrix products, dot(): lax.dot_general(left, right, ((contract[:1], contract[1:]), ((), ())), pr...  104 us
    all_to_all x2, waiting for transfers between devices, vector_cut(): lax.all_to_all(block, 'hil', split_axis=0, concat_axis=0, tiled=True)  103 us
    ppermute x18, waiting for transfers between devices, spread_step(): return [lax.ppermute(piece, 'vec', pairs) for piece in held]  101 us
    all_to_all x4, waiting for transfers between devices, vector_cut(): back = lax.all_to_all(piece, 'hil', split_axis=0, concat_axis=0, tiled=True)  51 us
    pallas_call x3, Pallas kernels, rotate_part(): pl.pallas_call(functools.partial(rotate_kernel, [len(cuts) for cuts in pi...  22.7 us
    all_to_all x4, starting transfers between devices, vector_cut(): back = lax.all_to_all(piece, 'hil', split_axis=0, concat_axis=0, tiled=True)  18.5 us
    all_to_all x2, starting transfers between devices, vector_cut(): lax.all_to_all(block, 'hil', split_axis=0, concat_axis=0, tiled=True)  11.8 us
    slice x7, local copies, waits for them, and re-layouts, rows(): values.reshape(hil_parts, 2, half_rows, -1)[:, half]  11.5 us
  transfers between devices with their start and end apart: 31, of which 17 were waited for; matrix products, arithmetic and copies ran while one was open for 27% of the time, Pallas kernels for 6%

profile of v8, /device:TPU:0, one launch (start us, length us, event | category | flops | bytes accessed | tf_op | source)
XLA Modules:
  0.0 498.7 jit_solution(4463350328566084524)
XLA Ops:
  0.0 5.0 %shard_map.73 = f32[8,128,1024]{2,1,0:T(8,128)} custom-call(s32[1]{0:T(128)} %bitcast.place_ref, f32[128,16,1024]{2,1,0:T(8,128)} %block_ref.3), custom_call_target="tpu_custom_call" | custom-call | tf_op jit(solution)/shard_map/pallas_call | solution.py:65
  5.0 7.3 %all-to-all-start = ((f32[8,128,1024]{2,1,0:T(8,128)}), f32[8,128,1024]{2,1,0:T(8,128)}, u32[]{:S(2)}, u32[]{:S(2)}) async-start(f32[8,128,1024]{2,1,0:T(8,128)} %shard_map.73), calls=%async_computation | async-start | bytes 8388608 | tf_op jit(solution)/shard_map/all_to_all | solution.py:249
  12.3 5.1 %shard_map.74 = f32[8,128,1024]{2,1,0:T(8,128)} custom-call(s32[1]{0:T(128)} %bitcast.place_ref, f32[128,16,1024]{2,1,0:T(8,128)} %block_ref.3), custom_call_target="tpu_custom_call" | custom-call | tf_op jit(solution)/shard_map/pallas_call | solution.py:65
  20.0 5.2 %convolution_add_fusion = f32[1024,1024]{1,0:T(8,128)} fusion(f32[10]{0:T(128)S(1)} %copy-done.27, s32[1024]{0:T(1024)S(1)} %shift_right_arithmetic.28), kind=kOutput, calls=%fused_computation.24 | convolution fusion | flops 126949376 | bytes 4198440 | tf_op jit(solution)/shard_map/dot_general | solution.py:254
  25.2 80.3 %all-to-all-done = f32[8,128,1024]{2,1,0:T(8,128)} async-done(((f32[8,128,1024]{2,1,0:T(8,128)}), f32[8,128,1024]{2,1,0:T(8,128)}, u32[]{:S(2)}, u32[]{:S(2)}) %all-to-all-start) | async-done | bytes 4194336 | tf_op jit(solution)/shard_map/all_to_all | solution.py:249
  105.5 4.6 all-to-all-start.1
  110.1 5.4 %select_add_fusion = f32[8,2,64,1024]{3,2,1,0:T(8,128)S(1)} fusion(f32[8,2,64]{2,1,0:T(2,128)S(1)} %get-tuple-element.98, s32[8,2,64]{2,1,0:T(2,128)S(1)} %get-tuple-element.79, f32[8,2,64]{2,1,0:T(2,128)S(1)} %get-tuple-element.97, s32[8,2,64]{2,1,0:T(2,128)S(1)} %get-tuple-element.78, f32[8,2,64]{2,1,0:T(2,128)S(1)} %get-tuple-element.96, ...), kind=kLoop, calls=%fused_computation.1 | loop fusion | flops 30408704 | bytes 4276224 | tf_op jit(solution)/shard_map/add | solution.py:32
  122.9 8.9 %fusion.120 = f32[1024,1024]{1,0:T(8,128)S(1)} fusion(f32[1024,1024]{1,0:T(8,128)} %bitcast.3, f32[1024,1024]{1,0:T(8,128)S(1)} %copy-done.1), kind=kOutput, calls=%fused_computation.219 | convolution fusion | flops 6442450944 | bytes 12582912 | tf_op jit(solution)/shard_map/dot_general | solution.py:37
  131.9 17.0 %add_multiply_fusion.1 = f32[1024,1024]{1,0:T(8,128)S(1)} fusion(f32[1024,1024]{1,0:T(8,128)S(1)} %copy-done.16, f32[1024,1024]{1,0:T(8,128)} %bitcast.3, f32[1024,1024]{1,0:T(8,128)S(1)} %fusion.120, f32[1024]{0:T(1024)S(1)} %broadcast_in_dim.182, s32[1024]{0:T(1024)S(1)} %eq.388, f32[1024]{0:T(1024)S(1)} %broadcast_in_dim.180, s32[1024]{0:T(1024)S(1)} %eq.384, ...), kind=kOutput, calls=%fused_computation.12 | convolution fusion | flops 6477053952 | bytes 16859136 | tf_op jit(solution)/shard_map/dot_general | solution.py:37
  152.0 3.6 fusion.122
  155.7 3.6 fusion.121
  159.3 5.5 %bitcast_subtract_fusion.2 = f32[512,1024]{1,0:T(8,128)} fusion(f32[8,1,64,1024]{3,2,1,0:T(8,128)S(1)} %get-tuple-element.65, f32[512,1024]{1,0:T(8,128)S(1)} %bitcast.162, f32[8,1,64,1024]{3,2,1,0:T(8,128)S(1)} %get-tuple-element.61, f32[512,1024]{1,0:T(8,128)S(1)} %fusion.122, f32[512,1024]{1,0:T(8,128)S(1)} %bitcast.163, ...), kind=kOutput, calls=%fused_computation.27 | convolution fusion | flops 3223846912 | bytes 16777216 | tf_op jit(solution)/shard_map/dot_general | solution.py:37
  164.8 14.9 %bitcast_subtract_fusion.3 = f32[512,1024]{1,0:T(8,128)} fusion(f32[8,1,64,1024]{3,2,1,0:T(8,128)S(1)} %get-tuple-element.66, f32[512,1024]{1,0:T(8,128)S(1)} %bitcast.160, f32[8,1,64,1024]{3,2,1,0:T(8,128)S(1)} %get-tuple-element.62, f32[512,1024]{1,0:T(8,128)S(1)} %fusion.121, f32[512,1024]{1,0:T(8,128)S(1)} %bitcast.165, ...), kind=kOutput, calls=%fused_computation.34 | convolution fusion | flops 3223846912 | bytes 16777216 | tf_op jit(solution)/shard_map/dot_general | solution.py:37
  179.7 22.9 %all-to-all-done.1 = f32[8,128,1024]{2,1,0:T(8,128)} async-done(((f32[8,128,1024]{2,1,0:T(8,128)}), f32[8,128,1024]{2,1,0:T(8,128)}, u32[]{:S(2)}, u32[]{:S(2)}) %all-to-all-start.1) | async-done | bytes 4194336 | tf_op jit(solution)/shard_map/all_to_all | solution.py:249
  206.3 10.6 %fusion.123 = f32[1024,1024]{1,0:T(8,128)S(1)} fusion(f32[1024,1024]{1,0:T(8,128)} %bitcast.37, f32[1024,1024]{1,0:T(8,128)} %param.8), kind=kOutput, calls=%fused_computation.222 | convolution fusion | flops 6442450944 | bytes 12582912 | tf_op jit(solution)/shard_map/dot_general | solution.py:37
  216.9 17.1 %add_multiply_fusion = f32[1024,1024]{1,0:T(8,128)S(1)} fusion(f32[1024,1024]{1,0:T(8,128)S(1)} %copy-done.17, f32[1024,1024]{1,0:T(8,128)} %bitcast.37, f32[1024,1024]{1,0:T(8,128)S(1)} %fusion.123, f32[1024]{0:T(1024)S(1)} %broadcast_in_dim.182, s32[1024]{0:T(1024)S(1)} %eq.388, f32[1024]{0:T(1024)S(1)} %broadcast_in_dim.180, s32[1024]{0:T(1024)S(1)} %eq.384, ...), kind=kOutput, calls=%fused_computation | convolution fusion | flops 6477053952 | bytes 16859136 | tf_op jit(solution)/shard_map/dot_general | solution.py:37
  234.3 5.3 %fusion.114 = (f32[8,1,64,1024]{3,2,1,0:T(8,128)}, f32[8,1,64,1024]{3,2,1,0:T(8,128)S(1)}) fusion(f32[8,2,64,1024]{3,2,1,0:T(8,128)} %bitcast.40), kind=kLoop, calls=%fused_computation.213 | loop fusion | bytes 8388608 | tf_op jit(solution)/shard_map/slice | solution.py:262
  243.2 5.6 %bitcast_subtract_fusion.1 = f32[512,1024]{1,0:T(8,128)} fusion(f32[8,1,64,1024]{3,2,1,0:T(8,128)S(1)} %get-tuple-element.58, f32[512,1024]{1,0:T(8,128)S(1)} %bitcast.156, f32[8,1,64,1024]{3,2,1,0:T(8,128)S(1)} %copy-done.15, f32[512,1024]{1,0:T(8,128)S(1)} %fusion.124, f32[512,1024]{1,0:T(8,128)S(1)} %bitcast.166, f32[1024,1024]{1,0:T(8,128)S(1)} %add_multiply_fusion), kind=kOutput, calls=%fused_computation.26 | convolution fusion | flops 3223846912 | bytes 16777216 | tf_op jit(solution)/shard_map/dot_general | solution.py:37
  248.8 5.9 %all-to-all-done.3.refs_0_ = f32[8,64,1024]{2,1,0:T(8,128)S(1)} async-done(((f32[8,64,1024]{2,1,0:T(8,128)}), f32[8,64,1024]{2,1,0:T(8,128)S(1)}, u32[]{:S(2)}, u32[]{:S(2)}) %all-to-all-start.3) | async-done | bytes 2097184 | tf_op jit(solution)/shard_map/all_to_all | solution.py:288
  261.2 46.0 %collective-permute-done.1.refs_2_ = f32[8,64,1024]{2,1,0:T(8,128)} collective-permute-done((f32[8,64,1024]{2,1,0:T(8,128)}, f32[8,64,1024]{2,1,0:T(8,128)}, u32[]{:S(2)}, u32[]{:S(2)}) %collective-permute-start.1) | collective-permute-done | bytes 2097184 | tf_op jit(solution)/shard_map/ppermute | solution.py:49
  308.1 5.2 %all-to-all-start.5 = ((f32[8,64,1024]{2,1,0:T(8,128)}), f32[8,64,1024]{2,1,0:T(8,128)}, u32[]{:S(2)}, u32[]{:S(2)}) async-start(f32[8,64,1024]{2,1,0:T(8,128)} %bitcast.170), calls=%async_computation.5 | async-start | bytes 4194304 | tf_op jit(solution)/shard_map/all_to_all | solution.py:288
  316.7 3.7 fusion.125
  320.4 6.5 %bitcast_subtract_fusion = f32[512,1024]{1,0:T(8,128)} fusion(f32[8,1,64,1024]{3,2,1,0:T(8,128)} %get-tuple-element.57, f32[512,1024]{1,0:T(8,128)S(1)} %bitcast.158, f32[8,1,64,1024]{3,2,1,0:T(8,128)S(1)} %copy-done.11, f32[512,1024]{1,0:T(8,128)S(1)} %fusion.125, f32[512,1024]{1,0:T(8,128)S(1)} %bitcast.164, f32[1024,1024]{1,0:T(8,128)S(1)} %copy-done.5), kind=kOutput, calls=%fused_computation.25 | convolution fusion | flops 3223846912 | bytes 16777216 | tf_op jit(solution)/shard_map/dot_general | solution.py:37
  326.9 32.5 %collective-permute-done.3.refs_2_ = f32[8,64,1024]{2,1,0:T(8,128)S(1)} collective-permute-done((f32[8,64,1024]{2,1,0:T(8,128)S(1)}, f32[8,64,1024]{2,1,0:T(8,128)S(1)}, u32[]{:S(2)}, u32[]{:S(2)}) %collective-permute-start.3) | collective-permute-done | bytes 2097184 | tf_op jit(solution)/shard_map/ppermute | solution.py:49
  360.7 6.1 %all-to-all-start.4 = ((f32[8,64,1024]{2,1,0:T(8,128)}), f32[8,64,1024]{2,1,0:T(8,128)}, u32[]{:S(2)}, u32[]{:S(2)}) async-start(f32[8,64,1024]{2,1,0:T(8,128)} %bitcast.171), calls=%async_computation.4 | async-start | bytes 4194304 | tf_op jit(solution)/shard_map/all_to_all | solution.py:288
  368.9 44.3 %all-to-all-done.4.refs_4_ = f32[8,64,1024]{2,1,0:T(8,128)} async-done(((f32[8,64,1024]{2,1,0:T(8,128)}), f32[8,64,1024]{2,1,0:T(8,128)}, u32[]{:S(2)}, u32[]{:S(2)}) %all-to-all-start.4) | async-done | bytes 2097184 | tf_op jit(solution)/shard_map/all_to_all | solution.py:288
  420.7 5.9 %shard_map.75 = (f32[256,256]{1,0:T(8,128)S(1)}, f32[256,256]{1,0:T(8,128)S(1)}) custom-call(s32[1]{0:T(128)} %bitcast.2.start_ref, f32[8,64,1024]{2,1,0:T(8,128)S(1)} %all-to-all-done.2.refs_0_, f32[8,64,1024]{2,1,0:T(8,128)} %collective-permute-done.refs_1_, f32[8,64,1024]{2,1,0:T(8,128)} %collective-permute-done.1.refs_2_, ...), custom_call_target="tpu_custom_call" | custom-call | flops 2147483648 | bytes 8388608 | tf_op jit(solution)/shard_map/pallas_call | solution.py:121
  454.9 8.6 %collective-permute-done.16.refs_8_ = f32[8,64,256]{2,1,0:T(8,128)} collective-permute-done((f32[8,64,256]{2,1,0:T(8,128)}, f32[8,64,256]{2,1,0:T(8,128)}, u32[]{:S(2)}, u32[]{:S(2)}) %collective-permute-start.16) | collective-permute-done | bytes 524320 | tf_op jit(solution)/shard_map/ppermute | solution.py:49
  464.0 8.4 %collective-permute-done.20.refs_6_ = f32[8,64,256]{2,1,0:T(8,128)S(1)} collective-permute-done((f32[8,64,256]{2,1,0:T(8,128)}, f32[8,64,256]{2,1,0:T(8,128)S(1)}, u32[]{:S(2)}, u32[]{:S(2)}) %collective-permute-start.20) | collective-permute-done | bytes 524320 | tf_op jit(solution)/shard_map/ppermute | solution.py:49
  472.4 9.8 %shard_map.76.refs_12_ = f32[128,16,1024]{2,1,0:T(8,128)} custom-call(s32[1]{0:T(128)} %bitcast.place_ref, f32[128,512]{1,0:T(8,128)} %convolution_select_fusion.mix_ref, f32[8,64,1024]{2,1,0:T(8,128)} %copy-done, f32[8,64,1024]{2,1,0:T(8,128)} %collective-permute-done.refs_1_, f32[8,64,1024]{2,1,0:T(8,128)} %collective-permute-done.1.refs_2_, ...), custom_call_target="tpu_custom_call" | custom-call | flops 3221225472 | bytes 20971520 | tf_op jit(solution)/shard_map/pallas_call | solution.py:181
  484.5 8.0 %shard_map.77.refs_8_ = f32[128,16,1024]{2,1,0:T(8,128)} custom-call(s32[1]{0:T(128)} %bitcast.place_ref, f32[128,512]{1,0:T(8,128)} %convolution_select_fusion.mix_ref, f32[8,64,1024]{2,1,0:T(8,128)} %copy-done.6, f32[8,64,1024]{2,1,0:T(8,128)} %collective-permute-done.17.refs_1_, f32[8,64,1024]{2,1,0:T(8,128)} %copy-done.18, ...), custom_call_target="tpu_custom_call", output_to_operand_aliasing={{}: (14, {})} | custom-call | flops 2415919104 | bytes 15728640 | tf_op jit(solution)/shard_map/pallas_call | solution.py:181
  493.3 4.9 shard_map.78
  (194 shorter events, 73.1 us)
Async XLA Ops:
  5.0 100.5 %all-to-all-start = ((f32[8,128,1024]{2,1,0:T(8,128)}), f32[8,128,1024]{2,1,0:T(8,128)}, u32[]{:S(2)}, u32[]{:S(2)}) async-start(f32[8,128,1024]{2,1,0:T(8,128)} %shard_map.73), calls=%async_computation | async-start | bytes 8388608 | tf_op jit(solution)/shard_map/all_to_all | solution.py:249
  105.5 97.1 %all-to-all-start.1 = ((f32[8,128,1024]{2,1,0:T(8,128)}), f32[8,128,1024]{2,1,0:T(8,128)}, u32[]{:S(2)}, u32[]{:S(2)}) async-start(f32[8,128,1024]{2,1,0:T(8,128)} %shard_map.74), calls=%async_computation.1 | async-start | bytes 8388608 | tf_op jit(solution)/shard_map/all_to_all | solution.py:249
  202.6 52.0 %all-to-all-start.3 = ((f32[8,64,1024]{2,1,0:T(8,128)}), f32[8,64,1024]{2,1,0:T(8,128)S(1)}, u32[]{:S(2)}, u32[]{:S(2)}) async-start(f32[8,64,1024]{2,1,0:T(8,128)} %bitcast.169), calls=%async_computation.3 | async-start | bytes 4194304 | tf_op jit(solution)/shard_map/all_to_all | solution.py:288
  256.0 52.1 %all-to-all-start.2 = ((f32[8,64,1024]{2,1,0:T(8,128)}), f32[8,64,1024]{2,1,0:T(8,128)S(1)}, u32[]{:S(2)}, u32[]{:S(2)}) async-start(f32[8,64,1024]{2,1,0:T(8,128)} %bitcast.168), calls=%async_computation.2 | async-start | bytes 4194304 | tf_op jit(solution)/shard_map/all_to_all | solution.py:288
  259.7 47.6 %collective-permute-start.1 = (f32[8,64,1024]{2,1,0:T(8,128)}, f32[8,64,1024]{2,1,0:T(8,128)}, u32[]{:S(2)}, u32[]{:S(2)}) collective-permute-start(f32[8,64,1024]{2,1,0:T(8,128)} %copy-done.6), channel_id=1, source_target_pairs={{0,2},{1,3},{2,0},{3,1},{4,6},{5,7},{6,4},{7,5},{8,10},{9,11},{10,... | collective-permute-start | bytes 6291464 | tf_op jit(solution)/shard_map/ppermute | solution.py:49
  308.1 112.6 %copy-start = (f32[8,64,1024]{2,1,0:T(8,128)}, f32[8,64,1024]{2,1,0:T(8,128)S(1)}, u32[]{:S(2)}) copy-start(f32[8,64,1024]{2,1,0:T(8,128)S(1)} %all-to-all-done.2.refs_0_) | copy-start | bytes 6291460
  308.1 52.7 %all-to-all-start.5 = ((f32[8,64,1024]{2,1,0:T(8,128)}), f32[8,64,1024]{2,1,0:T(8,128)}, u32[]{:S(2)}, u32[]{:S(2)}) async-start(f32[8,64,1024]{2,1,0:T(8,128)} %bitcast.170), calls=%async_computation.5 | async-start | bytes 4194304 | tf_op jit(solution)/shard_map/all_to_all | solution.py:288
  313.3 46.1 %collective-permute-start.3 = (f32[8,64,1024]{2,1,0:T(8,128)S(1)}, f32[8,64,1024]{2,1,0:T(8,128)S(1)}, u32[]{:S(2)}, u32[]{:S(2)}) collective-permute-start(f32[8,64,1024]{2,1,0:T(8,128)S(1)} %all-to-all-done.2.refs_0_), channel_id=1, source_target_pairs={{0,2},{1,3},{2,0},{3,1},{4,6},{5,7},{6,4},{7,5},{8,10},{9,11},{10,... | collective-permute-start | bytes 6291464 | tf_op jit(solution)/shard_map/ppermute | solution.py:49
  360.7 52.4 %all-to-all-start.4 = ((f32[8,64,1024]{2,1,0:T(8,128)}), f32[8,64,1024]{2,1,0:T(8,128)}, u32[]{:S(2)}, u32[]{:S(2)}) async-start(f32[8,64,1024]{2,1,0:T(8,128)} %bitcast.171), calls=%async_computation.4 | async-start | bytes 4194304 | tf_op jit(solution)/shard_map/all_to_all | solution.py:288
  366.8 46.4 %collective-permute-start.5 = (f32[8,64,1024]{2,1,0:T(8,128)}, f32[8,64,1024]{2,1,0:T(8,128)}, u32[]{:S(2)}, u32[]{:S(2)}) collective-permute-start(f32[8,64,1024]{2,1,0:T(8,128)} %all-to-all-done.5.refs_4_), channel_id=1, source_target_pairs={{0,2},{1,3},{2,0},{3,1},{4,6},{5,7},{6,4},{7,5},{8,10},{9,11},{10,... | collective-permute-start | bytes 6291464 | tf_op jit(solution)/shard_map/ppermute | solution.py:49
  368.4 49.1 %collective-permute-start = (f32[8,64,1024]{2,1,0:T(8,128)S(1)}, f32[8,64,1024]{2,1,0:T(8,128)}, u32[]{:S(2)}, u32[]{:S(2)}) collective-permute-start(f32[8,64,1024]{2,1,0:T(8,128)S(1)} %all-to-all-done.2.refs_0_), channel_id=1, source_target_pairs={{0,1},{1,0},{2,3},{3,2},{4,5},{5,4},{6,7},{7,6},{8,9},{9,8},{10,11... | collective-permute-start | bytes 6291464 | tf_op jit(solution)/shard_map/ppermute | solution.py:49
  368.4 49.1 %collective-permute-start.2 = (f32[8,64,1024]{2,1,0:T(8,128)}, f32[8,64,1024]{2,1,0:T(8,128)}, u32[]{:S(2)}, u32[]{:S(2)}) collective-permute-start(f32[8,64,1024]{2,1,0:T(8,128)} %collective-permute-done.1.refs_2_), channel_id=1, source_target_pairs={{0,1},{1,0},{2,3},{3,2},{4,5},{5,4},{6,7},{7,6},{8,9},{9,8},{10,11... | collective-permute-start | bytes 6291464 | tf_op jit(solution)/shard_map/ppermute | solution.py:49
  413.2 4.5 collective-permute-start.4
  413.2 7.5 %collective-permute-start.6 = (f32[8,64,1024]{2,1,0:T(8,128)}, f32[8,64,1024]{2,1,0:T(8,128)}, u32[]{:S(2)}, u32[]{:S(2)}) collective-permute-start(f32[8,64,1024]{2,1,0:T(8,128)} %collective-permute-done.5.refs_6_), channel_id=1, source_target_pairs={{0,1},{1,0},{2,3},{3,2},{4,5},{5,4},{6,7},{7,6},{8,9},{9,8},{10,11... | collective-permute-start | bytes 6291464 | tf_op jit(solution)/shard_map/ppermute | solution.py:49
  416.0 14.2 %collective-permute-start.7 = (f32[8,64,256]{2,1,0:T(8,128)}, f32[8,64,256]{2,1,0:T(8,128)}, u32[]{:S(2)}, u32[]{:S(2)}) collective-permute-start(f32[8,64,256]{2,1,0:T(8,128)} %slice.225), channel_id=1, source_target_pairs={{0,2},{1,3},{2,0},{3,1},{4,6},{5,7},{6,4},{7,5},{8,10},{9,11},{10,... | collective-permute-start | bytes 1572872 | tf_op jit(solution)/shard_map/ppermute | solution.py:49
  430.2 4.6 collective-permute-start.10
  430.4 4.3 collective-permute-start.8
  431.8 3.9 collective-permute-start.9
  435.7 14.0 %collective-permute-start.15 = (f32[8,64,256]{2,1,0:T(8,128)S(1)}, f32[8,64,256]{2,1,0:T(8,128)S(1)}, u32[]{:S(2)}, u32[]{:S(2)}) collective-permute-start(f32[8,64,256]{2,1,0:T(8,128)S(1)} %get-tuple-element.44), channel_id=1, source_target_pairs={{0,2},{1,3},{2,0},{3,1},{4,6},{5,7},{6,4},{7,5},{8,10},{9,11},{10,... | collective-permute-start | bytes 1572872 | tf_op jit(solution)/shard_map/ppermute | solution.py:49
  436.4 3.9 collective-permute-start.11
  437.6 3.9 collective-permute-start.12
  438.6 4.8 collective-permute-start.13
  443.4 4.9 collective-permute-start.14
  446.1 17.4 %collective-permute-start.17 = (f32[8,64,1024]{2,1,0:T(8,128)S(1)}, f32[8,64,1024]{2,1,0:T(8,128)}, u32[]{:S(2)}, u32[]{:S(2)}) collective-permute-start(f32[8,64,1024]{2,1,0:T(8,128)S(1)} %copy-done.7), channel_id=1, source_target_pairs={{0,1},{1,0},{2,3},{3,2},{4,5},{5,4},{6,7},{7,6},{8,9},{9,8},{10,11... | collective-permute-start | bytes 6291464 | tf_op jit(solution)/shard_map/ppermute | solution.py:49
  446.1 36.2 %collective-permute-start.18 = (f32[8,64,1024]{2,1,0:T(8,128)}, f32[8,64,1024]{2,1,0:T(8,128)}, u32[]{:S(2)}, u32[]{:S(2)}) collective-permute-start(f32[8,64,1024]{2,1,0:T(8,128)} %copy-done.18), channel_id=1, source_target_pairs={{0,1},{1,0},{2,3},{3,2},{4,5},{5,4},{6,7},{7,6},{8,9},{9,8},{10,11... | collective-permute-start | bytes 6291464 | tf_op jit(solution)/shard_map/ppermute | solution.py:49
  446.6 36.1 %collective-permute-start.19 = (f32[8,64,1024]{2,1,0:T(8,128)}, f32[8,64,1024]{2,1,0:T(8,128)}, u32[]{:S(2)}, u32[]{:S(2)}) collective-permute-start(f32[8,64,1024]{2,1,0:T(8,128)} %all-to-all-done.5.refs_4_), channel_id=1, source_target_pairs={{0,1},{1,0},{2,3},{3,2},{4,5},{5,4},{6,7},{7,6},{8,9},{9,8},{10,11... | collective-permute-start | bytes 6291464 | tf_op jit(solution)/shard_map/ppermute | solution.py:49
  448.3 15.2 %collective-permute-start.16 = (f32[8,64,256]{2,1,0:T(8,128)}, f32[8,64,256]{2,1,0:T(8,128)}, u32[]{:S(2)}, u32[]{:S(2)}) collective-permute-start(f32[8,64,256]{2,1,0:T(8,128)} %get-tuple-element.48), channel_id=1, source_target_pairs={{0,2},{1,3},{2,0},{3,1},{4,6},{5,7},{6,4},{7,5},{8,10},{9,11},{10,... | collective-permute-start | bytes 1572872 | tf_op jit(solution)/shard_map/ppermute | solution.py:49
  449.7 22.7 %collective-permute-start.20 = (f32[8,64,256]{2,1,0:T(8,128)}, f32[8,64,256]{2,1,0:T(8,128)S(1)}, u32[]{:S(2)}, u32[]{:S(2)}) collective-permute-start(f32[8,64,256]{2,1,0:T(8,128)} %get-tuple-element.51), channel_id=1, source_target_pairs={{0,2},{1,3},{2,0},{3,1},{4,6},{5,7},{6,4},{7,5},{8,10},{9,11},{10,... | collective-permute-start | bytes 1572872 | tf_op jit(solution)/shard_map/ppermute | solution.py:49
  463.5 19.2 %collective-permute-start.22 = (f32[8,64,256]{2,1,0:T(8,128)}, f32[8,64,256]{2,1,0:T(8,128)S(1)}, u32[]{:S(2)}, u32[]{:S(2)}) collective-permute-start(f32[8,64,256]{2,1,0:T(8,128)} %collective-permute-done.7.refs_6_), channel_id=1, source_target_pairs={{0,1},{1,0},{2,3},{3,2},{4,5},{5,4},{6,7},{7,6},{8,9},{9,8},{10,11... | collective-permute-start | bytes 1572872 | tf_op jit(solution)/shard_map/ppermute | solution.py:49
  463.5 19.2 %collective-permute-start.23 = (f32[8,64,256]{2,1,0:T(8,128)S(1)}, f32[8,64,256]{2,1,0:T(8,128)S(1)}, u32[]{:S(2)}, u32[]{:S(2)}) collective-permute-start(f32[8,64,256]{2,1,0:T(8,128)S(1)} %collective-permute-done.15.refs_7_), channel_id=1, source_target_pairs={{0,1},{1,0},{2,3},{3,2},{4,5},{5,4},{6,7},{7,6},{8,9},{9,8},{10,11... | collective-permute-start | bytes 1572872 | tf_op jit(solution)/shard_map/ppermute | solution.py:49
  472.4 10.3 %collective-permute-start.24 = (f32[8,64,256]{2,1,0:T(8,128)}, f32[8,64,256]{2,1,0:T(8,128)S(1)}, u32[]{:S(2)}, u32[]{:S(2)}) collective-permute-start(f32[8,64,256]{2,1,0:T(8,128)} %collective-permute-done.16.refs_8_), channel_id=1, source_target_pairs={{0,1},{1,0},{2,3},{3,2},{4,5},{5,4},{6,7},{7,6},{8,9},{9,8},{10,11... | collective-permute-start | bytes 1572872 | tf_op jit(solution)/shard_map/ppermute | solution.py:49
  482.3 10.2 %collective-permute-start.21 = (f32[8,64,256]{2,1,0:T(8,128)S(1)}, f32[8,64,256]{2,1,0:T(8,128)S(1)}, u32[]{:S(2)}, u32[]{:S(2)}) collective-permute-start(f32[8,64,256]{2,1,0:T(8,128)S(1)} %collective-permute-done.20.refs_6_), channel_id=1, source_target_pairs={{0,1},{1,0},{2,3},{3,2},{4,5},{5,4},{6,7},{7,6},{8,9},{9,8},{10,11... | collective-permute-start | bytes 1572872 | tf_op jit(solution)/shard_map/ppermute | solution.py:49
  (28 other events, 324.2 us)

commit v9 on v8

--- a/solution.py
+++ b/solution.py
@@ -192,11 +192,7 @@
         ),
         input_output_aliases=aliases,
         compiler_params=pltpu.CompilerParams(vmem_limit_bytes=56 * 1024 * 1024),
-        cost_estimate=pl.CostEstimate(
-            flops=6 * wide_mixing.size * width * half_rows // SUBLANES,
-            bytes_accessed=4 * half_rows * width * (sum(cuts[0].shape[0] for cuts in pieces) + own),
-            transcendentals=0,
-        ),
+        cost_estimate=pl.CostEstimate(flops=0, bytes_accessed=0, transcendentals=0),
     )(*operands)
 
 
@@ -328,19 +324,19 @@
     right = (jnp.arange(order.shape[0], dtype=jnp.int32)[:, None] == long[None, :] // SUBLANES).astype(jnp.float32)
     wide_mixing = dot(left, dot(mixing, right, (1, 0), highest), (1, 0), highest)
     wide_mixing = jnp.where(wide[:, None] // vec_local == long[None, :] % SUBLANES, wide_mixing, 0.0)
-    wide_mixing, cuts[:3] = lax.optimization_barrier((wide_mixing, cuts[:3]))
-    result = rotate_part(own_pieces, wide_mixing, place, mine, 0, down_count, None)
-    result, cuts[3] = lax.optimization_barrier((result, cuts[3]))
     here = [[piece] for turn in range(rounds) for piece in on_side([held[theirs][turn]])]
     there = [[piece] for turn in range(rounds - 1) for piece in on_side([crossed[2 * turn + 1]])]
-    exchanged = [on_side([cut]) for cut in cuts]
-    early = there + [list(pair) for pair in zip(*exchanged[:3])]
-    late = there + [[piece] for piece in exchanged[3]]
-    for arrays, column, width in ((early, 0, bounds[3]), (late, 3, down_count - bounds[3])):
+    exchanged = [on_side([cut]) for cut in cuts[:2]]
+    wide_mixing, here, there, exchanged = lax.optimization_barrier((wide_mixing, here, there, exchanged))
+    result = rotate_part(own_pieces, wide_mixing, place, mine, 0, down_count, None)
+    for column in range(2):
+        result, cuts[2 + column] = lax.optimization_barrier((result, cuts[2 + column]))
+        exchanged.append(on_side([cuts[2 + column]]))
+        arrays = there + [list(pair) for pair in zip(*exchanged[2 * column : 2 * column + 2])]
         pieces = []
         for begin in range(0, len(here), side):
             pieces += here[begin : begin + side] + arrays[begin : begin + side]
-        result = rotate_part(pieces, wide_mixing, place, theirs, column, width, result)
+        result = rotate_part(pieces, wide_mixing, place, theirs, column, down_count // 2, result)
     return result
 
 

time: 507 us -> 494 us (0.974)
  waiting for transfers between devices: 262 us -> 249 us
    ppermute x18, waiting for transfers between devices: 101 us -> 89.1 us  [spread_step(): return [lax.ppermute(piece, 'vec', pairs) for piece in held]]
  transfers between devices with their start and end apart: 31 -> 31, of which waited for: 17 -> 20; matrix products, arithmetic and copies ran while one was open for 27% -> 28% of each run, Pallas kernels for 6% -> 6%
where the time goes in v9:
time: 494 us; the launch traced here: 485 us
  waiting for transfers between devices  249 us (50%)
  matrix products  109 us (22%)
  starting transfers between devices  50.1 us (10%)
  Pallas kernels  38.5 us (8%)
  local copies, waits for them, and re-layouts  28.9 us (6%)
  other arithmetic  6.67 us (1%)
    dot_general x28, matrix products, dot(): lax.dot_general(left, right, ((contract[:1], contract[1:]), ((), ())), pr...  104 us
    all_to_all x2, waiting for transfers between devices, vector_cut(): lax.all_to_all(block, 'hil', split_axis=0, concat_axis=0, tiled=True)  103 us
    ppermute x18, waiting for transfers between devices, spread_step(): return [lax.ppermute(piece, 'vec', pairs) for piece in held]  89.1 us
    all_to_all x4, waiting for transfers between devices, vector_cut(): back = lax.all_to_all(piece, 'hil', split_axis=0, concat_axis=0, tiled=True)  51 us
    pallas_call x3, Pallas kernels, rotate_part(): pl.pallas_call(functools.partial(rotate_kernel, [len(cuts) for cuts in pi...  22.6 us
    all_to_all x4, starting transfers between devices, vector_cut(): back = lax.all_to_all(piece, 'hil', split_axis=0, concat_axis=0, tiled=True)  18.5 us
    all_to_all x2, starting transfers between devices, vector_cut(): lax.all_to_all(block, 'hil', split_axis=0, concat_axis=0, tiled=True)  11.8 us
    ppermute x18, starting transfers between devices, spread_step(): return [lax.ppermute(piece, 'vec', pairs) for piece in held]  11.7 us
  transfers between devices with their start and end apart: 31, of which 20 were waited for; matrix products, arithmetic and copies ran while one was open for 28% of the time, Pallas kernels for 6%

profile of v9, /device:TPU:0, one launch (start us, length us, event | category | flops | bytes accessed | tf_op | source)
XLA Modules:
  0.0 484.9 jit_solution(3263223021127205724)
XLA Ops:
  0.0 5.0 %shard_map.73 = f32[8,128,1024]{2,1,0:T(8,128)} custom-call(s32[1]{0:T(128)} %bitcast.place_ref, f32[128,16,1024]{2,1,0:T(8,128)} %block_ref.3), custom_call_target="tpu_custom_call" | custom-call | tf_op jit(solution)/shard_map/pallas_call | solution.py:65
  5.0 7.3 %all-to-all-start = ((f32[8,128,1024]{2,1,0:T(8,128)}), f32[8,128,1024]{2,1,0:T(8,128)}, u32[]{:S(2)}, u32[]{:S(2)}) async-start(f32[8,128,1024]{2,1,0:T(8,128)} %shard_map.73), calls=%async_computation | async-start | bytes 8388608 | tf_op jit(solution)/shard_map/all_to_all | solution.py:245
  12.3 5.1 %shard_map.74 = f32[8,128,1024]{2,1,0:T(8,128)} custom-call(s32[1]{0:T(128)} %bitcast.place_ref, f32[128,16,1024]{2,1,0:T(8,128)} %block_ref.3), custom_call_target="tpu_custom_call" | custom-call | tf_op jit(solution)/shard_map/pallas_call | solution.py:65
  20.0 5.2 %convolution_add_fusion = f32[1024,1024]{1,0:T(8,128)} fusion(f32[10]{0:T(128)S(1)} %copy-done.27, s32[1024]{0:T(1024)S(1)} %shift_right_arithmetic.28), kind=kOutput, calls=%fused_computation.24 | convolution fusion | flops 126949376 | bytes 4198440 | tf_op jit(solution)/shard_map/dot_general | solution.py:250
  25.2 80.3 %all-to-all-done = f32[8,128,1024]{2,1,0:T(8,128)} async-done(((f32[8,128,1024]{2,1,0:T(8,128)}), f32[8,128,1024]{2,1,0:T(8,128)}, u32[]{:S(2)}, u32[]{:S(2)}) %all-to-all-start) | async-done | bytes 4194336 | tf_op jit(solution)/shard_map/all_to_all | solution.py:245
  105.5 4.6 all-to-all-start.1
  110.1 5.4 %select_add_fusion = f32[8,2,64,1024]{3,2,1,0:T(8,128)S(1)} fusion(f32[8,2,64]{2,1,0:T(2,128)S(1)} %get-tuple-element.116, s32[8,2,64]{2,1,0:T(2,128)S(1)} %get-tuple-element.97, f32[8,2,64]{2,1,0:T(2,128)S(1)} %get-tuple-element.115, s32[8,2,64]{2,1,0:T(2,128)S(1)} %get-tuple-element.96, f32[8,2,64]{2,1,0:T(2,128)S(1)} %get-tuple-element.114, ...), kind=kLoop, calls=%fused_computation.1 | loop fusion | flops 30408704 | bytes 4276224 | tf_op jit(solution)/shard_map/add | solution.py:32
  122.9 8.9 %fusion.120 = f32[1024,1024]{1,0:T(8,128)S(1)} fusion(f32[1024,1024]{1,0:T(8,128)} %bitcast.3, f32[1024,1024]{1,0:T(8,128)S(1)} %copy-done.1), kind=kOutput, calls=%fused_computation.219 | convolution fusion | flops 6442450944 | bytes 12582912 | tf_op jit(solution)/shard_map/dot_general | solution.py:37
  131.9 17.0 %add_multiply_fusion.1 = f32[1024,1024]{1,0:T(8,128)S(1)} fusion(f32[1024,1024]{1,0:T(8,128)S(1)} %copy-done.16, f32[1024,1024]{1,0:T(8,128)} %bitcast.3, f32[1024,1024]{1,0:T(8,128)S(1)} %fusion.120, f32[1024]{0:T(1024)S(1)} %broadcast_in_dim.182, s32[1024]{0:T(1024)S(1)} %eq.388, f32[1024]{0:T(1024)S(1)} %broadcast_in_dim.180, s32[1024]{0:T(1024)S(1)} %eq.384, ...), kind=kOutput, calls=%fused_computation.12 | convolution fusion | flops 6477053952 | bytes 16859136 | tf_op jit(solution)/shard_map/dot_general | solution.py:37
  152.0 3.6 fusion.122
  155.7 3.6 fusion.121
  159.3 5.5 %bitcast_subtract_fusion.2 = f32[512,1024]{1,0:T(8,128)} fusion(f32[8,1,64,1024]{3,2,1,0:T(8,128)S(1)} %get-tuple-element.83, f32[512,1024]{1,0:T(8,128)S(1)} %bitcast.162, f32[8,1,64,1024]{3,2,1,0:T(8,128)S(1)} %get-tuple-element.79, f32[512,1024]{1,0:T(8,128)S(1)} %fusion.122, f32[512,1024]{1,0:T(8,128)S(1)} %bitcast.163, ...), kind=kOutput, calls=%fused_computation.27 | convolution fusion | flops 3223846912 | bytes 16777216 | tf_op jit(solution)/shard_map/dot_general | solution.py:37
  164.8 14.9 %bitcast_subtract_fusion.3 = f32[512,1024]{1,0:T(8,128)} fusion(f32[8,1,64,1024]{3,2,1,0:T(8,128)S(1)} %get-tuple-element.84, f32[512,1024]{1,0:T(8,128)S(1)} %bitcast.160, f32[8,1,64,1024]{3,2,1,0:T(8,128)S(1)} %get-tuple-element.80, f32[512,1024]{1,0:T(8,128)S(1)} %fusion.121, f32[512,1024]{1,0:T(8,128)S(1)} %bitcast.165, ...), kind=kOutput, calls=%fused_computation.34 | convolution fusion | flops 3223846912 | bytes 16777216 | tf_op jit(solution)/shard_map/dot_general | solution.py:37
  179.7 22.9 %all-to-all-done.1 = f32[8,128,1024]{2,1,0:T(8,128)} async-done(((f32[8,128,1024]{2,1,0:T(8,128)}), f32[8,128,1024]{2,1,0:T(8,128)}, u32[]{:S(2)}, u32[]{:S(2)}) %all-to-all-start.1) | async-done | bytes 4194336 | tf_op jit(solution)/shard_map/all_to_all | solution.py:245
  202.6 3.6 all-to-all-start.3
  206.3 10.6 %fusion.123 = f32[1024,1024]{1,0:T(8,128)S(1)} fusion(f32[1024,1024]{1,0:T(8,128)} %bitcast.37, f32[1024,1024]{1,0:T(8,128)} %param.8), kind=kOutput, calls=%fused_computation.222 | convolution fusion | flops 6442450944 | bytes 12582912 | tf_op jit(solution)/shard_map/dot_general | solution.py:37
  216.9 17.1 %add_multiply_fusion = f32[1024,1024]{1,0:T(8,128)S(1)} fusion(f32[1024,1024]{1,0:T(8,128)S(1)} %copy-done.17, f32[1024,1024]{1,0:T(8,128)} %bitcast.37, f32[1024,1024]{1,0:T(8,128)S(1)} %fusion.123, f32[1024]{0:T(1024)S(1)} %broadcast_in_dim.182, s32[1024]{0:T(1024)S(1)} %eq.388, f32[1024]{0:T(1024)S(1)} %broadcast_in_dim.180, s32[1024]{0:T(1024)S(1)} %eq.384, ...), kind=kOutput, calls=%fused_computation | convolution fusion | flops 6477053952 | bytes 16859136 | tf_op jit(solution)/shard_map/dot_general | solution.py:37
  234.3 5.3 %fusion.114 = (f32[8,1,64,1024]{3,2,1,0:T(8,128)}, f32[8,1,64,1024]{3,2,1,0:T(8,128)S(1)}) fusion(f32[8,2,64,1024]{3,2,1,0:T(8,128)} %bitcast.40), kind=kLoop, calls=%fused_computation.213 | loop fusion | bytes 8388608 | tf_op jit(solution)/shard_map/slice | solution.py:258
  243.2 5.6 %bitcast_subtract_fusion.1 = f32[512,1024]{1,0:T(8,128)} fusion(f32[8,1,64,1024]{3,2,1,0:T(8,128)S(1)} %get-tuple-element.76, f32[512,1024]{1,0:T(8,128)S(1)} %bitcast.156, f32[8,1,64,1024]{3,2,1,0:T(8,128)S(1)} %copy-done.15, f32[512,1024]{1,0:T(8,128)S(1)} %fusion.124, f32[512,1024]{1,0:T(8,128)S(1)} %bitcast.166, f32[1024,1024]{1,0:T(8,128)S(1)} %add_multiply_fusion), kind=kOutput, calls=%fused_computation.26 | convolution fusion | flops 3223846912 | bytes 16777216 | tf_op jit(solution)/shard_map/dot_general | solution.py:37
  248.8 5.9 %all-to-all-done.3.refs_0_ = f32[8,64,1024]{2,1,0:T(8,128)S(1)} async-done(((f32[8,64,1024]{2,1,0:T(8,128)}), f32[8,64,1024]{2,1,0:T(8,128)S(1)}, u32[]{:S(2)}, u32[]{:S(2)}) %all-to-all-start.3) | async-done | bytes 2097184 | tf_op jit(solution)/shard_map/all_to_all | solution.py:284
  256.0 3.6 all-to-all-start.2
  261.2 46.0 %collective-permute-done.1.refs_2_ = f32[8,64,1024]{2,1,0:T(8,128)} collective-permute-done((f32[8,64,1024]{2,1,0:T(8,128)}, f32[8,64,1024]{2,1,0:T(8,128)}, u32[]{:S(2)}, u32[]{:S(2)}) %collective-permute-start.1) | collective-permute-done | bytes 2097184 | tf_op jit(solution)/shard_map/ppermute | solution.py:49
  308.1 5.2 %all-to-all-start.5 = ((f32[8,64,1024]{2,1,0:T(8,128)}), f32[8,64,1024]{2,1,0:T(8,128)}, u32[]{:S(2)}, u32[]{:S(2)}) async-start(f32[8,64,1024]{2,1,0:T(8,128)} %bitcast.170), calls=%async_computation.5 | async-start | bytes 4194304 | tf_op jit(solution)/shard_map/all_to_all | solution.py:284
  316.7 3.7 fusion.125
  320.4 6.5 %bitcast_subtract_fusion = f32[512,1024]{1,0:T(8,128)} fusion(f32[8,1,64,1024]{3,2,1,0:T(8,128)} %get-tuple-element.75, f32[512,1024]{1,0:T(8,128)S(1)} %bitcast.158, f32[8,1,64,1024]{3,2,1,0:T(8,128)S(1)} %copy-done.11, f32[512,1024]{1,0:T(8,128)S(1)} %fusion.125, f32[512,1024]{1,0:T(8,128)S(1)} %bitcast.164, f32[1024,1024]{1,0:T(8,128)S(1)} %copy-done.5), kind=kOutput, calls=%fused_computation.25 | convolution fusion | flops 3223846912 | bytes 16777216 | tf_op jit(solution)/shard_map/dot_general | solution.py:37
  326.9 32.5 %collective-permute-done.3.refs_2_ = f32[8,64,1024]{2,1,0:T(8,128)S(1)} collective-permute-done((f32[8,64,1024]{2,1,0:T(8,128)S(1)}, f32[8,64,1024]{2,1,0:T(8,128)S(1)}, u32[]{:S(2)}, u32[]{:S(2)}) %collective-permute-start.3) | collective-permute-done | bytes 2097184 | tf_op jit(solution)/shard_map/ppermute | solution.py:49
  360.7 6.1 %all-to-all-start.4 = ((f32[8,64,1024]{2,1,0:T(8,128)}), f32[8,64,1024]{2,1,0:T(8,128)}, u32[]{:S(2)}, u32[]{:S(2)}) async-start(f32[8,64,1024]{2,1,0:T(8,128)} %bitcast.171), calls=%async_computation.4 | async-start | bytes 4194304 | tf_op jit(solution)/shard_map/all_to_all | solution.py:284
  368.9 44.3 %all-to-all-done.4.refs_4_ = f32[8,64,1024]{2,1,0:T(8,128)} async-done(((f32[8,64,1024]{2,1,0:T(8,128)}), f32[8,64,1024]{2,1,0:T(8,128)}, u32[]{:S(2)}, u32[]{:S(2)}) %all-to-all-start.4) | async-done | bytes 2097184 | tf_op jit(solution)/shard_map/all_to_all | solution.py:284
  420.7 5.9 %shard_map.75 = (f32[256,256]{1,0:T(8,128)S(1)}, f32[256,256]{1,0:T(8,128)S(1)}) custom-call(s32[1]{0:T(128)} %bitcast.2.start_ref, f32[8,64,1024]{2,1,0:T(8,128)S(1)} %all-to-all-done.2.refs_0_, f32[8,64,1024]{2,1,0:T(8,128)} %collective-permute-done.refs_1_, f32[8,64,1024]{2,1,0:T(8,128)} %collective-permute-done.1.refs_2_, ...), custom_call_target="tpu_custom_call" | custom-call | flops 2147483648 | bytes 8388608 | tf_op jit(solution)/shard_map/pallas_call | solution.py:121
  458.1 9.8 %shard_map.76.refs_10_ = f32[128,16,1024]{2,1,0:T(8,128)} custom-call(s32[1]{0:T(128)} %bitcast.place_ref, f32[128,512]{1,0:T(8,128)} %convolution_select_fusion.mix_ref, f32[8,64,1024]{2,1,0:T(8,128)} %copy-done, f32[8,64,1024]{2,1,0:T(8,128)} %collective-permute-done.refs_1_, f32[8,64,1024]{2,1,0:T(8,128)} %collective-permute-done.1.refs_2_, ...), custom_call_target="tpu_custom_call" | custom-call | tf_op jit(solution)/shard_map/pallas_call | solution.py:181
  468.0 6.4 %shard_map.77.refs_10_ = f32[128,16,1024]{2,1,0:T(8,128)} custom-call(s32[1]{0:T(128)} %bitcast.place_ref, f32[128,512]{1,0:T(8,128)} %convolution_select_fusion.mix_ref, f32[8,64,1024]{2,1,0:T(8,128)} %copy-done.6, f32[8,64,1024]{2,1,0:T(8,128)} %collective-permute-done.16.refs_1_, f32[8,64,1024]{2,1,0:T(8,128)} %copy-done.18, ...), custom_call_target="tpu_custom_call", output_to_operand_aliasing={{}: (12, {})} | custom-call | tf_op jit(solution)/shard_map/pallas_call | solution.py:181
  478.1 6.3 %shard_map.78 = f32[128,16,1024]{2,1,0:T(8,128)} custom-call(s32[1]{0:T(128)} %bitcast.place_ref, f32[128,512]{1,0:T(8,128)} %convolution_select_fusion.mix_ref, f32[8,64,1024]{2,1,0:T(8,128)} %copy-done.6, f32[8,64,1024]{2,1,0:T(8,128)} %collective-permute-done.16.refs_1_, f32[8,64,1024]{2,1,0:T(8,128)} %copy-done.18, ...), custom_call_target="tpu_custom_call", output_to_operand_aliasing={{}: (12, {})} | custom-call | tf_op jit(solution)/shard_map/pallas_call | solution.py:181
  (194 shorter events, 69.1 us)
Async XLA Ops:
  5.0 100.5 %all-to-all-start = ((f32[8,128,1024]{2,1,0:T(8,128)}), f32[8,128,1024]{2,1,0:T(8,128)}, u32[]{:S(2)}, u32[]{:S(2)}) async-start(f32[8,128,1024]{2,1,0:T(8,128)} %shard_map.73), calls=%async_computation | async-start | bytes 8388608 | tf_op jit(solution)/shard_map/all_to_all | solution.py:245
  105.5 97.1 %all-to-all-start.1 = ((f32[8,128,1024]{2,1,0:T(8,128)}), f32[8,128,1024]{2,1,0:T(8,128)}, u32[]{:S(2)}, u32[]{:S(2)}) async-start(f32[8,128,1024]{2,1,0:T(8,128)} %shard_map.74), calls=%async_computation.1 | async-start | bytes 8388608 | tf_op jit(solution)/shard_map/all_to_all | solution.py:245
  202.6 52.0 %all-to-all-start.3 = ((f32[8,64,1024]{2,1,0:T(8,128)}), f32[8,64,1024]{2,1,0:T(8,128)S(1)}, u32[]{:S(2)}, u32[]{:S(2)}) async-start(f32[8,64,1024]{2,1,0:T(8,128)} %bitcast.169), calls=%async_computation.3 | async-start | bytes 4194304 | tf_op jit(solution)/shard_map/all_to_all | solution.py:284
  256.0 52.1 %all-to-all-start.2 = ((f32[8,64,1024]{2,1,0:T(8,128)}), f32[8,64,1024]{2,1,0:T(8,128)S(1)}, u32[]{:S(2)}, u32[]{:S(2)}) async-start(f32[8,64,1024]{2,1,0:T(8,128)} %bitcast.168), calls=%async_computation.2 | async-start | bytes 4194304 | tf_op jit(solution)/shard_map/all_to_all | solution.py:284
  259.7 47.6 %collective-permute-start.1 = (f32[8,64,1024]{2,1,0:T(8,128)}, f32[8,64,1024]{2,1,0:T(8,128)}, u32[]{:S(2)}, u32[]{:S(2)}) collective-permute-start(f32[8,64,1024]{2,1,0:T(8,128)} %copy-done.6), channel_id=1, source_target_pairs={{0,2},{1,3},{2,0},{3,1},{4,6},{5,7},{6,4},{7,5},{8,10},{9,11},{10,... | collective-permute-start | bytes 6291464 | tf_op jit(solution)/shard_map/ppermute | solution.py:49
  308.1 112.6 %copy-start = (f32[8,64,1024]{2,1,0:T(8,128)}, f32[8,64,1024]{2,1,0:T(8,128)S(1)}, u32[]{:S(2)}) copy-start(f32[8,64,1024]{2,1,0:T(8,128)S(1)} %all-to-all-done.2.refs_0_) | copy-start | bytes 6291460
  308.1 52.7 %all-to-all-start.5 = ((f32[8,64,1024]{2,1,0:T(8,128)}), f32[8,64,1024]{2,1,0:T(8,128)}, u32[]{:S(2)}, u32[]{:S(2)}) async-start(f32[8,64,1024]{2,1,0:T(8,128)} %bitcast.170), calls=%async_computation.5 | async-start | bytes 4194304 | tf_op jit(solution)/shard_map/all_to_all | solution.py:284
  313.3 46.1 %collective-permute-start.3 = (f32[8,64,1024]{2,1,0:T(8,128)S(1)}, f32[8,64,1024]{2,1,0:T(8,128)S(1)}, u32[]{:S(2)}, u32[]{:S(2)}) collective-permute-start(f32[8,64,1024]{2,1,0:T(8,128)S(1)} %all-to-all-done.2.refs_0_), channel_id=1, source_target_pairs={{0,2},{1,3},{2,0},{3,1},{4,6},{5,7},{6,4},{7,5},{8,10},{9,11},{10,... | collective-permute-start | bytes 6291464 | tf_op jit(solution)/shard_map/ppermute | solution.py:49
  360.7 52.4 %all-to-all-start.4 = ((f32[8,64,1024]{2,1,0:T(8,128)}), f32[8,64,1024]{2,1,0:T(8,128)}, u32[]{:S(2)}, u32[]{:S(2)}) async-start(f32[8,64,1024]{2,1,0:T(8,128)} %bitcast.171), calls=%async_computation.4 | async-start | bytes 4194304 | tf_op jit(solution)/shard_map/all_to_all | solution.py:284
  366.8 46.4 %collective-permute-start.5 = (f32[8,64,1024]{2,1,0:T(8,128)}, f32[8,64,1024]{2,1,0:T(8,128)}, u32[]{:S(2)}, u32[]{:S(2)}) collective-permute-start(f32[8,64,1024]{2,1,0:T(8,128)} %all-to-all-done.5.refs_4_), channel_id=1, source_target_pairs={{0,2},{1,3},{2,0},{3,1},{4,6},{5,7},{6,4},{7,5},{8,10},{9,11},{10,... | collective-permute-start | bytes 6291464 | tf_op jit(solution)/shard_map/ppermute | solution.py:49
  368.4 49.1 %collective-permute-start = (f32[8,64,1024]{2,1,0:T(8,128)S(1)}, f32[8,64,1024]{2,1,0:T(8,128)}, u32[]{:S(2)}, u32[]{:S(2)}) collective-permute-start(f32[8,64,1024]{2,1,0:T(8,128)S(1)} %all-to-all-done.2.refs_0_), channel_id=1, source_target_pairs={{0,1},{1,0},{2,3},{3,2},{4,5},{5,4},{6,7},{7,6},{8,9},{9,8},{10,11... | collective-permute-start | bytes 6291464 | tf_op jit(solution)/shard_map/ppermute | solution.py:49
  368.4 49.1 %collective-permute-start.2 = (f32[8,64,1024]{2,1,0:T(8,128)}, f32[8,64,1024]{2,1,0:T(8,128)}, u32[]{:S(2)}, u32[]{:S(2)}) collective-permute-start(f32[8,64,1024]{2,1,0:T(8,128)} %collective-permute-done.1.refs_2_), channel_id=1, source_target_pairs={{0,1},{1,0},{2,3},{3,2},{4,5},{5,4},{6,7},{7,6},{8,9},{9,8},{10,11... | collective-permute-start | bytes 6291464 | tf_op jit(solution)/shard_map/ppermute | solution.py:49
  413.2 4.5 collective-permute-start.4
  413.2 7.5 %collective-permute-start.6 = (f32[8,64,1024]{2,1,0:T(8,128)}, f32[8,64,1024]{2,1,0:T(8,128)}, u32[]{:S(2)}, u32[]{:S(2)}) collective-permute-start(f32[8,64,1024]{2,1,0:T(8,128)} %collective-permute-done.5.refs_6_), channel_id=1, source_target_pairs={{0,1},{1,0},{2,3},{3,2},{4,5},{5,4},{6,7},{7,6},{8,9},{9,8},{10,11... | collective-permute-start | bytes 6291464 | tf_op jit(solution)/shard_map/ppermute | solution.py:49
  416.0 14.2 %collective-permute-start.7 = (f32[8,64,256]{2,1,0:T(8,128)}, f32[8,64,256]{2,1,0:T(8,128)}, u32[]{:S(2)}, u32[]{:S(2)}) collective-permute-start(f32[8,64,256]{2,1,0:T(8,128)} %slice.225), channel_id=1, source_target_pairs={{0,2},{1,3},{2,0},{3,1},{4,6},{5,7},{6,4},{7,5},{8,10},{9,11},{10,... | collective-permute-start | bytes 1572872 | tf_op jit(solution)/shard_map/ppermute | solution.py:49
  430.2 4.7 collective-permute-start.10
  430.4 4.4 collective-permute-start.8
  431.8 3.9 collective-permute-start.9
  435.7 12.7 %collective-permute-start.15 = (f32[8,64,256]{2,1,0:T(8,128)S(1)}, f32[8,64,256]{2,1,0:T(8,128)S(1)}, u32[]{:S(2)}, u32[]{:S(2)}) collective-permute-start(f32[8,64,256]{2,1,0:T(8,128)S(1)} %get-tuple-element.53), channel_id=1, source_target_pairs={{0,2},{1,3},{2,0},{3,1},{4,6},{5,7},{6,4},{7,5},{8,10},{9,11},{10,... | collective-permute-start | bytes 1572872 | tf_op jit(solution)/shard_map/ppermute | solution.py:49
  436.4 3.9 collective-permute-start.11
  437.6 3.9 collective-permute-start.12
  438.6 4.8 collective-permute-start.13
  443.4 4.9 %collective-permute-start.14 = (f32[64,64]{1,0:T(8,128)S(1)}, f32[64,64]{1,0:T(8,128)S(1)}, u32[]{:S(2)}, u32[]{:S(2)}) collective-permute-start(f32[64,64]{1,0:T(8,128)S(1)} %add_add_fusion), channel_id=1, source_target_pairs={{0,16},{4,20},{8,24},{12,28},{16,0},{20,4},{24,8},{28,12},{1,17},{... | collective-permute-start | bytes 49160 | tf_op jit(solution)/shard_map/ppermute | solution.py:208
  446.1 7.1 %collective-permute-start.16 = (f32[8,64,1024]{2,1,0:T(8,128)S(1)}, f32[8,64,1024]{2,1,0:T(8,128)}, u32[]{:S(2)}, u32[]{:S(2)}) collective-permute-start(f32[8,64,1024]{2,1,0:T(8,128)S(1)} %copy-done.7), channel_id=1, source_target_pairs={{0,1},{1,0},{2,3},{3,2},{4,5},{5,4},{6,7},{7,6},{8,9},{9,8},{10,11... | collective-permute-start | bytes 6291464 | tf_op jit(solution)/shard_map/ppermute | solution.py:49
  446.1 8.1 %collective-permute-start.18 = (f32[8,64,1024]{2,1,0:T(8,128)}, f32[8,64,1024]{2,1,0:T(8,128)}, u32[]{:S(2)}, u32[]{:S(2)}) collective-permute-start(f32[8,64,1024]{2,1,0:T(8,128)} %copy-done.18), channel_id=1, source_target_pairs={{0,1},{1,0},{2,3},{3,2},{4,5},{5,4},{6,7},{7,6},{8,9},{9,8},{10,11... | collective-permute-start | bytes 6291464 | tf_op jit(solution)/shard_map/ppermute | solution.py:49
  446.6 10.0 %collective-permute-start.17 = (f32[8,64,1024]{2,1,0:T(8,128)}, f32[8,64,1024]{2,1,0:T(8,128)}, u32[]{:S(2)}, u32[]{:S(2)}) collective-permute-start(f32[8,64,1024]{2,1,0:T(8,128)} %all-to-all-done.5.refs_4_), channel_id=1, source_target_pairs={{0,1},{1,0},{2,3},{3,2},{4,5},{5,4},{6,7},{7,6},{8,9},{9,8},{10,11... | collective-permute-start | bytes 6291464 | tf_op jit(solution)/shard_map/ppermute | solution.py:49
  448.3 9.8 %collective-permute-start.19 = (f32[8,64,256]{2,1,0:T(8,128)}, f32[8,64,256]{2,1,0:T(8,128)}, u32[]{:S(2)}, u32[]{:S(2)}) collective-permute-start(f32[8,64,256]{2,1,0:T(8,128)} %collective-permute-done.7.refs_6_), channel_id=1, source_target_pairs={{0,1},{1,0},{2,3},{3,2},{4,5},{5,4},{6,7},{7,6},{8,9},{9,8},{10,11... | collective-permute-start | bytes 1572872 | tf_op jit(solution)/shard_map/ppermute | solution.py:49
  448.5 19.5 %collective-permute-start.21 = (f32[8,64,256]{2,1,0:T(8,128)}, f32[8,64,256]{2,1,0:T(8,128)S(1)}, u32[]{:S(2)}, u32[]{:S(2)}) collective-permute-start(f32[8,64,256]{2,1,0:T(8,128)} %get-tuple-element.65), channel_id=1, source_target_pairs={{0,2},{1,3},{2,0},{3,1},{4,6},{5,7},{6,4},{7,5},{8,10},{9,11},{10,... | collective-permute-start | bytes 1572872 | tf_op jit(solution)/shard_map/ppermute | solution.py:49
  453.2 21.3 %collective-permute-start.22 = (f32[8,64,256]{2,1,0:T(8,128)}, f32[8,64,256]{2,1,0:T(8,128)S(1)}, u32[]{:S(2)}, u32[]{:S(2)}) collective-permute-start(f32[8,64,256]{2,1,0:T(8,128)} %get-tuple-element.72), channel_id=1, source_target_pairs={{0,2},{1,3},{2,0},{3,1},{4,6},{5,7},{6,4},{7,5},{8,10},{9,11},{10,... | collective-permute-start | bytes 1572872 | tf_op jit(solution)/shard_map/ppermute | solution.py:49
  454.2 3.9 collective-permute-start.20
  474.5 2.0 collective-permute-start.24
  474.7 2.5 collective-permute-start.23
  (28 other events, 318.8 us)

commit v10 on v9

--- a/solution.py
+++ b/solution.py
@@ -191,7 +191,7 @@
             scratch_shapes=[pltpu.VMEM((2 * wide_mixing.shape[0], wide_mixing.shape[1]), jnp.bfloat16)],
         ),
         input_output_aliases=aliases,
-        compiler_params=pltpu.CompilerParams(vmem_limit_bytes=56 * 1024 * 1024),
+        compiler_params=pltpu.CompilerParams(vmem_limit_bytes=30 * 1024 * 1024),
         cost_estimate=pl.CostEstimate(flops=0, bytes_accessed=0, transcendentals=0),
     )(*operands)
 

time: 494 us -> 490 us (level)
  transfers between devices with their start and end apart: 31 -> 31, of which waited for: 20 -> 22; matrix products, arithmetic and copies ran while one was open for 28% -> 28% of each run, Pallas kernels for 6% -> 5%
where the time goes in v10:
time: 490 us; the launch traced here: 481 us
  waiting for transfers between devices  251 us (51%)
  matrix products  109 us (22%)
  starting transfers between devices  49.4 us (10%)
  Pallas kernels  36.6 us (7%)
  local copies, waits for them, and re-layouts  25.4 us (5%)
  other arithmetic  7.59 us (2%)
    dot_general x28, matrix products, dot(): lax.dot_general(left, right, ((contract[:1], contract[1:]), ((), ())), pr...  104 us
    all_to_all x2, waiting for transfers between devices, vector_cut(): lax.all_to_all(block, 'hil', split_axis=0, concat_axis=0, tiled=True)  103 us
    ppermute x18, waiting for transfers between devices, spread_step(): return [lax.ppermute(piece, 'vec', pairs) for piece in held]  89.8 us
    all_to_all x4, waiting for transfers between devices, vector_cut(): back = lax.all_to_all(piece, 'hil', split_axis=0, concat_axis=0, tiled=True)  52.9 us
    pallas_call x3, Pallas kernels, rotate_part(): pl.pallas_call(functools.partial(rotate_kernel, [len(cuts) for cuts in pi...  20.5 us
    all_to_all x4, starting transfers between devices, vector_cut(): back = lax.all_to_all(piece, 'hil', split_axis=0, concat_axis=0, tiled=True)  18.1 us
    all_to_all x2, starting transfers between devices, vector_cut(): lax.all_to_all(block, 'hil', split_axis=0, concat_axis=0, tiled=True)  11.8 us
    slice x7, local copies, waits for them, and re-layouts, rows(): values.reshape(hil_parts, 2, half_rows, -1)[:, half]  11.5 us
  transfers between devices with their start and end apart: 31, of which 22 were waited for; matrix products, arithmetic and copies ran while one was open for 28% of the time, Pallas kernels for 5%

profile of v10, /device:TPU:0, one launch (start us, length us, event | category | flops | bytes accessed | tf_op | source)
XLA Modules:
  0.0 480.9 jit_solution(1032960182692119463)
XLA Ops:
  0.0 5.0 %shard_map.73 = f32[8,128,1024]{2,1,0:T(8,128)} custom-call(s32[1]{0:T(128)} %bitcast.place_ref, f32[128,16,1024]{2,1,0:T(8,128)} %block_ref.3), custom_call_target="tpu_custom_call" | custom-call | tf_op jit(solution)/shard_map/pallas_call | solution.py:65
  5.0 7.3 %all-to-all-start = ((f32[8,128,1024]{2,1,0:T(8,128)}), f32[8,128,1024]{2,1,0:T(8,128)}, u32[]{:S(2)}, u32[]{:S(2)}) async-start(f32[8,128,1024]{2,1,0:T(8,128)} %shard_map.73), calls=%async_computation | async-start | bytes 8388608 | tf_op jit(solution)/shard_map/all_to_all | solution.py:245
  12.3 5.1 %shard_map.74 = f32[8,128,1024]{2,1,0:T(8,128)} custom-call(s32[1]{0:T(128)} %bitcast.place_ref, f32[128,16,1024]{2,1,0:T(8,128)} %block_ref.3), custom_call_target="tpu_custom_call" | custom-call | tf_op jit(solution)/shard_map/pallas_call | solution.py:65
  20.1 5.2 %convolution_add_fusion = f32[1024,1024]{1,0:T(8,128)} fusion(f32[10]{0:T(128)S(1)} %copy-done.21, s32[1024]{0:T(1024)S(1)} %shift_right_arithmetic.28), kind=kOutput, calls=%fused_computation.24 | convolution fusion | flops 126949376 | bytes 4198440 | tf_op jit(solution)/shard_map/dot_general | solution.py:250
  25.3 80.2 %all-to-all-done = f32[8,128,1024]{2,1,0:T(8,128)} async-done(((f32[8,128,1024]{2,1,0:T(8,128)}), f32[8,128,1024]{2,1,0:T(8,128)}, u32[]{:S(2)}, u32[]{:S(2)}) %all-to-all-start) | async-done | bytes 4194336 | tf_op jit(solution)/shard_map/all_to_all | solution.py:245
  105.5 4.6 all-to-all-start.1
  110.1 5.4 %select_add_fusion = f32[8,2,64,1024]{3,2,1,0:T(8,128)S(1)} fusion(f32[8,2,64]{2,1,0:T(2,128)S(1)} %get-tuple-element.116, s32[8,2,64]{2,1,0:T(2,128)S(1)} %get-tuple-element.97, f32[8,2,64]{2,1,0:T(2,128)S(1)} %get-tuple-element.115, s32[8,2,64]{2,1,0:T(2,128)S(1)} %get-tuple-element.96, f32[8,2,64]{2,1,0:T(2,128)S(1)} %get-tuple-element.114, ...), kind=kLoop, calls=%fused_computation.1 | loop fusion | flops 30408704 | bytes 4276224 | tf_op jit(solution)/shard_map/add | solution.py:32
  122.9 9.1 %fusion.120 = f32[1024,1024]{1,0:T(8,128)S(1)} fusion(f32[1024,1024]{1,0:T(8,128)} %bitcast.3, f32[1024,1024]{1,0:T(8,128)S(1)} %copy-done.4), kind=kOutput, calls=%fused_computation.219 | convolution fusion | flops 6442450944 | bytes 12582912 | tf_op jit(solution)/shard_map/dot_general | solution.py:37
  132.1 17.0 %add_multiply_fusion.1 = f32[1024,1024]{1,0:T(8,128)S(1)} fusion(f32[1024,1024]{1,0:T(8,128)S(1)} %copy-done.17, f32[1024,1024]{1,0:T(8,128)} %bitcast.3, f32[1024,1024]{1,0:T(8,128)S(1)} %fusion.120, f32[1024]{0:T(1024)S(1)} %broadcast_in_dim.182, s32[1024]{0:T(1024)S(1)} %eq.388, f32[1024]{0:T(1024)S(1)} %broadcast_in_dim.180, s32[1024]{0:T(1024)S(1)} %eq.384, ...), kind=kOutput, calls=%fused_computation.12 | convolution fusion | flops 6477053952 | bytes 16859136 | tf_op jit(solution)/shard_map/dot_general | solution.py:37
  152.4 3.7 fusion.122
  156.1 3.7 fusion.121
  159.9 5.5 %bitcast_subtract_fusion.2 = f32[512,1024]{1,0:T(8,128)} fusion(f32[8,1,64,1024]{3,2,1,0:T(8,128)S(1)} %get-tuple-element.83, f32[512,1024]{1,0:T(8,128)S(1)} %bitcast.162, f32[8,1,64,1024]{3,2,1,0:T(8,128)S(1)} %get-tuple-element.79, f32[512,1024]{1,0:T(8,128)S(1)} %fusion.122, f32[512,1024]{1,0:T(8,128)S(1)} %bitcast.163, ...), kind=kOutput, calls=%fused_computation.27 | convolution fusion | flops 3223846912 | bytes 16777216 | tf_op jit(solution)/shard_map/dot_general | solution.py:37
  165.4 14.9 %bitcast_subtract_fusion.3 = f32[512,1024]{1,0:T(8,128)} fusion(f32[8,1,64,1024]{3,2,1,0:T(8,128)S(1)} %get-tuple-element.84, f32[512,1024]{1,0:T(8,128)S(1)} %bitcast.160, f32[8,1,64,1024]{3,2,1,0:T(8,128)S(1)} %get-tuple-element.80, f32[512,1024]{1,0:T(8,128)S(1)} %fusion.121, f32[512,1024]{1,0:T(8,128)S(1)} %bitcast.165, ...), kind=kOutput, calls=%fused_computation.34 | convolution fusion | flops 3223846912 | bytes 16777216 | tf_op jit(solution)/shard_map/dot_general | solution.py:37
  180.3 22.4 %all-to-all-done.1 = f32[8,128,1024]{2,1,0:T(8,128)} async-done(((f32[8,128,1024]{2,1,0:T(8,128)}), f32[8,128,1024]{2,1,0:T(8,128)}, u32[]{:S(2)}, u32[]{:S(2)}) %all-to-all-start.1) | async-done | bytes 4194336 | tf_op jit(solution)/shard_map/all_to_all | solution.py:245
  202.6 3.6 all-to-all-start.3
  206.3 10.6 %fusion.123 = f32[1024,1024]{1,0:T(8,128)S(1)} fusion(f32[1024,1024]{1,0:T(8,128)} %bitcast.37, f32[1024,1024]{1,0:T(8,128)} %param.8), kind=kOutput, calls=%fused_computation.222 | convolution fusion | flops 6442450944 | bytes 12582912 | tf_op jit(solution)/shard_map/dot_general | solution.py:37
  216.9 17.0 %add_multiply_fusion = f32[1024,1024]{1,0:T(8,128)S(1)} fusion(f32[1024,1024]{1,0:T(8,128)S(1)} %copy-done.18, f32[1024,1024]{1,0:T(8,128)} %bitcast.37, f32[1024,1024]{1,0:T(8,128)S(1)} %fusion.123, f32[1024]{0:T(1024)S(1)} %broadcast_in_dim.182, s32[1024]{0:T(1024)S(1)} %eq.388, f32[1024]{0:T(1024)S(1)} %broadcast_in_dim.180, s32[1024]{0:T(1024)S(1)} %eq.384, ...), kind=kOutput, calls=%fused_computation | convolution fusion | flops 6477053952 | bytes 16859136 | tf_op jit(solution)/shard_map/dot_general | solution.py:37
  234.3 5.4 %fusion.114 = (f32[8,1,64,1024]{3,2,1,0:T(8,128)}, f32[8,1,64,1024]{3,2,1,0:T(8,128)S(1)}) fusion(f32[8,2,64,1024]{3,2,1,0:T(8,128)} %bitcast.40), kind=kLoop, calls=%fused_computation.213 | loop fusion | bytes 8388608 | tf_op jit(solution)/shard_map/slice | solution.py:258
  243.2 5.5 %bitcast_subtract_fusion.1 = f32[512,1024]{1,0:T(8,128)} fusion(f32[8,1,64,1024]{3,2,1,0:T(8,128)S(1)} %get-tuple-element.76, f32[512,1024]{1,0:T(8,128)S(1)} %bitcast.156, f32[8,1,64,1024]{3,2,1,0:T(8,128)S(1)} %copy-done.16, f32[512,1024]{1,0:T(8,128)S(1)} %fusion.124, f32[512,1024]{1,0:T(8,128)S(1)} %bitcast.166, f32[1024,1024]{1,0:T(8,128)S(1)} %add_multiply_fusion), kind=kOutput, calls=%fused_computation.26 | convolution fusion | flops 3223846912 | bytes 16777216 | tf_op jit(solution)/shard_map/dot_general | solution.py:37
  248.7 6.0 %all-to-all-done.3.refs_0_ = f32[8,64,1024]{2,1,0:T(8,128)S(1)} async-done(((f32[8,64,1024]{2,1,0:T(8,128)}), f32[8,64,1024]{2,1,0:T(8,128)S(1)}, u32[]{:S(2)}, u32[]{:S(2)}) %all-to-all-start.3) | async-done | bytes 2097184 | tf_op jit(solution)/shard_map/all_to_all | solution.py:284
  254.7 4.3 all-to-all-start.2
  260.6 45.1 %collective-permute-done.1.refs_2_ = f32[8,64,1024]{2,1,0:T(8,128)} collective-permute-done((f32[8,64,1024]{2,1,0:T(8,128)S(1)}, f32[8,64,1024]{2,1,0:T(8,128)}, u32[]{:S(2)}, u32[]{:S(2)}) %collective-permute-start.1) | collective-permute-done | bytes 2097184 | tf_op jit(solution)/shard_map/ppermute | solution.py:49
  306.9 4.9 %all-to-all-start.5 = ((f32[8,64,1024]{2,1,0:T(8,128)}), f32[8,64,1024]{2,1,0:T(8,128)}, u32[]{:S(2)}, u32[]{:S(2)}) async-start(f32[8,64,1024]{2,1,0:T(8,128)} %bitcast.170), calls=%async_computation.5 | async-start | bytes 4194304 | tf_op jit(solution)/shard_map/all_to_all | solution.py:284
  315.1 3.7 fusion.125
  318.9 6.5 %bitcast_subtract_fusion = f32[512,1024]{1,0:T(8,128)} fusion(f32[8,1,64,1024]{3,2,1,0:T(8,128)} %get-tuple-element.75, f32[512,1024]{1,0:T(8,128)S(1)} %bitcast.158, f32[8,1,64,1024]{3,2,1,0:T(8,128)S(1)} %copy-done.12, f32[512,1024]{1,0:T(8,128)S(1)} %fusion.125, f32[512,1024]{1,0:T(8,128)S(1)} %bitcast.164, f32[1024,1024]{1,0:T(8,128)S(1)} %copy-done.8), kind=kOutput, calls=%fused_computation.25 | convolution fusion | flops 3223846912 | bytes 16777216 | tf_op jit(solution)/shard_map/dot_general | solution.py:37
  325.3 33.1 %collective-permute-done.3.refs_2_ = f32[8,64,1024]{2,1,0:T(8,128)} collective-permute-done((f32[8,64,1024]{2,1,0:T(8,128)}, f32[8,64,1024]{2,1,0:T(8,128)}, u32[]{:S(2)}, u32[]{:S(2)}) %collective-permute-start.3) | collective-permute-done | bytes 2097184 | tf_op jit(solution)/shard_map/ppermute | solution.py:49
  359.3 5.3 %all-to-all-start.4 = ((f32[8,64,1024]{2,1,0:T(8,128)}), f32[8,64,1024]{2,1,0:T(8,128)S(1)}, u32[]{:S(2)}, u32[]{:S(2)}) async-start(f32[8,64,1024]{2,1,0:T(8,128)} %bitcast.171), calls=%async_computation.4 | async-start | bytes 4194304 | tf_op jit(solution)/shard_map/all_to_all | solution.py:284
  366.6 45.0 %all-to-all-done.4.refs_4_ = f32[8,64,1024]{2,1,0:T(8,128)S(1)} async-done(((f32[8,64,1024]{2,1,0:T(8,128)}), f32[8,64,1024]{2,1,0:T(8,128)S(1)}, u32[]{:S(2)}, u32[]{:S(2)}) %all-to-all-start.4) | async-done | bytes 2097184 | tf_op jit(solution)/shard_map/all_to_all | solution.py:284
  419.1 6.0 %shard_map.75 = (f32[256,256]{1,0:T(8,128)S(1)}, f32[256,256]{1,0:T(8,128)S(1)}) custom-call(s32[1]{0:T(128)} %bitcast.2.start_ref, f32[8,64,1024]{2,1,0:T(8,128)} %all-to-all-done.2.refs_0_, f32[8,64,1024]{2,1,0:T(8,128)} %collective-permute-done.refs_1_, f32[8,64,1024]{2,1,0:T(8,128)} %collective-permute-done.1.refs_2_, ...), custom_call_target="tpu_custom_call" | custom-call | flops 2147483648 | bytes 8388608 | tf_op jit(solution)/shard_map/pallas_call | solution.py:121
  455.5 9.1 %shard_map.76.refs_10_ = f32[128,16,1024]{2,1,0:T(8,128)} custom-call(s32[1]{0:T(128)} %bitcast.place_ref, f32[128,512]{1,0:T(8,128)S(1)} %convolution_select_fusion.mix_ref, f32[8,64,1024]{2,1,0:T(8,128)} %all-to-all-done.2.refs_0_, f32[8,64,1024]{2,1,0:T(8,128)} %collective-permute-done.refs_1_, f32[8,64,1024]{2,1,0:T(8,128)} %collective-permute-done.1.refs_2_, ...), custom_call_target="tpu_custom_call" | custom-call | tf_op jit(solution)/shard_map/pallas_call | solution.py:181
  464.7 5.7 %shard_map.77.refs_10_ = f32[128,16,1024]{2,1,0:T(8,128)} custom-call(s32[1]{0:T(128)} %bitcast.place_ref, f32[128,512]{1,0:T(8,128)S(1)} %convolution_select_fusion.mix_ref, f32[8,64,1024]{2,1,0:T(8,128)S(1)} %copy-done.3, f32[8,64,1024]{2,1,0:T(8,128)} %collective-permute-done.16.refs_1_, ...), custom_call_target="tpu_custom_call", output_to_operand_aliasing={{}: (12, {})} | custom-call | tf_op jit(solution)/shard_map/pallas_call | solution.py:181
  474.8 5.7 %shard_map.78 = f32[128,16,1024]{2,1,0:T(8,128)} custom-call(s32[1]{0:T(128)} %bitcast.place_ref, f32[128,512]{1,0:T(8,128)S(1)} %convolution_select_fusion.mix_ref, f32[8,64,1024]{2,1,0:T(8,128)S(1)} %copy-done.3, f32[8,64,1024]{2,1,0:T(8,128)} %collective-permute-done.16.refs_1_, ...), custom_call_target="tpu_custom_call", output_to_operand_aliasing={{}: (12, {})} | custom-call | tf_op jit(solution)/shard_map/pallas_call | solution.py:181
  (182 shorter events, 67.4 us)
Async XLA Ops:
  5.0 100.5 %all-to-all-start = ((f32[8,128,1024]{2,1,0:T(8,128)}), f32[8,128,1024]{2,1,0:T(8,128)}, u32[]{:S(2)}, u32[]{:S(2)}) async-start(f32[8,128,1024]{2,1,0:T(8,128)} %shard_map.73), calls=%async_computation | async-start | bytes 8388608 | tf_op jit(solution)/shard_map/all_to_all | solution.py:245
  105.5 97.1 %all-to-all-start.1 = ((f32[8,128,1024]{2,1,0:T(8,128)}), f32[8,128,1024]{2,1,0:T(8,128)}, u32[]{:S(2)}, u32[]{:S(2)}) async-start(f32[8,128,1024]{2,1,0:T(8,128)} %shard_map.74), calls=%async_computation.1 | async-start | bytes 8388608 | tf_op jit(solution)/shard_map/all_to_all | solution.py:245
  202.6 52.0 %all-to-all-start.3 = ((f32[8,64,1024]{2,1,0:T(8,128)}), f32[8,64,1024]{2,1,0:T(8,128)S(1)}, u32[]{:S(2)}, u32[]{:S(2)}) async-start(f32[8,64,1024]{2,1,0:T(8,128)} %bitcast.169), calls=%async_computation.3 | async-start | bytes 4194304 | tf_op jit(solution)/shard_map/all_to_all | solution.py:284
  254.7 52.2 %copy-start.2 = (f32[8,64,1024]{2,1,0:T(8,128)}, f32[8,64,1024]{2,1,0:T(8,128)S(1)}, u32[]{:S(2)}) copy-start(f32[8,64,1024]{2,1,0:T(8,128)S(1)} %all-to-all-done.3.refs_0_) | copy-start | bytes 6291460
  254.7 52.2 %all-to-all-start.2 = ((f32[8,64,1024]{2,1,0:T(8,128)}), f32[8,64,1024]{2,1,0:T(8,128)}, u32[]{:S(2)}, u32[]{:S(2)}) async-start(f32[8,64,1024]{2,1,0:T(8,128)} %bitcast.168), calls=%async_computation.2 | async-start | bytes 4194304 | tf_op jit(solution)/shard_map/all_to_all | solution.py:284
  259.0 46.7 %collective-permute-start.1 = (f32[8,64,1024]{2,1,0:T(8,128)S(1)}, f32[8,64,1024]{2,1,0:T(8,128)}, u32[]{:S(2)}, u32[]{:S(2)}) collective-permute-start(f32[8,64,1024]{2,1,0:T(8,128)S(1)} %all-to-all-done.3.refs_0_), channel_id=1, source_target_pairs={{0,2},{1,3},{2,0},{3,1},{4,6},{5,7},{6,4},{7,5},{8,10},{9,11},{10,... | collective-permute-start | bytes 6291464 | tf_op jit(solution)/shard_map/ppermute | solution.py:49
  306.9 52.4 %all-to-all-start.5 = ((f32[8,64,1024]{2,1,0:T(8,128)}), f32[8,64,1024]{2,1,0:T(8,128)}, u32[]{:S(2)}, u32[]{:S(2)}) async-start(f32[8,64,1024]{2,1,0:T(8,128)} %bitcast.170), calls=%async_computation.5 | async-start | bytes 4194304 | tf_op jit(solution)/shard_map/all_to_all | solution.py:284
  311.8 46.7 %collective-permute-start.3 = (f32[8,64,1024]{2,1,0:T(8,128)}, f32[8,64,1024]{2,1,0:T(8,128)}, u32[]{:S(2)}, u32[]{:S(2)}) collective-permute-start(f32[8,64,1024]{2,1,0:T(8,128)} %all-to-all-done.2.refs_0_), channel_id=1, source_target_pairs={{0,2},{1,3},{2,0},{3,1},{4,6},{5,7},{6,4},{7,5},{8,10},{9,11},{10,... | collective-permute-start | bytes 6291464 | tf_op jit(solution)/shard_map/ppermute | solution.py:49
  359.3 52.3 %all-to-all-start.4 = ((f32[8,64,1024]{2,1,0:T(8,128)}), f32[8,64,1024]{2,1,0:T(8,128)S(1)}, u32[]{:S(2)}, u32[]{:S(2)}) async-start(f32[8,64,1024]{2,1,0:T(8,128)} %bitcast.171), calls=%async_computation.4 | async-start | bytes 4194304 | tf_op jit(solution)/shard_map/all_to_all | solution.py:284
  364.5 47.1 %collective-permute-start.5 = (f32[8,64,1024]{2,1,0:T(8,128)}, f32[8,64,1024]{2,1,0:T(8,128)}, u32[]{:S(2)}, u32[]{:S(2)}) collective-permute-start(f32[8,64,1024]{2,1,0:T(8,128)} %all-to-all-done.5.refs_4_), channel_id=1, source_target_pairs={{0,2},{1,3},{2,0},{3,1},{4,6},{5,7},{6,4},{7,5},{8,10},{9,11},{10,... | collective-permute-start | bytes 6291464 | tf_op jit(solution)/shard_map/ppermute | solution.py:49
  366.1 48.9 %collective-permute-start = (f32[8,64,1024]{2,1,0:T(8,128)}, f32[8,64,1024]{2,1,0:T(8,128)}, u32[]{:S(2)}, u32[]{:S(2)}) collective-permute-start(f32[8,64,1024]{2,1,0:T(8,128)} %all-to-all-done.2.refs_0_), channel_id=1, source_target_pairs={{0,1},{1,0},{2,3},{3,2},{4,5},{5,4},{6,7},{7,6},{8,9},{9,8},{10,11... | collective-permute-start | bytes 6291464 | tf_op jit(solution)/shard_map/ppermute | solution.py:49
  366.1 48.9 %collective-permute-start.2 = (f32[8,64,1024]{2,1,0:T(8,128)}, f32[8,64,1024]{2,1,0:T(8,128)}, u32[]{:S(2)}, u32[]{:S(2)}) collective-permute-start(f32[8,64,1024]{2,1,0:T(8,128)} %collective-permute-done.1.refs_2_), channel_id=1, source_target_pairs={{0,1},{1,0},{2,3},{3,2},{4,5},{5,4},{6,7},{7,6},{8,9},{9,8},{10,11... | collective-permute-start | bytes 6291464 | tf_op jit(solution)/shard_map/ppermute | solution.py:49
  411.6 6.5 %collective-permute-start.4 = (f32[8,64,1024]{2,1,0:T(8,128)S(1)}, f32[8,64,1024]{2,1,0:T(8,128)}, u32[]{:S(2)}, u32[]{:S(2)}) collective-permute-start(f32[8,64,1024]{2,1,0:T(8,128)S(1)} %all-to-all-done.4.refs_4_), channel_id=1, source_target_pairs={{0,1},{1,0},{2,3},{3,2},{4,5},{5,4},{6,7},{7,6},{8,9},{9,8},{10,11... | collective-permute-start | bytes 6291464 | tf_op jit(solution)/shard_map/ppermute | solution.py:49
  411.6 7.5 %collective-permute-start.6 = (f32[8,64,1024]{2,1,0:T(8,128)}, f32[8,64,1024]{2,1,0:T(8,128)}, u32[]{:S(2)}, u32[]{:S(2)}) collective-permute-start(f32[8,64,1024]{2,1,0:T(8,128)} %collective-permute-done.5.refs_6_), channel_id=1, source_target_pairs={{0,1},{1,0},{2,3},{3,2},{4,5},{5,4},{6,7},{7,6},{8,9},{9,8},{10,11... | collective-permute-start | bytes 6291464 | tf_op jit(solution)/shard_map/ppermute | solution.py:49
  413.4 14.3 %collective-permute-start.7 = (f32[8,64,256]{2,1,0:T(8,128)}, f32[8,64,256]{2,1,0:T(8,128)S(1)}, u32[]{:S(2)}, u32[]{:S(2)}) collective-permute-start(f32[8,64,256]{2,1,0:T(8,128)} %slice.225), channel_id=1, source_target_pairs={{0,2},{1,3},{2,0},{3,1},{4,6},{5,7},{6,4},{7,5},{8,10},{9,11},{10,... | collective-permute-start | bytes 1572872 | tf_op jit(solution)/shard_map/ppermute | solution.py:49
  427.8 4.8 collective-permute-start.10
  429.1 3.5 collective-permute-start.8
  429.5 3.9 collective-permute-start.9
  433.4 13.2 %collective-permute-start.15 = (f32[8,64,256]{2,1,0:T(8,128)}, f32[8,64,256]{2,1,0:T(8,128)S(1)}, u32[]{:S(2)}, u32[]{:S(2)}) collective-permute-start(f32[8,64,256]{2,1,0:T(8,128)} %get-tuple-element.53), channel_id=1, source_target_pairs={{0,2},{1,3},{2,0},{3,1},{4,6},{5,7},{6,4},{7,5},{8,10},{9,11},{10,... | collective-permute-start | bytes 1572872 | tf_op jit(solution)/shard_map/ppermute | solution.py:49
  434.2 3.9 collective-permute-start.11
  435.7 3.9 collective-permute-start.12
  436.3 4.8 %collective-permute-start.13 = (f32[64,64]{1,0:T(8,128)S(1)}, f32[64,64]{1,0:T(8,128)S(1)}, u32[]{:S(2)}, u32[]{:S(2)}) collective-permute-start(f32[64,64]{1,0:T(8,128)S(1)} %add_add_fusion.1), channel_id=1, source_target_pairs={{0,12},{4,8},{8,4},{12,0},{16,28},{20,24},{24,20},{28,16},{1,13},{... | collective-permute-start | bytes 49160 | tf_op jit(solution)/shard_map/ppermute | solution.py:208
  441.2 4.9 %collective-permute-start.14 = (f32[64,64]{1,0:T(8,128)S(1)}, f32[64,64]{1,0:T(8,128)S(1)}, u32[]{:S(2)}, u32[]{:S(2)}) collective-permute-start(f32[64,64]{1,0:T(8,128)S(1)} %add_add_fusion), channel_id=1, source_target_pairs={{0,16},{4,20},{8,24},{12,28},{16,0},{20,4},{24,8},{28,12},{1,17},{... | collective-permute-start | bytes 49160 | tf_op jit(solution)/shard_map/ppermute | solution.py:208
  443.8 7.3 %collective-permute-start.16 = (f32[8,64,1024]{2,1,0:T(8,128)}, f32[8,64,1024]{2,1,0:T(8,128)}, u32[]{:S(2)}, u32[]{:S(2)}) collective-permute-start(f32[8,64,1024]{2,1,0:T(8,128)} %copy-done.2), channel_id=1, source_target_pairs={{0,1},{1,0},{2,3},{3,2},{4,5},{5,4},{6,7},{7,6},{8,9},{9,8},{10,11... | collective-permute-start | bytes 6291464 | tf_op jit(solution)/shard_map/ppermute | solution.py:49
  443.9 8.2 %collective-permute-start.18 = (f32[8,64,1024]{2,1,0:T(8,128)}, f32[8,64,1024]{2,1,0:T(8,128)}, u32[]{:S(2)}, u32[]{:S(2)}) collective-permute-start(f32[8,64,1024]{2,1,0:T(8,128)} %collective-permute-done.3.refs_2_), channel_id=1, source_target_pairs={{0,1},{1,0},{2,3},{3,2},{4,5},{5,4},{6,7},{7,6},{8,9},{9,8},{10,11... | collective-permute-start | bytes 6291464 | tf_op jit(solution)/shard_map/ppermute | solution.py:49
  444.4 10.7 %collective-permute-start.17 = (f32[8,64,1024]{2,1,0:T(8,128)}, f32[8,64,1024]{2,1,0:T(8,128)}, u32[]{:S(2)}, u32[]{:S(2)}) collective-permute-start(f32[8,64,1024]{2,1,0:T(8,128)} %all-to-all-done.5.refs_4_), channel_id=1, source_target_pairs={{0,1},{1,0},{2,3},{3,2},{4,5},{5,4},{6,7},{7,6},{8,9},{9,8},{10,11... | collective-permute-start | bytes 6291464 | tf_op jit(solution)/shard_map/ppermute | solution.py:49
  446.0 9.1 %collective-permute-start.19 = (f32[8,64,256]{2,1,0:T(8,128)S(1)}, f32[8,64,256]{2,1,0:T(8,128)}, u32[]{:S(2)}, u32[]{:S(2)}) collective-permute-start(f32[8,64,256]{2,1,0:T(8,128)S(1)} %collective-permute-done.7.refs_6_), channel_id=1, source_target_pairs={{0,1},{1,0},{2,3},{3,2},{4,5},{5,4},{6,7},{7,6},{8,9},{9,8},{10,11... | collective-permute-start | bytes 1572872 | tf_op jit(solution)/shard_map/ppermute | solution.py:49
  446.6 18.1 %collective-permute-start.21 = (f32[8,64,256]{2,1,0:T(8,128)}, f32[8,64,256]{2,1,0:T(8,128)}, u32[]{:S(2)}, u32[]{:S(2)}) collective-permute-start(f32[8,64,256]{2,1,0:T(8,128)} %get-tuple-element.65), channel_id=1, source_target_pairs={{0,2},{1,3},{2,0},{3,1},{4,6},{5,7},{6,4},{7,5},{8,10},{9,11},{10,... | collective-permute-start | bytes 1572872 | tf_op jit(solution)/shard_map/ppermute | solution.py:49
  451.1 20.7 %collective-permute-start.22 = (f32[8,64,256]{2,1,0:T(8,128)}, f32[8,64,256]{2,1,0:T(8,128)S(1)}, u32[]{:S(2)}, u32[]{:S(2)}) collective-permute-start(f32[8,64,256]{2,1,0:T(8,128)} %get-tuple-element.72), channel_id=1, source_target_pairs={{0,2},{1,3},{2,0},{3,1},{4,6},{5,7},{6,4},{7,5},{8,10},{9,11},{10,... | collective-permute-start | bytes 1572872 | tf_op jit(solution)/shard_map/ppermute | solution.py:49
  452.1 3.4 collective-permute-start.20
  471.9 2.6 collective-permute-start.24
  471.9 2.9 collective-permute-start.23
  (22 other events, 309.0 us)
